TPU v7x, 32 devices: a whole 2x2x4 slice. The times are simulated.
32 devices in a mesh: lat: 4 (over y, x), lon: 8 (over z, core).
Axes of the slice: x: 2, y: 2, z: 4, core: 2. Of those that a mesh axis runs over, the one named last changes fastest.
Arguments:
- tokens: bfloat16 [2, 48, 192, 512], P(None, 'lat', 'lon'), may hold values from -6 to 6
- level_ids: int32 [2, 48, 192], P(None, 'lat', 'lon'), may hold values from 0 to 2
- coarse_ids: int32 [2, 24, 96], P(None, 'lat', 'lon'), may hold values from 0 to 2
- first_qkv: bfloat16 [512, 1536], replicated, may hold values from -1.25 to 1.25
- first_out: bfloat16 [512, 512], replicated, may hold values from -0.25 to 0.25
- merge_weight: bfloat16 [2048, 1024], P('lon'), may hold values from -0.125 to 0.125
- second_qkv: bfloat16 [1024, 3072], P('lon'), may hold values from -1.25 to 1.25
- second_out: bfloat16 [1024, 1024], P('lon'), may hold values from -0.1875 to 0.1875
Outputs:
- skip: bfloat16 [2, 48, 192, 512], P(None, 'lat', 'lon')
- coarse: bfloat16 [2, 24, 96, 1024], P(None, 'lat', 'lon')
All inputs are finite; a program needn't handle non-finite values.
Results may differ from a plain program's by a relative error of at most 0.012.
Values may be sent and summed in bfloat16 or wider, within the bound.
No kernel may reach another device: no remote copies, remote signals or barrier semaphores. Data moves between devices by JAX's collectives and lax.ppermute only.
A program may use at most 64 MiB of HBM per device.

v0:
```python
import math

import jax
import jax.numpy as jnp
from jax import lax
from jax.sharding import PartitionSpec as P

HEADS1 = 8
HEADS2 = 16
WIN_LEVELS = 2
WIN_ROWS = 6
WIN_COLS = 12


EPSILON = 1e-05


def from_behind(block, axis, distance):
    devices = range(lax.axis_size(axis))
    route = [((i - distance) % len(devices), i) for i in devices]
    return lax.ppermute(block, axis, route)


def normalized(values):
    widened = values.astype(jnp.float32)
    center = jnp.mean(widened, axis=-1, keepdims=True)
    spread = jnp.mean(jnp.square(widened - center), axis=-1, keepdims=True)
    return ((widened - center) * lax.rsqrt(spread + EPSILON)).astype(jnp.bfloat16)


def window_softmax(queries, keys, values, labels, heads):
    levels, rows, columns, width = queries.shape
    stacks = levels // WIN_LEVELS
    across = columns // WIN_COLS
    head_size = width // heads

    def windows(array):
        shaped = array.reshape(stacks, WIN_LEVELS, rows, across, WIN_COLS, heads, head_size)
        shaped = shaped.transpose(0, 3, 1, 2, 4, 5, 6)
        return shaped.reshape(stacks * across, WIN_LEVELS * rows * WIN_COLS, heads, head_size)

    marks = labels.reshape(stacks, WIN_LEVELS, rows, across, WIN_COLS).transpose(0, 3, 1, 2, 4)
    marks = marks.reshape(stacks * across, WIN_LEVELS * rows * WIN_COLS)
    scores = jnp.einsum(
        "wqhd,wkhd->whqk", windows(queries), windows(keys), preferred_element_type=jnp.float32
    )
    scores = scores / math.sqrt(head_size)
    allowed = marks[:, None, :, None] == marks[:, None, None, :]
    scores = jnp.where(allowed, scores, -1e30)
    highest = jnp.max(scores, axis=-1, keepdims=True)
    expos = jnp.exp(scores - highest)
    weights = (expos / jnp.sum(expos, axis=-1, keepdims=True)).astype(jnp.bfloat16)
    mixed = jnp.einsum(
        "whqk,wkhd->wqhd", weights, windows(values), preferred_element_type=jnp.float32
    )
    mixed = mixed.astype(jnp.bfloat16)
    mixed = mixed.reshape(stacks, across, WIN_LEVELS, rows, WIN_COLS, width).transpose(
        0, 2, 3, 1, 4, 5
    )
    return mixed.reshape(levels, rows, columns, width)


def attend_bands(queries, keys, values, labels, heads):
    levels, rows, columns, width = queries.shape
    bands = rows // WIN_ROWS

    def by_band(array):
        return jnp.moveaxis(array.reshape((levels, bands, WIN_ROWS) + array.shape[2:]), 1, 0)

    def one_band(group):
        return window_softmax(group[0], group[1], group[2], group[3], heads)

    result = lax.map(one_band, (by_band(queries), by_band(keys), by_band(values), by_band(labels)))
    return jnp.moveaxis(result, 0, 1).reshape(levels, rows, columns, width)


def shifted_layer(field, labels, qkv_product, out_product, heads):
    levels, height, breadth, width = field.shape
    half_rows = WIN_ROWS // 2
    half_cols = WIN_COLS // 2
    marks = labels.astype(jnp.bfloat16)
    below = from_behind((field[:, :half_rows], marks[:, :half_rows]), "lat", -1)
    moved = jnp.concatenate([field[:, half_rows:], below[0]], axis=1)
    moved_marks = jnp.concatenate([marks[:, half_rows:], below[1]], axis=1)
    beside = from_behind((moved[:, :, :half_cols], moved_marks[:, :, :half_cols]), "lon", -1)
    moved = jnp.concatenate([moved[:, :, half_cols:], beside[0]], axis=2)
    moved_marks = jnp.concatenate([moved_marks[:, :, half_cols:], beside[1]], axis=2)
    packed = qkv_product(normalized(moved).reshape(-1, width)).astype(jnp.bfloat16)
    packed = packed.reshape(levels, height, breadth, 3 * width)
    mixed = attend_bands(
        packed[..., :width],
        packed[..., width : 2 * width],
        packed[..., 2 * width :],
        moved_marks.astype(jnp.int32),
        heads,
    )
    update = out_product(mixed.reshape(-1, width)).reshape(field.shape)
    result = (moved.astype(jnp.float32) + update).astype(jnp.bfloat16)
    returned = from_behind(result[:, :, breadth - half_cols :], "lon", 1)
    result = jnp.concatenate([returned, result[:, :, : breadth - half_cols]], axis=2)
    returned = from_behind(result[:, height - half_rows :], "lat", 1)
    return jnp.concatenate([returned, result[:, : height - half_rows]], axis=1)


def edge_labels(ids):
    height = ids.shape[1]
    global_rows = lax.axis_index("lat") * height + jnp.arange(height)
    edge = (global_rows < WIN_ROWS // 2).astype(jnp.int32)
    return ids * 2 + edge[None, :, None]


def merge_patches(field):
    levels, height, breadth, width = field.shape
    shaped = field.reshape(levels, height // 2, 2, breadth // 2, 2, width).transpose(
        0, 1, 3, 4, 2, 5
    )
    return shaped.reshape(levels, height // 2, breadth // 2, 4 * width)


def add_rows(left, piece):
    return jnp.dot(left, piece, preferred_element_type=jnp.float32)


def per_device(
    tokens, level_ids, coarse_ids, first_qkv, first_out, merge_weight, second_qkv, second_out
):

    def second_qkv_product(left):
        return add_rows(left, lax.all_gather(second_qkv, "lon", axis=0, tiled=True))

    def second_out_product(left):
        return add_rows(left, lax.all_gather(second_out, "lon", axis=0, tiled=True))

    def first_qkv_product(left):
        return jnp.dot(left, first_qkv, preferred_element_type=jnp.float32)

    def first_out_product(left):
        return jnp.dot(left, first_out, preferred_element_type=jnp.float32)

    skip = shifted_layer(
        tokens, edge_labels(level_ids), first_qkv_product, first_out_product, HEADS1
    )
    joined = merge_patches(skip)
    levels, height, breadth, width = joined.shape
    left = normalized(joined).reshape(-1, width)
    merged = add_rows(left, lax.all_gather(merge_weight, "lon", axis=0, tiled=True)).astype(
        jnp.bfloat16
    )
    merged = merged.reshape(levels, height, breadth, merge_weight.shape[1])
    coarse = shifted_layer(
        merged, edge_labels(coarse_ids), second_qkv_product, second_out_product, HEADS2
    )
    return (skip, coarse)


def solution(mesh):
    placed = (
        P(None, "lat", "lon", None),
        P(None, "lat", "lon"),
        P(None, "lat", "lon"),
        P(),
        P(),
        P("lon", None),
        P("lon", None),
        P("lon", None),
    )
    return jax.shard_map(
        per_device,
        mesh=mesh,
        in_specs=placed,
        out_specs=(P(None, "lat", "lon", None), P(None, "lat", "lon", None)),
        check_vma=False,
    )
```

profile of v0, /device:TPU:0, one launch (start us, length us, event | category | flops | bytes accessed | tf_op | source)
XLA Modules:
  0.0 183.6 jit_solution(6962086006332394582)
XLA Ops:
  8.8 3.9 %collective-permute-start = (bf16[2,3,24,512]{3,2,1,0:T(8,128)(2,1)S(1)}, bf16[2,3,24,512]{3,2,1,0:T(8,128)(2,1)S(1)}, u32[]{:S(2)}, u32[]{:S(2)}) collective-permute-start(bf16[2,3,24,512]{3,2,1,0:T(8,128)(2,1)S(1)} %slice.91), channel_id=1, source_target_pairs={{8,0},{16,8},{24,16},{0,24},{9,1},{17,9},{25,17},{1,25},{10,2},{18... | collective-permute-start | bytes 442376 | tf_op jit(solution)/shard_map/ppermute | solution.py:21
  13.5 3.0 %collective-permute-done.2 = bf16[2,3,24]{2,0,1:T(2,128)(2,1)S(1)} collective-permute-done((bf16[2,3,24]{2,0,1:T(2,128)(2,1)S(1)}, bf16[2,3,24]{2,0,1:T(2,128)(2,1)S(1)}, u32[]{:S(2)}, u32[]{:S(2)}) %collective-permute-start.2) | collective-permute-done | bytes 320 | tf_op jit(solution)/shard_map/ppermute | solution.py:21
  16.5 2.0 %collective-permute-start.3 = (bf16[2,12,6]{2,0,1:T(2,128)(2,1)S(1)}, bf16[2,12,6]{2,0,1:T(2,128)(2,1)S(1)}, u32[]{:S(2)}, u32[]{:S(2)}) collective-permute-start(bf16[2,12,6]{2,0,1:T(2,128)(2,1)S(1)} %pad_maximum_fusion.7), channel_id=1, source_target_pairs={{1,0},{2,1},{3,2},{4,3},{5,4},{6,5},{7,6},{0,7},{9,8},{10,9},{11,1... | collective-permute-start | bytes 872 | tf_op jit(solution)/shard_map/ppermute | solution.py:21
  18.6 1.8 collective-permute-start.1
  20.7 6.8 %collective-permute-done.1 = bf16[2,12,6,512]{3,2,1,0:T(8,128)(2,1)S(1)} collective-permute-done((bf16[2,12,6,512]{3,2,1,0:T(8,128)(2,1)S(1)}, bf16[2,12,6,512]{3,2,1,0:T(8,128)(2,1)S(1)}, u32[]{:S(2)}, u32[]{:S(2)}) %collective-permute-start.1) | collective-permute-done | bytes 147488 | tf_op jit(solution)/shard_map/ppermute | solution.py:21
  28.6 1.1 convolution_convert_fusion.2
  29.7 1.0 fusion.75
  30.7 21.8 %while.2 = (s32[]{:T(128)}, bf16[2,2,6,24,512]{4,3,2,0,1:T(8,128)(2,1)}, bf16[2,2,6,24,512]{4,3,2,0,1:T(8,128)(2,1)}, s32[2,2,6,24]{3,1,2,0:T(2,128)S(1)}, bf16[...) while((s32[]{:T(128)}, bf16[2,2,6,24,512]{4,3,2,0,1:T(8,128)(2,1)}, ...), condition=%wide.region_5.6_spmd, body=%wide.region_2.5_spmd.sunk | while | flops 87114384 | bytes 23410532 | solution.py:73
  30.7 0.8 copy-done.2
  32.4 0.9 copy.116
  33.6 3.6 %fusion.99 = (f32[2,8,144]{2,1,0:T(8,128)S(1)}, f32[2,8,144,144]{2,3,1,0:T(8,128)}) fusion(pred[2,144,144]{1,2,0:T(8,128)(4,1)S(1)} %broadcast_compare_fusion.3, bf16[2,144,8,64]{3,2,1,0:T(8,128)(2,1)S(1)} %bitcast.117, bf16[2,144,8,64]{3,2,1,0:T(8,128)(2,1)} %bitcast.118), kind=kOutput, calls=%fused_computation.98.clone.1 | convolution fusion | flops 43794576 | bytes 1967616 | tf_op jit(solution)/shard_map/while/body/eval_jaxpr/sub | solution.py:51
  37.5 2.1 %fusion.100 = bf16[2,144,8,64]{1,3,2,0:T(8,128)(2,1)S(1)} fusion(f32[2,8,144,144]{2,3,1,0:T(8,128)} %get-tuple-element.140, f32[2,8,144]{2,1,0:T(8,128)S(1)} %get-tuple-element.141, bf16[2,144,8,64]{3,2,1,0:T(8,128)(2,1)S(1)} %bitcast.119), kind=kOutput, calls=%fused_computation.6.clone.1 | convolution fusion | flops 43278336 | bytes 1926144 | tf_op jit(solution)/shard_map/while/body/eval_jaxpr/whqk,wkhd->wqhd/dot_general | solution.py:53
  40.8 0.8 copy_dynamic-update-slice_fusion.2
  41.6 0.8 copy-done.2
  43.2 0.9 copy.116
  44.5 3.6 %fusion.99 = (f32[2,8,144]{2,1,0:T(8,128)S(1)}, f32[2,8,144,144]{2,3,1,0:T(8,128)}) fusion(pred[2,144,144]{1,2,0:T(8,128)(4,1)S(1)} %broadcast_compare_fusion.3, bf16[2,144,8,64]{3,2,1,0:T(8,128)(2,1)S(1)} %bitcast.117, bf16[2,144,8,64]{3,2,1,0:T(8,128)(2,1)} %bitcast.118), kind=kOutput, calls=%fused_computation.98.clone.1 | convolution fusion | flops 43794576 | bytes 1967616 | tf_op jit(solution)/shard_map/while/body/eval_jaxpr/sub | solution.py:51
  48.4 2.1 %fusion.100 = bf16[2,144,8,64]{1,3,2,0:T(8,128)(2,1)S(1)} fusion(f32[2,8,144,144]{2,3,1,0:T(8,128)} %get-tuple-element.140, f32[2,8,144]{2,1,0:T(8,128)S(1)} %get-tuple-element.141, bf16[2,144,8,64]{3,2,1,0:T(8,128)(2,1)S(1)} %bitcast.119), kind=kOutput, calls=%fused_computation.6.clone.1 | convolution fusion | flops 43278336 | bytes 1926144 | tf_op jit(solution)/shard_map/while/body/eval_jaxpr/whqk,wkhd->wqhd/dot_general | solution.py:53
  52.5 1.9 %fusion.28 = bf16[2,12,24,512]{3,2,1,0:T(8,128)(2,1)S(1)} fusion(bf16[2,12,24,512]{3,2,1,0:T(8,128)(2,1)} %bitcast.130, bf16[512,512]{1,0:T(8,128)(2,1)} %param.14, bf16[2,12,6,512]{3,2,1,0:T(8,128)(2,1)S(1)} %collective-permute-done.1, bf16[2,12,18,512]{3,2,1,0:T(8,128)(2,1)} %copy-done.1), kind=kOutput, calls=%fused_computation.32 | convolution fusion | flops 303759360 | bytes 2293760 | tf_op jit(solution)/shard_map/dot_general | solution.py:138
  54.6 7.1 %collective-permute-done.4 = bf16[2,12,6,512]{3,2,1,0:T(8,128)(2,1)S(1)} collective-permute-done((bf16[2,12,6,512]{3,2,1,0:T(8,128)(2,1)S(1)}, bf16[2,12,6,512]{3,2,1,0:T(8,128)(2,1)S(1)}, u32[]{:S(2)}, u32[]{:S(2)}) %collective-permute-start.4) | collective-permute-done | bytes 147488 | tf_op jit(solution)/shard_map/ppermute | solution.py:21
  61.7 1.8 collective-permute-start.5
  63.5 1.2 collective-permute-start.8
  64.8 3.0 %collective-permute-done.5 = bf16[2,3,24,512]{3,2,1,0:T(8,128)(2,1)S(1)} collective-permute-done((bf16[2,3,24,512]{3,2,1,0:T(8,128)(2,1)S(1)}, bf16[2,3,24,512]{3,2,1,0:T(8,128)(2,1)S(1)}, u32[]{:S(2)}, u32[]{:S(2)}) %collective-permute-start.5) | collective-permute-done | bytes 147488 | tf_op jit(solution)/shard_map/ppermute | solution.py:21
  68.7 1.1 fusion.69
  69.8 1.2 multiply_reduce_fusion
  71.0 2.0 %copy.99 = f32[2,6,2,12,2,512]{5,2,4,3,1,0:T(2,128)} copy(f32[2,6,2,12,2,512]{5,4,3,2,1,0:T(2,128)S(1)} %reshape.297) | data formatting | bytes 2359296 | tf_op jit(solution)/shard_map/convert_element_type | solution.py:25
  73.2 2.3 %reshape.293 = f32[144,2048]{1,0:T(8,128)S(1)} reshape(f32[2,6,12,2,2,512]{5,4,3,2,1,0:T(2,128)} %bitcast.123) | data formatting | bytes 2359296 | tf_op jit(solution)/shard_map/convert_element_type | solution.py:25
  75.5 3.0 %convolution_convert_fusion.4 = bf16[144,1024]{1,0:T(8,128)(2,1)S(1)} fusion(bf16[2048,1024]{1,0:T(8,128)(2,1)} %all-gather.4.cloned.1.call-done, f32[144,2048]{1,0:T(8,128)S(1)} %reshape.293, f32[144]{0:T(256)S(1)} %rsqrt.36, f32[144]{0:T(256)S(1)} %div.56), kind=kOutput, calls=%fused_computation.37 | convolution fusion | flops 605011968 | bytes 5670016 | tf_op jit(solution)/shard_map/dot_general | solution.py:121
  78.7 2.1 %collective-permute-start.6 = (bf16[2,3,12,1024]{3,2,1,0:T(8,128)(2,1)S(1)}, bf16[2,3,12,1024]{3,2,1,0:T(8,128)(2,1)S(1)}, u32[]{:S(2)}, u32[]{:S(2)}) collective-permute-start(bf16[2,3,12,1024]{3,2,1,0:T(8,128)(2,1)S(1)} %get-tuple-element.90), channel_id=1, source_target_pairs={{8,0},{16,8},{24,16},{0,24},{9,1},{17,9},{25,17},{1,25},{10,2},{18... | collective-permute-start | bytes 442376 | tf_op jit(solution)/shard_map/ppermute | solution.py:21
  80.8 1.3 collective-permute-done.9
  82.3 2.1 %collective-permute-done.6 = bf16[2,3,12,1024]{3,2,1,0:T(8,128)(2,1)S(1)} collective-permute-done((bf16[2,3,12,1024]{3,2,1,0:T(8,128)(2,1)S(1)}, bf16[2,3,12,1024]{3,2,1,0:T(8,128)(2,1)S(1)}, u32[]{:S(2)}, u32[]{:S(2)}) %collective-permute-start.6) | collective-permute-done | bytes 147488 | tf_op jit(solution)/shard_map/ppermute | solution.py:21
  84.5 1.9 %collective-permute-start.7 = (bf16[2,6,6,1024]{3,2,1,0:T(8,128)(2,1)S(1)}, bf16[2,6,6,1024]{3,2,1,0:T(8,128)(2,1)S(1)}, u32[]{:S(2)}, u32[]{:S(2)}) collective-permute-start(bf16[2,6,6,1024]{3,2,1,0:T(8,128)(2,1)S(1)} %get-tuple-element.88), channel_id=1, source_target_pairs={{1,0},{2,1},{3,2},{4,3},{5,4},{6,5},{7,6},{0,7},{9,8},{10,9},{11,1... | collective-permute-start | bytes 442376 | tf_op jit(solution)/shard_map/ppermute | solution.py:21
  87.1 6.7 %collective-permute-done.7 = bf16[2,6,6,1024]{3,2,1,0:T(8,128)(2,1)S(1)} collective-permute-done((bf16[2,6,6,1024]{3,2,1,0:T(8,128)(2,1)S(1)}, bf16[2,6,6,1024]{3,2,1,0:T(8,128)(2,1)S(1)}, u32[]{:S(2)}, u32[]{:S(2)}) %collective-permute-start.7) | collective-permute-done | bytes 147488 | tf_op jit(solution)/shard_map/ppermute | solution.py:21
  94.7 35.9 %all-gather.6.cloned.1.call-done = bf16[1024,3072]{1,0:T(8,128)(2,1)} async-done(((bf16[128,3072]{1,0:T(8,128)(2,1)}), bf16[1024,3072]{1,0:T(8,128)(2,1)}) %all-gather.6.cloned.1.call-update) | async-done | bytes 6291472 | tf_op jit(solution)/shard_map/all_gather | solution.py:129
  130.6 4.9 %convolution_convert_fusion.1 = bf16[144,3072]{1,0:T(8,128)(2,1)} fusion(bf16[1024,3072]{1,0:T(8,128)(2,1)} %all-gather.6.cloned.1.call-done, f32[144,1024]{1,0:T(8,128)S(1)} %reshape.294, f32[144]{0:T(256)S(1)} %rsqrt.38, f32[144]{0:T(256)S(1)} %div.59), kind=kOutput, calls=%fused_computation.23 | convolution fusion | flops 906854400 | bytes 7767168 | tf_op jit(solution)/shard_map/dot_general | solution.py:121
  135.5 1.3 reshape.288
  136.8 1.0 fusion.76
  137.8 1.5 reshape.290
  139.3 1.2 reshape.291
  140.5 1.2 reshape.289
  141.7 3.6 %fusion.80 = (f32[16,144]{1,0:T(8,128)S(1)}, f32[16,144,144]{1,2,0:T(8,128)}) fusion(pred[144,144]{0,1:T(8,128)(4,1)S(1)} %copy-done.13, bf16[144,16,64]{2,1,0:T(8,128)(2,1)} %reshape.291, bf16[144,16,64]{2,1,0:T(8,128)(2,1)S(1)} %reshape.290), kind=kOutput, calls=%fused_computation.104 | convolution fusion | flops 43794576 | bytes 1946880 | tf_op jit(solution)/shard_map/while/body/eval_jaxpr/sub | solution.py:51
  145.3 2.9 %fusion.35 = bf16[1,144,16,64]{1,3,2,0:T(8,128)(2,1)} fusion(f32[16,144,144]{1,2,0:T(8,128)} %get-tuple-element.96, f32[16,144]{1,0:T(8,128)S(1)} %get-tuple-element.95, bf16[144,16,64]{2,1,0:T(8,128)(2,1)S(1)} %copy-done.12), kind=kOutput, calls=%fused_computation.36 | convolution fusion | flops 43278336 | bytes 1926144 | tf_op jit(solution)/shard_map/while/body/eval_jaxpr/whqk,wkhd->wqhd/dot_general | solution.py:53
  148.3 1.6 copy.38
  150.3 9.7 %all-gather.8.cloned.1.call-done = bf16[1024,1024]{1,0:T(8,128)(2,1)} async-done(((bf16[128,1024]{1,0:T(8,128)(2,1)}), bf16[1024,1024]{1,0:T(8,128)(2,1)}) %all-gather.8.cloned.1.call-update) | async-done | bytes 2097168 | tf_op jit(solution)/shard_map/all_gather | solution.py:132
  160.0 2.2 %fusion.32 = bf16[2,6,12,1024]{3,2,1,0:T(8,128)(2,1)S(1)} fusion(bf16[2,6,12,1024]{3,2,1,0:T(8,128)(2,1)S(1)} %dot_general.40, bf16[1024,1024]{1,0:T(8,128)(2,1)} %all-gather.8.cloned.1.call-done, bf16[2,6,6,1024]{3,2,1,0:T(8,128)(2,1)S(1)} %copy-done.9, bf16[2,6,6,1024]{3,2,1,0:T(8,128)(2,1)S(1)} %get-tuple-element.87), kind=kOutput, calls=%fused_computation.35 | convolution fusion | flops 302874624 | bytes 2981888 | tf_op jit(solution)/shard_map/dot_general | solution.py:121
  162.6 6.7 %collective-permute-done.10 = bf16[2,6,6,1024]{3,2,1,0:T(8,128)(2,1)S(1)} collective-permute-done((bf16[2,6,6,1024]{3,2,1,0:T(8,128)(2,1)S(1)}, bf16[2,6,6,1024]{3,2,1,0:T(8,128)(2,1)S(1)}, u32[]{:S(2)}, u32[]{:S(2)}) %collective-permute-start.10) | collective-permute-done | bytes 147488 | tf_op jit(solution)/shard_map/ppermute | solution.py:21
  169.3 1.5 collective-permute-start.11
  170.8 5.1 %collective-permute-done.11 = bf16[2,3,12,1024]{3,2,1,0:T(8,128)(2,1)S(1)} collective-permute-done((bf16[2,3,12,1024]{3,2,1,0:T(8,128)(2,1)S(1)}, bf16[2,3,12,1024]{3,2,1,0:T(8,128)(2,1)S(1)}, u32[]{:S(2)}, u32[]{:S(2)}) %collective-permute-start.11) | collective-permute-done | bytes 147488 | tf_op jit(solution)/shard_map/ppermute | solution.py:21
  176.0 1.0 copy.39
  (135 shorter events, 14.2 us)
Async XLA Ops:
  7.2 21.4 %copy-start = (bf16[512,1536]{1,0:T(8,128)(2,1)S(1)}, bf16[512,1536]{1,0:T(8,128)(2,1)}, u32[]{:S(2)}) copy-start(bf16[512,1536]{1,0:T(8,128)(2,1)} %param.13) | copy-start | bytes 4718596
  7.2 1.6 copy-start.11
  7.2 5.5 %copy-start.14 = (s32[2,12,24]{2,0,1:T(2,128)S(1)}, s32[2,12,24]{2,0,1:T(2,128)}, u32[]{:S(2)}) copy-start(s32[2,12,24]{2,0,1:T(2,128)} %param.11) | copy-start | bytes 6916
  7.2 68.3 %all-gather.4.cloned.1.call-start = ((), (), s32[]{:S(2)}) async-start(), calls=%async_computation | async-start | bytes 4718592 | tf_op jit(solution)/shard_map/all_gather | solution.py:146
  7.9 122.7 %all-gather.6.cloned.1.call-start = ((), (), s32[]{:S(2)}) async-start(), calls=%async_computation.1 | async-start | bytes 7077888 | tf_op jit(solution)/shard_map/all_gather | solution.py:129
  8.7 151.3 %all-gather.8.cloned.1.call-start = ((), (), s32[]{:S(2)}) async-start(), calls=%async_computation.2 | async-start | bytes 2359296 | tf_op jit(solution)/shard_map/all_gather | solution.py:132
  8.8 9.8 %collective-permute-start = (bf16[2,3,24,512]{3,2,1,0:T(8,128)(2,1)S(1)}, bf16[2,3,24,512]{3,2,1,0:T(8,128)(2,1)S(1)}, u32[]{:S(2)}, u32[]{:S(2)}) collective-permute-start(bf16[2,3,24,512]{3,2,1,0:T(8,128)(2,1)S(1)} %slice.91), channel_id=1, source_target_pairs={{8,0},{16,8},{24,16},{0,24},{9,1},{17,9},{25,17},{1,25},{10,2},{18... | collective-permute-start | bytes 442376 | tf_op jit(solution)/shard_map/ppermute | solution.py:21
  12.8 3.6 %collective-permute-start.2 = (bf16[2,3,24]{2,0,1:T(2,128)(2,1)S(1)}, bf16[2,3,24]{2,0,1:T(2,128)(2,1)S(1)}, u32[]{:S(2)}, u32[]{:S(2)}) collective-permute-start(bf16[2,3,24]{2,0,1:T(2,128)(2,1)S(1)} %slice.124), channel_id=1, source_target_pairs={{8,0},{16,8},{24,16},{0,24},{9,1},{17,9},{25,17},{1,25},{10,2},{18... | collective-permute-start | bytes 872 | tf_op jit(solution)/shard_map/ppermute | solution.py:21
  16.5 3.9 %collective-permute-start.3 = (bf16[2,12,6]{2,0,1:T(2,128)(2,1)S(1)}, bf16[2,12,6]{2,0,1:T(2,128)(2,1)S(1)}, u32[]{:S(2)}, u32[]{:S(2)}) collective-permute-start(bf16[2,12,6]{2,0,1:T(2,128)(2,1)S(1)} %pad_maximum_fusion.7), channel_id=1, source_target_pairs={{1,0},{2,1},{3,2},{4,3},{5,4},{6,5},{7,6},{0,7},{9,8},{10,9},{11,1... | collective-permute-start | bytes 872 | tf_op jit(solution)/shard_map/ppermute | solution.py:21
  18.6 8.9 %collective-permute-start.1 = (bf16[2,12,6,512]{3,2,1,0:T(8,128)(2,1)S(1)}, bf16[2,12,6,512]{3,2,1,0:T(8,128)(2,1)S(1)}, u32[]{:S(2)}, u32[]{:S(2)}) collective-permute-start(bf16[2,12,6,512]{3,2,1,0:T(8,128)(2,1)S(1)} %pad_maximum_fusion.5), channel_id=1, source_target_pairs={{1,0},{2,1},{3,2},{4,3},{5,4},{6,5},{7,6},{0,7},{9,8},{10,9},{11,1... | collective-permute-start | bytes 442376 | tf_op jit(solution)/shard_map/ppermute | solution.py:21
  20.6 7.9 %copy-start.1 = (bf16[2,12,18,512]{3,2,1,0:T(8,128)(2,1)}, bf16[2,12,18,512]{3,2,1,0:T(8,128)(2,1)S(1)}, u32[]{:S(2)}) copy-start(bf16[2,12,18,512]{3,2,1,0:T(8,128)(2,1)S(1)} %slice_maximum_fusion) | copy-start | bytes 1327108
  30.7 0.8 copy-start.2
  30.7 1.0 copy-start.4
  33.6 3.6 %copy-start.6 = (bf16[2,2,6,24,512]{4,3,2,0,1:T(8,128)(2,1)S(1)}, bf16[2,2,6,24,512]{4,3,2,0,1:T(8,128)(2,1)}, u32[]{:S(2)}) copy-start(bf16[2,2,6,24,512]{4,3,2,0,1:T(8,128)(2,1)} %get-tuple-element.158) | copy-start | bytes 1769476 | tf_op jit(solution)/shard_map/while
  40.1 1.4 copy-start.3
  40.4 1.1 copy-start.5
  41.5 0.8 copy-start.2
  41.6 1.0 copy-start.4
  44.4 3.6 %copy-start.6 = (bf16[2,2,6,24,512]{4,3,2,0,1:T(8,128)(2,1)S(1)}, bf16[2,2,6,24,512]{4,3,2,0,1:T(8,128)(2,1)}, u32[]{:S(2)}) copy-start(bf16[2,2,6,24,512]{4,3,2,0,1:T(8,128)(2,1)} %get-tuple-element.158) | copy-start | bytes 1769476 | tf_op jit(solution)/shard_map/while
  51.0 1.4 copy-start.3
  51.3 1.1 copy-start.5
  52.5 2.0 %copy-start.15 = (s32[2,6,12]{2,0,1:T(2,128)S(1)}, s32[2,6,12]{2,0,1:T(2,128)}, u32[]{:S(2)}) copy-start(s32[2,6,12]{2,0,1:T(2,128)} %param.12) | copy-start | bytes 1732
  54.4 7.2 %collective-permute-start.4 = (bf16[2,12,6,512]{3,2,1,0:T(8,128)(2,1)S(1)}, bf16[2,12,6,512]{3,2,1,0:T(8,128)(2,1)S(1)}, u32[]{:S(2)}, u32[]{:S(2)}) collective-permute-start(bf16[2,12,6,512]{3,2,1,0:T(8,128)(2,1)S(1)} %slice.129), channel_id=1, source_target_pairs={{7,0},{0,1},{1,2},{2,3},{3,4},{4,5},{5,6},{6,7},{15,8},{8,9},{9,10... | collective-permute-start | bytes 442376 | tf_op jit(solution)/shard_map/ppermute | solution.py:21
  61.7 6.1 %collective-permute-start.5 = (bf16[2,3,24,512]{3,2,1,0:T(8,128)(2,1)S(1)}, bf16[2,3,24,512]{3,2,1,0:T(8,128)(2,1)S(1)}, u32[]{:S(2)}, u32[]{:S(2)}) collective-permute-start(bf16[2,3,24,512]{3,2,1,0:T(8,128)(2,1)S(1)} %pad_maximum_fusion.6), channel_id=1, source_target_pairs={{24,0},{0,8},{8,16},{16,24},{25,1},{1,9},{9,17},{17,25},{26,2},{2,... | collective-permute-start | bytes 442376 | tf_op jit(solution)/shard_map/ppermute | solution.py:21
  63.5 17.2 %collective-permute-start.8 = (bf16[2,3,12]{2,0,1:T(2,128)(2,1)S(1)}, bf16[2,3,12]{2,0,1:T(2,128)(2,1)S(1)}, u32[]{:S(2)}, u32[]{:S(2)}) collective-permute-start(bf16[2,3,12]{2,0,1:T(2,128)(2,1)S(1)} %get-tuple-element.94), channel_id=1, source_target_pairs={{8,0},{16,8},{24,16},{0,24},{9,1},{17,9},{25,17},{1,25},{10,2},{18... | collective-permute-start | bytes 440 | tf_op jit(solution)/shard_map/ppermute | solution.py:21
  68.0 1.8 %copy-start.7 = (bf16[2,12,24,512]{3,2,1,0:T(8,128)(2,1)}, bf16[2,12,24,512]{3,2,1,0:T(8,128)(2,1)S(1)}, u32[]{:S(2)}) copy-start(bf16[2,12,24,512]{3,2,1,0:T(8,128)(2,1)S(1)} %fusion.41) | copy-start | bytes 1769476
  78.7 5.7 %collective-permute-start.6 = (bf16[2,3,12,1024]{3,2,1,0:T(8,128)(2,1)S(1)}, bf16[2,3,12,1024]{3,2,1,0:T(8,128)(2,1)S(1)}, u32[]{:S(2)}, u32[]{:S(2)}) collective-permute-start(bf16[2,3,12,1024]{3,2,1,0:T(8,128)(2,1)S(1)} %get-tuple-element.90), channel_id=1, source_target_pairs={{8,0},{16,8},{24,16},{0,24},{9,1},{17,9},{25,17},{1,25},{10,2},{18... | collective-permute-start | bytes 442376 | tf_op jit(solution)/shard_map/ppermute | solution.py:21
  80.8 1.3 collective-permute-start.9
  84.5 9.2 %collective-permute-start.7 = (bf16[2,6,6,1024]{3,2,1,0:T(8,128)(2,1)S(1)}, bf16[2,6,6,1024]{3,2,1,0:T(8,128)(2,1)S(1)}, u32[]{:S(2)}, u32[]{:S(2)}) collective-permute-start(bf16[2,6,6,1024]{3,2,1,0:T(8,128)(2,1)S(1)} %get-tuple-element.88), channel_id=1, source_target_pairs={{1,0},{2,1},{3,2},{4,3},{5,4},{6,5},{7,6},{0,7},{9,8},{10,9},{11,1... | collective-permute-start | bytes 442376 | tf_op jit(solution)/shard_map/ppermute | solution.py:21
  93.7 0.9 copy-start.8
  137.8 1.5 copy-start.10
  139.3 2.5 %copy-start.13 = (pred[144,144]{0,1:T(8,128)(4,1)S(1)}, pred[144,144]{0,1:T(8,128)(4,1)}, u32[]{:S(2)}) copy-start(pred[144,144]{0,1:T(8,128)(4,1)} %broadcast_compare_fusion.1) | copy-start | bytes 62212
  141.7 3.6 %copy-start.12 = (bf16[144,16,64]{2,1,0:T(8,128)(2,1)S(1)}, bf16[144,16,64]{2,1,0:T(8,128)(2,1)}, u32[]{:S(2)}) copy-start(bf16[144,16,64]{2,1,0:T(8,128)(2,1)} %reshape.289) | copy-start | bytes 884740
  148.3 11.8 %copy-start.9 = (bf16[2,6,6,1024]{3,2,1,0:T(8,128)(2,1)S(1)}, bf16[2,6,6,1024]{3,2,1,0:T(8,128)(2,1)}, u32[]{:S(2)}) copy-start(bf16[2,6,6,1024]{3,2,1,0:T(8,128)(2,1)} %copy-done.8) | copy-start | bytes 442372
  162.3 6.9 %collective-permute-start.10 = (bf16[2,6,6,1024]{3,2,1,0:T(8,128)(2,1)S(1)}, bf16[2,6,6,1024]{3,2,1,0:T(8,128)(2,1)S(1)}, u32[]{:S(2)}, u32[]{:S(2)}) collective-permute-start(bf16[2,6,6,1024]{3,2,1,0:T(8,128)(2,1)S(1)} %get-tuple-element.85), channel_id=1, source_target_pairs={{7,0},{0,1},{1,2},{2,3},{3,4},{4,5},{5,6},{6,7},{15,8},{8,9},{9,10... | collective-permute-start | bytes 442376 | tf_op jit(solution)/shard_map/ppermute | solution.py:21
  169.3 6.6 %collective-permute-start.11 = (bf16[2,3,12,1024]{3,2,1,0:T(8,128)(2,1)S(1)}, bf16[2,3,12,1024]{3,2,1,0:T(8,128)(2,1)S(1)}, u32[]{:S(2)}, u32[]{:S(2)}) collective-permute-start(bf16[2,3,12,1024]{3,2,1,0:T(8,128)(2,1)S(1)} %fusion.52), channel_id=1, source_target_pairs={{24,0},{0,8},{8,16},{16,24},{25,1},{1,9},{9,17},{17,25},{26,2},{2,... | collective-permute-start | bytes 442376 | tf_op jit(solution)/shard_map/ppermute | solution.py:21
Sparse Core Ops, SparseCore 0:
  9.6 49.8 all-gather.3
  61.2 69.3 all-gather.5
  132.2 27.7 all-gather.7
where the time goes:
time: 184 us
  waiting for transfers between devices  88.8 us (48%)
  matrix products  30.9 us (17%)
  local copies, waits for them, and re-layouts  26.3 us (14%)
  starting transfers between devices  17.3 us (9%)
  between operations  14.2 us (8%)
  other arithmetic  5.87 us (3%)
    ppermute x12, waiting for transfers between devices, from_behind(): return lax.ppermute(block, axis, route)  41.7 us
    all_gather x1, waiting for transfers between devices, second_qkv_product(): return add_rows(left, lax.all_gather(second_qkv, 'lon', axis=0, tiled=True))  35.9 us
    ppermute x12, starting transfers between devices, from_behind(): return lax.ppermute(block, axis, route)  17.2 us
    sub x3, matrix products, window_softmax(): expos = jnp.exp(scores - highest)  10.7 us
    dot_general x3, matrix products, add_rows(): return jnp.dot(left, piece, preferred_element_type=jnp.float32)  10.1 us
    all_gather x1, waiting for transfers between devices, second_out_product(): return add_rows(left, lax.all_gather(second_out, 'lon', axis=0, tiled=True))  9.71 us
    dot_general x3, matrix products, window_softmax(): jnp.einsum('whqk,wkhd->wqhd', weights, windows(values), preferred_element...  7.09 us
    convert_element_type x3, local copies, waits for them, and re-layouts, normalized(): widened = values.astype(jnp.float32)  5.03 us
  transfers between devices with their start and end apart: 15, of which 11 were waited for; matrix products, arithmetic and copies ran while one was open for 31% of the time, Pallas kernels for 0%

commit v1 on v0

--- a/solution.py
+++ b/solution.py
@@ -121,12 +121,53 @@
     return jnp.dot(left, piece, preferred_element_type=jnp.float32)
 
 
+def exchange(block, axis, mask):
+    return lax.ppermute(block, axis, [(i, i ^ mask) for i in range(lax.axis_size(axis))])
+
+
+def spread(shard):
+    ranks, rows, columns = lax.axis_size("lon"), shard.shape[0], shard.shape[1]
+    stops = ranks // 2
+    quarter = columns // 4
+    corner = lax.axis_index("lat") % 4
+    mine = lax.dynamic_slice(shard, (0, corner * quarter), (rows, quarter))
+    far = [
+        lax.ppermute(mine, "lon", [(i, (i + 2 * d) % ranks) for i in range(ranks)])
+        for d in range(1, stops)
+    ]
+    near = jnp.concatenate(far, axis=0)
+    half = near.shape[0] // 2
+    first = exchange(near, "lat", 1)
+    second = exchange(near, "lat", 2)
+    third = jnp.concatenate([exchange(first[:half], "lat", 2), exchange(second[half:], "lat", 1)], axis=0)
+    whole = jnp.zeros((stops * rows, columns), shard.dtype)
+    whole = lax.dynamic_update_slice(whole, shard, (0, 0))
+    for mask, part in enumerate((near, first, second, third)):
+        whole = lax.dynamic_update_slice(whole, part, (rows, (corner ^ mask) * quarter))
+    return jnp.concatenate([whole, exchange(whole, "lon", 1)], axis=0)
+
+
+def reordered(left, rows):
+    ranks = lax.axis_size("lon")
+    stops = ranks // 2
+    me = lax.axis_index("lon")
+    pieces = [
+        lax.dynamic_slice(left, (0, (((me // 2 - d) % stops) * 2 + (me % 2 ^ side)) * rows), (left.shape[0], rows))
+        for side in range(2)
+        for d in range(stops)
+    ]
+    return jnp.concatenate(pieces, axis=1)
+
+
 def per_device(
     tokens, level_ids, coarse_ids, first_qkv, first_out, merge_weight, second_qkv, second_out
 ):
 
+    merge_whole = spread(merge_weight)
+    second_qkv_whole = spread(second_qkv)
+
     def second_qkv_product(left):
-        return add_rows(left, lax.all_gather(second_qkv, "lon", axis=0, tiled=True))
+        return add_rows(reordered(left, second_qkv.shape[0]), second_qkv_whole)
 
     def second_out_product(left):
         return add_rows(left, lax.all_gather(second_out, "lon", axis=0, tiled=True))
@@ -143,9 +184,7 @@
     joined = merge_patches(skip)
     levels, height, breadth, width = joined.shape
     left = normalized(joined).reshape(-1, width)
-    merged = add_rows(left, lax.all_gather(merge_weight, "lon", axis=0, tiled=True)).astype(
-        jnp.bfloat16
-    )
+    merged = add_rows(reordered(left, merge_weight.shape[0]), merge_whole).astype(jnp.bfloat16)
     merged = merged.reshape(levels, height, breadth, merge_weight.shape[1])
     coarse = shifted_layer(
         merged, edge_labels(coarse_ids), second_qkv_product, second_out_product, HEADS2

time: 184 us -> 198 us (1.076)
  waiting for transfers between devices: 88.8 us -> 44.9 us
  local copies, waits for them, and re-layouts: 26.3 us -> 61 us
  starting transfers between devices: 17.3 us -> 36.5 us
  other arithmetic: 5.87 us -> 9.66 us
    all_gather x2 -> x0, waiting for transfers between devices: 35.9 us -> none  [the longest x1 35.9 us: second_qkv_product(): return add_rows(left, lax.all_gather(second_qkv, 'lon', axis=0, tiled=True))]
    ppermute x0 -> x16, waiting for transfers between devices: none -> 19.9 us  [the longest x10 12.8 us: exchange(): lax.ppermute(block, axis, [(i, i ^ mask) for i in range(lax.axis_size(axi...]
    ppermute x12, waiting for transfers between devices: 41.7 us -> 25 us  [from_behind(): return lax.ppermute(block, axis, route)]
    ppermute x0 -> x16, starting transfers between devices: none -> 15.7 us  [the longest x6 9.66 us: spread(): lax.ppermute(mine, 'lon', [(i, (i + 2 * d) % ranks) for i in range(ranks)])]
    dynamic_update_slice x0 -> x8, local copies, waits for them, and re-layouts: none -> 15 us  [the longest x6 11.4 us: spread(): lax.dynamic_update_slice(whole, part, (rows, (corner ^ mask) * quarter))]
    all_gather x1, waiting for transfers between devices: 9.71 us -> 0.02 us  [second_out_product(): return add_rows(left, lax.all_gather(second_out, 'lon', axis=0, tiled=True))]
    unnamed x23 -> x41, local copies, waits for them, and re-layouts: 1.07 us -> 6.91 us
    slice x0 -> x4, local copies, waits for them, and re-layouts: none -> 4.65 us  [the longest x2 2.73 us: spread(): first[:half]]
  transfers between devices with their start and end apart: 15 -> 29, of which waited for: 11 -> 12; matrix products, arithmetic and copies ran while one was open for 31% -> 48% of each run, Pallas kernels for 0% -> 0%
where the time goes in v1:
time: 198 us; the launch traced here: 197 us
  local copies, waits for them, and re-layouts  61 us (31%)
  waiting for transfers between devices  44.9 us (23%)
  starting transfers between devices  36.5 us (18%)
  matrix products  30 us (15%)
  between operations  14.8 us (7%)
  other arithmetic  9.66 us (5%)
    ppermute x12, waiting for transfers between devices, from_behind(): return lax.ppermute(block, axis, route)  25 us
    ppermute x12, starting transfers between devices, from_behind(): return lax.ppermute(block, axis, route)  20.7 us
    ppermute x10, waiting for transfers between devices, exchange(): lax.ppermute(block, axis, [(i, i ^ mask) for i in range(lax.axis_size(axi...  12.8 us
    dynamic_update_slice x6, local copies, waits for them, and re-layouts, spread(): lax.dynamic_update_slice(whole, part, (rows, (corner ^ mask) * quarter))  11.4 us
    sub x3, matrix products, window_softmax(): expos = jnp.exp(scores - highest)  10.4 us
    ppermute x6, starting transfers between devices, spread(): lax.ppermute(mine, 'lon', [(i, (i + 2 * d) % ranks) for i in range(ranks)])  9.66 us
    dot_general x3, matrix products, add_rows(): return jnp.dot(left, piece, preferred_element_type=jnp.float32)  9.53 us
    ppermute x6, waiting for transfers between devices, spread(): lax.ppermute(mine, 'lon', [(i, (i + 2 * d) % ranks) for i in range(ranks)])  7.15 us
  transfers between devices with their start and end apart: 29, of which 12 were waited for; matrix products, arithmetic and copies ran while one was open for 48% of the time, Pallas kernels for 0%

profile of v1, /device:TPU:0, one launch (start us, length us, event | category | flops | bytes accessed | tf_op | source)
XLA Modules:
  0.0 197.0 jit_solution(12572990370063241904)
XLA Ops:
  7.3 1.7 constant_dynamic-slice_fusion.2
  9.0 3.0 %collective-permute-start.6 = (bf16[256,256]{1,0:T(8,128)(2,1)}, bf16[256,256]{1,0:T(8,128)(2,1)}, u32[]{:S(2)}, u32[]{:S(2)}) collective-permute-start(bf16[256,256]{1,0:T(8,128)(2,1)} %constant_dynamic-slice_fusion.2), channel_id=1, source_target_pairs={{0,2},{1,3},{2,4},{3,5},{4,6},{5,7},{6,0},{7,1},{8,10},{9,11},{10,... | collective-permute-start | bytes 393224 | tf_op jit(solution)/shard_map/ppermute | solution.py:135
  12.0 2.6 %collective-permute-start.7 = (bf16[256,256]{1,0:T(8,128)(2,1)}, bf16[256,256]{1,0:T(8,128)(2,1)}, u32[]{:S(2)}, u32[]{:S(2)}) collective-permute-start(bf16[256,256]{1,0:T(8,128)(2,1)} %constant_dynamic-slice_fusion.2), channel_id=1, source_target_pairs={{0,4},{1,5},{2,6},{3,7},{4,0},{5,1},{6,2},{7,3},{8,12},{9,13},{10,... | collective-permute-start | bytes 393224 | tf_op jit(solution)/shard_map/ppermute | solution.py:135
  16.7 2.5 %collective-permute-start.2 = (bf16[2,3,24]{2,0,1:T(2,128)(2,1)S(1)}, bf16[2,3,24]{2,0,1:T(2,128)(2,1)S(1)}, u32[]{:S(2)}, u32[]{:S(2)}) collective-permute-start(bf16[2,3,24]{2,0,1:T(2,128)(2,1)S(1)} %slice.140), channel_id=1, source_target_pairs={{8,0},{16,8},{24,16},{0,24},{9,1},{17,9},{25,17},{1,25},{10,2},{18... | collective-permute-start | bytes 872 | tf_op jit(solution)/shard_map/ppermute | solution.py:21
  19.2 1.6 constant_dynamic-slice_fusion.1
  21.6 1.6 slice.103
  24.5 1.7 dynamic_update_slice.37
  26.1 2.0 %dynamic_update_slice.42 = bf16[512,3072]{1,0:T(8,128)(2,1)} pad(bf16[128,3072]{1,0:T(8,128)(2,1)S(1)} %copy-done.7, bf16[]{:T(256)} %constant.214.clone.1), padding=0_384x0_0 | pad | bytes 3932162 | tf_op jit(solution)/shard_map/dynamic_update_slice | solution.py:144
  31.4 2.0 %collective-permute-start.18 = (bf16[128,768]{1,0:T(8,128)(2,1)}, bf16[128,768]{1,0:T(8,128)(2,1)S(1)}, u32[]{:S(2)}, u32[]{:S(2)}) collective-permute-start(bf16[128,768]{1,0:T(8,128)(2,1)} %constant_dynamic-slice_fusion.1), channel_id=1, source_target_pairs={{0,6},{1,7},{2,0},{3,1},{4,2},{5,3},{6,4},{7,5},{8,14},{9,15},{10,... | collective-permute-start | bytes 589832 | tf_op jit(solution)/shard_map/ppermute | solution.py:135
  33.5 1.6 constant_dynamic-update-slice_fusion.2
  35.6 1.6 constant_dynamic-update-slice_fusion.1
  38.6 1.6 constant_dynamic-update-slice_fusion
  40.2 1.8 constant_dynamic-update-slice_fusion.19
  43.6 1.7 constant_dynamic-update-slice_fusion.13
  45.3 7.1 %collective-permute-done.17 = bf16[128,768]{1,0:T(8,128)(2,1)S(1)} collective-permute-done((bf16[128,768]{1,0:T(8,128)(2,1)}, bf16[128,768]{1,0:T(8,128)(2,1)S(1)}, u32[]{:S(2)}, u32[]{:S(2)}) %collective-permute-start.17) | collective-permute-done | bytes 196640 | tf_op jit(solution)/shard_map/ppermute | solution.py:135
  53.4 2.4 %collective-permute-done.1 = bf16[2,12,6,512]{3,2,1,0:T(8,128)(2,1)S(1)} collective-permute-done((bf16[2,12,6,512]{3,2,1,0:T(8,128)(2,1)S(1)}, bf16[2,12,6,512]{3,2,1,0:T(8,128)(2,1)S(1)}, u32[]{:S(2)}, u32[]{:S(2)}) %collective-permute-start.1) | collective-permute-done | bytes 147488 | tf_op jit(solution)/shard_map/ppermute | solution.py:21
  59.2 21.7 %while.2 = (s32[]{:T(128)}, bf16[2,2,6,24,512]{4,3,2,0,1:T(8,128)(2,1)}, bf16[2,2,6,24,512]{4,3,2,0,1:T(8,128)(2,1)}, s32[2,2,6,24]{3,1,2,0:T(2,128)S(1)}, bf16[...) while((s32[]{:T(128)}, bf16[2,2,6,24,512]{4,3,2,0,1:T(8,128)(2,1)}, ...), condition=%wide.region_5.6_spmd, body=%wide.region_2.5_spmd.sunk | while | flops 87114384 | bytes 13972737 | solution.py:73
  62.2 3.6 %fusion.111 = (f32[2,8,144]{2,1,0:T(8,128)S(1)}, f32[2,8,144,144]{2,3,1,0:T(8,128)}) fusion(pred[2,144,144]{1,2,0:T(8,128)(4,1)S(1)} %broadcast_compare_fusion.3, bf16[2,144,8,64]{3,2,1,0:T(8,128)(2,1)S(1)} %bitcast.117, bf16[2,144,8,64]{3,2,1,0:T(8,128)(2,1)} %bitcast.118), kind=kOutput, calls=%fused_computation.136.clone.1 | convolution fusion | flops 43794576 | bytes 1967616 | tf_op jit(solution)/shard_map/while/body/eval_jaxpr/sub | solution.py:51
  66.1 2.1 %fusion.112 = bf16[2,144,8,64]{1,3,2,0:T(8,128)(2,1)S(1)} fusion(f32[2,8,144,144]{2,3,1,0:T(8,128)} %get-tuple-element.140, f32[2,8,144]{2,1,0:T(8,128)S(1)} %get-tuple-element.141, bf16[2,144,8,64]{3,2,1,0:T(8,128)(2,1)S(1)} %bitcast.119), kind=kOutput, calls=%fused_computation.6.clone.1 | convolution fusion | flops 43278336 | bytes 1926144 | tf_op jit(solution)/shard_map/while/body/eval_jaxpr/whqk,wkhd->wqhd/dot_general | solution.py:53
  73.0 3.5 %fusion.111 = (f32[2,8,144]{2,1,0:T(8,128)S(1)}, f32[2,8,144,144]{2,3,1,0:T(8,128)}) fusion(pred[2,144,144]{1,2,0:T(8,128)(4,1)S(1)} %broadcast_compare_fusion.3, bf16[2,144,8,64]{3,2,1,0:T(8,128)(2,1)S(1)} %bitcast.117, bf16[2,144,8,64]{3,2,1,0:T(8,128)(2,1)} %bitcast.118), kind=kOutput, calls=%fused_computation.136.clone.1 | convolution fusion | flops 43794576 | bytes 1967616 | tf_op jit(solution)/shard_map/while/body/eval_jaxpr/sub | solution.py:51
  77.0 2.1 %fusion.112 = bf16[2,144,8,64]{1,3,2,0:T(8,128)(2,1)S(1)} fusion(f32[2,8,144,144]{2,3,1,0:T(8,128)} %get-tuple-element.140, f32[2,8,144]{2,1,0:T(8,128)S(1)} %get-tuple-element.141, bf16[2,144,8,64]{3,2,1,0:T(8,128)(2,1)S(1)} %bitcast.119), kind=kOutput, calls=%fused_computation.6.clone.1 | convolution fusion | flops 43278336 | bytes 1926144 | tf_op jit(solution)/shard_map/while/body/eval_jaxpr/whqk,wkhd->wqhd/dot_general | solution.py:53
  80.9 1.9 fusion.39
  82.9 2.3 %collective-permute-start.4 = (bf16[2,12,6,512]{3,2,1,0:T(8,128)(2,1)S(1)}, bf16[2,12,6,512]{3,2,1,0:T(8,128)(2,1)S(1)}, u32[]{:S(2)}, u32[]{:S(2)}) collective-permute-start(bf16[2,12,6,512]{3,2,1,0:T(8,128)(2,1)S(1)} %slice.145), channel_id=1, source_target_pairs={{7,0},{0,1},{1,2},{2,3},{3,4},{4,5},{5,6},{6,7},{15,8},{8,9},{9,10... | collective-permute-start | bytes 442376 | tf_op jit(solution)/shard_map/ppermute | solution.py:21
  86.8 2.0 %constant_dynamic-update-slice_fusion.16 = bf16[512,3072]{1,0:T(8,128)(2,1)} fusion(bf16[512,3072]{1,0:T(8,128)(2,1)} %dynamic_update_slice.42, bf16[384,768]{1,0:T(8,128)(2,1)} %constant_dynamic-update-slice_fusion.11, s32[]{:T(128)S(6)} %select_n.213), kind=kLoop, calls=%fused_computation.126 | loop fusion | bytes 1179652 | tf_op jit(solution)/shard_map/dynamic_update_slice | solution.py:146
  88.8 5.8 %collective-permute-done.4 = bf16[2,12,6,512]{3,2,1,0:T(8,128)(2,1)S(1)} collective-permute-done((bf16[2,12,6,512]{3,2,1,0:T(8,128)(2,1)S(1)}, bf16[2,12,6,512]{3,2,1,0:T(8,128)(2,1)S(1)}, u32[]{:S(2)}, u32[]{:S(2)}) %collective-permute-start.4) | collective-permute-done | bytes 147488 | tf_op jit(solution)/shard_map/ppermute | solution.py:21
  97.4 2.0 collective-permute-start.12
  99.4 1.8 constant_dynamic-update-slice_fusion.18
  101.2 1.6 slice.147
  102.8 1.8 constant_dynamic-update-slice_fusion.17
  107.6 7.8 %collective-permute-done.11 = bf16[384,256]{1,0:T(8,128)(2,1)} collective-permute-done((bf16[384,256]{1,0:T(8,128)(2,1)}, bf16[384,256]{1,0:T(8,128)(2,1)}, u32[]{:S(2)}, u32[]{:S(2)}) %collective-permute-start.11) | collective-permute-done | bytes 196640 | tf_op jit(solution)/shard_map/ppermute | solution.py:125
  115.3 1.8 maximum_dynamic-update-slice_fusion.1
  118.5 1.9 copy.101
  120.5 2.3 %reshape.293 = f32[144,2048]{1,0:T(8,128)S(1)} reshape(f32[2,6,12,2,2,512]{5,4,3,2,1,0:T(2,128)} %bitcast.121) | data formatting | bytes 2359296 | tf_op jit(solution)/shard_map/convert_element_type | solution.py:25
  125.9 2.0 %constant_dynamic-update-slice_fusion.15 = bf16[512,3072]{1,0:T(8,128)(2,1)} fusion(bf16[512,3072]{1,0:T(8,128)(2,1)} %constant_dynamic-update-slice_fusion.16, bf16[384,768]{1,0:T(8,128)(2,1)} %collective-permute-done.19, s32[]{:T(128)S(6)} %select_n.214), kind=kLoop, calls=%fused_computation.125 | loop fusion | bytes 1179652 | tf_op jit(solution)/shard_map/dynamic_update_slice | solution.py:146
  127.9 2.0 constant_dynamic-update-slice_fusion.14
  129.9 3.8 %collective-permute-done.22 = bf16[192,768]{1,0:T(8,128)(2,1)S(1)} collective-permute-done((bf16[192,768]{1,0:T(8,128)(2,1)S(1)}, bf16[192,768]{1,0:T(8,128)(2,1)S(1)}, u32[]{:S(2)}, u32[]{:S(2)}) %collective-permute-start.22) | collective-permute-done | bytes 294944 | tf_op jit(solution)/shard_map/ppermute | solution.py:125
  135.9 2.4 %fusion.47 = bf16[144,1024]{1,0:T(8,128)(2,1)S(1)} fusion(bf16[144,2048]{1,0:T(8,128)(2,1)S(1)} %dynamic-slice_dynamic-update-slice_fusion, bf16[1024,1024]{1,0:T(8,128)(2,1)} %collective-permute-done.13, bf16[1024,1024]{1,0:T(8,128)(2,1)S(1)} %copy-done.4), kind=kOutput, calls=%fused_computation.45 | convolution fusion | flops 612515840 | bytes 5079040 | tf_op jit(solution)/shard_map/dot_general | solution.py:121
  139.8 3.6 %collective-permute-start.25 = (bf16[2,6,6]{2,0,1:T(2,128)(2,1)S(1)}, bf16[2,6,6]{2,0,1:T(2,128)(2,1)S(1)}, u32[]{:S(2)}, u32[]{:S(2)}) collective-permute-start(bf16[2,6,6]{2,0,1:T(2,128)(2,1)S(1)} %get-tuple-element.92), channel_id=1, source_target_pairs={{1,0},{2,1},{3,2},{4,3},{5,4},{6,5},{7,6},{0,7},{9,8},{10,9},{11,1... | collective-permute-start | bytes 440 | tf_op jit(solution)/shard_map/ppermute | solution.py:21
  145.8 3.0 %collective-permute-start.15 = (bf16[2,6,6,1024]{3,2,1,0:T(8,128)(2,1)S(1)}, bf16[2,6,6,1024]{3,2,1,0:T(8,128)(2,1)S(1)}, u32[]{:S(2)}, u32[]{:S(2)}) collective-permute-start(bf16[2,6,6,1024]{3,2,1,0:T(8,128)(2,1)S(1)} %get-tuple-element.88), channel_id=1, source_target_pairs={{1,0},{2,1},{3,2},{4,3},{5,4},{6,5},{7,6},{0,7},{9,8},{10,9},{11,1... | collective-permute-start | bytes 442376 | tf_op jit(solution)/shard_map/ppermute | solution.py:21
  149.5 2.5 %collective-permute-done.15 = bf16[2,6,6,1024]{3,2,1,0:T(8,128)(2,1)S(1)} collective-permute-done((bf16[2,6,6,1024]{3,2,1,0:T(8,128)(2,1)S(1)}, bf16[2,6,6,1024]{3,2,1,0:T(8,128)(2,1)S(1)}, u32[]{:S(2)}, u32[]{:S(2)}) %collective-permute-start.15) | collective-permute-done | bytes 147488 | tf_op jit(solution)/shard_map/ppermute | solution.py:21
  153.4 5.0 %fusion.33 = bf16[144,3072]{1,0:T(8,128)(2,1)} fusion(bf16[144,1024]{1,0:T(8,128)(2,1)S(1)} %constant_dynamic-update-slice_fusion.3, bf16[512,3072]{1,0:T(8,128)(2,1)} %collective-permute-done.23, bf16[512,3072]{1,0:T(8,128)(2,1)} %maximum_dynamic-update-slice_fusion), kind=kOutput, calls=%fused_computation.31 | convolution fusion | flops 918994944 | bytes 7471104 | tf_op jit(solution)/shard_map/dot_general | solution.py:121
  164.7 3.3 %fusion.92 = (f32[16,144]{1,0:T(8,128)S(1)}, f32[16,144,144]{1,2,0:T(8,128)}) fusion(pred[144,144]{0,1:T(8,128)(4,1)} %broadcast_compare_fusion.1, bf16[144,16,64]{2,1,0:T(8,128)(2,1)S(1)} %reshape.291, bf16[144,16,64]{2,1,0:T(8,128)(2,1)S(1)} %reshape.290), kind=kOutput, calls=%fused_computation.142 | convolution fusion | flops 43794576 | bytes 1946880 | tf_op jit(solution)/shard_map/while/body/eval_jaxpr/sub | solution.py:51
  168.0 2.9 %fusion.46 = bf16[1,144,16,64]{1,3,2,0:T(8,128)(2,1)} fusion(f32[16,144,144]{1,2,0:T(8,128)} %get-tuple-element.96, f32[16,144]{1,0:T(8,128)S(1)} %get-tuple-element.95, bf16[144,16,64]{2,1,0:T(8,128)(2,1)S(1)} %copy-done.9), kind=kOutput, calls=%fused_computation.44 | convolution fusion | flops 43278336 | bytes 1926144 | tf_op jit(solution)/shard_map/while/body/eval_jaxpr/whqk,wkhd->wqhd/dot_general | solution.py:53
  170.9 1.6 copy.38
  173.0 2.2 %fusion.43 = bf16[2,6,12,1024]{3,2,1,0:T(8,128)(2,1)S(1)} fusion(bf16[2,6,12,1024]{3,2,1,0:T(8,128)(2,1)S(1)} %dot_general.40, bf16[1024,1024]{1,0:T(8,128)(2,1)} %all-gather.2.cloned.1.call-done, bf16[2,6,6,1024]{3,2,1,0:T(8,128)(2,1)S(1)} %copy-done.6, bf16[2,6,6,1024]{3,2,1,0:T(8,128)(2,1)S(1)} %get-tuple-element.87), kind=kOutput, calls=%fused_computation.43 | convolution fusion | flops 302874624 | bytes 2981888 | tf_op jit(solution)/shard_map/dot_general | solution.py:121
  176.1 6.2 %collective-permute-done.26 = bf16[2,6,6,1024]{3,2,1,0:T(8,128)(2,1)S(1)} collective-permute-done((bf16[2,6,6,1024]{3,2,1,0:T(8,128)(2,1)S(1)}, bf16[2,6,6,1024]{3,2,1,0:T(8,128)(2,1)S(1)}, u32[]{:S(2)}, u32[]{:S(2)}) %collective-permute-start.26) | collective-permute-done | bytes 147488 | tf_op jit(solution)/shard_map/ppermute | solution.py:21
  182.4 2.1 %collective-permute-start.27 = (bf16[2,3,12,1024]{3,2,1,0:T(8,128)(2,1)S(1)}, bf16[2,3,12,1024]{3,2,1,0:T(8,128)(2,1)S(1)}, u32[]{:S(2)}, u32[]{:S(2)}) collective-permute-start(bf16[2,3,12,1024]{3,2,1,0:T(8,128)(2,1)S(1)} %fusion.62), channel_id=1, source_target_pairs={{24,0},{0,8},{8,16},{16,24},{25,1},{1,9},{9,17},{17,25},{26,2},{2,... | collective-permute-start | bytes 442376 | tf_op jit(solution)/shard_map/ppermute | solution.py:21
  184.5 4.5 %collective-permute-done.27 = bf16[2,3,12,1024]{3,2,1,0:T(8,128)(2,1)S(1)} collective-permute-done((bf16[2,3,12,1024]{3,2,1,0:T(8,128)(2,1)S(1)}, bf16[2,3,12,1024]{3,2,1,0:T(8,128)(2,1)S(1)}, u32[]{:S(2)}, u32[]{:S(2)}) %collective-permute-start.27) | collective-permute-done | bytes 147488 | tf_op jit(solution)/shard_map/ppermute | solution.py:21
  (185 shorter events, 54.2 us)
Async XLA Ops:
  7.2 49.7 %copy-start = (bf16[512,1536]{1,0:T(8,128)(2,1)S(1)}, bf16[512,1536]{1,0:T(8,128)(2,1)}, u32[]{:S(2)}) copy-start(bf16[512,1536]{1,0:T(8,128)(2,1)} %param.13) | copy-start | bytes 4718596
  7.2 17.3 %copy-start.8 = (bf16[256,1024]{1,0:T(8,128)(2,1)S(1)}, bf16[256,1024]{1,0:T(8,128)(2,1)}, u32[]{:S(2)}) copy-start(bf16[256,1024]{1,0:T(8,128)(2,1)} %param.15) | copy-start | bytes 1572868
  7.2 165.8 %all-gather.2.cloned.1.call-start = ((), (), s32[]{:S(2)}) async-start(), calls=%async_computation | async-start | bytes 2359296 | tf_op jit(solution)/shard_map/all_gather | solution.py:173
  9.0 22.5 %collective-permute-start.6 = (bf16[256,256]{1,0:T(8,128)(2,1)}, bf16[256,256]{1,0:T(8,128)(2,1)}, u32[]{:S(2)}, u32[]{:S(2)}) collective-permute-start(bf16[256,256]{1,0:T(8,128)(2,1)} %constant_dynamic-slice_fusion.2), channel_id=1, source_target_pairs={{0,2},{1,3},{2,4},{3,5},{4,6},{5,7},{6,0},{7,1},{8,10},{9,11},{10,... | collective-permute-start | bytes 393224 | tf_op jit(solution)/shard_map/ppermute | solution.py:135
  12.0 23.0 %collective-permute-start.7 = (bf16[256,256]{1,0:T(8,128)(2,1)}, bf16[256,256]{1,0:T(8,128)(2,1)}, u32[]{:S(2)}, u32[]{:S(2)}) collective-permute-start(bf16[256,256]{1,0:T(8,128)(2,1)} %constant_dynamic-slice_fusion.2), channel_id=1, source_target_pairs={{0,4},{1,5},{2,6},{3,7},{4,0},{5,1},{6,2},{7,3},{8,12},{9,13},{10,... | collective-permute-start | bytes 393224 | tf_op jit(solution)/shard_map/ppermute | solution.py:135
  14.6 22.6 %collective-permute-start.8 = (bf16[256,256]{1,0:T(8,128)(2,1)}, bf16[256,256]{1,0:T(8,128)(2,1)}, u32[]{:S(2)}, u32[]{:S(2)}) collective-permute-start(bf16[256,256]{1,0:T(8,128)(2,1)} %constant_dynamic-slice_fusion.2), channel_id=1, source_target_pairs={{0,6},{1,7},{2,0},{3,1},{4,2},{5,3},{6,4},{7,5},{8,14},{9,15},{10,... | collective-permute-start | bytes 393224 | tf_op jit(solution)/shard_map/ppermute | solution.py:135
  16.7 12.0 %collective-permute-start.2 = (bf16[2,3,24]{2,0,1:T(2,128)(2,1)S(1)}, bf16[2,3,24]{2,0,1:T(2,128)(2,1)S(1)}, u32[]{:S(2)}, u32[]{:S(2)}) collective-permute-start(bf16[2,3,24]{2,0,1:T(2,128)(2,1)S(1)} %slice.140), channel_id=1, source_target_pairs={{8,0},{16,8},{24,16},{0,24},{9,1},{17,9},{25,17},{1,25},{10,2},{18... | collective-permute-start | bytes 872 | tf_op jit(solution)/shard_map/ppermute | solution.py:21
  20.9 21.9 %collective-permute-start.16 = (bf16[128,768]{1,0:T(8,128)(2,1)}, bf16[128,768]{1,0:T(8,128)(2,1)}, u32[]{:S(2)}, u32[]{:S(2)}) collective-permute-start(bf16[128,768]{1,0:T(8,128)(2,1)} %constant_dynamic-slice_fusion.1), channel_id=1, source_target_pairs={{0,2},{1,3},{2,4},{3,5},{4,6},{5,7},{6,0},{7,1},{8,10},{9,11},{10,... | collective-permute-start | bytes 589832 | tf_op jit(solution)/shard_map/ppermute | solution.py:135
  21.6 4.6 %copy-start.7 = (bf16[128,3072]{1,0:T(8,128)(2,1)S(1)}, bf16[128,3072]{1,0:T(8,128)(2,1)}, u32[]{:S(2)}) copy-start(bf16[128,3072]{1,0:T(8,128)(2,1)} %param.16) | copy-start | bytes 2359300
  26.1 2.0 %copy-start.11 = (s32[2,6,12]{2,0,1:T(2,128)S(1)}, s32[2,6,12]{2,0,1:T(2,128)}, u32[]{:S(2)}) copy-start(s32[2,6,12]{2,0,1:T(2,128)} %param.12) | copy-start | bytes 1732
  26.1 8.9 %copy-start.10 = (bf16[2,3,24,512]{3,2,1,0:T(8,128)(2,1)S(1)}, bf16[2,3,24,512]{3,2,1,0:T(8,128)(2,1)}, u32[]{:S(2)}) copy-start(bf16[2,3,24,512]{3,2,1,0:T(8,128)(2,1)} %slice.103) | copy-start | bytes 442372
  28.8 2.6 %collective-permute-start.3 = (bf16[2,12,6]{2,0,1:T(2,128)(2,1)S(1)}, bf16[2,12,6]{2,0,1:T(2,128)(2,1)S(1)}, u32[]{:S(2)}, u32[]{:S(2)}) collective-permute-start(bf16[2,12,6]{2,0,1:T(2,128)(2,1)S(1)} %pad_maximum_fusion.7), channel_id=1, source_target_pairs={{1,0},{2,1},{3,2},{4,3},{5,4},{6,5},{7,6},{0,7},{9,8},{10,9},{11,1... | collective-permute-start | bytes 872 | tf_op jit(solution)/shard_map/ppermute | solution.py:21
  31.4 21.1 %collective-permute-start.17 = (bf16[128,768]{1,0:T(8,128)(2,1)}, bf16[128,768]{1,0:T(8,128)(2,1)S(1)}, u32[]{:S(2)}, u32[]{:S(2)}) collective-permute-start(bf16[128,768]{1,0:T(8,128)(2,1)} %constant_dynamic-slice_fusion.1), channel_id=1, source_target_pairs={{0,4},{1,5},{2,6},{3,7},{4,0},{5,1},{6,2},{7,3},{8,12},{9,13},{10,... | collective-permute-start | bytes 589832 | tf_op jit(solution)/shard_map/ppermute | solution.py:135
  31.4 53.8 %collective-permute-start.18 = (bf16[128,768]{1,0:T(8,128)(2,1)}, bf16[128,768]{1,0:T(8,128)(2,1)S(1)}, u32[]{:S(2)}, u32[]{:S(2)}) collective-permute-start(bf16[128,768]{1,0:T(8,128)(2,1)} %constant_dynamic-slice_fusion.1), channel_id=1, source_target_pairs={{0,6},{1,7},{2,0},{3,1},{4,2},{5,3},{6,4},{7,5},{8,14},{9,15},{10,... | collective-permute-start | bytes 589832 | tf_op jit(solution)/shard_map/ppermute | solution.py:135
  35.0 6.9 %collective-permute-start = (bf16[2,3,24,512]{3,2,1,0:T(8,128)(2,1)S(1)}, bf16[2,3,24,512]{3,2,1,0:T(8,128)(2,1)S(1)}, u32[]{:S(2)}, u32[]{:S(2)}) collective-permute-start(bf16[2,3,24,512]{3,2,1,0:T(8,128)(2,1)S(1)} %copy-done.10), channel_id=1, source_target_pairs={{8,0},{16,8},{24,16},{0,24},{9,1},{17,9},{25,17},{1,25},{10,2},{18... | collective-permute-start | bytes 442376 | tf_op jit(solution)/shard_map/ppermute | solution.py:21
  37.2 102.5 %collective-permute-start.24 = (bf16[2,3,12]{2,0,1:T(2,128)(2,1)}, bf16[2,3,12]{2,0,1:T(2,128)(2,1)S(1)}, u32[]{:S(2)}, u32[]{:S(2)}) collective-permute-start(bf16[2,3,12]{2,0,1:T(2,128)(2,1)} %get-tuple-element.94), channel_id=1, source_target_pairs={{8,0},{16,8},{24,16},{0,24},{9,1},{17,9},{25,17},{1,25},{10,2},{18... | collective-permute-start | bytes 440 | tf_op jit(solution)/shard_map/ppermute | solution.py:21
  42.0 55.5 %collective-permute-start.9 = (bf16[768,256]{1,0:T(8,128)(2,1)}, bf16[768,256]{1,0:T(8,128)(2,1)}, u32[]{:S(2)}, u32[]{:S(2)}) collective-permute-start(bf16[768,256]{1,0:T(8,128)(2,1)} %constant_dynamic-update-slice_fusion), channel_id=1, source_target_pairs={{0,8},{8,0},{16,24},{24,16},{1,9},{9,1},{17,25},{25,17},{2,10},{10... | collective-permute-start | bytes 1179656 | tf_op jit(solution)/shard_map/ppermute | solution.py:125
  42.7 14.2 %copy-start.1 = (bf16[2,12,18,512]{3,2,1,0:T(8,128)(2,1)}, bf16[2,12,18,512]{3,2,1,0:T(8,128)(2,1)S(1)}, u32[]{:S(2)}) copy-start(bf16[2,12,18,512]{3,2,1,0:T(8,128)(2,1)S(1)} %slice_maximum_fusion) | copy-start | bytes 1327108
  42.8 13.0 %collective-permute-start.1 = (bf16[2,12,6,512]{3,2,1,0:T(8,128)(2,1)S(1)}, bf16[2,12,6,512]{3,2,1,0:T(8,128)(2,1)S(1)}, u32[]{:S(2)}, u32[]{:S(2)}) collective-permute-start(bf16[2,12,6,512]{3,2,1,0:T(8,128)(2,1)S(1)} %pad_maximum_fusion.5), channel_id=1, source_target_pairs={{1,0},{2,1},{3,2},{4,3},{5,4},{6,5},{7,6},{0,7},{9,8},{10,9},{11,1... | collective-permute-start | bytes 442376 | tf_op jit(solution)/shard_map/ppermute | solution.py:21
  52.4 43.2 %collective-permute-start.10 = (bf16[768,256]{1,0:T(8,128)(2,1)}, bf16[768,256]{1,0:T(8,128)(2,1)}, u32[]{:S(2)}, u32[]{:S(2)}) collective-permute-start(bf16[768,256]{1,0:T(8,128)(2,1)} %constant_dynamic-update-slice_fusion), channel_id=1, source_target_pairs={{0,16},{8,24},{16,0},{24,8},{1,17},{9,25},{17,1},{25,9},{2,18},{10... | collective-permute-start | bytes 1179656 | tf_op jit(solution)/shard_map/ppermute | solution.py:125
  62.2 3.6 %copy-start.2 = (bf16[2,2,6,24,512]{4,3,2,0,1:T(8,128)(2,1)S(1)}, bf16[2,2,6,24,512]{4,3,2,0,1:T(8,128)(2,1)}, u32[]{:S(2)}) copy-start(bf16[2,2,6,24,512]{4,3,2,0,1:T(8,128)(2,1)} %get-tuple-element.158) | copy-start | bytes 1769476 | tf_op jit(solution)/shard_map/while
  73.0 3.6 %copy-start.2 = (bf16[2,2,6,24,512]{4,3,2,0,1:T(8,128)(2,1)S(1)}, bf16[2,2,6,24,512]{4,3,2,0,1:T(8,128)(2,1)}, u32[]{:S(2)}) copy-start(bf16[2,2,6,24,512]{4,3,2,0,1:T(8,128)(2,1)} %get-tuple-element.158) | copy-start | bytes 1769476 | tf_op jit(solution)/shard_map/while
  82.9 11.7 %collective-permute-start.4 = (bf16[2,12,6,512]{3,2,1,0:T(8,128)(2,1)S(1)}, bf16[2,12,6,512]{3,2,1,0:T(8,128)(2,1)S(1)}, u32[]{:S(2)}, u32[]{:S(2)}) collective-permute-start(bf16[2,12,6,512]{3,2,1,0:T(8,128)(2,1)S(1)} %slice.145), channel_id=1, source_target_pairs={{7,0},{0,1},{1,2},{2,3},{3,4},{4,5},{5,6},{6,7},{15,8},{8,9},{9,10... | collective-permute-start | bytes 442376 | tf_op jit(solution)/shard_map/ppermute | solution.py:21
  85.9 38.4 %collective-permute-start.19 = (bf16[384,768]{1,0:T(8,128)(2,1)}, bf16[384,768]{1,0:T(8,128)(2,1)}, u32[]{:S(2)}, u32[]{:S(2)}) collective-permute-start(bf16[384,768]{1,0:T(8,128)(2,1)} %constant_dynamic-update-slice_fusion.11), channel_id=1, source_target_pairs={{0,8},{8,0},{16,24},{24,16},{1,9},{9,1},{17,25},{25,17},{2,10},{10... | collective-permute-start | bytes 1769480 | tf_op jit(solution)/shard_map/ppermute | solution.py:125
  94.6 28.7 %collective-permute-start.20 = (bf16[384,768]{1,0:T(8,128)(2,1)}, bf16[384,768]{1,0:T(8,128)(2,1)}, u32[]{:S(2)}, u32[]{:S(2)}) collective-permute-start(bf16[384,768]{1,0:T(8,128)(2,1)} %constant_dynamic-update-slice_fusion.11), channel_id=1, source_target_pairs={{0,16},{8,24},{16,0},{24,8},{1,17},{9,25},{17,1},{25,9},{2,18},{10... | collective-permute-start | bytes 1769480 | tf_op jit(solution)/shard_map/ppermute | solution.py:125
  95.6 9.0 %collective-permute-start.5 = (bf16[2,3,24,512]{3,2,1,0:T(8,128)(2,1)S(1)}, bf16[2,3,24,512]{3,2,1,0:T(8,128)(2,1)S(1)}, u32[]{:S(2)}, u32[]{:S(2)}) collective-permute-start(bf16[2,3,24,512]{3,2,1,0:T(8,128)(2,1)S(1)} %pad_maximum_fusion.6), channel_id=1, source_target_pairs={{24,0},{0,8},{8,16},{16,24},{25,1},{1,9},{9,17},{17,25},{26,2},{2,... | collective-permute-start | bytes 442376 | tf_op jit(solution)/shard_map/ppermute | solution.py:21
  97.4 10.1 %collective-permute-start.12 = (bf16[384,256]{1,0:T(8,128)(2,1)S(1)}, bf16[384,256]{1,0:T(8,128)(2,1)}, u32[]{:S(2)}, u32[]{:S(2)}) collective-permute-start(bf16[384,256]{1,0:T(8,128)(2,1)S(1)} %slice.148), channel_id=1, source_target_pairs={{0,8},{8,0},{16,24},{24,16},{1,9},{9,1},{17,25},{25,17},{2,10},{10... | collective-permute-start | bytes 589832 | tf_op jit(solution)/shard_map/ppermute | solution.py:125
  104.6 10.7 %collective-permute-start.11 = (bf16[384,256]{1,0:T(8,128)(2,1)}, bf16[384,256]{1,0:T(8,128)(2,1)}, u32[]{:S(2)}, u32[]{:S(2)}) collective-permute-start(bf16[384,256]{1,0:T(8,128)(2,1)} %slice.147), channel_id=1, source_target_pairs={{0,16},{8,24},{16,0},{24,8},{1,17},{9,25},{17,1},{25,9},{2,18},{10... | collective-permute-start | bytes 589832 | tf_op jit(solution)/shard_map/ppermute | solution.py:125
  105.7 12.8 %copy-start.3 = (bf16[2,12,24,512]{3,2,1,0:T(8,128)(2,1)}, bf16[2,12,24,512]{3,2,1,0:T(8,128)(2,1)S(1)}, u32[]{:S(2)}) copy-start(bf16[2,12,24,512]{3,2,1,0:T(8,128)(2,1)S(1)} %fusion.55) | copy-start | bytes 1769476
  117.2 18.7 %collective-permute-start.13 = (bf16[1024,1024]{1,0:T(8,128)(2,1)}, bf16[1024,1024]{1,0:T(8,128)(2,1)}, u32[]{:S(2)}, u32[]{:S(2)}) collective-permute-start(bf16[1024,1024]{1,0:T(8,128)(2,1)} %maximum_dynamic-update-slice_fusion.1), channel_id=1, source_target_pairs={{0,1},{1,0},{2,3},{3,2},{4,5},{5,4},{6,7},{7,6},{8,9},{9,8},{10,11... | collective-permute-start | bytes 6291464 | tf_op jit(solution)/shard_map/ppermute | solution.py:125
  124.3 11.6 %copy-start.4 = (bf16[1024,1024]{1,0:T(8,128)(2,1)S(1)}, bf16[1024,1024]{1,0:T(8,128)(2,1)}, u32[]{:S(2)}) copy-start(bf16[1024,1024]{1,0:T(8,128)(2,1)} %maximum_dynamic-update-slice_fusion.1) | copy-start | bytes 6291460
  124.3 9.4 %collective-permute-start.22 = (bf16[192,768]{1,0:T(8,128)(2,1)S(1)}, bf16[192,768]{1,0:T(8,128)(2,1)S(1)}, u32[]{:S(2)}, u32[]{:S(2)}) collective-permute-start(bf16[192,768]{1,0:T(8,128)(2,1)S(1)} %slice.154), channel_id=1, source_target_pairs={{0,8},{8,0},{16,24},{24,16},{1,9},{9,1},{17,25},{25,17},{2,10},{10... | collective-permute-start | bytes 884744 | tf_op jit(solution)/shard_map/ppermute | solution.py:125
  125.5 9.4 %collective-permute-start.21 = (bf16[192,768]{1,0:T(8,128)(2,1)S(1)}, bf16[192,768]{1,0:T(8,128)(2,1)S(1)}, u32[]{:S(2)}, u32[]{:S(2)}) collective-permute-start(bf16[192,768]{1,0:T(8,128)(2,1)S(1)} %slice.153), channel_id=1, source_target_pairs={{0,16},{8,24},{16,0},{24,8},{1,17},{9,25},{17,1},{25,9},{2,18},{10... | collective-permute-start | bytes 884744 | tf_op jit(solution)/shard_map/ppermute | solution.py:125
  135.8 17.5 %collective-permute-start.23 = (bf16[512,3072]{1,0:T(8,128)(2,1)}, bf16[512,3072]{1,0:T(8,128)(2,1)}, u32[]{:S(2)}, u32[]{:S(2)}) collective-permute-start(bf16[512,3072]{1,0:T(8,128)(2,1)} %maximum_dynamic-update-slice_fusion), channel_id=1, source_target_pairs={{0,1},{1,0},{2,3},{3,2},{4,5},{5,4},{6,7},{7,6},{8,9},{9,8},{10,11... | collective-permute-start | bytes 9437192 | tf_op jit(solution)/shard_map/ppermute | solution.py:125
  138.4 7.4 %collective-permute-start.14 = (bf16[2,3,12,1024]{3,2,1,0:T(8,128)(2,1)S(1)}, bf16[2,3,12,1024]{3,2,1,0:T(8,128)(2,1)S(1)}, u32[]{:S(2)}, u32[]{:S(2)}) collective-permute-start(bf16[2,3,12,1024]{3,2,1,0:T(8,128)(2,1)S(1)} %get-tuple-element.90), channel_id=1, source_target_pairs={{8,0},{16,8},{24,16},{0,24},{9,1},{17,9},{25,17},{1,25},{10,2},{18... | collective-permute-start | bytes 442376 | tf_op jit(solution)/shard_map/ppermute | solution.py:21
  139.8 4.9 %collective-permute-start.25 = (bf16[2,6,6]{2,0,1:T(2,128)(2,1)S(1)}, bf16[2,6,6]{2,0,1:T(2,128)(2,1)S(1)}, u32[]{:S(2)}, u32[]{:S(2)}) collective-permute-start(bf16[2,6,6]{2,0,1:T(2,128)(2,1)S(1)} %get-tuple-element.92), channel_id=1, source_target_pairs={{1,0},{2,1},{3,2},{4,3},{5,4},{6,5},{7,6},{0,7},{9,8},{10,9},{11,1... | collective-permute-start | bytes 440 | tf_op jit(solution)/shard_map/ppermute | solution.py:21
  145.8 6.2 %collective-permute-start.15 = (bf16[2,6,6,1024]{3,2,1,0:T(8,128)(2,1)S(1)}, bf16[2,6,6,1024]{3,2,1,0:T(8,128)(2,1)S(1)}, u32[]{:S(2)}, u32[]{:S(2)}) collective-permute-start(bf16[2,6,6,1024]{3,2,1,0:T(8,128)(2,1)S(1)} %get-tuple-element.88), channel_id=1, source_target_pairs={{1,0},{2,1},{3,2},{4,3},{5,4},{6,5},{7,6},{0,7},{9,8},{10,9},{11,1... | collective-permute-start | bytes 442376 | tf_op jit(solution)/shard_map/ppermute | solution.py:21
  152.0 1.1 copy-start.5
  164.7 3.3 %copy-start.9 = (bf16[144,16,64]{2,1,0:T(8,128)(2,1)S(1)}, bf16[144,16,64]{2,1,0:T(8,128)(2,1)}, u32[]{:S(2)}) copy-start(bf16[144,16,64]{2,1,0:T(8,128)(2,1)} %reshape.289) | copy-start | bytes 884740
  170.9 2.1 %copy-start.6 = (bf16[2,6,6,1024]{3,2,1,0:T(8,128)(2,1)S(1)}, bf16[2,6,6,1024]{3,2,1,0:T(8,128)(2,1)}, u32[]{:S(2)}) copy-start(bf16[2,6,6,1024]{3,2,1,0:T(8,128)(2,1)} %copy-done.5) | copy-start | bytes 442372
  175.2 7.1 %collective-permute-start.26 = (bf16[2,6,6,1024]{3,2,1,0:T(8,128)(2,1)S(1)}, bf16[2,6,6,1024]{3,2,1,0:T(8,128)(2,1)S(1)}, u32[]{:S(2)}, u32[]{:S(2)}) collective-permute-start(bf16[2,6,6,1024]{3,2,1,0:T(8,128)(2,1)S(1)} %get-tuple-element.85), channel_id=1, source_target_pairs={{7,0},{0,1},{1,2},{2,3},{3,4},{4,5},{5,6},{6,7},{15,8},{8,9},{9,10... | collective-permute-start | bytes 442376 | tf_op jit(solution)/shard_map/ppermute | solution.py:21
  182.4 6.6 %collective-permute-start.27 = (bf16[2,3,12,1024]{3,2,1,0:T(8,128)(2,1)S(1)}, bf16[2,3,12,1024]{3,2,1,0:T(8,128)(2,1)S(1)}, u32[]{:S(2)}, u32[]{:S(2)}) collective-permute-start(bf16[2,3,12,1024]{3,2,1,0:T(8,128)(2,1)S(1)} %fusion.62), channel_id=1, source_target_pairs={{24,0},{0,8},{8,16},{16,24},{25,1},{1,9},{9,17},{17,25},{26,2},{2,... | collective-permute-start | bytes 442376 | tf_op jit(solution)/shard_map/ppermute | solution.py:21
Sparse Core Ops, SparseCore 0:
  21.7 38.6 all-gather.1

commit v2 on v0

v2 whole, which is shorter than its diff:
```python
import math

import jax
import jax.numpy as jnp
import numpy as np
from jax import lax
from jax.experimental import pallas as pl
from jax.experimental.pallas import tpu as pltpu
from jax.sharding import PartitionSpec as P

HEADS1 = 8
HEADS2 = 16
WIN_LEVELS = 2
WIN_ROWS = 6
WIN_COLS = 12
HALF_ROWS = WIN_ROWS // 2
HALF_COLS = WIN_COLS // 2

EPSILON = 1e-05
EXCLUDED = -1e30
LANES = 128
PACK = 16
VMEM_LIMIT = 48 * 1024 * 1024
NT = (((1,), (1,)), ((), ()))


def up(count, unit):
    return -(-count // unit) * unit


def places(levels, rows, columns):
    return np.arange(levels * rows * columns).reshape(levels, rows, columns)


def regions(levels, rows, columns, row_from, column_from):
    at = places(levels, rows, columns)
    in_rows = (np.arange(rows) >= row_from) & (np.arange(rows) < row_from + HALF_ROWS)
    in_columns = (np.arange(columns) >= column_from) & (np.arange(columns) < column_from + HALF_COLS)
    picked = (
        at[:, in_rows][:, :, ~in_columns],
        at[:, ~in_rows][:, :, in_columns],
        at[:, in_rows][:, :, in_columns],
    )
    return [part.reshape(-1) for part in picked]


def window_order(levels, rows, columns):
    at = places(levels, rows, columns)
    order = []
    for band in range(rows // WIN_ROWS):
        for across in range(columns // WIN_COLS):
            r = (HALF_ROWS + WIN_ROWS * band + np.arange(WIN_ROWS)) % rows
            c = (HALF_COLS + WIN_COLS * across + np.arange(WIN_COLS)) % columns
            order.append(at[:, r][:, :, c].reshape(-1))
    return np.concatenate(order)


def matrix(sources, columns, height=None):
    out = np.zeros((height or len(sources), columns), np.float32)
    out[np.arange(len(sources)), sources] = 1
    return jnp.asarray(out, jnp.bfloat16)


def offsets(sizes):
    return np.concatenate([[0], np.cumsum([up(size, LANES) for size in sizes])]).tolist()


def replaced(count, parts, held=None):
    starts = offsets([count] + [up(len(part) + 2, PACK) for part in parts])
    source = np.arange(count) if held is None else held.copy()
    for start, part in zip(starts[1:], parts):
        source[part] = start + np.arange(len(part))
    return source, starts[-1]


def fill(stage_ref, parts):
    start = 0
    for part in parts:
        rows = part.shape[0]
        stage_ref[start : start + rows] = part[...]
        if rows % LANES:
            stage_ref[start + rows : start + up(rows, LANES)] = jnp.zeros(
                (up(rows, LANES) - rows, part.shape[1]), stage_ref.dtype
            )
        start += up(rows, LANES)


def dot(left, right):
    return jnp.dot(left, right, preferred_element_type=jnp.float32)


def dot_nt(left, right):
    return lax.dot_general(left, right, NT, preferred_element_type=jnp.float32)


def normalized(values):
    center = jnp.mean(values, axis=-1, keepdims=True)
    moved = values - center
    spread = jnp.mean(moved * moved, axis=-1, keepdims=True)
    return (moved * lax.rsqrt(spread + EPSILON)).astype(jnp.bfloat16)


def label_bias(wide, select):
    along = dot_nt(wide, select)[:1]
    down = dot_nt(select, wide)[:, :1]
    return jnp.where(down == along, 0.0, EXCLUDED)


def attend(packed_ref, mixed_ref, first, count, width, heads, bias):
    head_size = width // heads
    lane = lax.broadcasted_iota(jnp.int32, (1, LANES), 1)
    ones = jnp.ones((count, LANES), jnp.bfloat16)
    rows = slice(first, first + count)
    for start in range(0, width, LANES):
        queries = packed_ref[rows, start : start + LANES]
        keys = packed_ref[rows, width + start : width + start + LANES]
        values = packed_ref[rows, 2 * width + start : 2 * width + start + LANES]
        values = jnp.concatenate([values, ones], axis=1)
        mixed = None
        for low in range(0, LANES, head_size):
            own = (lane >= low) & (lane < low + head_size)
            chosen = jnp.where(own, 1.0 / math.sqrt(head_size), 0.0).astype(jnp.bfloat16)
            scores = dot_nt(queries * chosen, keys) + bias
            highest = jnp.max(scores, axis=-1, keepdims=True)
            expos = jnp.exp(scores - highest).astype(jnp.bfloat16)
            summed = dot(expos, values)
            result = summed[:, :LANES] / summed[:, LANES:]
            mixed = result if mixed is None else jnp.where(own, result, mixed)
        mixed_ref[rows, start : start + LANES] = mixed.astype(jnp.bfloat16)


def flat_labels(ids, spread, rows):
    flat = jnp.sum(dot(ids.astype(jnp.bfloat16), spread) * rows.astype(jnp.float32), axis=0, keepdims=True)
    return jnp.broadcast_to(flat, (8, flat.shape[1])).astype(jnp.bfloat16)


def pack_kernel(
    heights, counts, at_ref, x_ref, ids_ref, coarse_ids_ref, spread1, rows1, spread2, rows2,
    pick_lat, pick_lon, pick_both, coarse_lat, coarse_lon, coarse_both, merge_ref, qkv_ref,
    lat_ref, lon_ref, both_ref, labels_ref, coarse_labels_ref, merge_part, qkv_part, sems,
):
    corner = at_ref[0]
    copies = []
    for slot, (whole, part) in enumerate(((merge_ref, merge_part), (qkv_ref, qkv_part))):
        wide = part.shape[1]
        start = pl.multiple_of(corner * wide, LANES)
        copies.append(pltpu.make_async_copy(whole.at[:, pl.ds(start, wide)], part, sems.at[slot]))
        copies[-1].start()

    def labels_of(ref, height):
        row = lax.broadcasted_iota(jnp.int32, ref.shape, 0)
        edge = jnp.zeros(ref.shape, jnp.bool_)
        for level in range(ref.shape[0] // height):
            edge = edge | ((row >= level * height) & (row < level * height + HALF_ROWS))
        return (ref[...] * 2 + jnp.where(edge, at_ref[1], 0)).astype(jnp.float32)

    labels = flat_labels(labels_of(ids_ref, heights[0]), spread1[...], rows1[...])
    coarse_labels = flat_labels(labels_of(coarse_ids_ref, heights[1]), spread2[...], rows2[...])
    labels_ref[...] = labels
    coarse_labels_ref[...] = coarse_labels
    trio = ((pick_lat, coarse_lat, lat_ref), (pick_lon, coarse_lon, lon_ref), (pick_both, coarse_both, both_ref))
    for (pick, coarse_pick, out_ref), count in zip(trio, counts):
        height = out_ref.shape[0]
        body = dot(pick[:height], x_ref[...])
        row = lax.broadcasted_iota(jnp.int32, (height, LANES), 0)
        fine = dot_nt(labels, pick[...])[:1]
        coarse = dot_nt(coarse_labels, coarse_pick[...])[:1]
        extra = jnp.where(row == count, fine, jnp.where(row == count + 1, coarse, 0.0))
        out_ref[:, :LANES] = (body[:, :LANES] + extra).astype(out_ref.dtype)
        out_ref[:, LANES:] = body[:, LANES:].astype(out_ref.dtype)
    for copy in copies:
        copy.wait()


def wide_labels(labels_ref, packets, counts, line):
    count = labels_ref.shape[1]
    pad = up(count, LANES) - count
    parts = [labels_ref[...].astype(jnp.float32)]
    if pad:
        parts[0] = jnp.concatenate([parts[0], jnp.zeros((8, pad), jnp.float32)], axis=1)
    for packet, size in zip(packets, counts):
        block = packet[size // PACK * PACK : size // PACK * PACK + PACK, :LANES].astype(jnp.float32)
        row = lax.broadcasted_iota(jnp.int32, block.shape, 0)
        picked = jnp.sum(jnp.where(row == size % PACK + line, block, 0.0), axis=0, keepdims=True)
        parts.append(jnp.broadcast_to(picked, (8, LANES)))
    return jnp.concatenate(parts, axis=1).astype(jnp.bfloat16)


def first_kernel(
    heads, counts, x_ref, labels_ref, lat_ref, lon_ref, both_ref, select_ref, qkv_ref, out_ref,
    mid_lat, mid_lon, mid_both, skip_lat, skip_lon, skip_both,
    y_ref, mid_lat_out, mid_lon_out, mid_both_out, skip_lat_out, skip_lon_out, skip_both_out,
    stage_ref, rolled_ref, packed_ref, mixed_ref,
):
    width = x_ref.shape[1]
    window = WIN_LEVELS * WIN_ROWS * WIN_COLS
    fill(stage_ref, (x_ref, lat_ref, lon_ref, both_ref))
    wide = wide_labels(labels_ref, (lat_ref, lon_ref, both_ref), counts, 0)
    rolled = dot(select_ref[...], stage_ref[...])
    rolled_ref[...] = rolled
    packed_ref[...] = dot(normalized(rolled), qkv_ref[...]).astype(jnp.bfloat16)
    for first in range(0, x_ref.shape[0], window):
        bias = label_bias(wide, select_ref[first : first + window])
        attend(packed_ref, mixed_ref, first, window, width, heads, bias)
    y_ref[...] = (rolled_ref[...] + dot(mixed_ref[...], out_ref[...])).astype(jnp.bfloat16)
    for pick, packet in (
        (mid_lat, mid_lat_out), (mid_lon, mid_lon_out), (mid_both, mid_both_out),
        (skip_lat, skip_lat_out), (skip_lon, skip_lon_out), (skip_both, skip_both_out),
    ):
        packet[...] = dot(pick[...], y_ref[...]).astype(jnp.bfloat16)


def start_pieces(whole_ref, pieces, at_ref, sem):
    corner, side = at_ref[0], at_ref[2]
    stops, _, rows, columns = whole_ref.shape
    quarter = columns // 4
    copies = []
    for piece, (other, mask, stop) in pieces:
        start = pl.multiple_of((corner ^ mask) * quarter, LANES)
        count = piece.shape[0]
        copies.append(
            pltpu.make_async_copy(
                piece, whole_ref.at[pl.ds(stop, count), side ^ other, :, pl.ds(start, quarter)], sem.at[len(copies)]
            )
        )
        copies[-1].start()
    return copies


def piece_keys(stops):
    half = stops // 2
    keys = [(0, 0), (1, 0), (2, 0), (3, 0), (3, half)]
    return [(other, mask, stop) for other in range(2) for mask, stop in keys]


def merge_kernel(keys, at_ref, y_ref, lat_ref, lon_ref, both_ref, select_ref, *refs):
    pieces, (out_ref, stage_ref, whole_ref, sem) = refs[: len(keys)], refs[len(keys) :]
    copies = start_pieces(whole_ref, list(zip(pieces, keys)), at_ref, sem)
    fill(stage_ref, (y_ref, lat_ref, lon_ref, both_ref))
    cells = out_ref.shape[0]
    patches = [
        dot(select_ref[first : first + cells], stage_ref[...]) for first in range(0, select_ref.shape[0], cells)
    ]
    total = 1.0 / (len(patches) * y_ref.shape[1])
    center = sum(jnp.sum(patch, axis=-1, keepdims=True) for patch in patches) * total
    moved = [patch - center for patch in patches]
    spread = sum(jnp.sum(patch * patch, axis=-1, keepdims=True) for patch in moved) * total
    scale = lax.rsqrt(spread + EPSILON)
    left = jnp.concatenate([(patch * scale).astype(jnp.bfloat16) for patch in moved], axis=1)
    for copy in copies:
        copy.wait()
    stops, sides, rows, columns = whole_ref.shape
    out_ref[...] = dot(left, whole_ref[...].reshape(stops * sides * rows, columns)).astype(jnp.bfloat16)


def second_kernel(
    heads, counts, keys, at_ref, merged_ref, labels_ref, lat_ref, lon_ref, both_ref, select_ref, out_weight,
    end_lat, end_lon, end_both, *refs
):
    pieces = refs[: len(keys)]
    z_ref, lat_out, lon_out, both_out, whole_ref, packed_ref, mixed_ref, sem = refs[len(keys) :]
    copies = start_pieces(whole_ref, list(zip(pieces, keys)), at_ref, sem)
    count, width = merged_ref.shape
    merged = merged_ref[...].astype(jnp.float32)
    left = normalized(merged)
    wide = wide_labels(labels_ref, (lat_ref, lon_ref, both_ref), counts, 1)
    bias = label_bias(wide, select_ref[...])
    for copy in copies:
        copy.wait()
    stops, sides, rows, columns = whole_ref.shape
    packed_ref[...] = dot(left, whole_ref[...].reshape(stops * sides * rows, columns)).astype(jnp.bfloat16)
    attend(packed_ref, mixed_ref, 0, count, width, heads, bias)
    z_ref[...] = (merged + dot(mixed_ref[...], out_weight[...])).astype(jnp.bfloat16)
    for pick, packet in ((end_lat, lat_out), (end_lon, lon_out), (end_both, both_out)):
        packet[...] = dot(pick[...], z_ref[...]).astype(jnp.bfloat16)


def place_kernel(own_ref, lat_ref, lon_ref, both_ref, select_ref, out_ref, stage_ref):
    fill(stage_ref, (own_ref, lat_ref, lon_ref, both_ref))
    out_ref[...] = dot(select_ref[...], stage_ref[...]).astype(out_ref.dtype)


def call(kernel, outs, scratch, *operands, scalars=0, anywhere=(), outs_anywhere=()):
    spaces = []
    for number in range(len(operands)):
        space = pltpu.VMEM
        if number < scalars:
            space = pltpu.SMEM
        elif number in anywhere:
            space = pl.ANY
        spaces.append(pl.BlockSpec(memory_space=space))
    return pl.pallas_call(
        kernel,
        out_shape=[jax.ShapeDtypeStruct(shape, jnp.bfloat16) for shape in outs],
        in_specs=spaces,
        out_specs=[
            pl.BlockSpec(memory_space=pl.ANY if number in outs_anywhere else pltpu.VMEM)
            for number in range(len(outs))
        ],
        scratch_shapes=scratch,
        compiler_params=pltpu.CompilerParams(vmem_limit_bytes=VMEM_LIMIT),
    )(*operands)


def shifted(blocks, step):
    lat, lon = lax.axis_size("lat"), lax.axis_size("lon")
    return (
        lax.ppermute(blocks[0], "lat", [(i, (i + step) % lat) for i in range(lat)]),
        lax.ppermute(blocks[1], "lon", [(i, (i + step) % lon) for i in range(lon)]),
        lax.ppermute(
            blocks[2],
            ("lat", "lon"),
            [(i * lon + j, (i + step) % lat * lon + (j + step) % lon) for i in range(lat) for j in range(lon)],
        ),
    )


def exchange(block, axis, mask):
    return lax.ppermute(block, axis, [(i, i ^ mask) for i in range(lax.axis_size(axis))])


def spread_pieces(part):
    ranks = lax.axis_size("lon")
    stops = ranks // 2
    groups = [[2 * stop + side for stop in range(stops)] for side in range(2)]
    own = lax.all_gather(part, "lon", axis=0, axis_index_groups=groups)
    half = stops // 2
    first = exchange(own, "lat", 1)
    second = exchange(own, "lat", 2)
    pieces = [own, first, second, exchange(first[:half], "lat", 2), exchange(second[half:], "lat", 1)]
    return pieces + [exchange(piece, "lon", 1) for piece in pieces]


def per_device(
    tokens, level_ids, coarse_ids, first_qkv, first_out, merge_weight, second_qkv, second_out
):
    levels, height, breadth, width = tokens.shape
    _, low, narrow = coarse_ids.shape
    wider = merge_weight.shape[1]
    cells, coarse_cells = levels * height * breadth, levels * low * narrow
    window = WIN_LEVELS * WIN_ROWS * WIN_COLS
    stops = lax.axis_size("lon") // 2
    lat, lon = lax.axis_index("lat"), lax.axis_index("lon")
    at = jnp.stack([lat % 4, (lat == 0).astype(jnp.int32), lon % 2]).astype(jnp.int32)

    start = regions(levels, height, breadth, 0, 0)
    middle = regions(levels, height, breadth, HALF_ROWS, HALF_COLS)
    end = regions(levels, low, narrow, 0, 0)
    counts = [len(part) for part in start]
    packet_rows = [up(len(part) + 2, PACK) for part in start]
    end_rows = [up(len(part) + 2, PACK) for part in end]
    order = window_order(levels, height, breadth)
    inverse = np.argsort(order)
    coarse_order = np.arange(coarse_cells)

    def flat_pair(rows, columns):
        index = np.arange(rows * columns)
        return matrix(index % columns, columns).T, matrix(index // columns, rows).T

    x = tokens.reshape(cells, width)
    lat_pk, lon_pk, both_pk, labels, coarse_labels, merge_part, qkv_part = call(
        lambda *refs: pack_kernel((height, low), counts, *refs),
        [(rows, width) for rows in packet_rows]
        + [
            (8, cells),
            (8, coarse_cells),
            (merge_weight.shape[0], wider // 4),
            (second_qkv.shape[0], second_qkv.shape[1] // 4),
        ],
        [pltpu.SemaphoreType.DMA((2,))],
        at,
        x,
        level_ids.reshape(levels * height, breadth),
        coarse_ids.reshape(levels * low, narrow),
        *flat_pair(levels * height, breadth),
        *flat_pair(levels * low, narrow),
        *[matrix(part, cells, LANES) for part in start],
        *[matrix(part, coarse_cells, LANES) for part in end],
        merge_weight,
        second_qkv,
        scalars=1,
        anywhere=(14, 15),
        outs_anywhere=(5, 6),
    )
    got = shifted((lat_pk, lon_pk, both_pk), -1)
    merge_pieces = spread_pieces(merge_part)
    qkv_pieces = spread_pieces(qkv_part)
    out_whole = lax.all_gather(second_out, "lon", axis=0, tiled=True)

    source, depth = replaced(cells, start)
    select = matrix(source[order], depth)
    held = np.empty_like(order)
    held[order] = np.arange(cells)
    y, *packets = call(
        lambda *refs: first_kernel(HEADS1, counts, *refs),
        [(cells, width)] + [(rows, width) for rows in packet_rows] * 2,
        [
            pltpu.VMEM((depth, width), jnp.bfloat16),
            pltpu.VMEM((cells, width), jnp.float32),
            pltpu.VMEM((cells, 3 * width), jnp.bfloat16),
            pltpu.VMEM((cells, width), jnp.bfloat16),
        ],
        x,
        labels,
        *got,
        select,
        first_qkv,
        first_out,
        *[matrix(inverse[part], cells, rows) for part, rows in zip(middle, packet_rows)],
        *[matrix(inverse[part], cells, rows) for part, rows in zip(start, packet_rows)],
    )
    mid = shifted(packets[:3], -1)
    back = shifted(packets[3:], 1)

    source, depth = replaced(cells, middle, held)
    fine = source.reshape(levels, low, 2, narrow, 2)
    patches = [fine[:, :, r, :, c].reshape(-1) for r, c in ((0, 0), (1, 0), (0, 1), (1, 1))]
    keys = piece_keys(stops)
    whole_shape = (stops, 2, merge_weight.shape[0], wider)
    (merged,) = call(
        lambda *refs: merge_kernel(keys, *refs),
        [(coarse_cells, wider)],
        [
            pltpu.VMEM((depth, width), jnp.bfloat16),
            pltpu.VMEM(whole_shape, jnp.bfloat16),
            pltpu.SemaphoreType.DMA((len(keys),)),
        ],
        at,
        y,
        *mid,
        matrix(np.concatenate(patches), depth),
        *merge_pieces,
        scalars=1,
        anywhere=range(6, 6 + len(keys)),
    )

    source, depth = replaced(cells, start, held)
    (skip,) = call(
        place_kernel,
        [(cells, width)],
        [pltpu.VMEM((depth, width), jnp.bfloat16)],
        y,
        *back,
        matrix(source, depth),
    )

    source, depth = replaced(coarse_cells, end)
    z, *packets = call(
        lambda *refs: second_kernel(HEADS2, counts, keys, *refs),
        [(coarse_cells, wider)] + [(rows, wider) for rows in end_rows],
        [
            pltpu.VMEM((stops, 2) + second_qkv.shape, jnp.bfloat16),
            pltpu.VMEM((coarse_cells, 3 * wider), jnp.bfloat16),
            pltpu.VMEM((coarse_cells, wider), jnp.bfloat16),
            pltpu.SemaphoreType.DMA((len(keys),)),
        ],
        at,
        merged,
        coarse_labels,
        *got,
        matrix(source, depth),
        out_whole,
        *[matrix(part, coarse_cells, rows) for part, rows in zip(end, end_rows)],
        *qkv_pieces,
        scalars=1,
        anywhere=range(11, 11 + len(keys)),
    )
    done = shifted(packets, 1)
    (coarse,) = call(
        place_kernel,
        [(coarse_cells, wider)],
        [pltpu.VMEM((depth, wider), jnp.bfloat16)],
        z,
        *done,
        matrix(source, depth),
    )
    return skip.reshape(tokens.shape), coarse.reshape(levels, low, narrow, wider)


def solution(mesh):
    placed = (
        P(None, "lat", "lon", None),
        P(None, "lat", "lon"),
        P(None, "lat", "lon"),
        P(),
        P(),
        P("lon", None),
        P("lon", None),
        P("lon", None),
    )
    return jax.shard_map(
        per_device,
        mesh=mesh,
        in_specs=placed,
        out_specs=(P(None, "lat", "lon", None), P(None, "lat", "lon", None)),
        check_vma=False,
    )
```

time: 184 us -> 179 us (0.973)
  waiting for transfers between devices: 88.8 us -> 45.1 us
  blocking collectives: 0 us -> 42.3 us
  matrix products: 30.9 us -> 0 us
  Pallas kernels: 0 us -> 20.9 us
  starting transfers between devices: 17.3 us -> 27.8 us
  other arithmetic: 5.87 us -> 0.08 us
    all_gather x3 -> x1, waiting for transfers between devices: 45.7 us -> 0.01 us  [per_device(): out_whole = lax.all_gather(second_out, 'lon', axis=0, tiled=True)]
    all_gather x0 -> x2, blocking collectives: none -> 42.3 us  [spread_pieces(): own = lax.all_gather(part, 'lon', axis=0, axis_index_groups=groups)]
    unnamed x23 -> x91, local copies, waits for them, and re-layouts: 1.07 us -> 27.3 us
    pallas_call x0 -> x6, Pallas kernels: none -> 20.9 us  [call(): pl.pallas_call(kernel, out_shape=[jax.ShapeDtypeStruct(shape, jnp.bfloat1...]
    dot_general x8 -> x0, matrix products: 20.1 us -> none  [the longest x3 10.1 us: add_rows(): return jnp.dot(left, piece, preferred_element_type=jnp.float32)]
    sub x3 -> x0, matrix products: 10.7 us -> none  [window_softmax(): expos = jnp.exp(scores - highest)]
    ppermute x12 -> x30, starting transfers between devices: 17.2 us -> 27.8 us  [the longest x18 10.2 us: exchange(): lax.ppermute(block, axis, [(i, i ^ mask) for i in range(lax.axis_size(axi...]
    convert_element_type x9 -> x0, local copies, waits for them, and re-layouts: 7.85 us -> none  [the longest x3 5.03 us: normalized(): widened = values.astype(jnp.float32)]
  transfers between devices with their start and end apart: 15 -> 31, of which waited for: 11 -> 12; matrix products, arithmetic and copies ran while one was open for 31% -> 1% of each run, Pallas kernels for 0% -> 11%
where the time goes in v2:
time: 179 us; the launch traced here: 178 us
  waiting for transfers between devices  45.1 us (25%)
  blocking collectives  42.3 us (24%)
  starting transfers between devices  27.8 us (16%)
  local copies, waits for them, and re-layouts  27.5 us (15%)
  Pallas kernels  20.9 us (12%)
  between operations  14.4 us (8%)
    all_gather x2, blocking collectives, spread_pieces(): own = lax.all_gather(part, 'lon', axis=0, axis_index_groups=groups)  42.3 us
    ppermute x18, waiting for transfers between devices, exchange(): lax.ppermute(block, axis, [(i, i ^ mask) for i in range(lax.axis_size(axi...  32.4 us
    unnamed x91, local copies, waits for them, and re-layouts  27.3 us
    pallas_call x6, Pallas kernels, call(): pl.pallas_call(kernel, out_shape=[jax.ShapeDtypeStruct(shape, jnp.bfloat1...  20.9 us
    ppermute x18, starting transfers between devices, exchange(): lax.ppermute(block, axis, [(i, i ^ mask) for i in range(lax.axis_size(axi...  10.2 us
    ppermute x4, waiting for transfers between devices, shifted(): lax.ppermute(blocks[2], ('lat', 'lon'), [(i * lon + j, (i + step) % lat *...  9.09 us
    ppermute x4, starting transfers between devices, shifted(): lax.ppermute(blocks[2], ('lat', 'lon'), [(i * lon + j, (i + step) % lat *...  8.5 us
    ppermute x4, starting transfers between devices, shifted(): lax.ppermute(blocks[1], 'lon', [(i, (i + step) % lon) for i in range(lon)])  4.92 us
  transfers between devices with their start and end apart: 31, of which 12 were waited for; matrix products, arithmetic and copies ran while one was open for 1% of the time, Pallas kernels for 11%

profile of v2, /device:TPU:0, one launch (start us, length us, event | category | flops | bytes accessed | tf_op | source)
XLA Modules:
  0.0 178.0 jit_solution(7595927019568800498)
XLA Ops:
  9.5 1.1 copy-done
  10.5 1.1 copy-done.7
  11.7 1.0 copy-done.10
  12.7 0.9 copy-done.23
  13.6 0.9 copy-done.24
  14.5 0.9 copy-done.25
  15.4 0.8 copy-done.30
  16.3 0.8 copy-done.31
  17.1 0.8 copy-done.32
  18.0 0.8 copy-done.35
  18.7 0.8 copy-done.36
  20.9 1.3 shard_map.311
  22.2 24.3 %all-gather = bf16[1024,256]{1,0:T(8,128)(2,1)S(1)} all-gather(bf16[256,256]{1,0:T(8,128)(2,1)S(1)} %get-tuple-element.31), channel_id=2, replica_groups={{0,2,4,6},{1,3,5,7},{8,10,12,14},{9,11,13,15},{16,18,20,22},{17,19,21,2..., dimensions={0}, use_global_device_ids=true | all-gather | bytes 655360 | tf_op jit(solution)/shard_map/all_gather | solution.py:326
  46.5 1.5 collective-permute-start.9
  48.0 1.5 collective-permute-start.10
  50.0 0.9 collective-permute-start.1
  50.9 3.3 %collective-permute-start.2 = (bf16[48,512]{1,0:T(8,128)(2,1)S(1)}, bf16[48,512]{1,0:T(8,128)(2,1)S(1)}, u32[]{:S(2)}, u32[]{:S(2)}) collective-permute-start(bf16[48,512]{1,0:T(8,128)(2,1)S(1)} %get-tuple-element.23), channel_id=1, source_target_pairs={{0,31},{1,24},{2,25},{3,26},{4,27},{5,28},{6,29},{7,30},{8,7},{9,0... | collective-permute-start | bytes 147464 | tf_op jit(solution)/shard_map/ppermute | solution.py:310
  54.2 5.5 %collective-permute-done.2.refs_4_.refs_5_ = bf16[48,512]{1,0:T(8,128)(2,1)S(1)} collective-permute-done((bf16[48,512]{1,0:T(8,128)(2,1)S(1)}, bf16[48,512]{1,0:T(8,128)(2,1)S(1)}, u32[]{:S(2)}, u32[]{:S(2)}) %collective-permute-start.2) | collective-permute-done | bytes 49184 | tf_op jit(solution)/shard_map/ppermute | solution.py:310
  59.7 2.3 %collective-permute-done.refs_2_.refs_3_ = bf16[112,512]{1,0:T(8,128)(2,1)S(1)} collective-permute-done((bf16[112,512]{1,0:T(8,128)(2,1)S(1)}, bf16[112,512]{1,0:T(8,128)(2,1)S(1)}, u32[]{:S(2)}, u32[]{:S(2)}) %collective-permute-start) | collective-permute-done | bytes 114720 | tf_op jit(solution)/shard_map/ppermute | solution.py:308
  62.1 1.0 copy-done.9
  63.1 0.9 copy-done.28
  64.1 0.9 copy-done.29
  65.0 6.5 %shard_map.312 = (bf16[576,512]{1,0:T(8,128)(2,1)S(1)}, bf16[112,512]{1,0:T(8,128)(2,1)S(1)}, bf16[112,512]{1,0:T(8,128)(2,1)S(1)}, bf16[48,512]{1,0:T(8,128)(2,...) custom-call(bf16[576,512]{1,0:T(8,128)(2,1)S(1)} %bitcast.12, ...), custom_call_target="tpu_custom_call" | custom-call | tf_op jit(solution)/shard_map/pallas_call | solution.py:292
  71.5 2.6 %collective-permute-start.8 = (bf16[48,512]{1,0:T(8,128)(2,1)S(1)}, bf16[48,512]{1,0:T(8,128)(2,1)S(1)}, u32[]{:S(2)}, u32[]{:S(2)}) collective-permute-start(bf16[48,512]{1,0:T(8,128)(2,1)S(1)} %get-tuple-element.30), channel_id=1, source_target_pairs={{0,31},{1,24},{2,25},{3,26},{4,27},{5,28},{6,29},{7,30},{8,7},{9,0... | collective-permute-start | bytes 147464 | tf_op jit(solution)/shard_map/ppermute | solution.py:310
  74.1 1.0 collective-permute-start.6
  75.9 3.4 %collective-permute-start.7 = (bf16[112,512]{1,0:T(8,128)(2,1)S(1)}, bf16[112,512]{1,0:T(8,128)(2,1)S(1)}, u32[]{:S(2)}, u32[]{:S(2)}) collective-permute-start(bf16[112,512]{1,0:T(8,128)(2,1)S(1)} %get-tuple-element.29), channel_id=1, source_target_pairs={{0,7},{1,0},{2,1},{3,2},{4,3},{5,4},{6,5},{7,6},{8,15},{9,8},{10,9... | collective-permute-start | bytes 344072 | tf_op jit(solution)/shard_map/ppermute | solution.py:309
  79.2 18.1 %all-gather.1 = bf16[512,768]{1,0:T(8,128)(2,1)S(1)} all-gather(bf16[128,768]{1,0:T(8,128)(2,1)S(1)} %get-tuple-element.33), channel_id=3, replica_groups={{0,2,4,6},{1,3,5,7},{8,10,12,14},{9,11,13,15},{16,18,20,22},{17,19,21,2..., dimensions={0}, use_global_device_ids=true | all-gather | bytes 983040 | tf_op jit(solution)/shard_map/all_gather | solution.py:326
  97.3 2.5 %collective-permute-start.18 = (bf16[4,128,768]{2,1,0:T(8,128)(2,1)S(1)}, bf16[4,128,768]{2,1,0:T(8,128)(2,1)S(1)}, u32[]{:S(2)}, u32[]{:S(2)}) collective-permute-start(bf16[4,128,768]{2,1,0:T(8,128)(2,1)S(1)} %bitcast.7), channel_id=1, source_target_pairs={{0,8},{8,0},{16,24},{24,16},{1,9},{9,1},{17,25},{25,17},{2,10},{10... | collective-permute-start | bytes 2359304 | tf_op jit(solution)/shard_map/ppermute | solution.py:319
  100.3 1.7 collective-permute-start.11
  102.2 19.7 %collective-permute-done.11.refs_9_ = bf16[2,256,256]{2,1,0:T(8,128)(2,1)S(1)} collective-permute-done((bf16[2,256,256]{2,1,0:T(8,128)(2,1)S(1)}, bf16[2,256,256]{2,1,0:T(8,128)(2,1)S(1)}, u32[]{:S(2)}, u32[]{:S(2)}) %collective-permute-start.11) | collective-permute-done | bytes 262176 | tf_op jit(solution)/shard_map/ppermute | solution.py:319
  124.7 9.5 %collective-permute-done.20.refs_14_ = bf16[2,128,768]{2,1,0:T(8,128)(2,1)S(1)} collective-permute-done((bf16[2,128,768]{2,1,0:T(8,128)(2,1)S(1)}, bf16[2,128,768]{2,1,0:T(8,128)(2,1)S(1)}, u32[]{:S(2)}, u32[]{:S(2)}) %collective-permute-start.20) | collective-permute-done | bytes 393248 | tf_op jit(solution)/shard_map/ppermute | solution.py:319
  134.1 0.8 collective-permute-done.21.refs_15_
  135.4 1.6 collective-permute-done.17.refs_15_
  137.1 2.1 %collective-permute-start.3 = (bf16[112,512]{1,0:T(8,128)(2,1)}, bf16[112,512]{1,0:T(8,128)(2,1)}, u32[]{:S(2)}, u32[]{:S(2)}) collective-permute-start(bf16[112,512]{1,0:T(8,128)(2,1)} %get-tuple-element.25), channel_id=1, source_target_pairs={{0,8},{8,16},{16,24},{24,0},{1,9},{9,17},{17,25},{25,1},{2,10},{10... | collective-permute-start | bytes 344072 | tf_op jit(solution)/shard_map/ppermute | solution.py:308
  139.7 3.9 %shard_map.314.refs_1_ = bf16[144,1024]{1,0:T(8,128)(2,1)S(1)} custom-call(s32[3]{0:T(128)S(1)} %pad_add_fusion.refs_0_, bf16[576,512]{1,0:T(8,128)(2,1)S(1)} %get-tuple-element.24.own_ref.refs_1_, bf16[112,512]{1,0:T(8,128)(2,1)S(1)} %collective-permute-done.6.refs_2_, bf16[112,512]{1,0:T(8,128)(2,1)S(1)} %collective-permute-done.7.refs_3_, ...), custom_call_target="tpu_custom_call" | custom-call | tf_op jit(solution)/shard_map/pallas_call | solution.py:292
  144.4 0.8 copy-done.19
  145.2 1.1 copy-done.6
  146.3 0.9 copy-done.12
  147.2 1.0 copy-done.14
  148.2 1.0 copy-done.16
  149.2 1.0 copy-done.18
  150.2 1.0 copy-done.20
  151.2 0.8 copy-done.22
  154.2 6.2 %shard_map.315 = (bf16[144,1024]{1,0:T(8,128)(2,1)S(1)}, bf16[48,1024]{1,0:T(8,128)(2,1)S(1)}, bf16[48,1024]{1,0:T(8,128)(2,1)S(1)}, bf16[48,1024]{1,0:T(8,128)(2,1)S(1)}) custom-call(s32[3]{0:T(128)S(1)} %pad_add_fusion.refs_0_, bf16[144,1024]{1,0:T(8,128)(2,1)S(1)} %shard_map.314.refs_1_, bf16[8,144]{1,0:T(8,128)(2,1)S(1)} %get-tuple-element.32.refs_2_, ...), custom_call_target="tpu_custom_call" | custom-call | tf_op jit(solution)/shard_map/pallas_call | solution.py:292
  161.1 2.5 %collective-permute-start.29 = (bf16[48,1024]{1,0:T(8,128)(2,1)S(1)}, bf16[48,1024]{1,0:T(8,128)(2,1)S(1)}, u32[]{:S(2)}, u32[]{:S(2)}) collective-permute-start(bf16[48,1024]{1,0:T(8,128)(2,1)S(1)} %get-tuple-element.37), channel_id=1, source_target_pairs={{0,9},{1,10},{2,11},{3,12},{4,13},{5,14},{6,15},{7,8},{8,17},{9,18... | collective-permute-start | bytes 294920 | tf_op jit(solution)/shard_map/ppermute | solution.py:310
  163.6 2.5 %shard_map.313 = bf16[576,512]{1,0:T(8,128)(2,1)} custom-call(bf16[576,512]{1,0:T(8,128)(2,1)S(1)} %get-tuple-element.24.own_ref.refs_1_, bf16[112,512]{1,0:T(8,128)(2,1)} %collective-permute-done.3.lat_ref, bf16[112,512]{1,0:T(8,128)(2,1)} %collective-permute-done.4.lon_ref, bf16[48,512]{1,0:T(8,128)(2,1)} %collective-permute-done.5.both_ref, ...), custom_call_target="tpu_custom_call" | custom-call | tf_op jit(solution)/shard_map/pallas_call | solution.py:292
  166.8 2.9 %collective-permute-done.29.both_ref = bf16[48,1024]{1,0:T(8,128)(2,1)S(1)} collective-permute-done((bf16[48,1024]{1,0:T(8,128)(2,1)S(1)}, bf16[48,1024]{1,0:T(8,128)(2,1)S(1)}, u32[]{:S(2)}, u32[]{:S(2)}) %collective-permute-start.29) | collective-permute-done | bytes 98336 | tf_op jit(solution)/shard_map/ppermute | solution.py:310
  170.2 1.0 copy.39
  (122 shorter events, 14.1 us)
Async XLA Ops:
  7.2 138.0 %all-gather.4.cloned.1.call-start = ((), (), s32[]{:S(2)}) async-start(), calls=%async_computation | async-start | bytes 2359296 | tf_op jit(solution)/shard_map/all_gather | solution.py:388
  7.2 54.8 %copy-start.27 = (bf16[112,576]{1,0:T(8,128)(2,1)S(1)}, bf16[112,576]{1,0:T(8,128)(2,1)}, u32[]{:S(2)}) copy-start(bf16[112,576]{1,0:T(8,128)(2,1)} %constant.90.clone.refs_9_) | copy-start | bytes 387076
  7.2 54.8 %copy-start.33 = (bf16[48,576]{1,0:T(8,128)(2,1)S(1)}, bf16[48,576]{1,0:T(8,128)(2,1)}, u32[]{:S(2)}) copy-start(bf16[48,576]{1,0:T(8,128)(2,1)} %constant.91.clone.refs_10_) | copy-start | bytes 165892
  7.2 54.8 %copy-start.34 = (bf16[48,576]{1,0:T(8,128)(2,1)S(1)}, bf16[48,576]{1,0:T(8,128)(2,1)}, u32[]{:S(2)}) copy-start(bf16[48,576]{1,0:T(8,128)(2,1)} %constant.94.clone.refs_13_) | copy-start | bytes 165892
  7.9 54.2 %copy-start.26 = (bf16[112,576]{1,0:T(8,128)(2,1)S(1)}, bf16[112,576]{1,0:T(8,128)(2,1)}, u32[]{:S(2)}) copy-start(bf16[112,576]{1,0:T(8,128)(2,1)} %constant.89.clone.refs_8_) | copy-start | bytes 387076
  20.9 41.2 %copy-start.1 = (bf16[2,12,24,512]{3,2,1,0:T(8,128)(2,1)S(1)}, bf16[2,12,24,512]{3,2,1,0:T(8,128)(2,1)}, u32[]{:S(2)}) copy-start(bf16[2,12,24,512]{3,2,1,0:T(8,128)(2,1)} %param.32) | copy-start | bytes 1769476
  20.9 41.2 %copy-start.2 = (bf16[512,1536]{1,0:T(8,128)(2,1)S(1)}, bf16[512,1536]{1,0:T(8,128)(2,1)}, u32[]{:S(2)}) copy-start(bf16[512,1536]{1,0:T(8,128)(2,1)} %refs_6_.2) | copy-start | bytes 4718596
  20.9 41.2 %copy-start.4 = (bf16[576,1024]{1,0:T(8,128)(2,1)S(1)}, bf16[576,1024]{1,0:T(8,128)(2,1)}, u32[]{:S(2)}) copy-start(bf16[576,1024]{1,0:T(8,128)(2,1)} %constant.88.clone.refs_5_) | copy-start | bytes 3538948
  46.5 53.3 %collective-permute-start.9 = (bf16[4,256,256]{2,1,0:T(8,128)(2,1)S(1)}, bf16[4,256,256]{2,1,0:T(8,128)(2,1)S(1)}, u32[]{:S(2)}, u32[]{:S(2)}) collective-permute-start(bf16[4,256,256]{2,1,0:T(8,128)(2,1)S(1)} %bitcast.13), channel_id=1, source_target_pairs={{0,8},{8,0},{16,24},{24,16},{1,9},{9,1},{17,25},{25,17},{2,10},{10... | collective-permute-start | bytes 1572872 | tf_op jit(solution)/shard_map/ppermute | solution.py:319
  48.0 52.3 %collective-permute-start.10 = (bf16[4,256,256]{2,1,0:T(8,128)(2,1)S(1)}, bf16[4,256,256]{2,1,0:T(8,128)(2,1)S(1)}, u32[]{:S(2)}, u32[]{:S(2)}) collective-permute-start(bf16[4,256,256]{2,1,0:T(8,128)(2,1)S(1)} %bitcast.14), channel_id=1, source_target_pairs={{0,16},{8,24},{16,0},{24,8},{1,17},{9,25},{17,1},{25,9},{2,18},{10... | collective-permute-start | bytes 1572872 | tf_op jit(solution)/shard_map/ppermute | solution.py:319
  49.5 12.5 %collective-permute-start = (bf16[112,512]{1,0:T(8,128)(2,1)S(1)}, bf16[112,512]{1,0:T(8,128)(2,1)S(1)}, u32[]{:S(2)}, u32[]{:S(2)}) collective-permute-start(bf16[112,512]{1,0:T(8,128)(2,1)S(1)} %get-tuple-element.21), channel_id=1, source_target_pairs={{0,24},{8,0},{16,8},{24,16},{1,25},{9,1},{17,9},{25,17},{2,26},{10... | collective-permute-start | bytes 344072 | tf_op jit(solution)/shard_map/ppermute | solution.py:308
  50.0 12.1 %collective-permute-start.1 = (bf16[112,512]{1,0:T(8,128)(2,1)S(1)}, bf16[112,512]{1,0:T(8,128)(2,1)S(1)}, u32[]{:S(2)}, u32[]{:S(2)}) collective-permute-start(bf16[112,512]{1,0:T(8,128)(2,1)S(1)} %get-tuple-element.22), channel_id=1, source_target_pairs={{0,7},{1,0},{2,1},{3,2},{4,3},{5,4},{6,5},{7,6},{8,15},{9,8},{10,9... | collective-permute-start | bytes 344072 | tf_op jit(solution)/shard_map/ppermute | solution.py:309
  50.9 8.8 %collective-permute-start.2 = (bf16[48,512]{1,0:T(8,128)(2,1)S(1)}, bf16[48,512]{1,0:T(8,128)(2,1)S(1)}, u32[]{:S(2)}, u32[]{:S(2)}) collective-permute-start(bf16[48,512]{1,0:T(8,128)(2,1)S(1)} %get-tuple-element.23), channel_id=1, source_target_pairs={{0,31},{1,24},{2,25},{3,26},{4,27},{5,28},{6,29},{7,30},{8,7},{9,0... | collective-permute-start | bytes 147464 | tf_op jit(solution)/shard_map/ppermute | solution.py:310
  59.7 11.8 %copy-start.21 = (bf16[48,512]{1,0:T(8,128)(2,1)}, bf16[48,512]{1,0:T(8,128)(2,1)S(1)}, u32[]{:S(2)}) copy-start(bf16[48,512]{1,0:T(8,128)(2,1)S(1)} %collective-permute-done.2.refs_4_.refs_5_) | copy-start | bytes 147460
  62.0 9.5 %copy-start.11 = (bf16[112,512]{1,0:T(8,128)(2,1)}, bf16[112,512]{1,0:T(8,128)(2,1)S(1)}, u32[]{:S(2)}) copy-start(bf16[112,512]{1,0:T(8,128)(2,1)S(1)} %collective-permute-done.1.refs_3_.refs_4_) | copy-start | bytes 344068
  71.5 4.4 %collective-permute-start.8 = (bf16[48,512]{1,0:T(8,128)(2,1)S(1)}, bf16[48,512]{1,0:T(8,128)(2,1)S(1)}, u32[]{:S(2)}, u32[]{:S(2)}) collective-permute-start(bf16[48,512]{1,0:T(8,128)(2,1)S(1)} %get-tuple-element.30), channel_id=1, source_target_pairs={{0,31},{1,24},{2,25},{3,26},{4,27},{5,28},{6,29},{7,30},{8,7},{9,0... | collective-permute-start | bytes 147464 | tf_op jit(solution)/shard_map/ppermute | solution.py:310
  74.1 27.9 %collective-permute-start.13 = (bf16[4,256,256]{2,1,0:T(8,128)(2,1)S(1)}, bf16[4,256,256]{2,1,0:T(8,128)(2,1)S(1)}, u32[]{:S(2)}, u32[]{:S(2)}) collective-permute-start(bf16[4,256,256]{2,1,0:T(8,128)(2,1)S(1)} %bitcast.15), channel_id=1, source_target_pairs={{0,1},{1,0},{2,3},{3,2},{4,5},{5,4},{6,7},{7,6},{8,9},{9,8},{10,11... | collective-permute-start | bytes 1572872 | tf_op jit(solution)/shard_map/ppermute | solution.py:319
  74.1 23.2 %collective-permute-start.6 = (bf16[112,512]{1,0:T(8,128)(2,1)S(1)}, bf16[112,512]{1,0:T(8,128)(2,1)S(1)}, u32[]{:S(2)}, u32[]{:S(2)}) collective-permute-start(bf16[112,512]{1,0:T(8,128)(2,1)S(1)} %get-tuple-element.28), channel_id=1, source_target_pairs={{0,24},{8,0},{16,8},{24,16},{1,25},{9,1},{17,9},{25,17},{2,26},{10... | collective-permute-start | bytes 344072 | tf_op jit(solution)/shard_map/ppermute | solution.py:308
  75.9 24.3 %collective-permute-start.7 = (bf16[112,512]{1,0:T(8,128)(2,1)S(1)}, bf16[112,512]{1,0:T(8,128)(2,1)S(1)}, u32[]{:S(2)}, u32[]{:S(2)}) collective-permute-start(bf16[112,512]{1,0:T(8,128)(2,1)S(1)} %get-tuple-element.29), channel_id=1, source_target_pairs={{0,7},{1,0},{2,1},{3,2},{4,3},{5,4},{6,5},{7,6},{8,15},{9,8},{10,9... | collective-permute-start | bytes 344072 | tf_op jit(solution)/shard_map/ppermute | solution.py:309
  97.3 25.1 %collective-permute-start.18 = (bf16[4,128,768]{2,1,0:T(8,128)(2,1)S(1)}, bf16[4,128,768]{2,1,0:T(8,128)(2,1)S(1)}, u32[]{:S(2)}, u32[]{:S(2)}) collective-permute-start(bf16[4,128,768]{2,1,0:T(8,128)(2,1)S(1)} %bitcast.7), channel_id=1, source_target_pairs={{0,8},{8,0},{16,24},{24,16},{1,9},{9,1},{17,25},{25,17},{2,10},{10... | collective-permute-start | bytes 2359304 | tf_op jit(solution)/shard_map/ppermute | solution.py:319
  99.8 22.6 %collective-permute-start.19 = (bf16[4,128,768]{2,1,0:T(8,128)(2,1)S(1)}, bf16[4,128,768]{2,1,0:T(8,128)(2,1)S(1)}, u32[]{:S(2)}, u32[]{:S(2)}) collective-permute-start(bf16[4,128,768]{2,1,0:T(8,128)(2,1)S(1)} %bitcast.8), channel_id=1, source_target_pairs={{0,16},{8,24},{16,0},{24,8},{1,17},{9,25},{17,1},{25,9},{2,18},{10... | collective-permute-start | bytes 2359304 | tf_op jit(solution)/shard_map/ppermute | solution.py:319
  100.2 22.8 %collective-permute-start.22 = (bf16[4,128,768]{2,1,0:T(8,128)(2,1)S(1)}, bf16[4,128,768]{2,1,0:T(8,128)(2,1)S(1)}, u32[]{:S(2)}, u32[]{:S(2)}) collective-permute-start(bf16[4,128,768]{2,1,0:T(8,128)(2,1)S(1)} %bitcast.9), channel_id=1, source_target_pairs={{0,1},{1,0},{2,3},{3,2},{4,5},{5,4},{6,7},{7,6},{8,9},{9,8},{10,11... | collective-permute-start | bytes 2359304 | tf_op jit(solution)/shard_map/ppermute | solution.py:319
  100.3 21.6 %collective-permute-start.11 = (bf16[2,256,256]{2,1,0:T(8,128)(2,1)S(1)}, bf16[2,256,256]{2,1,0:T(8,128)(2,1)S(1)}, u32[]{:S(2)}, u32[]{:S(2)}) collective-permute-start(bf16[2,256,256]{2,1,0:T(8,128)(2,1)S(1)} %slice.16), channel_id=1, source_target_pairs={{0,16},{8,24},{16,0},{24,8},{1,17},{9,25},{17,1},{25,9},{2,18},{10... | collective-permute-start | bytes 786440 | tf_op jit(solution)/shard_map/ppermute | solution.py:319
  102.1 19.8 %collective-permute-start.12 = (bf16[2,256,256]{2,1,0:T(8,128)(2,1)S(1)}, bf16[2,256,256]{2,1,0:T(8,128)(2,1)S(1)}, u32[]{:S(2)}, u32[]{:S(2)}) collective-permute-start(bf16[2,256,256]{2,1,0:T(8,128)(2,1)S(1)} %slice.17), channel_id=1, source_target_pairs={{0,8},{8,0},{16,24},{24,16},{1,9},{9,1},{17,25},{25,17},{2,10},{10... | collective-permute-start | bytes 786440 | tf_op jit(solution)/shard_map/ppermute | solution.py:319
  121.9 1.9 %collective-permute-start.14 = (bf16[4,256,256]{2,1,0:T(8,128)(2,1)S(1)}, bf16[4,256,256]{2,1,0:T(8,128)(2,1)S(1)}, u32[]{:S(2)}, u32[]{:S(2)}) collective-permute-start(bf16[4,256,256]{2,1,0:T(8,128)(2,1)S(1)} %collective-permute-done.9.refs_7_), channel_id=1, source_target_pairs={{0,1},{1,0},{2,3},{3,2},{4,5},{5,4},{6,7},{7,6},{8,9},{9,8},{10,11... | collective-permute-start | bytes 1572872 | tf_op jit(solution)/shard_map/ppermute | solution.py:319
  121.9 2.7 %collective-permute-start.15 = (bf16[4,256,256]{2,1,0:T(8,128)(2,1)S(1)}, bf16[4,256,256]{2,1,0:T(8,128)(2,1)S(1)}, u32[]{:S(2)}, u32[]{:S(2)}) collective-permute-start(bf16[4,256,256]{2,1,0:T(8,128)(2,1)S(1)} %collective-permute-done.10.refs_8_), channel_id=1, source_target_pairs={{0,1},{1,0},{2,3},{3,2},{4,5},{5,4},{6,7},{7,6},{8,9},{9,8},{10,11... | collective-permute-start | bytes 1572872 | tf_op jit(solution)/shard_map/ppermute | solution.py:319
  122.4 14.7 %collective-permute-start.23 = (bf16[4,128,768]{2,1,0:T(8,128)(2,1)S(1)}, bf16[4,128,768]{2,1,0:T(8,128)(2,1)S(1)}, u32[]{:S(2)}, u32[]{:S(2)}) collective-permute-start(bf16[4,128,768]{2,1,0:T(8,128)(2,1)S(1)} %collective-permute-done.18.refs_12_), channel_id=1, source_target_pairs={{0,1},{1,0},{2,3},{3,2},{4,5},{5,4},{6,7},{7,6},{8,9},{9,8},{10,11... | collective-permute-start | bytes 2359304 | tf_op jit(solution)/shard_map/ppermute | solution.py:319
  122.5 16.7 %collective-permute-start.24 = (bf16[4,128,768]{2,1,0:T(8,128)(2,1)S(1)}, bf16[4,128,768]{2,1,0:T(8,128)(2,1)S(1)}, u32[]{:S(2)}, u32[]{:S(2)}) collective-permute-start(bf16[4,128,768]{2,1,0:T(8,128)(2,1)S(1)} %collective-permute-done.19.refs_13_), channel_id=1, source_target_pairs={{0,1},{1,0},{2,3},{3,2},{4,5},{5,4},{6,7},{7,6},{8,9},{9,8},{10,11... | collective-permute-start | bytes 2359304 | tf_op jit(solution)/shard_map/ppermute | solution.py:319
  123.0 20.6 %copy-start.5 = (bf16[4,128,768]{2,1,0:T(8,128)(2,1)}, bf16[4,128,768]{2,1,0:T(8,128)(2,1)S(1)}, u32[]{:S(2)}) copy-start(bf16[4,128,768]{2,1,0:T(8,128)(2,1)S(1)} %collective-permute-done.22.refs_16_) | copy-start | bytes 2359300
  123.0 11.2 %collective-permute-start.20 = (bf16[2,128,768]{2,1,0:T(8,128)(2,1)S(1)}, bf16[2,128,768]{2,1,0:T(8,128)(2,1)S(1)}, u32[]{:S(2)}, u32[]{:S(2)}) collective-permute-start(bf16[2,128,768]{2,1,0:T(8,128)(2,1)S(1)} %slice.18), channel_id=1, source_target_pairs={{0,16},{8,24},{16,0},{24,8},{1,17},{9,25},{17,1},{25,9},{2,18},{10... | collective-permute-start | bytes 1179656 | tf_op jit(solution)/shard_map/ppermute | solution.py:319
  123.8 11.2 %collective-permute-start.21 = (bf16[2,128,768]{2,1,0:T(8,128)(2,1)S(1)}, bf16[2,128,768]{2,1,0:T(8,128)(2,1)S(1)}, u32[]{:S(2)}, u32[]{:S(2)}) collective-permute-start(bf16[2,128,768]{2,1,0:T(8,128)(2,1)S(1)} %slice.19), channel_id=1, source_target_pairs={{0,8},{8,0},{16,24},{24,16},{1,9},{9,1},{17,25},{25,17},{2,10},{10... | collective-permute-start | bytes 1179656 | tf_op jit(solution)/shard_map/ppermute | solution.py:319
  124.5 10.4 %collective-permute-start.16 = (bf16[2,256,256]{2,1,0:T(8,128)(2,1)S(1)}, bf16[2,256,256]{2,1,0:T(8,128)(2,1)S(1)}, u32[]{:S(2)}, u32[]{:S(2)}) collective-permute-start(bf16[2,256,256]{2,1,0:T(8,128)(2,1)S(1)} %collective-permute-done.11.refs_9_), channel_id=1, source_target_pairs={{0,1},{1,0},{2,3},{3,2},{4,5},{5,4},{6,7},{7,6},{8,9},{9,8},{10,11... | collective-permute-start | bytes 786440 | tf_op jit(solution)/shard_map/ppermute | solution.py:319
  134.1 9.5 %copy-start.13 = (bf16[2,128,768]{2,1,0:T(8,128)(2,1)}, bf16[2,128,768]{2,1,0:T(8,128)(2,1)S(1)}, u32[]{:S(2)}) copy-start(bf16[2,128,768]{2,1,0:T(8,128)(2,1)S(1)} %collective-permute-done.20.refs_14_) | copy-start | bytes 1179652
  134.1 9.5 %collective-permute-start.25 = (bf16[2,128,768]{2,1,0:T(8,128)(2,1)S(1)}, bf16[2,128,768]{2,1,0:T(8,128)(2,1)S(1)}, u32[]{:S(2)}, u32[]{:S(2)}) collective-permute-start(bf16[2,128,768]{2,1,0:T(8,128)(2,1)S(1)} %collective-permute-done.20.refs_14_), channel_id=1, source_target_pairs={{0,1},{1,0},{2,3},{3,2},{4,5},{5,4},{6,7},{7,6},{8,9},{9,8},{10,11... | collective-permute-start | bytes 1179656 | tf_op jit(solution)/shard_map/ppermute | solution.py:319
  134.9 8.7 %copy-start.15 = (bf16[2,128,768]{2,1,0:T(8,128)(2,1)}, bf16[2,128,768]{2,1,0:T(8,128)(2,1)S(1)}, u32[]{:S(2)}) copy-start(bf16[2,128,768]{2,1,0:T(8,128)(2,1)S(1)} %collective-permute-done.21.refs_15_) | copy-start | bytes 1179652
  134.9 9.5 %collective-permute-start.26 = (bf16[2,128,768]{2,1,0:T(8,128)(2,1)S(1)}, bf16[2,128,768]{2,1,0:T(8,128)(2,1)S(1)}, u32[]{:S(2)}, u32[]{:S(2)}) collective-permute-start(bf16[2,128,768]{2,1,0:T(8,128)(2,1)S(1)} %collective-permute-done.21.refs_15_), channel_id=1, source_target_pairs={{0,1},{1,0},{2,3},{3,2},{4,5},{5,4},{6,7},{7,6},{8,9},{9,8},{10,11... | collective-permute-start | bytes 1179656 | tf_op jit(solution)/shard_map/ppermute | solution.py:319
  134.9 2.1 %collective-permute-start.17 = (bf16[2,256,256]{2,1,0:T(8,128)(2,1)S(1)}, bf16[2,256,256]{2,1,0:T(8,128)(2,1)S(1)}, u32[]{:S(2)}, u32[]{:S(2)}) collective-permute-start(bf16[2,256,256]{2,1,0:T(8,128)(2,1)S(1)} %collective-permute-done.12.refs_10_), channel_id=1, source_target_pairs={{0,1},{1,0},{2,3},{3,2},{4,5},{5,4},{6,7},{7,6},{8,9},{9,8},{10,11... | collective-permute-start | bytes 786440 | tf_op jit(solution)/shard_map/ppermute | solution.py:319
  137.0 24.1 %collective-permute-start.5 = (bf16[48,512]{1,0:T(8,128)(2,1)}, bf16[48,512]{1,0:T(8,128)(2,1)}, u32[]{:S(2)}, u32[]{:S(2)}) collective-permute-start(bf16[48,512]{1,0:T(8,128)(2,1)} %get-tuple-element.27), channel_id=1, source_target_pairs={{0,9},{1,10},{2,11},{3,12},{4,13},{5,14},{6,15},{7,8},{8,17},{9,18... | collective-permute-start | bytes 147464 | tf_op jit(solution)/shard_map/ppermute | solution.py:310
  137.1 6.5 %copy-start.42 = (bf16[4,128,768]{2,1,0:T(8,128)(2,1)}, bf16[4,128,768]{2,1,0:T(8,128)(2,1)S(1)}, u32[]{:S(2)}) copy-start(bf16[4,128,768]{2,1,0:T(8,128)(2,1)S(1)} %collective-permute-done.23.refs_17_) | copy-start | bytes 2359300
  137.1 26.5 %collective-permute-start.3 = (bf16[112,512]{1,0:T(8,128)(2,1)}, bf16[112,512]{1,0:T(8,128)(2,1)}, u32[]{:S(2)}, u32[]{:S(2)}) collective-permute-start(bf16[112,512]{1,0:T(8,128)(2,1)} %get-tuple-element.25), channel_id=1, source_target_pairs={{0,8},{8,16},{16,24},{24,0},{1,9},{9,17},{17,25},{25,1},{2,10},{10... | collective-permute-start | bytes 344072 | tf_op jit(solution)/shard_map/ppermute | solution.py:308
  139.2 4.4 %copy-start.43 = (bf16[4,128,768]{2,1,0:T(8,128)(2,1)}, bf16[4,128,768]{2,1,0:T(8,128)(2,1)S(1)}, u32[]{:S(2)}) copy-start(bf16[4,128,768]{2,1,0:T(8,128)(2,1)S(1)} %collective-permute-done.24.refs_18_) | copy-start | bytes 2359300
  139.2 24.4 %collective-permute-start.4 = (bf16[112,512]{1,0:T(8,128)(2,1)}, bf16[112,512]{1,0:T(8,128)(2,1)}, u32[]{:S(2)}, u32[]{:S(2)}) collective-permute-start(bf16[112,512]{1,0:T(8,128)(2,1)} %get-tuple-element.26), channel_id=1, source_target_pairs={{0,1},{1,2},{2,3},{3,4},{4,5},{5,6},{6,7},{7,0},{8,9},{9,10},{10,1... | collective-permute-start | bytes 344072 | tf_op jit(solution)/shard_map/ppermute | solution.py:309
  139.7 5.5 %copy-start.8 = (bf16[144,640]{1,0:T(8,128)(2,1)S(1)}, bf16[144,640]{1,0:T(8,128)(2,1)}, u32[]{:S(2)}) copy-start(bf16[144,640]{1,0:T(8,128)(2,1)} %constant.97.clone.refs_6_.select_ref) | copy-start | bytes 552964
  145.2 1.1 copy-start.6
  154.2 9.4 %copy-start.3 = (bf16[576,1024]{1,0:T(8,128)(2,1)S(1)}, bf16[576,1024]{1,0:T(8,128)(2,1)}, u32[]{:S(2)}) copy-start(bf16[576,1024]{1,0:T(8,128)(2,1)} %constant.96.clone.select_ref) | copy-start | bytes 3538948
  160.4 6.2 %collective-permute-start.27 = (bf16[48,1024]{1,0:T(8,128)(2,1)S(1)}, bf16[48,1024]{1,0:T(8,128)(2,1)S(1)}, u32[]{:S(2)}, u32[]{:S(2)}) collective-permute-start(bf16[48,1024]{1,0:T(8,128)(2,1)S(1)} %get-tuple-element.35), channel_id=1, source_target_pairs={{0,8},{8,16},{16,24},{24,0},{1,9},{9,17},{17,25},{25,1},{2,10},{10... | collective-permute-start | bytes 294920 | tf_op jit(solution)/shard_map/ppermute | solution.py:308
  161.0 5.8 %collective-permute-start.28 = (bf16[48,1024]{1,0:T(8,128)(2,1)S(1)}, bf16[48,1024]{1,0:T(8,128)(2,1)S(1)}, u32[]{:S(2)}, u32[]{:S(2)}) collective-permute-start(bf16[48,1024]{1,0:T(8,128)(2,1)S(1)} %get-tuple-element.36), channel_id=1, source_target_pairs={{0,1},{1,2},{2,3},{3,4},{4,5},{5,6},{6,7},{7,0},{8,9},{9,10},{10,1... | collective-permute-start | bytes 294920 | tf_op jit(solution)/shard_map/ppermute | solution.py:309
  161.1 8.6 %collective-permute-start.29 = (bf16[48,1024]{1,0:T(8,128)(2,1)S(1)}, bf16[48,1024]{1,0:T(8,128)(2,1)S(1)}, u32[]{:S(2)}, u32[]{:S(2)}) collective-permute-start(bf16[48,1024]{1,0:T(8,128)(2,1)S(1)} %get-tuple-element.37), channel_id=1, source_target_pairs={{0,9},{1,10},{2,11},{3,12},{4,13},{5,14},{6,15},{7,8},{8,17},{9,18... | collective-permute-start | bytes 294920 | tf_op jit(solution)/shard_map/ppermute | solution.py:310
  (27 other events, 23.7 us)
Sparse Core Ops, SparseCore 0:
  9.6 40.2 all-gather.3

commit v3 on v2

v3 whole, which is shorter than its diff:
```python
import math

import jax
import jax.numpy as jnp
import numpy as np
from jax import lax
from jax.experimental import pallas as pl
from jax.experimental.pallas import tpu as pltpu
from jax.sharding import PartitionSpec as P

HEADS1 = 8
HEADS2 = 16
WIN_LEVELS = 2
WIN_ROWS = 6
WIN_COLS = 12
HALF_ROWS = WIN_ROWS // 2
HALF_COLS = WIN_COLS // 2

EPSILON = 1e-05
EXCLUDED = -1e30
LANES = 128
PACK = 16
VMEM_LIMIT = 32 * 1024 * 1024
NT = (((1,), (1,)), ((), ()))


def up(count, unit):
    return -(-count // unit) * unit


def places(levels, rows, columns):
    return np.arange(levels * rows * columns).reshape(levels, rows, columns)


def regions(levels, rows, columns, row_from, column_from):
    at = places(levels, rows, columns)
    in_rows = (np.arange(rows) >= row_from) & (np.arange(rows) < row_from + HALF_ROWS)
    in_columns = (np.arange(columns) >= column_from) & (np.arange(columns) < column_from + HALF_COLS)
    picked = (
        at[:, in_rows][:, :, ~in_columns],
        at[:, ~in_rows][:, :, in_columns],
        at[:, in_rows][:, :, in_columns],
    )
    return [part.reshape(-1) for part in picked]


def window_order(levels, rows, columns):
    at = places(levels, rows, columns)
    order = []
    for band in range(rows // WIN_ROWS):
        for across in range(columns // WIN_COLS):
            r = (HALF_ROWS + WIN_ROWS * band + np.arange(WIN_ROWS)) % rows
            c = (HALF_COLS + WIN_COLS * across + np.arange(WIN_COLS)) % columns
            order.append(at[:, r][:, :, c].reshape(-1))
    return np.concatenate(order)


def matrix(sources, columns, height=None):
    out = np.zeros((height or len(sources), columns), np.float32)
    out[np.arange(len(sources)), sources] = 1
    return jnp.asarray(out, jnp.bfloat16)


def offsets(sizes):
    return np.concatenate([[0], np.cumsum([up(size, LANES) for size in sizes])]).tolist()


def replaced(count, parts, held=None):
    starts = offsets([count] + [up(len(part) + 2, PACK) for part in parts])
    source = np.arange(count) if held is None else held.copy()
    for start, part in zip(starts[1:], parts):
        source[part] = start + np.arange(len(part))
    return source, starts[-1]


def fill(stage_ref, parts, held=0):
    start = 0
    for part in parts:
        rows = held if part is None else part.shape[0]
        if part is not None:
            stage_ref[start : start + rows] = part[...]
        if rows % LANES:
            stage_ref[start + rows : start + up(rows, LANES)] = jnp.zeros(
                (up(rows, LANES) - rows, stage_ref.shape[1]), stage_ref.dtype
            )
        start += up(rows, LANES)


def dot(left, right):
    return jnp.dot(left, right, preferred_element_type=jnp.float32)


def dot_nt(left, right):
    return lax.dot_general(left, right, NT, preferred_element_type=jnp.float32)


def normalized(values):
    center = jnp.mean(values, axis=-1, keepdims=True)
    moved = values - center
    spread = jnp.mean(moved * moved, axis=-1, keepdims=True)
    return (moved * lax.rsqrt(spread + EPSILON)).astype(jnp.bfloat16)


def label_bias(wide, select):
    along = dot_nt(wide, select)[:1]
    down = dot_nt(select, wide)[:, :1]
    return jnp.where(down == along, 0.0, EXCLUDED)


def attend(packed_ref, mixed_ref, first, count, width, heads, bias):
    head_size = width // heads
    lane = lax.broadcasted_iota(jnp.int32, (1, LANES), 1)
    ones = jnp.ones((count, LANES), jnp.bfloat16)
    rows = slice(first, first + count)
    for start in range(0, width, LANES):
        queries = packed_ref[rows, start : start + LANES]
        keys = packed_ref[rows, width + start : width + start + LANES]
        values = packed_ref[rows, 2 * width + start : 2 * width + start + LANES]
        values = jnp.concatenate([values, ones], axis=1)
        mixed = None
        for low in range(0, LANES, head_size):
            own = (lane >= low) & (lane < low + head_size)
            chosen = jnp.where(own, 1.0 / math.sqrt(head_size), 0.0).astype(jnp.bfloat16)
            scores = dot_nt(queries * chosen, keys) + bias
            highest = jnp.max(scores, axis=-1, keepdims=True)
            expos = jnp.exp(scores - highest).astype(jnp.bfloat16)
            summed = dot(expos, values)
            result = summed[:, :LANES] / summed[:, LANES:]
            mixed = result if mixed is None else jnp.where(own, result, mixed)
        mixed_ref[rows, start : start + LANES] = mixed.astype(jnp.bfloat16)


def fetch(sems, *pairs):
    copies = [pltpu.make_async_copy(source, target, sems.at[n]) for n, (source, target) in enumerate(pairs)]
    for copy in copies:
        copy.start()
    return copies


def flat_labels(ids_ref, edge, spread):
    levels, rows, columns = ids_ref.shape
    total = 0.0
    for level in range(levels):
        row = lax.broadcasted_iota(jnp.int32, (rows, columns), 0)
        labels = ids_ref[level] * 2 + jnp.where(row < HALF_ROWS, edge, 0)
        wide = dot(labels.astype(jnp.float32).astype(jnp.bfloat16), spread)
        place = lax.broadcasted_iota(jnp.int32, wide.shape, 1)
        low = (level * rows + lax.broadcasted_iota(jnp.int32, wide.shape, 0)) * columns
        own = (place >= low) & (place < low + columns)
        total += jnp.sum(jnp.where(own, wide, 0.0), axis=0, keepdims=True)
    return jnp.broadcast_to(total, (8, total.shape[1])).astype(jnp.bfloat16)


def pack_kernel(
    counts, at_ref, x_hbm, ids_hbm, coarse_ids_hbm, fine_hbm, coarse_hbm, *refs
):
    wholes, refs = refs[:3], refs[3:]
    outs, labels_ref, coarse_labels_ref, parts = refs[:3], refs[3], refs[4], refs[5:8]
    x_ref, ids_ref, coarse_ids_ref, fine_ref, coarse_ref, sems = refs[8:]
    corner, edge = at_ref[0], at_ref[1]
    loads = fetch(
        sems,
        (ids_hbm, ids_ref),
        (coarse_ids_hbm, coarse_ids_ref),
        (coarse_hbm, coarse_ref),
        (fine_hbm, fine_ref),
        (x_hbm, x_ref),
    )
    copies = []
    for whole, part in zip(wholes, parts):
        wide = part.shape[1]
        start = pl.multiple_of(corner * wide, LANES)
        copies.append(
            pltpu.make_async_copy(whole.at[:, pl.ds(start, wide)], part, sems.at[len(loads) + len(copies)])
        )
        copies[-1].start()
    for load in loads[:4]:
        load.wait()
    picks = 3 * LANES
    labels = flat_labels(ids_ref, edge, fine_ref[picks : picks + ids_ref.shape[2]])
    coarse_labels = flat_labels(coarse_ids_ref, edge, coarse_ref[picks : picks + coarse_ids_ref.shape[2]])
    labels_ref[...] = labels
    coarse_labels_ref[...] = coarse_labels
    loads[4].wait()
    for number, (out_ref, count) in enumerate(zip(outs, counts)):
        height = out_ref.shape[0]
        first = number * LANES
        body = dot(fine_ref[first : first + height], x_ref[...])
        row = lax.broadcasted_iota(jnp.int32, (height, LANES), 0)
        fine = dot_nt(labels, fine_ref[first : first + LANES])[:1]
        coarse = dot_nt(coarse_labels, coarse_ref[first : first + LANES])[:1]
        extra = jnp.where(row == count, fine, jnp.where(row == count + 1, coarse, 0.0))
        out_ref[:, :LANES] = (body[:, :LANES] + extra).astype(out_ref.dtype)
        out_ref[:, LANES:] = body[:, LANES:].astype(out_ref.dtype)
    for copy in copies:
        copy.wait()


def wide_labels(labels_ref, packets, counts, line):
    count = labels_ref.shape[1]
    pad = up(count, LANES) - count
    parts = [labels_ref[...].astype(jnp.float32)]
    if pad:
        parts[0] = jnp.concatenate([parts[0], jnp.zeros((8, pad), jnp.float32)], axis=1)
    for packet, size in zip(packets, counts):
        block = packet[size // PACK * PACK : size // PACK * PACK + PACK, :LANES].astype(jnp.float32)
        row = lax.broadcasted_iota(jnp.int32, block.shape, 0)
        picked = jnp.sum(jnp.where(row == size % PACK + line, block, 0.0), axis=0, keepdims=True)
        parts.append(jnp.broadcast_to(picked, (8, LANES)))
    return jnp.concatenate(parts, axis=1).astype(jnp.bfloat16)


def first_kernel(
    heads, counts, x_hbm, select_hbm, qkv_hbm, out_hbm, pick_hbm,
    labels_ref, lat_ref, lon_ref, both_ref, y_ref, *refs,
):
    packets, refs = refs[:6], refs[6:]
    select_ref, qkv_ref, out_ref, pick_ref, stage_ref, rolled_ref, packed_ref, mixed_ref, sems = refs
    cells, width = x_hbm.shape
    window = WIN_LEVELS * WIN_ROWS * WIN_COLS
    loads = fetch(
        sems,
        (x_hbm, stage_ref.at[pl.ds(0, cells)]),
        (select_hbm, select_ref),
        (qkv_hbm, qkv_ref),
        (out_hbm, out_ref),
        (pick_hbm, pick_ref),
    )
    fill(stage_ref, (None, lat_ref, lon_ref, both_ref), cells)
    wide = wide_labels(labels_ref, (lat_ref, lon_ref, both_ref), counts, 0)
    loads[0].wait()
    loads[1].wait()
    rolled = dot(select_ref[...], stage_ref[...])
    rolled_ref[...] = rolled
    loads[2].wait()
    packed_ref[...] = dot(normalized(rolled), qkv_ref[...]).astype(jnp.bfloat16)
    for first in range(0, cells, window):
        bias = label_bias(wide, select_ref[first : first + window])
        attend(packed_ref, mixed_ref, first, window, width, heads, bias)
    loads[3].wait()
    y_ref[...] = (rolled_ref[...] + dot(mixed_ref[...], out_ref[...])).astype(jnp.bfloat16)
    loads[4].wait()
    first = 0
    for packet in packets:
        height = packet.shape[0]
        packet[...] = dot(pick_ref[first : first + height], y_ref[...]).astype(jnp.bfloat16)
        first += height


def join_kernel(*refs):
    parts, (out_ref, sems) = refs[:-2], refs[-2:]
    copies = fetch(sems, *[(part, out_ref.at[number]) for number, part in enumerate(parts)])
    for copy in copies:
        copy.wait()


def start_pieces(whole_ref, pieces, at_ref, sems):
    corner, side, here = at_ref[0], at_ref[2], at_ref[3]
    stops, _, _, columns = whole_ref.shape
    quarter = columns // 4
    copies = []
    for number, piece in enumerate(pieces):
        other, mask = number // 5, number % 5 - 1
        held = whole_ref.at[:, side ^ other]
        if mask < 0:
            pairs = [(piece, held.at[here])]
        else:
            start = pl.multiple_of((corner ^ mask) * quarter, LANES)
            pairs = [
                (piece.at[back - 1], held.at[lax.rem(here + (stops - back), stops), :, pl.ds(start, quarter)])
                for back in range(1, stops)
            ]
        for source, target in pairs:
            copies.append(pltpu.make_async_copy(source, target, sems.at[len(copies)]))
            copies[-1].start()
    return copies


def piece_copies(stops):
    return 2 * (1 + 4 * (stops - 1))


def flat(whole_ref):
    stops, sides, rows, columns = whole_ref.shape
    return whole_ref[...].reshape(stops * sides * rows, columns)


def merge_kernel(at_ref, select_hbm, *refs):
    pieces, (y_ref, lat_ref, lon_ref, both_ref, out_ref) = refs[:10], refs[10:15]
    select_ref, stage_ref, whole_ref, sems, piece_sems = refs[15:]
    loads = fetch(sems, (select_hbm, select_ref))
    copies = start_pieces(whole_ref, pieces, at_ref, piece_sems)
    fill(stage_ref, (y_ref, lat_ref, lon_ref, both_ref))
    cells = out_ref.shape[0]
    loads[0].wait()
    patches = [
        dot(select_ref[first : first + cells], stage_ref[...]) for first in range(0, select_ref.shape[0], cells)
    ]
    total = 1.0 / (len(patches) * y_ref.shape[1])
    center = sum(jnp.sum(patch, axis=-1, keepdims=True) for patch in patches) * total
    moved = [patch - center for patch in patches]
    spread = sum(jnp.sum(patch * patch, axis=-1, keepdims=True) for patch in moved) * total
    scale = lax.rsqrt(spread + EPSILON)
    left = jnp.concatenate([(patch * scale).astype(jnp.bfloat16) for patch in moved], axis=1)
    for copy in copies:
        copy.wait()
    out_ref[...] = dot(left, flat(whole_ref)).astype(jnp.bfloat16)


def second_kernel(heads, counts, at_ref, select_hbm, *refs):
    pieces, (merged_ref, labels_ref, lat_ref, lon_ref, both_ref, mixed_ref) = refs[:10], refs[10:16]
    select_ref, whole_ref, packed_ref, sems, piece_sems = refs[16:]
    loads = fetch(sems, (select_hbm, select_ref))
    copies = start_pieces(whole_ref, pieces, at_ref, piece_sems)
    count, width = merged_ref.shape
    left = normalized(merged_ref[...].astype(jnp.float32))
    wide = wide_labels(labels_ref, (lat_ref, lon_ref, both_ref), counts, 1)
    loads[0].wait()
    bias = label_bias(wide, select_ref[...])
    for copy in copies:
        copy.wait()
    packed_ref[...] = dot(left, flat(whole_ref)).astype(jnp.bfloat16)
    attend(packed_ref, mixed_ref, 0, count, width, heads, bias)


def close_kernel(at_ref, pick_hbm, *refs):
    pieces, (merged_ref, mixed_ref, z_ref), packets = refs[:10], refs[10:13], refs[13:16]
    pick_ref, whole_ref, sems, piece_sems = refs[16:]
    copies = fetch(sems, (pick_hbm, pick_ref)) + start_pieces(whole_ref, pieces, at_ref, piece_sems)
    for copy in copies:
        copy.wait()
    result = merged_ref[...].astype(jnp.float32) + dot(mixed_ref[...], flat(whole_ref))
    z_ref[...] = result.astype(jnp.bfloat16)
    first = 0
    for packet in packets:
        height = packet.shape[0]
        packet[...] = dot(pick_ref[first : first + height], z_ref[...]).astype(jnp.bfloat16)
        first += height


def place_kernel(select_hbm, own_ref, lat_ref, lon_ref, both_ref, out_ref, select_ref, stage_ref, sems):
    loads = fetch(sems, (select_hbm, select_ref))
    fill(stage_ref, (own_ref, lat_ref, lon_ref, both_ref))
    loads[0].wait()
    out_ref[...] = dot(select_ref[...], stage_ref[...]).astype(out_ref.dtype)


def call(kernel, outs, scratch, scalars=(), hbm=(), vmem=(), hbm_outs=()):
    spaces = [pltpu.SMEM] * len(scalars) + [pltpu.HBM] * len(hbm) + [pltpu.VMEM] * len(vmem)
    return pl.pallas_call(
        kernel,
        out_shape=[jax.ShapeDtypeStruct(shape, jnp.bfloat16) for shape in outs],
        in_specs=[pl.BlockSpec(memory_space=space) for space in spaces],
        out_specs=[
            pl.BlockSpec(memory_space=pltpu.HBM if number in hbm_outs else pltpu.VMEM)
            for number in range(len(outs))
        ],
        scratch_shapes=scratch,
        compiler_params=pltpu.CompilerParams(vmem_limit_bytes=VMEM_LIMIT),
    )(*scalars, *hbm, *vmem)


def shifted(blocks, step):
    lat, lon = lax.axis_size("lat"), lax.axis_size("lon")
    return (
        lax.ppermute(blocks[0], "lat", [(i, (i + step) % lat) for i in range(lat)]),
        lax.ppermute(blocks[1], "lon", [(i, (i + step) % lon) for i in range(lon)]),
        lax.ppermute(
            blocks[2],
            ("lat", "lon"),
            [(i * lon + j, (i + step) % lat * lon + (j + step) % lon) for i in range(lat) for j in range(lon)],
        ),
    )


def exchange(block, axis, mask):
    return lax.ppermute(block, axis, [(i, i ^ mask) for i in range(lax.axis_size(axis))])


def spread_pieces(shard, part, by_first):
    ranks = lax.axis_size("lon")
    stops = ranks // 2
    far = [
        lax.ppermute(part, "lon", [(i, (i + 2 * back) % ranks) for i in range(ranks)]) for back in range(1, stops)
    ]
    (near,) = call(
        join_kernel,
        [(stops - 1,) + part.shape],
        [pltpu.SemaphoreType.DMA((stops - 1,))],
        hbm=far,
        hbm_outs=(0,),
    )
    first = exchange(near, "lat", 1)
    second = exchange(near, "lat", 2)
    third = exchange(first, "lat", 2) if by_first else exchange(second, "lat", 1)
    pieces = [shard, near, first, second, third]
    return pieces + [exchange(piece, "lon", 1) for piece in pieces]


def dma(count):
    return pltpu.SemaphoreType.DMA((count,))


def bf16(*shape):
    return pltpu.VMEM(shape, jnp.bfloat16)


def per_device(
    tokens, level_ids, coarse_ids, first_qkv, first_out, merge_weight, second_qkv, second_out
):
    levels, height, breadth, width = tokens.shape
    _, low, narrow = coarse_ids.shape
    wider = merge_weight.shape[1]
    cells, coarse_cells = levels * height * breadth, levels * low * narrow
    stops = lax.axis_size("lon") // 2
    lat, lon = lax.axis_index("lat"), lax.axis_index("lon")
    at = jnp.stack([lat % 4, (lat == 0).astype(jnp.int32), lon % 2, lon // 2]).astype(jnp.int32)

    start = regions(levels, height, breadth, 0, 0)
    middle = regions(levels, height, breadth, HALF_ROWS, HALF_COLS)
    end = regions(levels, low, narrow, 0, 0)
    counts = [len(part) for part in start]
    packet_rows = [up(len(part) + 2, PACK) for part in start]
    end_rows = [up(len(part) + 2, PACK) for part in end]
    order = window_order(levels, height, breadth)
    inverse = np.argsort(order)
    weights = (merge_weight, second_qkv, second_out)

    def picks(parts, rows, columns):
        return [matrix(part, columns, count) for part, count in zip(parts, rows)]

    def spreader(columns, count):
        return matrix(np.arange(count) % columns, up(columns, PACK)).T

    fine = jnp.concatenate(picks(start, [LANES] * 3, cells) + [spreader(breadth, cells)])
    coarse = jnp.concatenate(picks(end, [LANES] * 3, coarse_cells) + [spreader(narrow, coarse_cells)])
    x = tokens.reshape(cells, width)
    *packets, labels, coarse_labels, merge_part, qkv_part, out_part = call(
        lambda *refs: pack_kernel(counts, *refs),
        [(rows, width) for rows in packet_rows]
        + [(8, cells), (8, coarse_cells)]
        + [(weight.shape[0], weight.shape[1] // 4) for weight in weights],
        [
            bf16(cells, width),
            pltpu.VMEM(level_ids.shape, jnp.int32),
            pltpu.VMEM(coarse_ids.shape, jnp.int32),
            bf16(*fine.shape),
            bf16(*coarse.shape),
            dma(8),
        ],
        scalars=(at,),
        hbm=(x, level_ids, coarse_ids, fine, coarse, *weights),
        hbm_outs=(5, 6, 7),
    )
    got = shifted(packets, -1)
    merge_pieces = spread_pieces(merge_weight, merge_part, True)
    qkv_pieces = spread_pieces(second_qkv, qkv_part, False)
    out_pieces = spread_pieces(second_out, out_part, True)

    source, depth = replaced(cells, start)
    held = np.empty_like(order)
    held[order] = np.arange(cells)
    select = matrix(source[order], depth)
    pick = jnp.concatenate(
        picks([inverse[part] for part in middle], packet_rows, cells)
        + picks([inverse[part] for part in start], packet_rows, cells)
    )
    y, *packets = call(
        lambda *refs: first_kernel(HEADS1, counts, *refs),
        [(cells, width)] + [(rows, width) for rows in packet_rows] * 2,
        [
            bf16(*select.shape),
            bf16(*first_qkv.shape),
            bf16(*first_out.shape),
            bf16(*pick.shape),
            bf16(depth, width),
            pltpu.VMEM((cells, width), jnp.float32),
            bf16(cells, 3 * width),
            bf16(cells, width),
            dma(5),
        ],
        hbm=(x, select, first_qkv, first_out, pick),
        vmem=(labels, *got),
    )
    mid = shifted(packets[:3], -1)
    back = shifted(packets[3:], 1)

    source, depth = replaced(cells, middle, held)
    fine = source.reshape(levels, low, 2, narrow, 2)
    patches = [fine[:, :, r, :, c].reshape(-1) for r, c in ((0, 0), (1, 0), (0, 1), (1, 1))]
    select = matrix(np.concatenate(patches), depth)
    (merged,) = call(
        merge_kernel,
        [(coarse_cells, wider)],
        [
            bf16(*select.shape),
            bf16(depth, width),
            bf16(stops, 2, *merge_weight.shape),
            dma(1),
            dma(piece_copies(stops)),
        ],
        scalars=(at,),
        hbm=(select, *merge_pieces),
        vmem=(y, *mid),
    )

    source, depth = replaced(cells, start, held)
    select = matrix(source, depth)
    (skip,) = call(
        place_kernel,
        [(cells, width)],
        [bf16(*select.shape), bf16(depth, width), dma(1)],
        hbm=(select,),
        vmem=(y, *back),
    )

    source, depth = replaced(coarse_cells, end)
    select = matrix(source, depth)
    (mixed,) = call(
        lambda *refs: second_kernel(HEADS2, counts, *refs),
        [(coarse_cells, wider)],
        [
            bf16(*select.shape),
            bf16(stops, 2, *second_qkv.shape),
            bf16(coarse_cells, 3 * wider),
            dma(1),
            dma(piece_copies(stops)),
        ],
        scalars=(at,),
        hbm=(select, *qkv_pieces),
        vmem=(merged, coarse_labels, *got),
    )
    pick = jnp.concatenate(picks(end, end_rows, coarse_cells))
    z, *packets = call(
        close_kernel,
        [(coarse_cells, wider)] + [(rows, wider) for rows in end_rows],
        [
            bf16(*pick.shape),
            bf16(stops, 2, *second_out.shape),
            dma(1),
            dma(piece_copies(stops)),
        ],
        scalars=(at,),
        hbm=(pick, *out_pieces),
        vmem=(merged, mixed),
    )
    done = shifted(packets, 1)
    (coarse,) = call(
        place_kernel,
        [(coarse_cells, wider)],
        [bf16(*select.shape), bf16(depth, wider), dma(1)],
        hbm=(select,),
        vmem=(z, *done),
    )
    return skip.reshape(tokens.shape), coarse.reshape(levels, low, narrow, wider)


def solution(mesh):
    placed = (
        P(None, "lat", "lon", None),
        P(None, "lat", "lon"),
        P(None, "lat", "lon"),
        P(),
        P(),
        P("lon", None),
        P("lon", None),
        P("lon", None),
    )
    return jax.shard_map(
        per_device,
        mesh=mesh,
        in_specs=placed,
        out_specs=(P(None, "lat", "lon", None), P(None, "lat", "lon", None)),
        check_vma=False,
    )
```

time: 179 us -> 133 us (0.74)
  blocking collectives: 42.3 us -> 0 us
  local copies, waits for them, and re-layouts: 27.5 us -> 11 us
  between operations: 14.4 us -> 0.92 us
  starting transfers between devices: 27.8 us -> 40.5 us
  waiting for transfers between devices: 45.1 us -> 57.3 us
  Pallas kernels: 20.9 us -> 22.9 us
    all_gather x2 -> x0, blocking collectives: 42.3 us -> none  [spread_pieces(): own = lax.all_gather(part, 'lon', axis=0, axis_index_groups=groups)]
    unnamed x91 -> x39, local copies, waits for them, and re-layouts: 27.3 us -> 10.9 us
    ppermute x0 -> x9, starting transfers between devices: none -> 13.9 us  [spread_pieces(): lax.ppermute(part, 'lon', [(i, (i + 2 * back) % ranks) for i in range(ran...]
    ppermute x18 -> x24, waiting for transfers between devices: 32.4 us -> 42 us  [exchange(): lax.ppermute(block, axis, [(i, i ^ mask) for i in range(lax.axis_size(axi...]
    ppermute x0 -> x9, waiting for transfers between devices: none -> 6.41 us  [spread_pieces(): lax.ppermute(part, 'lon', [(i, (i + 2 * back) % ranks) for i in range(ran...]
    ppermute x18 -> x24, starting transfers between devices: 10.2 us -> 14 us  [exchange(): lax.ppermute(block, axis, [(i, i ^ mask) for i in range(lax.axis_size(axi...]
    ppermute x4, starting transfers between devices: 4.92 us -> 2.34 us  [shifted(): lax.ppermute(blocks[1], 'lon', [(i, (i + step) % lon) for i in range(lon)])]
    ppermute x4, starting transfers between devices: 8.5 us -> 6.31 us  [shifted(): lax.ppermute(blocks[2], ('lat', 'lon'), [(i * lon + j, (i + step) % lat *...]
  transfers between devices with their start and end apart: 31 -> 45, of which waited for: 12 -> 13; matrix products, arithmetic and copies ran while one was open for 1% -> 0% of each run, Pallas kernels for 11% -> 15%
where the time goes in v3:
time: 133 us
  waiting for transfers between devices  57.3 us (43%)
  starting transfers between devices  40.5 us (30%)
  Pallas kernels  22.9 us (17%)
  local copies, waits for them, and re-layouts  11 us (8%)
    ppermute x24, waiting for transfers between devices, exchange(): lax.ppermute(block, axis, [(i, i ^ mask) for i in range(lax.axis_size(axi...  42 us
    pallas_call x10, Pallas kernels, call(): pl.pallas_call(kernel, out_shape=[jax.ShapeDtypeStruct(shape, jnp.bfloat1...  22.9 us
    ppermute x24, starting transfers between devices, exchange(): lax.ppermute(block, axis, [(i, i ^ mask) for i in range(lax.axis_size(axi...  14 us
    ppermute x9, starting transfers between devices, spread_pieces(): lax.ppermute(part, 'lon', [(i, (i + 2 * back) % ranks) for i in range(ran...  13.9 us
    unnamed x39, local copies, waits for them, and re-layouts  10.9 us
    ppermute x4, waiting for transfers between devices, shifted(): lax.ppermute(blocks[2], ('lat', 'lon'), [(i * lon + j, (i + step) % lat *...  6.99 us
    ppermute x9, waiting for transfers between devices, spread_pieces(): lax.ppermute(part, 'lon', [(i, (i + 2 * back) % ranks) for i in range(ran...  6.41 us
    ppermute x4, starting transfers between devices, shifted(): lax.ppermute(blocks[2], ('lat', 'lon'), [(i * lon + j, (i + step) % lat *...  6.31 us
  transfers between devices with their start and end apart: 45, of which 13 were waited for; matrix products, arithmetic and copies ran while one was open for 0% of the time, Pallas kernels for 15%

profile of v3, /device:TPU:0, one launch (start us, length us, event | category | flops | bytes accessed | tf_op | source)
XLA Modules:
  0.0 132.8 jit_solution(16601387399127279275)
XLA Ops:
  2.1 1.1 copy-done
  3.3 1.1 copy-done.2
  4.3 1.0 copy-done.4
  5.4 0.9 copy-done.10
  6.3 1.0 copy-done.14
  7.4 0.9 copy-done.16
  8.3 1.9 %shard_map.284 = (bf16[112,512]{1,0:T(8,128)(2,1)S(1)}, bf16[112,512]{1,0:T(8,128)(2,1)S(1)}, bf16[48,512]{1,0:T(8,128)(2,1)S(1)}, bf16[8,576]{1,0:T(8,128)(2,1)...) custom-call(s32[4]{0:T(128)S(1)} %pad_add_fusion.refs_0_.at_ref, ...), custom_call_target="tpu_custom_call" | custom-call | tf_op jit(solution)/shard_map/pallas_call | solution.py:350
  10.3 3.1 %collective-permute-start.6 = (bf16[128,256]{1,0:T(8,128)(2,1)S(1)}, bf16[128,256]{1,0:T(8,128)(2,1)S(1)}, u32[]{:S(2)}, u32[]{:S(2)}) collective-permute-start(bf16[128,256]{1,0:T(8,128)(2,1)S(1)} %get-tuple-element.29), channel_id=1, source_target_pairs={{0,2},{1,3},{2,4},{3,5},{4,6},{5,7},{6,0},{7,1},{8,10},{9,11},{10,... | collective-permute-start | bytes 196616 | tf_op jit(solution)/shard_map/ppermute | solution.py:384
  13.3 3.4 %collective-permute-start.2 = (bf16[48,512]{1,0:T(8,128)(2,1)S(1)}, bf16[48,512]{1,0:T(8,128)(2,1)S(1)}, u32[]{:S(2)}, u32[]{:S(2)}) collective-permute-start(bf16[48,512]{1,0:T(8,128)(2,1)S(1)} %get-tuple-element.24), channel_id=1, source_target_pairs={{0,31},{1,24},{2,25},{3,26},{4,27},{5,28},{6,29},{7,30},{8,7},{9,0... | collective-permute-start | bytes 147464 | tf_op jit(solution)/shard_map/ppermute | solution.py:368
  18.6 1.8 %collective-permute-start.7 = (bf16[128,256]{1,0:T(8,128)(2,1)S(1)}, bf16[128,256]{1,0:T(8,128)(2,1)S(1)}, u32[]{:S(2)}, u32[]{:S(2)}) collective-permute-start(bf16[128,256]{1,0:T(8,128)(2,1)S(1)} %get-tuple-element.29), channel_id=1, source_target_pairs={{0,4},{1,5},{2,6},{3,7},{4,0},{5,1},{6,2},{7,3},{8,12},{9,13},{10,... | collective-permute-start | bytes 196616 | tf_op jit(solution)/shard_map/ppermute | solution.py:384
  20.4 1.5 %collective-permute-start.8 = (bf16[128,256]{1,0:T(8,128)(2,1)S(1)}, bf16[128,256]{1,0:T(8,128)(2,1)S(1)}, u32[]{:S(2)}, u32[]{:S(2)}) collective-permute-start(bf16[128,256]{1,0:T(8,128)(2,1)S(1)} %get-tuple-element.29), channel_id=1, source_target_pairs={{0,6},{1,7},{2,0},{3,1},{4,2},{5,3},{6,4},{7,5},{8,14},{9,15},{10,... | collective-permute-start | bytes 196616 | tf_op jit(solution)/shard_map/ppermute | solution.py:384
  21.9 6.4 %collective-permute-done.7.refs_1_ = bf16[128,256]{1,0:T(8,128)(2,1)S(1)} collective-permute-done((bf16[128,256]{1,0:T(8,128)(2,1)S(1)}, bf16[128,256]{1,0:T(8,128)(2,1)S(1)}, u32[]{:S(2)}, u32[]{:S(2)}) %collective-permute-start.7) | collective-permute-done | bytes 65568 | tf_op jit(solution)/shard_map/ppermute | solution.py:384
  28.3 3.2 %collective-permute-start.31 = (bf16[128,768]{1,0:T(8,128)(2,1)S(1)}, bf16[128,768]{1,0:T(8,128)(2,1)S(1)}, u32[]{:S(2)}, u32[]{:S(2)}) collective-permute-start(bf16[128,768]{1,0:T(8,128)(2,1)S(1)} %get-tuple-element.34), channel_id=1, source_target_pairs={{0,2},{1,3},{2,4},{3,5},{4,6},{5,7},{6,0},{7,1},{8,10},{9,11},{10,... | collective-permute-start | bytes 589832 | tf_op jit(solution)/shard_map/ppermute | solution.py:384
  32.1 1.1 collective-permute-start.32
  33.3 2.6 %collective-permute-start.33 = (bf16[128,768]{1,0:T(8,128)(2,1)S(1)}, bf16[128,768]{1,0:T(8,128)(2,1)S(1)}, u32[]{:S(2)}, u32[]{:S(2)}) collective-permute-start(bf16[128,768]{1,0:T(8,128)(2,1)S(1)} %get-tuple-element.34), channel_id=1, source_target_pairs={{0,6},{1,7},{2,0},{3,1},{4,2},{5,3},{6,4},{7,5},{8,14},{9,15},{10,... | collective-permute-start | bytes 589832 | tf_op jit(solution)/shard_map/ppermute | solution.py:384
  35.9 1.3 copy-done.9
  37.1 1.0 copy-done.15
  38.2 7.1 %shard_map.285 = (bf16[576,512]{1,0:T(8,128)(2,1)S(1)}, bf16[112,512]{1,0:T(8,128)(2,1)S(1)}, bf16[112,512]{1,0:T(8,128)(2,1)S(1)}, bf16[48,512]{1,0:T(8,128)(2,...) custom-call(bf16[576,512]{1,0:T(8,128)(2,1)S(1)} %bitcast.7, ...), custom_call_target="tpu_custom_call" | custom-call | tf_op jit(solution)/shard_map/pallas_call | solution.py:350
  45.3 0.8 collective-permute-start.28
  46.1 4.0 %collective-permute-done.30.refs_13_ = bf16[48,512]{1,0:T(8,128)(2,1)S(1)} collective-permute-done((bf16[48,512]{1,0:T(8,128)(2,1)S(1)}, bf16[48,512]{1,0:T(8,128)(2,1)S(1)}, u32[]{:S(2)}, u32[]{:S(2)}) %collective-permute-start.30) | collective-permute-done | bytes 49184 | tf_op jit(solution)/shard_map/ppermute | solution.py:368
  50.2 3.2 %collective-permute-start.12 = (bf16[128,1024]{1,0:T(8,128)(2,1)S(1)}, bf16[128,1024]{1,0:T(8,128)(2,1)S(1)}, u32[]{:S(2)}, u32[]{:S(2)}) collective-permute-start(bf16[128,1024]{1,0:T(8,128)(2,1)S(1)} %copy-done.10), channel_id=1, source_target_pairs={{0,1},{1,0},{2,3},{3,2},{4,5},{5,4},{6,7},{7,6},{8,9},{9,8},{10,11... | collective-permute-start | bytes 786440 | tf_op jit(solution)/shard_map/ppermute | solution.py:377
  53.7 1.0 collective-permute-start.9
  54.7 1.1 collective-permute-start.10
  56.3 0.8 collective-permute-start.20
  57.1 3.9 %collective-permute-done.9.refs_2_ = bf16[3,128,256]{2,1,0:T(8,128)(2,1)S(1)} collective-permute-done((bf16[3,128,256]{2,1,0:T(8,128)(2,1)S(1)}, bf16[3,128,256]{2,1,0:T(8,128)(2,1)S(1)}, u32[]{:S(2)}, u32[]{:S(2)}) %collective-permute-start.9) | collective-permute-done | bytes 196640 | tf_op jit(solution)/shard_map/ppermute | solution.py:377
  61.7 1.3 %collective-permute-start.21 = (bf16[3,256,256]{2,1,0:T(8,128)(2,1)S(1)}, bf16[3,256,256]{2,1,0:T(8,128)(2,1)S(1)}, u32[]{:S(2)}, u32[]{:S(2)}) collective-permute-start(bf16[3,256,256]{2,1,0:T(8,128)(2,1)S(1)} %shard_map.288.refs_1_), channel_id=1, source_target_pairs={{0,16},{8,24},{16,0},{24,8},{1,17},{9,25},{17,1},{25,9},{2,18},{10... | collective-permute-start | bytes 1179656 | tf_op jit(solution)/shard_map/ppermute | solution.py:377
  63.1 0.8 shard_map.290.refs_3_
  63.8 0.8 collective-permute-start.35
  64.8 3.9 %collective-permute-done.11.refs_4_ = bf16[3,128,256]{2,1,0:T(8,128)(2,1)S(1)} collective-permute-done((bf16[3,128,256]{2,1,0:T(8,128)(2,1)S(1)}, bf16[3,128,256]{2,1,0:T(8,128)(2,1)S(1)}, u32[]{:S(2)}, u32[]{:S(2)}) %collective-permute-start.11) | collective-permute-done | bytes 196640 | tf_op jit(solution)/shard_map/ppermute | solution.py:377
  68.7 1.0 collective-permute-start.34
  69.8 7.4 %collective-permute-done.21.refs_3_ = bf16[3,256,256]{2,1,0:T(8,128)(2,1)S(1)} collective-permute-done((bf16[3,256,256]{2,1,0:T(8,128)(2,1)S(1)}, bf16[3,256,256]{2,1,0:T(8,128)(2,1)S(1)}, u32[]{:S(2)}, u32[]{:S(2)}) %collective-permute-start.21) | collective-permute-done | bytes 393248 | tf_op jit(solution)/shard_map/ppermute | solution.py:377
  77.7 11.8 %collective-permute-done.35.refs_5_ = bf16[3,128,768]{2,1,0:T(8,128)(2,1)S(1)} collective-permute-done((bf16[3,128,768]{2,1,0:T(8,128)(2,1)S(1)}, bf16[3,128,768]{2,1,0:T(8,128)(2,1)S(1)}, u32[]{:S(2)}, u32[]{:S(2)}) %collective-permute-start.35) | collective-permute-done | bytes 589856 | tf_op jit(solution)/shard_map/ppermute | solution.py:377
  89.5 1.1 collective-permute-start.36
  90.6 0.8 collective-permute-start.22
  92.0 12.5 %collective-permute-done.36.refs_6_ = bf16[3,128,768]{2,1,0:T(8,128)(2,1)S(1)} collective-permute-done((bf16[3,128,768]{2,1,0:T(8,128)(2,1)S(1)}, bf16[3,128,768]{2,1,0:T(8,128)(2,1)S(1)}, u32[]{:S(2)}, u32[]{:S(2)}) %collective-permute-start.36) | collective-permute-done | bytes 589856 | tf_op jit(solution)/shard_map/ppermute | solution.py:377
  105.1 2.0 %collective-permute-done.26.refs_8_ = bf16[3,256,256]{2,1,0:T(8,128)(2,1)S(1)} collective-permute-done((bf16[3,256,256]{2,1,0:T(8,128)(2,1)S(1)}, bf16[3,256,256]{2,1,0:T(8,128)(2,1)S(1)}, u32[]{:S(2)}, u32[]{:S(2)}) %collective-permute-start.26) | collective-permute-done | bytes 393248 | tf_op jit(solution)/shard_map/ppermute | solution.py:377
  107.8 1.4 %collective-permute-start.5 = (bf16[48,512]{1,0:T(8,128)(2,1)S(1)}, bf16[48,512]{1,0:T(8,128)(2,1)S(1)}, u32[]{:S(2)}, u32[]{:S(2)}) collective-permute-start(bf16[48,512]{1,0:T(8,128)(2,1)S(1)} %get-tuple-element.28), channel_id=1, source_target_pairs={{0,9},{1,10},{2,11},{3,12},{4,13},{5,14},{6,15},{7,8},{8,17},{9,18... | collective-permute-start | bytes 147464 | tf_op jit(solution)/shard_map/ppermute | solution.py:368
  109.2 1.4 %collective-permute-start.3 = (bf16[112,512]{1,0:T(8,128)(2,1)S(1)}, bf16[112,512]{1,0:T(8,128)(2,1)S(1)}, u32[]{:S(2)}, u32[]{:S(2)}) collective-permute-start(bf16[112,512]{1,0:T(8,128)(2,1)S(1)} %get-tuple-element.26), channel_id=1, source_target_pairs={{0,8},{8,16},{16,24},{24,0},{1,9},{9,17},{17,25},{25,1},{2,10},{10... | collective-permute-start | bytes 344072 | tf_op jit(solution)/shard_map/ppermute | solution.py:366
  110.6 1.1 collective-permute-start.4
  111.7 3.5 %shard_map.289.refs_12_.refs_10_ = bf16[144,1024]{1,0:T(8,128)(2,1)S(1)} custom-call(s32[4]{0:T(128)S(1)} %pad_add_fusion.refs_0_.at_ref, bf16[576,1024]{1,0:T(8,128)(2,1)S(1)} %copy-done.8, bf16[256,1024]{1,0:T(8,128)(2,1)S(1)} %copy-done.5, bf16[3,256,256]{2,1,0:T(8,128)(2,1)S(1)} %shard_map.288.refs_1_, ...), custom_call_target="tpu_custom_call" | custom-call | tf_op jit(solution)/shard_map/pallas_call | solution.py:350
  115.2 4.3 %shard_map.291.refs_11_ = bf16[144,1024]{1,0:T(8,128)(2,1)S(1)} custom-call(s32[4]{0:T(128)S(1)} %pad_add_fusion.refs_0_.at_ref, bf16[144,640]{1,0:T(8,128)(2,1)S(1)} %copy-done.12, bf16[128,3072]{1,0:T(8,128)(2,1)S(1)} %copy-done.1, bf16[3,128,768]{2,1,0:T(8,128)(2,1)S(1)} %shard_map.290.refs_3_, bf16[3,128,768]{2,1,0:T(8,128)(2,1)S(1)} %collective-permute-done.34.refs_4_, ...), custom_call_target="tpu_custom_call" | custom-call | tf_op jit(solution)/shard_map/pallas_call | solution.py:350
  119.6 1.9 %shard_map.292 = (bf16[144,1024]{1,0:T(8,128)(2,1)S(1)}, bf16[48,1024]{1,0:T(8,128)(2,1)S(1)}, bf16[48,1024]{1,0:T(8,128)(2,1)S(1)}, bf16[48,1024]{1,0:T(8,128)(2,1)S(1)}) custom-call(s32[4]{0:T(128)S(1)} %pad_add_fusion.refs_0_.at_ref, bf16[144,144]{1,0:T(8,128)(2,1)S(1)} %copy-done.17, bf16[128,1024]{1,0:T(8,128)(2,1)S(1)} %copy-done.11, ...), custom_call_target="tpu_custom_call" | custom-call | tf_op jit(solution)/shard_map/pallas_call | solution.py:350
  121.6 1.3 collective-permute-start.42
  123.4 1.5 %collective-permute-start.44 = (bf16[48,1024]{1,0:T(8,128)(2,1)S(1)}, bf16[48,1024]{1,0:T(8,128)(2,1)S(1)}, u32[]{:S(2)}, u32[]{:S(2)}) collective-permute-start(bf16[48,1024]{1,0:T(8,128)(2,1)S(1)} %get-tuple-element.39), channel_id=1, source_target_pairs={{0,9},{1,10},{2,11},{3,12},{4,13},{5,14},{6,15},{7,8},{8,17},{9,18... | collective-permute-start | bytes 294920 | tf_op jit(solution)/shard_map/ppermute | solution.py:368
  124.9 1.9 %shard_map.286 = bf16[576,512]{1,0:T(8,128)(2,1)} custom-call(bf16[576,1024]{1,0:T(8,128)(2,1)S(1)} %copy-done.7, bf16[576,512]{1,0:T(8,128)(2,1)S(1)} %get-tuple-element.25.own_ref.refs_10_, bf16[112,512]{1,0:T(8,128)(2,1)S(1)} %collective-permute-done.3.lat_ref, bf16[112,512]{1,0:T(8,128)(2,1)S(1)} %collective-permute-done.4.lon_ref, ...), custom_call_target="tpu_custom_call" | custom-call | tf_op jit(solution)/shard_map/pallas_call | solution.py:350
  126.8 1.3 collective-permute-done.42.lat_ref
  128.7 2.3 %collective-permute-done.44.both_ref = bf16[48,1024]{1,0:T(8,128)(2,1)S(1)} collective-permute-done((bf16[48,1024]{1,0:T(8,128)(2,1)S(1)}, bf16[48,1024]{1,0:T(8,128)(2,1)S(1)}, u32[]{:S(2)}, u32[]{:S(2)}) %collective-permute-start.44) | collective-permute-done | bytes 98336 | tf_op jit(solution)/shard_map/ppermute | solution.py:368
  131.8 1.0 copy.36
  (93 shorter events, 10.2 us)
Async XLA Ops:
  8.3 27.6 %copy-start.6 = (bf16[512,1536]{1,0:T(8,128)(2,1)S(1)}, bf16[512,1536]{1,0:T(8,128)(2,1)}, u32[]{:S(2)}) copy-start(bf16[512,1536]{1,0:T(8,128)(2,1)} %refs_2_.3) | copy-start | bytes 4718596
  8.3 27.6 %copy-start.13 = (bf16[544,576]{1,0:T(8,128)(2,1)S(1)}, bf16[544,576]{1,0:T(8,128)(2,1)}, u32[]{:S(2)}) copy-start(bf16[544,576]{1,0:T(8,128)(2,1)} %constant.107.refs_4_) | copy-start | bytes 1880068
  10.3 10.1 %collective-permute-start.6 = (bf16[128,256]{1,0:T(8,128)(2,1)S(1)}, bf16[128,256]{1,0:T(8,128)(2,1)S(1)}, u32[]{:S(2)}, u32[]{:S(2)}) collective-permute-start(bf16[128,256]{1,0:T(8,128)(2,1)S(1)} %get-tuple-element.29), channel_id=1, source_target_pairs={{0,2},{1,3},{2,4},{3,5},{4,6},{5,7},{6,0},{7,1},{8,10},{9,11},{10,... | collective-permute-start | bytes 196616 | tf_op jit(solution)/shard_map/ppermute | solution.py:384
  13.3 5.3 %collective-permute-start.2 = (bf16[48,512]{1,0:T(8,128)(2,1)S(1)}, bf16[48,512]{1,0:T(8,128)(2,1)S(1)}, u32[]{:S(2)}, u32[]{:S(2)}) collective-permute-start(bf16[48,512]{1,0:T(8,128)(2,1)S(1)} %get-tuple-element.24), channel_id=1, source_target_pairs={{0,31},{1,24},{2,25},{3,26},{4,27},{5,28},{6,29},{7,30},{8,7},{9,0... | collective-permute-start | bytes 147464 | tf_op jit(solution)/shard_map/ppermute | solution.py:368
  16.8 14.7 %collective-permute-start = (bf16[112,512]{1,0:T(8,128)(2,1)S(1)}, bf16[112,512]{1,0:T(8,128)(2,1)S(1)}, u32[]{:S(2)}, u32[]{:S(2)}) collective-permute-start(bf16[112,512]{1,0:T(8,128)(2,1)S(1)} %get-tuple-element.22), channel_id=1, source_target_pairs={{0,24},{8,0},{16,8},{24,16},{1,25},{9,1},{17,9},{25,17},{2,26},{10... | collective-permute-start | bytes 344072 | tf_op jit(solution)/shard_map/ppermute | solution.py:366
  17.3 14.8 %collective-permute-start.1 = (bf16[112,512]{1,0:T(8,128)(2,1)S(1)}, bf16[112,512]{1,0:T(8,128)(2,1)S(1)}, u32[]{:S(2)}, u32[]{:S(2)}) collective-permute-start(bf16[112,512]{1,0:T(8,128)(2,1)S(1)} %get-tuple-element.23), channel_id=1, source_target_pairs={{0,7},{1,0},{2,1},{3,2},{4,3},{5,4},{6,5},{7,6},{8,15},{9,8},{10,9... | collective-permute-start | bytes 344072 | tf_op jit(solution)/shard_map/ppermute | solution.py:367
  18.0 15.2 %collective-permute-start.17 = (bf16[256,256]{1,0:T(8,128)(2,1)S(1)}, bf16[256,256]{1,0:T(8,128)(2,1)S(1)}, u32[]{:S(2)}, u32[]{:S(2)}) collective-permute-start(bf16[256,256]{1,0:T(8,128)(2,1)S(1)} %get-tuple-element.30), channel_id=1, source_target_pairs={{0,2},{1,3},{2,4},{3,5},{4,6},{5,7},{6,0},{7,1},{8,10},{9,11},{10,... | collective-permute-start | bytes 393224 | tf_op jit(solution)/shard_map/ppermute | solution.py:384
  18.6 9.7 %collective-permute-start.7 = (bf16[128,256]{1,0:T(8,128)(2,1)S(1)}, bf16[128,256]{1,0:T(8,128)(2,1)S(1)}, u32[]{:S(2)}, u32[]{:S(2)}) collective-permute-start(bf16[128,256]{1,0:T(8,128)(2,1)S(1)} %get-tuple-element.29), channel_id=1, source_target_pairs={{0,4},{1,5},{2,6},{3,7},{4,0},{5,1},{6,2},{7,3},{8,12},{9,13},{10,... | collective-permute-start | bytes 196616 | tf_op jit(solution)/shard_map/ppermute | solution.py:384
  20.4 7.9 %collective-permute-start.8 = (bf16[128,256]{1,0:T(8,128)(2,1)S(1)}, bf16[128,256]{1,0:T(8,128)(2,1)S(1)}, u32[]{:S(2)}, u32[]{:S(2)}) collective-permute-start(bf16[128,256]{1,0:T(8,128)(2,1)S(1)} %get-tuple-element.29), channel_id=1, source_target_pairs={{0,6},{1,7},{2,0},{3,1},{4,2},{5,3},{6,4},{7,5},{8,14},{9,15},{10,... | collective-permute-start | bytes 196616 | tf_op jit(solution)/shard_map/ppermute | solution.py:384
  28.3 17.0 %collective-permute-start.18 = (bf16[256,256]{1,0:T(8,128)(2,1)S(1)}, bf16[256,256]{1,0:T(8,128)(2,1)S(1)}, u32[]{:S(2)}, u32[]{:S(2)}) collective-permute-start(bf16[256,256]{1,0:T(8,128)(2,1)S(1)} %get-tuple-element.30), channel_id=1, source_target_pairs={{0,4},{1,5},{2,6},{3,7},{4,0},{5,1},{6,2},{7,3},{8,12},{9,13},{10,... | collective-permute-start | bytes 393224 | tf_op jit(solution)/shard_map/ppermute | solution.py:384
  28.3 25.1 %collective-permute-start.31 = (bf16[128,768]{1,0:T(8,128)(2,1)S(1)}, bf16[128,768]{1,0:T(8,128)(2,1)S(1)}, u32[]{:S(2)}, u32[]{:S(2)}) collective-permute-start(bf16[128,768]{1,0:T(8,128)(2,1)S(1)} %get-tuple-element.34), channel_id=1, source_target_pairs={{0,2},{1,3},{2,4},{3,5},{4,6},{5,7},{6,0},{7,1},{8,10},{9,11},{10,... | collective-permute-start | bytes 589832 | tf_op jit(solution)/shard_map/ppermute | solution.py:384
  31.5 14.7 %collective-permute-start.19 = (bf16[256,256]{1,0:T(8,128)(2,1)S(1)}, bf16[256,256]{1,0:T(8,128)(2,1)S(1)}, u32[]{:S(2)}, u32[]{:S(2)}) collective-permute-start(bf16[256,256]{1,0:T(8,128)(2,1)S(1)} %get-tuple-element.30), channel_id=1, source_target_pairs={{0,6},{1,7},{2,0},{3,1},{4,2},{5,3},{6,4},{7,5},{8,14},{9,15},{10,... | collective-permute-start | bytes 393224 | tf_op jit(solution)/shard_map/ppermute | solution.py:384
  32.1 21.6 %collective-permute-start.32 = (bf16[128,768]{1,0:T(8,128)(2,1)S(1)}, bf16[128,768]{1,0:T(8,128)(2,1)S(1)}, u32[]{:S(2)}, u32[]{:S(2)}) collective-permute-start(bf16[128,768]{1,0:T(8,128)(2,1)S(1)} %get-tuple-element.34), channel_id=1, source_target_pairs={{0,4},{1,5},{2,6},{3,7},{4,0},{5,1},{6,2},{7,3},{8,12},{9,13},{10,... | collective-permute-start | bytes 589832 | tf_op jit(solution)/shard_map/ppermute | solution.py:384
  33.3 21.4 %collective-permute-start.33 = (bf16[128,768]{1,0:T(8,128)(2,1)S(1)}, bf16[128,768]{1,0:T(8,128)(2,1)S(1)}, u32[]{:S(2)}, u32[]{:S(2)}) collective-permute-start(bf16[128,768]{1,0:T(8,128)(2,1)S(1)} %get-tuple-element.34), channel_id=1, source_target_pairs={{0,6},{1,7},{2,0},{3,1},{4,2},{5,3},{6,4},{7,5},{8,14},{9,15},{10,... | collective-permute-start | bytes 589832 | tf_op jit(solution)/shard_map/ppermute | solution.py:384
  38.2 73.5 %copy-start.8 = (bf16[576,1024]{1,0:T(8,128)(2,1)S(1)}, bf16[576,1024]{1,0:T(8,128)(2,1)}, u32[]{:S(2)}) copy-start(bf16[576,1024]{1,0:T(8,128)(2,1)} %constant.100.clone.select_hbm) | copy-start | bytes 3538948
  45.3 10.4 %collective-permute-start.28 = (bf16[112,512]{1,0:T(8,128)(2,1)S(1)}, bf16[112,512]{1,0:T(8,128)(2,1)S(1)}, u32[]{:S(2)}, u32[]{:S(2)}) collective-permute-start(bf16[112,512]{1,0:T(8,128)(2,1)S(1)} %get-tuple-element.31), channel_id=1, source_target_pairs={{0,24},{8,0},{16,8},{24,16},{1,25},{9,1},{17,9},{25,17},{2,26},{10... | collective-permute-start | bytes 344072 | tf_op jit(solution)/shard_map/ppermute | solution.py:366
  46.1 4.0 %collective-permute-start.30 = (bf16[48,512]{1,0:T(8,128)(2,1)S(1)}, bf16[48,512]{1,0:T(8,128)(2,1)S(1)}, u32[]{:S(2)}, u32[]{:S(2)}) collective-permute-start(bf16[48,512]{1,0:T(8,128)(2,1)S(1)} %get-tuple-element.33), channel_id=1, source_target_pairs={{0,31},{1,24},{2,25},{3,26},{4,27},{5,28},{6,29},{7,30},{8,7},{9,0... | collective-permute-start | bytes 147464 | tf_op jit(solution)/shard_map/ppermute | solution.py:368
  50.2 14.4 %collective-permute-start.12 = (bf16[128,1024]{1,0:T(8,128)(2,1)S(1)}, bf16[128,1024]{1,0:T(8,128)(2,1)S(1)}, u32[]{:S(2)}, u32[]{:S(2)}) collective-permute-start(bf16[128,1024]{1,0:T(8,128)(2,1)S(1)} %copy-done.10), channel_id=1, source_target_pairs={{0,1},{1,0},{2,3},{3,2},{4,5},{5,4},{6,7},{7,6},{8,9},{9,8},{10,11... | collective-permute-start | bytes 786440 | tf_op jit(solution)/shard_map/ppermute | solution.py:377
  53.4 2.9 %collective-permute-start.29 = (bf16[112,512]{1,0:T(8,128)(2,1)S(1)}, bf16[112,512]{1,0:T(8,128)(2,1)S(1)}, u32[]{:S(2)}, u32[]{:S(2)}) collective-permute-start(bf16[112,512]{1,0:T(8,128)(2,1)S(1)} %get-tuple-element.32), channel_id=1, source_target_pairs={{0,7},{1,0},{2,1},{3,2},{4,3},{5,4},{6,5},{7,6},{8,15},{9,8},{10,9... | collective-permute-start | bytes 344072 | tf_op jit(solution)/shard_map/ppermute | solution.py:367
  53.7 7.3 %collective-permute-start.9 = (bf16[3,128,256]{2,1,0:T(8,128)(2,1)S(1)}, bf16[3,128,256]{2,1,0:T(8,128)(2,1)S(1)}, u32[]{:S(2)}, u32[]{:S(2)}) collective-permute-start(bf16[3,128,256]{2,1,0:T(8,128)(2,1)S(1)} %shard_map.287.refs_1_), channel_id=1, source_target_pairs={{0,8},{8,0},{16,24},{24,16},{1,9},{9,1},{17,25},{25,17},{2,10},{10... | collective-permute-start | bytes 589832 | tf_op jit(solution)/shard_map/ppermute | solution.py:377
  54.7 7.1 %collective-permute-start.10 = (bf16[3,128,256]{2,1,0:T(8,128)(2,1)S(1)}, bf16[3,128,256]{2,1,0:T(8,128)(2,1)S(1)}, u32[]{:S(2)}, u32[]{:S(2)}) collective-permute-start(bf16[3,128,256]{2,1,0:T(8,128)(2,1)S(1)} %shard_map.287.refs_1_), channel_id=1, source_target_pairs={{0,16},{8,24},{16,0},{24,8},{1,17},{9,25},{17,1},{25,9},{2,18},{10... | collective-permute-start | bytes 589832 | tf_op jit(solution)/shard_map/ppermute | solution.py:377
  55.8 8.1 %collective-permute-start.13 = (bf16[3,128,256]{2,1,0:T(8,128)(2,1)S(1)}, bf16[3,128,256]{2,1,0:T(8,128)(2,1)S(1)}, u32[]{:S(2)}, u32[]{:S(2)}) collective-permute-start(bf16[3,128,256]{2,1,0:T(8,128)(2,1)S(1)} %shard_map.287.refs_1_), channel_id=1, source_target_pairs={{0,1},{1,0},{2,3},{3,2},{4,5},{5,4},{6,7},{7,6},{8,9},{9,8},{10,11... | collective-permute-start | bytes 589832 | tf_op jit(solution)/shard_map/ppermute | solution.py:377
  56.3 13.5 %collective-permute-start.20 = (bf16[3,256,256]{2,1,0:T(8,128)(2,1)S(1)}, bf16[3,256,256]{2,1,0:T(8,128)(2,1)S(1)}, u32[]{:S(2)}, u32[]{:S(2)}) collective-permute-start(bf16[3,256,256]{2,1,0:T(8,128)(2,1)S(1)} %shard_map.288.refs_1_), channel_id=1, source_target_pairs={{0,8},{8,0},{16,24},{24,16},{1,9},{9,1},{17,25},{25,17},{2,10},{10... | collective-permute-start | bytes 1179656 | tf_op jit(solution)/shard_map/ppermute | solution.py:377
  61.0 7.7 %collective-permute-start.11 = (bf16[3,128,256]{2,1,0:T(8,128)(2,1)S(1)}, bf16[3,128,256]{2,1,0:T(8,128)(2,1)S(1)}, u32[]{:S(2)}, u32[]{:S(2)}) collective-permute-start(bf16[3,128,256]{2,1,0:T(8,128)(2,1)S(1)} %collective-permute-done.9.refs_2_), channel_id=1, source_target_pairs={{0,16},{8,24},{16,0},{24,8},{1,17},{9,25},{17,1},{25,9},{2,18},{10... | collective-permute-start | bytes 589832 | tf_op jit(solution)/shard_map/ppermute | solution.py:377
  61.7 15.4 %collective-permute-start.21 = (bf16[3,256,256]{2,1,0:T(8,128)(2,1)S(1)}, bf16[3,256,256]{2,1,0:T(8,128)(2,1)S(1)}, u32[]{:S(2)}, u32[]{:S(2)}) collective-permute-start(bf16[3,256,256]{2,1,0:T(8,128)(2,1)S(1)} %shard_map.288.refs_1_), channel_id=1, source_target_pairs={{0,16},{8,24},{16,0},{24,8},{1,17},{9,25},{17,1},{25,9},{2,18},{10... | collective-permute-start | bytes 1179656 | tf_op jit(solution)/shard_map/ppermute | solution.py:377
  63.8 25.6 %collective-permute-start.35 = (bf16[3,128,768]{2,1,0:T(8,128)(2,1)S(1)}, bf16[3,128,768]{2,1,0:T(8,128)(2,1)S(1)}, u32[]{:S(2)}, u32[]{:S(2)}) collective-permute-start(bf16[3,128,768]{2,1,0:T(8,128)(2,1)S(1)} %shard_map.290.refs_3_), channel_id=1, source_target_pairs={{0,16},{8,24},{16,0},{24,8},{1,17},{9,25},{17,1},{25,9},{2,18},{10... | collective-permute-start | bytes 1769480 | tf_op jit(solution)/shard_map/ppermute | solution.py:377
  64.6 4.1 %collective-permute-start.14 = (bf16[3,128,256]{2,1,0:T(8,128)(2,1)S(1)}, bf16[3,128,256]{2,1,0:T(8,128)(2,1)S(1)}, u32[]{:S(2)}, u32[]{:S(2)}) collective-permute-start(bf16[3,128,256]{2,1,0:T(8,128)(2,1)S(1)} %collective-permute-done.9.refs_2_), channel_id=1, source_target_pairs={{0,1},{1,0},{2,3},{3,2},{4,5},{5,4},{6,7},{7,6},{8,9},{9,8},{10,11... | collective-permute-start | bytes 589832 | tf_op jit(solution)/shard_map/ppermute | solution.py:377
  68.7 8.4 %collective-permute-start.24 = (bf16[3,256,256]{2,1,0:T(8,128)(2,1)S(1)}, bf16[3,256,256]{2,1,0:T(8,128)(2,1)S(1)}, u32[]{:S(2)}, u32[]{:S(2)}) collective-permute-start(bf16[3,256,256]{2,1,0:T(8,128)(2,1)S(1)} %shard_map.288.refs_1_), channel_id=1, source_target_pairs={{0,1},{1,0},{2,3},{3,2},{4,5},{5,4},{6,7},{7,6},{8,9},{9,8},{10,11... | collective-permute-start | bytes 1179656 | tf_op jit(solution)/shard_map/ppermute | solution.py:377
  68.7 22.7 %collective-permute-start.34 = (bf16[3,128,768]{2,1,0:T(8,128)(2,1)S(1)}, bf16[3,128,768]{2,1,0:T(8,128)(2,1)S(1)}, u32[]{:S(2)}, u32[]{:S(2)}) collective-permute-start(bf16[3,128,768]{2,1,0:T(8,128)(2,1)S(1)} %shard_map.290.refs_3_), channel_id=1, source_target_pairs={{0,8},{8,0},{16,24},{24,16},{1,9},{9,1},{17,25},{25,17},{2,10},{10... | collective-permute-start | bytes 1769480 | tf_op jit(solution)/shard_map/ppermute | solution.py:377
  69.8 20.9 %collective-permute-start.23 = (bf16[256,1024]{1,0:T(8,128)(2,1)S(1)}, bf16[256,1024]{1,0:T(8,128)(2,1)S(1)}, u32[]{:S(2)}, u32[]{:S(2)}) collective-permute-start(bf16[256,1024]{1,0:T(8,128)(2,1)S(1)} %copy-done.5), channel_id=1, source_target_pairs={{0,1},{1,0},{2,3},{3,2},{4,5},{5,4},{6,7},{7,6},{8,9},{9,8},{10,11... | collective-permute-start | bytes 1572872 | tf_op jit(solution)/shard_map/ppermute | solution.py:377
  77.2 14.8 %collective-permute-start.37 = (bf16[128,3072]{1,0:T(8,128)(2,1)S(1)}, bf16[128,3072]{1,0:T(8,128)(2,1)S(1)}, u32[]{:S(2)}, u32[]{:S(2)}) collective-permute-start(bf16[128,3072]{1,0:T(8,128)(2,1)S(1)} %copy-done.1), channel_id=1, source_target_pairs={{0,1},{1,0},{2,3},{3,2},{4,5},{5,4},{6,7},{7,6},{8,9},{9,8},{10,11... | collective-permute-start | bytes 2359304 | tf_op jit(solution)/shard_map/ppermute | solution.py:377
  77.2 14.3 %collective-permute-start.38 = (bf16[3,128,768]{2,1,0:T(8,128)(2,1)S(1)}, bf16[3,128,768]{2,1,0:T(8,128)(2,1)S(1)}, u32[]{:S(2)}, u32[]{:S(2)}) collective-permute-start(bf16[3,128,768]{2,1,0:T(8,128)(2,1)S(1)} %shard_map.290.refs_3_), channel_id=1, source_target_pairs={{0,1},{1,0},{2,3},{3,2},{4,5},{5,4},{6,7},{7,6},{8,9},{9,8},{10,11... | collective-permute-start | bytes 1769480 | tf_op jit(solution)/shard_map/ppermute | solution.py:377
  89.5 15.0 %collective-permute-start.36 = (bf16[3,128,768]{2,1,0:T(8,128)(2,1)S(1)}, bf16[3,128,768]{2,1,0:T(8,128)(2,1)S(1)}, u32[]{:S(2)}, u32[]{:S(2)}) collective-permute-start(bf16[3,128,768]{2,1,0:T(8,128)(2,1)S(1)} %collective-permute-done.35.refs_5_), channel_id=1, source_target_pairs={{0,8},{8,0},{16,24},{24,16},{1,9},{9,1},{17,25},{25,17},{2,10},{10... | collective-permute-start | bytes 1769480 | tf_op jit(solution)/shard_map/ppermute | solution.py:377
  90.6 13.9 %collective-permute-start.22 = (bf16[3,256,256]{2,1,0:T(8,128)(2,1)S(1)}, bf16[3,256,256]{2,1,0:T(8,128)(2,1)S(1)}, u32[]{:S(2)}, u32[]{:S(2)}) collective-permute-start(bf16[3,256,256]{2,1,0:T(8,128)(2,1)S(1)} %collective-permute-done.20.refs_2_), channel_id=1, source_target_pairs={{0,16},{8,24},{16,0},{24,8},{1,17},{9,25},{17,1},{25,9},{2,18},{10... | collective-permute-start | bytes 1179656 | tf_op jit(solution)/shard_map/ppermute | solution.py:377
  91.4 13.6 %collective-permute-start.25 = (bf16[3,256,256]{2,1,0:T(8,128)(2,1)S(1)}, bf16[3,256,256]{2,1,0:T(8,128)(2,1)S(1)}, u32[]{:S(2)}, u32[]{:S(2)}) collective-permute-start(bf16[3,256,256]{2,1,0:T(8,128)(2,1)S(1)} %collective-permute-done.20.refs_2_), channel_id=1, source_target_pairs={{0,1},{1,0},{2,3},{3,2},{4,5},{5,4},{6,7},{7,6},{8,9},{9,8},{10,11... | collective-permute-start | bytes 1179656 | tf_op jit(solution)/shard_map/ppermute | solution.py:377
  91.4 16.3 %collective-permute-start.39 = (bf16[3,128,768]{2,1,0:T(8,128)(2,1)S(1)}, bf16[3,128,768]{2,1,0:T(8,128)(2,1)S(1)}, u32[]{:S(2)}, u32[]{:S(2)}) collective-permute-start(bf16[3,128,768]{2,1,0:T(8,128)(2,1)S(1)} %collective-permute-done.34.refs_4_), channel_id=1, source_target_pairs={{0,1},{1,0},{2,3},{3,2},{4,5},{5,4},{6,7},{7,6},{8,9},{9,8},{10,11... | collective-permute-start | bytes 1769480 | tf_op jit(solution)/shard_map/ppermute | solution.py:377
  91.9 17.3 %collective-permute-start.40 = (bf16[3,128,768]{2,1,0:T(8,128)(2,1)S(1)}, bf16[3,128,768]{2,1,0:T(8,128)(2,1)S(1)}, u32[]{:S(2)}, u32[]{:S(2)}) collective-permute-start(bf16[3,128,768]{2,1,0:T(8,128)(2,1)S(1)} %collective-permute-done.35.refs_5_), channel_id=1, source_target_pairs={{0,1},{1,0},{2,3},{3,2},{4,5},{5,4},{6,7},{7,6},{8,9},{9,8},{10,11... | collective-permute-start | bytes 1769480 | tf_op jit(solution)/shard_map/ppermute | solution.py:377
  104.5 6.1 %collective-permute-start.41 = (bf16[3,128,768]{2,1,0:T(8,128)(2,1)S(1)}, bf16[3,128,768]{2,1,0:T(8,128)(2,1)S(1)}, u32[]{:S(2)}, u32[]{:S(2)}) collective-permute-start(bf16[3,128,768]{2,1,0:T(8,128)(2,1)S(1)} %collective-permute-done.36.refs_6_), channel_id=1, source_target_pairs={{0,1},{1,0},{2,3},{3,2},{4,5},{5,4},{6,7},{7,6},{8,9},{9,8},{10,11... | collective-permute-start | bytes 1769480 | tf_op jit(solution)/shard_map/ppermute | solution.py:377
  104.5 2.6 %collective-permute-start.26 = (bf16[3,256,256]{2,1,0:T(8,128)(2,1)S(1)}, bf16[3,256,256]{2,1,0:T(8,128)(2,1)S(1)}, u32[]{:S(2)}, u32[]{:S(2)}) collective-permute-start(bf16[3,256,256]{2,1,0:T(8,128)(2,1)S(1)} %collective-permute-done.21.refs_3_), channel_id=1, source_target_pairs={{0,1},{1,0},{2,3},{3,2},{4,5},{5,4},{6,7},{7,6},{8,9},{9,8},{10,11... | collective-permute-start | bytes 1179656 | tf_op jit(solution)/shard_map/ppermute | solution.py:377
  105.0 2.6 %collective-permute-start.27 = (bf16[3,256,256]{2,1,0:T(8,128)(2,1)S(1)}, bf16[3,256,256]{2,1,0:T(8,128)(2,1)S(1)}, u32[]{:S(2)}, u32[]{:S(2)}) collective-permute-start(bf16[3,256,256]{2,1,0:T(8,128)(2,1)S(1)} %collective-permute-done.22.refs_4_), channel_id=1, source_target_pairs={{0,1},{1,0},{2,3},{3,2},{4,5},{5,4},{6,7},{7,6},{8,9},{9,8},{10,11... | collective-permute-start | bytes 1179656 | tf_op jit(solution)/shard_map/ppermute | solution.py:377
  107.1 12.5 %collective-permute-start.15 = (bf16[3,128,256]{2,1,0:T(8,128)(2,1)S(1)}, bf16[3,128,256]{2,1,0:T(8,128)(2,1)S(1)}, u32[]{:S(2)}, u32[]{:S(2)}) collective-permute-start(bf16[3,128,256]{2,1,0:T(8,128)(2,1)S(1)} %collective-permute-done.10.refs_3_), channel_id=1, source_target_pairs={{0,1},{1,0},{2,3},{3,2},{4,5},{5,4},{6,7},{7,6},{8,9},{9,8},{10,11... | collective-permute-start | bytes 589832 | tf_op jit(solution)/shard_map/ppermute | solution.py:377
  107.6 11.9 %collective-permute-start.16 = (bf16[3,128,256]{2,1,0:T(8,128)(2,1)S(1)}, bf16[3,128,256]{2,1,0:T(8,128)(2,1)S(1)}, u32[]{:S(2)}, u32[]{:S(2)}) collective-permute-start(bf16[3,128,256]{2,1,0:T(8,128)(2,1)S(1)} %collective-permute-done.11.refs_4_), channel_id=1, source_target_pairs={{0,1},{1,0},{2,3},{3,2},{4,5},{5,4},{6,7},{7,6},{8,9},{9,8},{10,11... | collective-permute-start | bytes 589832 | tf_op jit(solution)/shard_map/ppermute | solution.py:377
  107.8 15.6 %collective-permute-start.5 = (bf16[48,512]{1,0:T(8,128)(2,1)S(1)}, bf16[48,512]{1,0:T(8,128)(2,1)S(1)}, u32[]{:S(2)}, u32[]{:S(2)}) collective-permute-start(bf16[48,512]{1,0:T(8,128)(2,1)S(1)} %get-tuple-element.28), channel_id=1, source_target_pairs={{0,9},{1,10},{2,11},{3,12},{4,13},{5,14},{6,15},{7,8},{8,17},{9,18... | collective-permute-start | bytes 147464 | tf_op jit(solution)/shard_map/ppermute | solution.py:368
  109.2 15.6 %collective-permute-start.3 = (bf16[112,512]{1,0:T(8,128)(2,1)S(1)}, bf16[112,512]{1,0:T(8,128)(2,1)S(1)}, u32[]{:S(2)}, u32[]{:S(2)}) collective-permute-start(bf16[112,512]{1,0:T(8,128)(2,1)S(1)} %get-tuple-element.26), channel_id=1, source_target_pairs={{0,8},{8,16},{16,24},{24,0},{1,9},{9,17},{17,25},{25,1},{2,10},{10... | collective-permute-start | bytes 344072 | tf_op jit(solution)/shard_map/ppermute | solution.py:366
  110.6 14.3 %collective-permute-start.4 = (bf16[112,512]{1,0:T(8,128)(2,1)S(1)}, bf16[112,512]{1,0:T(8,128)(2,1)S(1)}, u32[]{:S(2)}, u32[]{:S(2)}) collective-permute-start(bf16[112,512]{1,0:T(8,128)(2,1)S(1)} %get-tuple-element.27), channel_id=1, source_target_pairs={{0,1},{1,2},{2,3},{3,4},{4,5},{5,6},{6,7},{7,0},{8,9},{9,10},{10,1... | collective-permute-start | bytes 344072 | tf_op jit(solution)/shard_map/ppermute | solution.py:367
  121.6 6.5 %collective-permute-start.42 = (bf16[48,1024]{1,0:T(8,128)(2,1)S(1)}, bf16[48,1024]{1,0:T(8,128)(2,1)S(1)}, u32[]{:S(2)}, u32[]{:S(2)}) collective-permute-start(bf16[48,1024]{1,0:T(8,128)(2,1)S(1)} %get-tuple-element.37), channel_id=1, source_target_pairs={{0,8},{8,16},{16,24},{24,0},{1,9},{9,17},{17,25},{25,1},{2,10},{10... | collective-permute-start | bytes 294920 | tf_op jit(solution)/shard_map/ppermute | solution.py:366
  122.9 5.8 %collective-permute-start.43 = (bf16[48,1024]{1,0:T(8,128)(2,1)S(1)}, bf16[48,1024]{1,0:T(8,128)(2,1)S(1)}, u32[]{:S(2)}, u32[]{:S(2)}) collective-permute-start(bf16[48,1024]{1,0:T(8,128)(2,1)S(1)} %get-tuple-element.38), channel_id=1, source_target_pairs={{0,1},{1,2},{2,3},{3,4},{4,5},{5,6},{6,7},{7,0},{8,9},{9,10},{10,1... | collective-permute-start | bytes 294920 | tf_op jit(solution)/shard_map/ppermute | solution.py:367
  123.4 7.6 %collective-permute-start.44 = (bf16[48,1024]{1,0:T(8,128)(2,1)S(1)}, bf16[48,1024]{1,0:T(8,128)(2,1)S(1)}, u32[]{:S(2)}, u32[]{:S(2)}) collective-permute-start(bf16[48,1024]{1,0:T(8,128)(2,1)S(1)} %get-tuple-element.39), channel_id=1, source_target_pairs={{0,9},{1,10},{2,11},{3,12},{4,13},{5,14},{6,15},{7,8},{8,17},{9,18... | collective-permute-start | bytes 294920 | tf_op jit(solution)/shard_map/ppermute | solution.py:368
  (15 other events, 93.8 us)

commit v4 on v3

--- a/solution.py
+++ b/solution.py
@@ -107,26 +107,43 @@
     return jnp.where(down == along, 0.0, EXCLUDED)
 
 
-def attend(packed_ref, mixed_ref, first, count, width, heads, bias):
+def lane_heads(width, heads):
     head_size = width // heads
     lane = lax.broadcasted_iota(jnp.int32, (1, LANES), 1)
-    ones = jnp.ones((count, LANES), jnp.bfloat16)
+    for start in range(0, width, LANES):
+        yield start, [
+            ((start + low) // head_size, (lane >= low) & (lane < low + head_size))
+            for low in range(0, LANES, head_size)
+        ]
+
+
+def head_expos(queries, keys, own, head_size, bias):
+    chosen = jnp.where(own, 1.0 / math.sqrt(head_size), 0.0).astype(jnp.bfloat16)
+    scores = dot_nt(queries * chosen, keys) + bias
+    highest = jnp.max(scores, axis=-1, keepdims=True)
+    return jnp.exp(scores - highest).astype(jnp.bfloat16)
+
+
+def head_mix(expos, values, own, mixed):
+    summed = dot(expos, values)
+    result = summed[:, :LANES] / summed[:, LANES:]
+    return result if mixed is None else jnp.where(own, result, mixed)
+
+
+def with_ones(values):
+    return jnp.concatenate([values, jnp.ones(values.shape, values.dtype)], axis=1)
+
+
+def attend(packed_ref, mixed_ref, first, count, width, heads, bias):
     rows = slice(first, first + count)
-    for start in range(0, width, LANES):
+    for start, members in lane_heads(width, heads):
         queries = packed_ref[rows, start : start + LANES]
         keys = packed_ref[rows, width + start : width + start + LANES]
-        values = packed_ref[rows, 2 * width + start : 2 * width + start + LANES]
-        values = jnp.concatenate([values, ones], axis=1)
+        values = with_ones(packed_ref[rows, 2 * width + start : 2 * width + start + LANES])
         mixed = None
-        for low in range(0, LANES, head_size):
-            own = (lane >= low) & (lane < low + head_size)
-            chosen = jnp.where(own, 1.0 / math.sqrt(head_size), 0.0).astype(jnp.bfloat16)
-            scores = dot_nt(queries * chosen, keys) + bias
-            highest = jnp.max(scores, axis=-1, keepdims=True)
-            expos = jnp.exp(scores - highest).astype(jnp.bfloat16)
-            summed = dot(expos, values)
-            result = summed[:, :LANES] / summed[:, LANES:]
-            mixed = result if mixed is None else jnp.where(own, result, mixed)
+        for _, own in members:
+            expos = head_expos(queries, keys, own, width // heads, bias)
+            mixed = head_mix(expos, values, own, mixed)
         mixed_ref[rows, start : start + LANES] = mixed.astype(jnp.bfloat16)
 
 
@@ -138,11 +155,11 @@
 
 
 def flat_labels(ids_ref, edge, spread):
-    levels, rows, columns = ids_ref.shape
+    rows, levels, columns = ids_ref.shape
     total = 0.0
     for level in range(levels):
         row = lax.broadcasted_iota(jnp.int32, (rows, columns), 0)
-        labels = ids_ref[level] * 2 + jnp.where(row < HALF_ROWS, edge, 0)
+        labels = ids_ref[:, level, :] * 2 + jnp.where(row < HALF_ROWS, edge, 0)
         wide = dot(labels.astype(jnp.float32).astype(jnp.bfloat16), spread)
         place = lax.broadcasted_iota(jnp.int32, wide.shape, 1)
         low = (level * rows + lax.broadcasted_iota(jnp.int32, wide.shape, 0)) * columns
@@ -151,48 +168,62 @@
     return jnp.broadcast_to(total, (8, total.shape[1])).astype(jnp.bfloat16)
 
 
-def pack_kernel(
-    counts, at_ref, x_hbm, ids_hbm, coarse_ids_hbm, fine_hbm, coarse_hbm, *refs
-):
-    wholes, refs = refs[:3], refs[3:]
-    outs, labels_ref, coarse_labels_ref, parts = refs[:3], refs[3], refs[4], refs[5:8]
-    x_ref, ids_ref, coarse_ids_ref, fine_ref, coarse_ref, sems = refs[8:]
-    corner, edge = at_ref[0], at_ref[1]
-    loads = fetch(
+def quarters_kernel(at_ref, merge_ref, qkv_ref, out_ref, merge_part, score_part, value_part, sems):
+    corner = at_ref[0]
+    wide = out_ref.shape[1] // 4
+
+    def quarter(ref, first, columns):
+        start = pl.multiple_of(first + corner * columns, LANES)
+        return ref.at[:, pl.ds(start, columns)]
+
+    copies = fetch(
+        sems,
+        (quarter(merge_ref, 0, merge_part.shape[1]), merge_part),
+        (quarter(qkv_ref, 0, 2 * wide), score_part),
+        (quarter(qkv_ref, 8 * wide, wide), value_part.at[:, pl.ds(0, wide)]),
+        (quarter(out_ref, 0, wide), value_part.at[:, pl.ds(wide, wide)]),
+    )
+    for copy in copies:
+        copy.wait()
+
+
+def pack_kernel(counts, at_ref, x_hbm, ids_hbm, coarse_ids_hbm, fine_hbm, coarse_hbm, qkv_ref, out_ref, *refs):
+    outs, labels_ref, coarse_labels_ref, score_own, value_own = refs[:3], refs[3], refs[4], refs[5], refs[6]
+    x_ref, ids_ref, coarse_ids_ref, fine_ref, coarse_ref, sems = refs[7:]
+    edge = at_ref[1]
+    wide = out_ref.shape[1] // 4
+    pairs = [(qkv_ref.at[:, pl.ds(0, 8 * wide)], score_own)]
+    for number in range(4):
+        pairs.append((qkv_ref.at[:, pl.ds((8 + number) * wide, wide)], value_own.at[:, pl.ds(2 * number * wide, wide)]))
+        pairs.append((out_ref.at[:, pl.ds(number * wide, wide)], value_own.at[:, pl.ds((2 * number + 1) * wide, wide)]))
+    copies = fetch(
         sems,
         (ids_hbm, ids_ref),
         (coarse_ids_hbm, coarse_ids_ref),
         (coarse_hbm, coarse_ref),
         (fine_hbm, fine_ref),
         (x_hbm, x_ref),
-    )
-    copies = []
-    for whole, part in zip(wholes, parts):
-        wide = part.shape[1]
-        start = pl.multiple_of(corner * wide, LANES)
-        copies.append(
-            pltpu.make_async_copy(whole.at[:, pl.ds(start, wide)], part, sems.at[len(loads) + len(copies)])
-        )
-        copies[-1].start()
-    for load in loads[:4]:
+        *pairs,
+    )
+    for load in copies[:4]:
         load.wait()
     picks = 3 * LANES
     labels = flat_labels(ids_ref, edge, fine_ref[picks : picks + ids_ref.shape[2]])
     coarse_labels = flat_labels(coarse_ids_ref, edge, coarse_ref[picks : picks + coarse_ids_ref.shape[2]])
     labels_ref[...] = labels
     coarse_labels_ref[...] = coarse_labels
-    loads[4].wait()
-    for number, (out_ref, count) in enumerate(zip(outs, counts)):
-        height = out_ref.shape[0]
+    copies[4].wait()
+    for number, (packet, count) in enumerate(zip(outs, counts)):
+        height = packet.shape[0]
         first = number * LANES
         body = dot(fine_ref[first : first + height], x_ref[...])
         row = lax.broadcasted_iota(jnp.int32, (height, LANES), 0)
         fine = dot_nt(labels, fine_ref[first : first + LANES])[:1]
         coarse = dot_nt(coarse_labels, coarse_ref[first : first + LANES])[:1]
         extra = jnp.where(row == count, fine, jnp.where(row == count + 1, coarse, 0.0))
-        out_ref[:, :LANES] = (body[:, :LANES] + extra).astype(out_ref.dtype)
-        out_ref[:, LANES:] = body[:, LANES:].astype(out_ref.dtype)
-    for copy in copies:
+        packet[:, :LANES] = (body[:, :LANES] + extra).astype(packet.dtype)
+        packet[:, LANES:] = body[:, LANES:].astype(packet.dtype)
+    for copy in copies[5:]:
         copy.wait()
 
 
@@ -260,9 +291,11 @@
     quarter = columns // 4
     copies = []
     for number, piece in enumerate(pieces):
-        other, mask = number // 5, number % 5 - 1
-        held = whole_ref.at[:, side ^ other]
-        if mask < 0:
+        other, kind = number // 5, number % 5
+        from_side = side ^ other
+        held = whole_ref.at[:, from_side]
+        mask = (None, 0, 1 + from_side, 2 - from_side, 3)[kind]
+        if mask is None:
             pairs = [(piece, held.at[here])]
         else:
             start = pl.multiple_of((corner ^ mask) * quarter, LANES)
@@ -307,30 +340,52 @@
     out_ref[...] = dot(left, flat(whole_ref)).astype(jnp.bfloat16)
 
 
-def second_kernel(heads, counts, at_ref, select_hbm, *refs):
-    pieces, (merged_ref, labels_ref, lat_ref, lon_ref, both_ref, mixed_ref) = refs[:10], refs[10:16]
+def scores_kernel(heads, counts, at_ref, select_hbm, *refs):
+    pieces, (merged_ref, labels_ref, lat_ref, lon_ref, both_ref, expos_ref) = refs[:10], refs[10:16]
     select_ref, whole_ref, packed_ref, sems, piece_sems = refs[16:]
-    loads = fetch(sems, (select_hbm, select_ref))
-    copies = start_pieces(whole_ref, pieces, at_ref, piece_sems)
+    copies = fetch(sems, (select_hbm, select_ref)) + start_pieces(whole_ref, pieces, at_ref, piece_sems)
     count, width = merged_ref.shape
     left = normalized(merged_ref[...].astype(jnp.float32))
     wide = wide_labels(labels_ref, (lat_ref, lon_ref, both_ref), counts, 1)
-    loads[0].wait()
+    copies[0].wait()
     bias = label_bias(wide, select_ref[...])
+    for copy in copies[1:]:
+        copy.wait()
+    packed_ref[...] = dot(left, flat(whole_ref)).astype(jnp.bfloat16)
+    for start, members in lane_heads(width, heads):
+        queries = packed_ref[:, start : start + LANES]
+        keys = packed_ref[:, width + start : width + start + LANES]
+        for head, own in members:
+            expos = head_expos(queries, keys, own, width // heads, bias)
+            expos_ref[head * count : (head + 1) * count] = expos
+
+
+def close_kernel(heads, at_ref, pick_hbm, *refs):
+    pieces, (merged_ref, expos_ref, z_ref), packets = refs[:10], refs[10:13], refs[13:16]
+    pick_ref, whole_ref, values_ref, mixed_ref, sems, piece_sems = refs[16:]
+    copies = fetch(sems, (pick_hbm, pick_ref)) + start_pieces(whole_ref, pieces, at_ref, piece_sems)
+    count, width = merged_ref.shape
+    merged = merged_ref[...].astype(jnp.float32)
+    left = normalized(merged)
     for copy in copies:
         copy.wait()
-    packed_ref[...] = dot(left, flat(whole_ref)).astype(jnp.bfloat16)
-    attend(packed_ref, mixed_ref, 0, count, width, heads, bias)
-
-
-def close_kernel(at_ref, pick_hbm, *refs):
-    pieces, (merged_ref, mixed_ref, z_ref), packets = refs[:10], refs[10:13], refs[13:16]
-    pick_ref, whole_ref, sems, piece_sems = refs[16:]
-    copies = fetch(sems, (pick_hbm, pick_ref)) + start_pieces(whole_ref, pieces, at_ref, piece_sems)
-    for copy in copies:
-        copy.wait()
-    result = merged_ref[...].astype(jnp.float32) + dot(mixed_ref[...], flat(whole_ref))
-    z_ref[...] = result.astype(jnp.bfloat16)
+    whole = flat(whole_ref)
+    wide = width // 4
+    for number in range(4):
+        columns = slice(number * wide, (number + 1) * wide)
+        first = 2 * number * wide
+        values_ref[:, columns] = dot(left, whole[:, first : first + wide]).astype(jnp.bfloat16)
+    for start, members in lane_heads(width, heads):
+        values = with_ones(values_ref[:, start : start + LANES])
+        mixed = None
+        for head, own in members:
+            mixed = head_mix(expos_ref[head * count : (head + 1) * count], values, own, mixed)
+        mixed_ref[:, start : start + LANES] = mixed.astype(jnp.bfloat16)
+    mixed = mixed_ref[...]
+    for number in range(4):
+        columns = slice(number * wide, (number + 1) * wide)
+        first = (2 * number + 1) * wide
+        z_ref[:, columns] = (merged[:, columns] + dot(mixed, whole[:, first : first + wide])).astype(jnp.bfloat16)
     first = 0
     for packet in packets:
         height = packet.shape[0]
@@ -345,7 +400,9 @@
     out_ref[...] = dot(select_ref[...], stage_ref[...]).astype(out_ref.dtype)
 
 
-def call(kernel, outs, scratch, scalars=(), hbm=(), vmem=(), hbm_outs=()):
+def call(kernel, outs, scratch, scalars=(), hbm=(), vmem=(), hbm_outs=(), pinned=False):
+    if pinned:
+        hbm = [pltpu.with_memory_space_constraint(array, pltpu.HBM) for array in hbm]
     spaces = [pltpu.SMEM] * len(scalars) + [pltpu.HBM] * len(hbm) + [pltpu.VMEM] * len(vmem)
     return pl.pallas_call(
         kernel,
@@ -377,24 +434,39 @@
     return lax.ppermute(block, axis, [(i, i ^ mask) for i in range(lax.axis_size(axis))])
 
 
-def spread_pieces(shard, part, by_first):
+def far_parts(part):
     ranks = lax.axis_size("lon")
-    stops = ranks // 2
-    far = [
-        lax.ppermute(part, "lon", [(i, (i + 2 * back) % ranks) for i in range(ranks)]) for back in range(1, stops)
+    return [
+        lax.ppermute(part, "lon", [(i, (i + 2 * back) % ranks) for i in range(ranks)])
+        for back in range(1, ranks // 2)
     ]
+
+
+def routed(block, turn):
+    lat, lon = lax.axis_size("lat"), lax.axis_size("lon")
+    pairs = [
+        (i * lon + j, (i ^ (1 + (j + turn) % 2)) * lon + j) for i in range(lat) for j in range(lon)
+    ]
+    return lax.ppermute(block, ("lat", "lon"), pairs)
+
+
+def joined_parts(far):
     (near,) = call(
         join_kernel,
-        [(stops - 1,) + part.shape],
-        [pltpu.SemaphoreType.DMA((stops - 1,))],
+        [(len(far),) + far[0].shape],
+        [pltpu.SemaphoreType.DMA((len(far),))],
         hbm=far,
         hbm_outs=(0,),
     )
-    first = exchange(near, "lat", 1)
-    second = exchange(near, "lat", 2)
-    third = exchange(first, "lat", 2) if by_first else exchange(second, "lat", 1)
-    pieces = [shard, near, first, second, third]
+    return near
+
+
+def own_and_swapped(pieces):
     return pieces + [exchange(piece, "lon", 1) for piece in pieces]
+
+
+def after(value, *earlier):
+    return lax.optimization_barrier((value, earlier))[0]
 
 
 def dma(count):
@@ -424,7 +496,16 @@
     end_rows = [up(len(part) + 2, PACK) for part in end]
     order = window_order(levels, height, breadth)
     inverse = np.argsort(order)
-    weights = (merge_weight, second_qkv, second_out)
+    rows = second_out.shape[0]
+    merge_part, score_part, value_part = call(
+        quarters_kernel,
+        [(merge_weight.shape[0], wider // 4), (rows, wider // 2), (rows, wider // 2)],
+        [dma(4)],
+        scalars=(at,),
+        hbm=(merge_weight, second_qkv, second_out),
+        hbm_outs=(0, 1, 2),
+        pinned=True,
+    )
 
     def picks(parts, rows, columns):
         return [matrix(part, columns, count) for part, count in zip(parts, rows)]
@@ -435,27 +516,33 @@
     fine = jnp.concatenate(picks(start, [LANES] * 3, cells) + [spreader(breadth, cells)])
     coarse = jnp.concatenate(picks(end, [LANES] * 3, coarse_cells) + [spreader(narrow, coarse_cells)])
     x = tokens.reshape(cells, width)
-    *packets, labels, coarse_labels, merge_part, qkv_part, out_part = call(
+    *packets, labels, coarse_labels, score_own, value_own = call(
         lambda *refs: pack_kernel(counts, *refs),
-        [(rows, width) for rows in packet_rows]
-        + [(8, cells), (8, coarse_cells)]
-        + [(weight.shape[0], weight.shape[1] // 4) for weight in weights],
+        [(count, width) for count in packet_rows]
+        + [(8, cells), (8, coarse_cells), (rows, 2 * wider), (rows, 2 * wider)],
         [
             bf16(cells, width),
-            pltpu.VMEM(level_ids.shape, jnp.int32),
-            pltpu.VMEM(coarse_ids.shape, jnp.int32),
+            *[pltpu.VMEM((ids.shape[1], levels, ids.shape[2]), jnp.int32) for ids in (level_ids, coarse_ids)],
             bf16(*fine.shape),
             bf16(*coarse.shape),
-            dma(8),
+            dma(14),
         ],
-        scalars=(at,),
-        hbm=(x, level_ids, coarse_ids, fine, coarse, *weights),
-        hbm_outs=(5, 6, 7),
+        scalars=(after(at, merge_part),),
+        hbm=(x, *[ids.transpose(1, 0, 2) for ids in (level_ids, coarse_ids)], fine, coarse, second_qkv, second_out),
+        hbm_outs=(5, 6),
+        pinned=True,
     )
     got = shifted(packets, -1)
-    merge_pieces = spread_pieces(merge_weight, merge_part, True)
-    qkv_pieces = spread_pieces(second_qkv, qkv_part, False)
-    out_pieces = spread_pieces(second_out, out_part, True)
+    nears, routes = [], []
+    for part in (merge_part, score_part, value_part):
+        near = joined_parts(far_parts(after(part, nears[-1]) if nears else part))
+        first, second = routed(near, 0), routed(near, 1)
+        nears.append(near)
+        routes.append([near, first, second, routed(first, 1)])
+    owns = after((merge_weight, score_own, value_own), routes[0][1])
+    merge_pieces, score_pieces, value_pieces = [
+        own_and_swapped([own] + route) for own, route in zip(owns, routes)
+    ]
 
     source, depth = replaced(cells, start)
     held = np.empty_like(order)
@@ -465,9 +552,10 @@
         picks([inverse[part] for part in middle], packet_rows, cells)
         + picks([inverse[part] for part in start], packet_rows, cells)
     )
+    got_first = after(got, nears[0])
     y, *packets = call(
         lambda *refs: first_kernel(HEADS1, counts, *refs),
-        [(cells, width)] + [(rows, width) for rows in packet_rows] * 2,
+        [(cells, width)] + [(count, width) for count in packet_rows] * 2,
         [
             bf16(*select.shape),
             bf16(*first_qkv.shape),
@@ -480,10 +568,10 @@
             dma(5),
         ],
         hbm=(x, select, first_qkv, first_out, pick),
-        vmem=(labels, *got),
+        vmem=(labels, *got_first),
     )
     mid = shifted(packets[:3], -1)
-    back = shifted(packets[3:], 1)
+    back = shifted(after(packets[3:], routes[2][1]), 1)
 
     source, depth = replaced(cells, middle, held)
     fine = source.reshape(levels, low, 2, narrow, 2)
@@ -516,33 +604,35 @@
 
     source, depth = replaced(coarse_cells, end)
     select = matrix(source, depth)
-    (mixed,) = call(
-        lambda *refs: second_kernel(HEADS2, counts, *refs),
-        [(coarse_cells, wider)],
+    (expos,) = call(
+        lambda *refs: scores_kernel(HEADS2, counts, *refs),
+        [(HEADS2 * coarse_cells, coarse_cells)],
         [
             bf16(*select.shape),
-            bf16(stops, 2, *second_qkv.shape),
-            bf16(coarse_cells, 3 * wider),
+            bf16(stops, 2, *score_own.shape),
+            bf16(coarse_cells, 2 * wider),
             dma(1),
             dma(piece_copies(stops)),
         ],
         scalars=(at,),
-        hbm=(select, *qkv_pieces),
+        hbm=(select, *score_pieces),
         vmem=(merged, coarse_labels, *got),
     )
     pick = jnp.concatenate(picks(end, end_rows, coarse_cells))
     z, *packets = call(
-        close_kernel,
-        [(coarse_cells, wider)] + [(rows, wider) for rows in end_rows],
+        lambda *refs: close_kernel(HEADS2, *refs),
+        [(coarse_cells, wider)] + [(count, wider) for count in end_rows],
         [
             bf16(*pick.shape),
-            bf16(stops, 2, *second_out.shape),
+            bf16(stops, 2, *value_own.shape),
+            bf16(coarse_cells, wider),
+            bf16(coarse_cells, wider),
             dma(1),
             dma(piece_copies(stops)),
         ],
         scalars=(at,),
-        hbm=(pick, *out_pieces),
-        vmem=(merged, mixed),
+        hbm=(pick, *value_pieces),
+        vmem=(merged, expos),
     )
     done = shifted(packets, 1)
     (coarse,) = call(

time: 133 us -> 113 us (0.85)
  waiting for transfers between devices: 57.3 us -> 38.7 us
  local copies, waits for them, and re-layouts: 11 us -> 1.14 us
  starting transfers between devices: 40.5 us -> 46.6 us
  Pallas kernels: 22.9 us -> 25.7 us
    ppermute x24 -> x15, waiting for transfers between devices: 42 us -> 0.04 us  [exchange(): lax.ppermute(block, axis, [(i, i ^ mask) for i in range(lax.axis_size(axi...]
    ppermute x9 -> x18, waiting for transfers between devices: 6.41 us -> 32.5 us  [the longest x9 20.8 us: routed(): return lax.ppermute(block, ('lat', 'lon'), pairs)]
    ppermute x9 -> x18, starting transfers between devices: 13.9 us -> 31.8 us  [the longest x9 19.4 us: far_parts(): lax.ppermute(part, 'lon', [(i, (i + 2 * back) % ranks) for i in range(ran...]
    ppermute x24 -> x15, starting transfers between devices: 14 us -> 2.14 us  [exchange(): lax.ppermute(block, axis, [(i, i ^ mask) for i in range(lax.axis_size(axi...]
    unnamed x39 -> x21, local copies, waits for them, and re-layouts: 10.9 us -> 1.07 us
    ppermute x4, waiting for transfers between devices: 6.99 us -> 1.93 us  [shifted(): lax.ppermute(blocks[2], ('lat', 'lon'), [(i * lon + j, (i + step) % lat *...]
    pallas_call x10 -> x11, Pallas kernels: 22.9 us -> 25.7 us  [call(): pl.pallas_call(kernel, out_shape=[jax.ShapeDtypeStruct(shape, jnp.bfloat1...]
    ppermute x4, starting transfers between devices: 6.31 us -> 4.61 us  [shifted(): lax.ppermute(blocks[2], ('lat', 'lon'), [(i * lon + j, (i + step) % lat *...]
  transfers between devices with their start and end apart: 45 -> 45, of which waited for: 13 -> 14; matrix products, arithmetic and copies ran while one was open for 0% -> 0% of each run, Pallas kernels for 15% -> 21%
where the time goes in v4:
time: 113 us
  starting transfers between devices  46.6 us (41%)
  waiting for transfers between devices  38.7 us (34%)
  Pallas kernels  25.7 us (23%)
  local copies, waits for them, and re-layouts  1.14 us (1%)
    pallas_call x11, Pallas kernels, call(): pl.pallas_call(kernel, out_shape=[jax.ShapeDtypeStruct(shape, jnp.bfloat1...  25.7 us
    ppermute x9, waiting for transfers between devices, routed(): return lax.ppermute(block, ('lat', 'lon'), pairs)  20.8 us
    ppermute x9, starting transfers between devices, far_parts(): lax.ppermute(part, 'lon', [(i, (i + 2 * back) % ranks) for i in range(ran...  19.4 us
    ppermute x9, starting transfers between devices, routed(): return lax.ppermute(block, ('lat', 'lon'), pairs)  12.4 us
    ppermute x9, waiting for transfers between devices, far_parts(): lax.ppermute(part, 'lon', [(i, (i + 2 * back) % ranks) for i in range(ran...  11.7 us
    ppermute x4, starting transfers between devices, shifted(): lax.ppermute(blocks[0], 'lat', [(i, (i + step) % lat) for i in range(lat)])  5.2 us
    ppermute x4, starting transfers between devices, shifted(): lax.ppermute(blocks[2], ('lat', 'lon'), [(i * lon + j, (i + step) % lat *...  4.61 us
    ppermute x4, starting transfers between devices, shifted(): lax.ppermute(blocks[1], 'lon', [(i, (i + step) % lon) for i in range(lon)])  2.82 us
  transfers between devices with their start and end apart: 45, of which 14 were waited for; matrix products, arithmetic and copies ran while one was open for 0% of the time, Pallas kernels for 21%

profile of v4, /device:TPU:0, one launch (start us, length us, event | category | flops | bytes accessed | tf_op | source)
XLA Modules:
  0.0 113.2 jit_solution(9624048522930552392)
XLA Ops:
  0.7 1.6 %shard_map.284 = (bf16[256,256]{1,0:T(8,128)(2,1)S(1)}, bf16[128,512]{1,0:T(8,128)(2,1)S(1)}, bf16[128,512]{1,0:T(8,128)(2,1)S(1)}) custom-call(s32[4]{0:T(128)S(1)} %pad_add_fusion.at_ref.refs_0_, bf16[256,1024]{1,0:T(8,128)(2,1)} %refs_0_, bf16[128,3072]{1,0:T(8,128)(2,1)} %refs_6_.1, bf16[128,1024]{1,0:T(8,128)(2,1)} %refs_7_.1), custom_call_target="tpu_custom_call" | custom-call | tf_op jit(solution)/shard_map/pallas_call | solution.py:407
  2.3 3.1 %collective-permute-start.3 = (bf16[256,256]{1,0:T(8,128)(2,1)S(1)}, bf16[256,256]{1,0:T(8,128)(2,1)S(1)}, u32[]{:S(2)}, u32[]{:S(2)}) collective-permute-start(bf16[256,256]{1,0:T(8,128)(2,1)S(1)} %get-tuple-element.35), channel_id=1, source_target_pairs={{0,2},{1,3},{2,4},{3,5},{4,6},{5,7},{6,0},{7,1},{8,10},{9,11},{10,... | collective-permute-start | bytes 393224 | tf_op jit(solution)/shard_map/ppermute | solution.py:440
  5.4 2.6 %collective-permute-start.4 = (bf16[256,256]{1,0:T(8,128)(2,1)S(1)}, bf16[256,256]{1,0:T(8,128)(2,1)S(1)}, u32[]{:S(2)}, u32[]{:S(2)}) collective-permute-start(bf16[256,256]{1,0:T(8,128)(2,1)S(1)} %get-tuple-element.35), channel_id=1, source_target_pairs={{0,4},{1,5},{2,6},{3,7},{4,0},{5,1},{6,2},{7,3},{8,12},{9,13},{10,... | collective-permute-start | bytes 393224 | tf_op jit(solution)/shard_map/ppermute | solution.py:440
  8.0 1.3 %collective-permute-start.5 = (bf16[256,256]{1,0:T(8,128)(2,1)S(1)}, bf16[256,256]{1,0:T(8,128)(2,1)S(1)}, u32[]{:S(2)}, u32[]{:S(2)}) collective-permute-start(bf16[256,256]{1,0:T(8,128)(2,1)S(1)} %get-tuple-element.35), channel_id=1, source_target_pairs={{0,6},{1,7},{2,0},{3,1},{4,2},{5,3},{6,4},{7,5},{8,14},{9,15},{10,... | collective-permute-start | bytes 393224 | tf_op jit(solution)/shard_map/ppermute | solution.py:440
  9.4 3.0 %shard_map.285 = (bf16[112,512]{1,0:T(8,128)(2,1)S(1)}, bf16[112,512]{1,0:T(8,128)(2,1)S(1)}, bf16[48,512]{1,0:T(8,128)(2,1)S(1)}, bf16[8,576]{1,0:T(8,128)(2,1)...) custom-call(s32[4]{0:T(128)S(1)} %pad_add_fusion.at_ref.refs_0_, ...), custom_call_target="tpu_custom_call" | custom-call | tf_op jit(solution)/shard_map/pallas_call | solution.py:407
  12.3 1.0 collective-permute-start.2
  13.3 1.6 %collective-permute-start = (bf16[112,512]{1,0:T(8,128)(2,1)S(1)}, bf16[112,512]{1,0:T(8,128)(2,1)S(1)}, u32[]{:S(2)}, u32[]{:S(2)}) collective-permute-start(bf16[112,512]{1,0:T(8,128)(2,1)S(1)} %get-tuple-element.38), channel_id=1, source_target_pairs={{0,24},{8,0},{16,8},{24,16},{1,25},{9,1},{17,9},{25,17},{2,26},{10... | collective-permute-start | bytes 344072 | tf_op jit(solution)/shard_map/ppermute | solution.py:423
  15.3 1.4 %collective-permute-done.4.refs_1_ = bf16[256,256]{1,0:T(8,128)(2,1)S(1)} collective-permute-done((bf16[256,256]{1,0:T(8,128)(2,1)S(1)}, bf16[256,256]{1,0:T(8,128)(2,1)S(1)}, u32[]{:S(2)}, u32[]{:S(2)}) %collective-permute-start.4) | collective-permute-done | bytes 131104 | tf_op jit(solution)/shard_map/ppermute | solution.py:440
  16.6 0.5 shard_map.286.refs_1_
  17.2 3.3 %collective-permute-start.6 = (bf16[128,512]{1,0:T(8,128)(2,1)S(1)}, bf16[128,512]{1,0:T(8,128)(2,1)S(1)}, u32[]{:S(2)}, u32[]{:S(2)}) collective-permute-start(bf16[128,512]{1,0:T(8,128)(2,1)S(1)} %get-tuple-element.50), channel_id=1, source_target_pairs={{0,2},{1,3},{2,4},{3,5},{4,6},{5,7},{6,0},{7,1},{8,10},{9,11},{10,... | collective-permute-start | bytes 393224 | tf_op jit(solution)/shard_map/ppermute | solution.py:440
  20.5 3.4 %collective-permute-start.7 = (bf16[128,512]{1,0:T(8,128)(2,1)S(1)}, bf16[128,512]{1,0:T(8,128)(2,1)S(1)}, u32[]{:S(2)}, u32[]{:S(2)}) collective-permute-start(bf16[128,512]{1,0:T(8,128)(2,1)S(1)} %get-tuple-element.50), channel_id=1, source_target_pairs={{0,4},{1,5},{2,6},{3,7},{4,0},{5,1},{6,2},{7,3},{8,12},{9,13},{10,... | collective-permute-start | bytes 393224 | tf_op jit(solution)/shard_map/ppermute | solution.py:440
  24.0 7.1 %shard_map.287 = (bf16[576,512]{1,0:T(8,128)(2,1)S(1)}, bf16[112,512]{1,0:T(8,128)(2,1)S(1)}, bf16[112,512]{1,0:T(8,128)(2,1)S(1)}, bf16[48,512]{1,0:T(8,128)(2,...) custom-call(bf16[576,512]{1,0:T(8,128)(2,1)S(1)} %bitcast.9, ...), custom_call_target="tpu_custom_call" | custom-call | tf_op jit(solution)/shard_map/pallas_call | solution.py:407
  31.1 1.7 %collective-permute-start.33 = (bf16[48,512]{1,0:T(8,128)(2,1)S(1)}, bf16[48,512]{1,0:T(8,128)(2,1)S(1)}, u32[]{:S(2)}, u32[]{:S(2)}) collective-permute-start(bf16[48,512]{1,0:T(8,128)(2,1)S(1)} %get-tuple-element.61), channel_id=1, source_target_pairs={{0,31},{1,24},{2,25},{3,26},{4,27},{5,28},{6,29},{7,30},{8,7},{9,0... | collective-permute-start | bytes 147464 | tf_op jit(solution)/shard_map/ppermute | solution.py:425
  32.9 0.8 collective-permute-start.31
  33.7 0.5 shard_map.288.refs_3_
  34.3 1.6 %collective-permute-start.10 = (bf16[128,512]{1,0:T(8,128)(2,1)S(1)}, bf16[128,512]{1,0:T(8,128)(2,1)S(1)}, u32[]{:S(2)}, u32[]{:S(2)}) collective-permute-start(bf16[128,512]{1,0:T(8,128)(2,1)S(1)} %get-tuple-element.51), channel_id=1, source_target_pairs={{0,4},{1,5},{2,6},{3,7},{4,0},{5,1},{6,2},{7,3},{8,12},{9,13},{10,... | collective-permute-start | bytes 393224 | tf_op jit(solution)/shard_map/ppermute | solution.py:440
  35.9 2.5 %collective-permute-start.32 = (bf16[112,512]{1,0:T(8,128)(2,1)S(1)}, bf16[112,512]{1,0:T(8,128)(2,1)S(1)}, u32[]{:S(2)}, u32[]{:S(2)}) collective-permute-start(bf16[112,512]{1,0:T(8,128)(2,1)S(1)} %get-tuple-element.60), channel_id=1, source_target_pairs={{0,7},{1,0},{2,1},{3,2},{4,3},{5,4},{6,5},{7,6},{8,15},{9,8},{10,9... | collective-permute-start | bytes 344072 | tf_op jit(solution)/shard_map/ppermute | solution.py:424
  38.3 1.5 %collective-permute-start.16 = (bf16[3,256,256]{2,1,0:T(8,128)(2,1)S(1)}, bf16[3,256,256]{2,1,0:T(8,128)(2,1)S(1)}, u32[]{:S(2)}, u32[]{:S(2)}) collective-permute-start(bf16[3,256,256]{2,1,0:T(8,128)(2,1)S(1)} %shard_map.286.refs_1_), channel_id=1, source_target_pairs={{0,8},{1,17},{2,10},{3,19},{4,12},{5,21},{6,14},{7,23},{8,0},{9,25... | collective-permute-start | bytes 1179656 | tf_op jit(solution)/shard_map/ppermute | solution.py:450
  40.7 1.5 %collective-permute-start.34 = (bf16[3,128,512]{2,1,0:T(8,128)(2,1)S(1)}, bf16[3,128,512]{2,1,0:T(8,128)(2,1)S(1)}, u32[]{:S(2)}, u32[]{:S(2)}) collective-permute-start(bf16[3,128,512]{2,1,0:T(8,128)(2,1)S(1)} %shard_map.288.refs_3_), channel_id=1, source_target_pairs={{0,8},{1,17},{2,10},{3,19},{4,12},{5,21},{6,14},{7,23},{8,0},{9,25... | collective-permute-start | bytes 1179656 | tf_op jit(solution)/shard_map/ppermute | solution.py:450
  42.2 1.5 %collective-permute-done.10.refs_1_ = bf16[128,512]{1,0:T(8,128)(2,1)S(1)} collective-permute-done((bf16[128,512]{1,0:T(8,128)(2,1)S(1)}, bf16[128,512]{1,0:T(8,128)(2,1)S(1)}, u32[]{:S(2)}, u32[]{:S(2)}) %collective-permute-start.10) | collective-permute-done | bytes 131104 | tf_op jit(solution)/shard_map/ppermute | solution.py:440
  43.7 3.0 %collective-permute-start.11 = (bf16[128,512]{1,0:T(8,128)(2,1)S(1)}, bf16[128,512]{1,0:T(8,128)(2,1)S(1)}, u32[]{:S(2)}, u32[]{:S(2)}) collective-permute-start(bf16[128,512]{1,0:T(8,128)(2,1)S(1)} %get-tuple-element.51), channel_id=1, source_target_pairs={{0,6},{1,7},{2,0},{3,1},{4,2},{5,3},{6,4},{7,5},{8,14},{9,15},{10,... | collective-permute-start | bytes 393224 | tf_op jit(solution)/shard_map/ppermute | solution.py:440
  46.7 2.8 %collective-permute-done.11.refs_2_ = bf16[128,512]{1,0:T(8,128)(2,1)S(1)} collective-permute-done((bf16[128,512]{1,0:T(8,128)(2,1)S(1)}, bf16[128,512]{1,0:T(8,128)(2,1)S(1)}, u32[]{:S(2)}, u32[]{:S(2)}) %collective-permute-start.11) | collective-permute-done | bytes 131104 | tf_op jit(solution)/shard_map/ppermute | solution.py:440
  49.5 1.1 %collective-permute-start.9 = (bf16[128,512]{1,0:T(8,128)(2,1)S(1)}, bf16[128,512]{1,0:T(8,128)(2,1)S(1)}, u32[]{:S(2)}, u32[]{:S(2)}) collective-permute-start(bf16[128,512]{1,0:T(8,128)(2,1)S(1)} %get-tuple-element.51), channel_id=1, source_target_pairs={{0,2},{1,3},{2,4},{3,5},{4,6},{5,7},{6,0},{7,1},{8,10},{9,11},{10,... | collective-permute-start | bytes 393224 | tf_op jit(solution)/shard_map/ppermute | solution.py:440
  50.7 6.0 %collective-permute-done.9.refs_0_ = bf16[128,512]{1,0:T(8,128)(2,1)S(1)} collective-permute-done((bf16[128,512]{1,0:T(8,128)(2,1)S(1)}, bf16[128,512]{1,0:T(8,128)(2,1)S(1)}, u32[]{:S(2)}, u32[]{:S(2)}) %collective-permute-start.9) | collective-permute-done | bytes 131104 | tf_op jit(solution)/shard_map/ppermute | solution.py:440
  56.6 1.4 %collective-permute-start.35 = (bf16[3,128,512]{2,1,0:T(8,128)(2,1)S(1)}, bf16[3,128,512]{2,1,0:T(8,128)(2,1)S(1)}, u32[]{:S(2)}, u32[]{:S(2)}) collective-permute-start(bf16[3,128,512]{2,1,0:T(8,128)(2,1)S(1)} %shard_map.288.refs_3_), channel_id=1, source_target_pairs={{0,16},{1,9},{2,18},{3,11},{4,20},{5,13},{6,22},{7,15},{8,24},{9,1... | collective-permute-start | bytes 1179656 | tf_op jit(solution)/shard_map/ppermute | solution.py:450
  58.7 1.5 %collective-permute-start.12 = (bf16[3,128,512]{2,1,0:T(8,128)(2,1)S(1)}, bf16[3,128,512]{2,1,0:T(8,128)(2,1)S(1)}, u32[]{:S(2)}, u32[]{:S(2)}) collective-permute-start(bf16[3,128,512]{2,1,0:T(8,128)(2,1)S(1)} %shard_map.289.refs_3_), channel_id=1, source_target_pairs={{0,8},{1,17},{2,10},{3,19},{4,12},{5,21},{6,14},{7,23},{8,0},{9,25... | collective-permute-start | bytes 1179656 | tf_op jit(solution)/shard_map/ppermute | solution.py:450
  60.2 0.8 collective-permute-start.17
  61.0 6.0 %collective-permute-done.35.refs_5_ = bf16[3,128,512]{2,1,0:T(8,128)(2,1)S(1)} collective-permute-done((bf16[3,128,512]{2,1,0:T(8,128)(2,1)S(1)}, bf16[3,128,512]{2,1,0:T(8,128)(2,1)S(1)}, u32[]{:S(2)}, u32[]{:S(2)}) %collective-permute-start.35) | collective-permute-done | bytes 393248 | tf_op jit(solution)/shard_map/ppermute | solution.py:450
  67.0 2.4 %collective-permute-start.25 = (bf16[3,256,256]{2,1,0:T(8,128)(2,1)S(1)}, bf16[3,256,256]{2,1,0:T(8,128)(2,1)S(1)}, u32[]{:S(2)}, u32[]{:S(2)}) collective-permute-start(bf16[3,256,256]{2,1,0:T(8,128)(2,1)S(1)} %collective-permute-done.16.refs_2_), channel_id=1, source_target_pairs={{0,16},{1,9},{2,18},{3,11},{4,20},{5,13},{6,22},{7,15},{8,24},{9,1... | collective-permute-start | bytes 1179656 | tf_op jit(solution)/shard_map/ppermute | solution.py:450
  69.4 1.3 %collective-permute-done.12.refs_4_ = bf16[3,128,512]{2,1,0:T(8,128)(2,1)S(1)} collective-permute-done((bf16[3,128,512]{2,1,0:T(8,128)(2,1)S(1)}, bf16[3,128,512]{2,1,0:T(8,128)(2,1)S(1)}, u32[]{:S(2)}, u32[]{:S(2)}) %collective-permute-start.12) | collective-permute-done | bytes 393248 | tf_op jit(solution)/shard_map/ppermute | solution.py:450
  70.7 2.1 %collective-permute-done.17.refs_5_ = bf16[3,128,512]{2,1,0:T(8,128)(2,1)S(1)} collective-permute-done((bf16[3,128,512]{2,1,0:T(8,128)(2,1)S(1)}, bf16[3,128,512]{2,1,0:T(8,128)(2,1)S(1)}, u32[]{:S(2)}, u32[]{:S(2)}) %collective-permute-start.17) | collective-permute-done | bytes 393248 | tf_op jit(solution)/shard_map/ppermute | solution.py:450
  73.4 3.7 %collective-permute-done.25.refs_4_ = bf16[3,256,256]{2,1,0:T(8,128)(2,1)S(1)} collective-permute-done((bf16[3,256,256]{2,1,0:T(8,128)(2,1)S(1)}, bf16[3,256,256]{2,1,0:T(8,128)(2,1)S(1)}, u32[]{:S(2)}, u32[]{:S(2)}) %collective-permute-start.25) | collective-permute-done | bytes 393248 | tf_op jit(solution)/shard_map/ppermute | solution.py:450
  77.1 1.4 %collective-permute-start.36 = (bf16[3,128,512]{2,1,0:T(8,128)(2,1)S(1)}, bf16[3,128,512]{2,1,0:T(8,128)(2,1)S(1)}, u32[]{:S(2)}, u32[]{:S(2)}) collective-permute-start(bf16[3,128,512]{2,1,0:T(8,128)(2,1)S(1)} %collective-permute-done.34.refs_4_), channel_id=1, source_target_pairs={{0,16},{1,9},{2,18},{3,11},{4,20},{5,13},{6,22},{7,15},{8,24},{9,1... | collective-permute-start | bytes 1179656 | tf_op jit(solution)/shard_map/ppermute | solution.py:450
  79.0 1.3 %collective-permute-start.18 = (bf16[3,128,512]{2,1,0:T(8,128)(2,1)S(1)}, bf16[3,128,512]{2,1,0:T(8,128)(2,1)S(1)}, u32[]{:S(2)}, u32[]{:S(2)}) collective-permute-start(bf16[3,128,512]{2,1,0:T(8,128)(2,1)S(1)} %collective-permute-done.12.refs_4_), channel_id=1, source_target_pairs={{0,16},{1,9},{2,18},{3,11},{4,20},{5,13},{6,22},{7,15},{8,24},{9,1... | collective-permute-start | bytes 1179656 | tf_op jit(solution)/shard_map/ppermute | solution.py:450
  80.3 4.6 %collective-permute-done.36.refs_6_ = bf16[3,128,512]{2,1,0:T(8,128)(2,1)S(1)} collective-permute-done((bf16[3,128,512]{2,1,0:T(8,128)(2,1)S(1)}, bf16[3,128,512]{2,1,0:T(8,128)(2,1)S(1)}, u32[]{:S(2)}, u32[]{:S(2)}) %collective-permute-start.36) | collective-permute-done | bytes 393248 | tf_op jit(solution)/shard_map/ppermute | solution.py:450
  85.9 3.2 %collective-permute-done.18.refs_6_ = bf16[3,128,512]{2,1,0:T(8,128)(2,1)S(1)} collective-permute-done((bf16[3,128,512]{2,1,0:T(8,128)(2,1)S(1)}, bf16[3,128,512]{2,1,0:T(8,128)(2,1)S(1)}, u32[]{:S(2)}, u32[]{:S(2)}) %collective-permute-start.18) | collective-permute-done | bytes 393248 | tf_op jit(solution)/shard_map/ppermute | solution.py:450
  89.1 1.8 %collective-permute-start.15 = (bf16[48,512]{1,0:T(8,128)(2,1)S(1)}, bf16[48,512]{1,0:T(8,128)(2,1)S(1)}, u32[]{:S(2)}, u32[]{:S(2)}) collective-permute-start(bf16[48,512]{1,0:T(8,128)(2,1)S(1)} %get-tuple-element.54), channel_id=1, source_target_pairs={{0,9},{1,10},{2,11},{3,12},{4,13},{5,14},{6,15},{7,8},{8,17},{9,18... | collective-permute-start | bytes 147464 | tf_op jit(solution)/shard_map/ppermute | solution.py:425
  90.8 1.2 %collective-permute-start.13 = (bf16[112,512]{1,0:T(8,128)(2,1)S(1)}, bf16[112,512]{1,0:T(8,128)(2,1)S(1)}, u32[]{:S(2)}, u32[]{:S(2)}) collective-permute-start(bf16[112,512]{1,0:T(8,128)(2,1)S(1)} %get-tuple-element.52), channel_id=1, source_target_pairs={{0,8},{8,16},{16,24},{24,0},{1,9},{9,17},{17,25},{25,1},{2,10},{10... | collective-permute-start | bytes 344072 | tf_op jit(solution)/shard_map/ppermute | solution.py:423
  92.1 3.5 %shard_map.291.refs_12_ = bf16[144,1024]{1,0:T(8,128)(2,1)S(1)} custom-call(s32[4]{0:T(128)S(1)} %pad_add_fusion.at_ref.refs_0_, bf16[576,1024]{1,0:T(8,128)(2,1)S(1)} %copy-done.4, bf16[256,1024]{1,0:T(8,128)(2,1)S(1)} %copy-done.1, bf16[3,256,256]{2,1,0:T(8,128)(2,1)S(1)} %shard_map.286.refs_1_, bf16[3,256,256]{2,1,0:T(8,128)(2,1)S(1)} %collective-permute-done.16.refs_2_, ...), custom_call_target="tpu_custom_call" | custom-call | tf_op jit(solution)/shard_map/pallas_call | solution.py:407
  95.7 3.5 %shard_map.292.refs_13_ = bf16[2304,144]{1,0:T(8,128)(2,1)S(1)} custom-call(s32[4]{0:T(128)S(1)} %pad_add_fusion.at_ref.refs_0_, bf16[144,640]{1,0:T(8,128)(2,1)S(1)} %copy-done.6, bf16[128,2048]{1,0:T(8,128)(2,1)S(1)} %get-tuple-element.62.refs_2_, bf16[3,128,512]{2,1,0:T(8,128)(2,1)S(1)} %shard_map.288.refs_3_, ...), custom_call_target="tpu_custom_call" | custom-call | tf_op jit(solution)/shard_map/pallas_call | solution.py:407
  99.2 3.0 %shard_map.293 = (bf16[144,1024]{1,0:T(8,128)(2,1)S(1)}, bf16[48,1024]{1,0:T(8,128)(2,1)S(1)}, bf16[48,1024]{1,0:T(8,128)(2,1)S(1)}, bf16[48,1024]{1,0:T(8,128)(2,1)S(1)}) custom-call(s32[4]{0:T(128)S(1)} %pad_add_fusion.at_ref.refs_0_, bf16[144,144]{1,0:T(8,128)(2,1)S(1)} %copy-done.9, bf16[128,2048]{1,0:T(8,128)(2,1)S(1)} %get-tuple-element.57.refs_2_, ...), custom_call_target="tpu_custom_call" | custom-call | tf_op jit(solution)/shard_map/pallas_call | solution.py:407
  102.2 1.5 %collective-permute-start.42 = (bf16[48,1024]{1,0:T(8,128)(2,1)S(1)}, bf16[48,1024]{1,0:T(8,128)(2,1)S(1)}, u32[]{:S(2)}, u32[]{:S(2)}) collective-permute-start(bf16[48,1024]{1,0:T(8,128)(2,1)S(1)} %get-tuple-element.65), channel_id=1, source_target_pairs={{0,8},{8,16},{16,24},{24,0},{1,9},{9,17},{17,25},{25,1},{2,10},{10... | collective-permute-start | bytes 294920 | tf_op jit(solution)/shard_map/ppermute | solution.py:423
  103.8 1.9 %shard_map.290 = bf16[576,512]{1,0:T(8,128)(2,1)} custom-call(bf16[576,1024]{1,0:T(8,128)(2,1)S(1)} %copy-done.3, bf16[576,512]{1,0:T(8,128)(2,1)S(1)} %get-tuple-element.44.own_ref.refs_10_, bf16[112,512]{1,0:T(8,128)(2,1)S(1)} %collective-permute-done.13.lat_ref, bf16[112,512]{1,0:T(8,128)(2,1)S(1)} %collective-permute-done.14.lon_ref, ...), custom_call_target="tpu_custom_call" | custom-call | tf_op jit(solution)/shard_map/pallas_call | solution.py:407
  105.7 2.0 %collective-permute-done.42.lat_ref = bf16[48,1024]{1,0:T(8,128)(2,1)S(1)} collective-permute-done((bf16[48,1024]{1,0:T(8,128)(2,1)S(1)}, bf16[48,1024]{1,0:T(8,128)(2,1)S(1)}, u32[]{:S(2)}, u32[]{:S(2)}) %collective-permute-start.42) | collective-permute-done | bytes 98336 | tf_op jit(solution)/shard_map/ppermute | solution.py:423
  107.7 1.8 %collective-permute-done.43.lon_ref = bf16[48,1024]{1,0:T(8,128)(2,1)S(1)} collective-permute-done((bf16[48,1024]{1,0:T(8,128)(2,1)S(1)}, bf16[48,1024]{1,0:T(8,128)(2,1)S(1)}, u32[]{:S(2)}, u32[]{:S(2)}) %collective-permute-start.43) | collective-permute-done | bytes 98336 | tf_op jit(solution)/shard_map/ppermute | solution.py:424
  109.5 1.9 %collective-permute-done.44.both_ref = bf16[48,1024]{1,0:T(8,128)(2,1)S(1)} collective-permute-done((bf16[48,1024]{1,0:T(8,128)(2,1)S(1)}, bf16[48,1024]{1,0:T(8,128)(2,1)S(1)}, u32[]{:S(2)}, u32[]{:S(2)}) %collective-permute-start.44) | collective-permute-done | bytes 98336 | tf_op jit(solution)/shard_map/ppermute | solution.py:425
  111.5 0.6 shard_map.294
  112.2 1.0 copy.32
  (76 shorter events, 4.3 us)
Async XLA Ops:
  0.7 23.2 %copy-start.8 = (bf16[512,512]{1,0:T(8,128)(2,1)S(1)}, bf16[512,512]{1,0:T(8,128)(2,1)}, u32[]{:S(2)}) copy-start(bf16[512,512]{1,0:T(8,128)(2,1)} %refs_3_.1) | copy-start | bytes 1572868
  2.3 12.6 %collective-permute-start.3 = (bf16[256,256]{1,0:T(8,128)(2,1)S(1)}, bf16[256,256]{1,0:T(8,128)(2,1)S(1)}, u32[]{:S(2)}, u32[]{:S(2)}) collective-permute-start(bf16[256,256]{1,0:T(8,128)(2,1)S(1)} %get-tuple-element.35), channel_id=1, source_target_pairs={{0,2},{1,3},{2,4},{3,5},{4,6},{5,7},{6,0},{7,1},{8,10},{9,11},{10,... | collective-permute-start | bytes 393224 | tf_op jit(solution)/shard_map/ppermute | solution.py:440
  5.4 11.2 %collective-permute-start.4 = (bf16[256,256]{1,0:T(8,128)(2,1)S(1)}, bf16[256,256]{1,0:T(8,128)(2,1)S(1)}, u32[]{:S(2)}, u32[]{:S(2)}) collective-permute-start(bf16[256,256]{1,0:T(8,128)(2,1)S(1)} %get-tuple-element.35), channel_id=1, source_target_pairs={{0,4},{1,5},{2,6},{3,7},{4,0},{5,1},{6,2},{7,3},{8,12},{9,13},{10,... | collective-permute-start | bytes 393224 | tf_op jit(solution)/shard_map/ppermute | solution.py:440
  8.0 8.6 %collective-permute-start.5 = (bf16[256,256]{1,0:T(8,128)(2,1)S(1)}, bf16[256,256]{1,0:T(8,128)(2,1)S(1)}, u32[]{:S(2)}, u32[]{:S(2)}) collective-permute-start(bf16[256,256]{1,0:T(8,128)(2,1)S(1)} %get-tuple-element.35), channel_id=1, source_target_pairs={{0,6},{1,7},{2,0},{3,1},{4,2},{5,3},{6,4},{7,5},{8,14},{9,15},{10,... | collective-permute-start | bytes 393224 | tf_op jit(solution)/shard_map/ppermute | solution.py:440
  12.3 11.6 %collective-permute-start.2 = (bf16[48,512]{1,0:T(8,128)(2,1)S(1)}, bf16[48,512]{1,0:T(8,128)(2,1)S(1)}, u32[]{:S(2)}, u32[]{:S(2)}) collective-permute-start(bf16[48,512]{1,0:T(8,128)(2,1)S(1)} %get-tuple-element.40), channel_id=1, source_target_pairs={{0,31},{1,24},{2,25},{3,26},{4,27},{5,28},{6,29},{7,30},{8,7},{9,0... | collective-permute-start | bytes 147464 | tf_op jit(solution)/shard_map/ppermute | solution.py:425
  13.3 10.6 %collective-permute-start = (bf16[112,512]{1,0:T(8,128)(2,1)S(1)}, bf16[112,512]{1,0:T(8,128)(2,1)S(1)}, u32[]{:S(2)}, u32[]{:S(2)}) collective-permute-start(bf16[112,512]{1,0:T(8,128)(2,1)S(1)} %get-tuple-element.38), channel_id=1, source_target_pairs={{0,24},{8,0},{16,8},{24,16},{1,25},{9,1},{17,9},{25,17},{2,26},{10... | collective-permute-start | bytes 344072 | tf_op jit(solution)/shard_map/ppermute | solution.py:423
  14.9 9.0 %collective-permute-start.1 = (bf16[112,512]{1,0:T(8,128)(2,1)S(1)}, bf16[112,512]{1,0:T(8,128)(2,1)S(1)}, u32[]{:S(2)}, u32[]{:S(2)}) collective-permute-start(bf16[112,512]{1,0:T(8,128)(2,1)S(1)} %get-tuple-element.39), channel_id=1, source_target_pairs={{0,7},{1,0},{2,1},{3,2},{4,3},{5,4},{6,5},{7,6},{8,15},{9,8},{10,9... | collective-permute-start | bytes 344072 | tf_op jit(solution)/shard_map/ppermute | solution.py:424
  17.2 16.5 %collective-permute-start.6 = (bf16[128,512]{1,0:T(8,128)(2,1)S(1)}, bf16[128,512]{1,0:T(8,128)(2,1)S(1)}, u32[]{:S(2)}, u32[]{:S(2)}) collective-permute-start(bf16[128,512]{1,0:T(8,128)(2,1)S(1)} %get-tuple-element.50), channel_id=1, source_target_pairs={{0,2},{1,3},{2,4},{3,5},{4,6},{5,7},{6,0},{7,1},{8,10},{9,11},{10,... | collective-permute-start | bytes 393224 | tf_op jit(solution)/shard_map/ppermute | solution.py:440
  20.5 13.2 %collective-permute-start.7 = (bf16[128,512]{1,0:T(8,128)(2,1)S(1)}, bf16[128,512]{1,0:T(8,128)(2,1)S(1)}, u32[]{:S(2)}, u32[]{:S(2)}) collective-permute-start(bf16[128,512]{1,0:T(8,128)(2,1)S(1)} %get-tuple-element.50), channel_id=1, source_target_pairs={{0,4},{1,5},{2,6},{3,7},{4,0},{5,1},{6,2},{7,3},{8,12},{9,13},{10,... | collective-permute-start | bytes 393224 | tf_op jit(solution)/shard_map/ppermute | solution.py:440
  23.9 9.8 %collective-permute-start.8 = (bf16[128,512]{1,0:T(8,128)(2,1)S(1)}, bf16[128,512]{1,0:T(8,128)(2,1)S(1)}, u32[]{:S(2)}, u32[]{:S(2)}) collective-permute-start(bf16[128,512]{1,0:T(8,128)(2,1)S(1)} %get-tuple-element.50), channel_id=1, source_target_pairs={{0,6},{1,7},{2,0},{3,1},{4,2},{5,3},{6,4},{7,5},{8,14},{9,15},{10,... | collective-permute-start | bytes 393224 | tf_op jit(solution)/shard_map/ppermute | solution.py:440
  24.0 68.1 %copy-start.4 = (bf16[576,1024]{1,0:T(8,128)(2,1)S(1)}, bf16[576,1024]{1,0:T(8,128)(2,1)}, u32[]{:S(2)}) copy-start(bf16[576,1024]{1,0:T(8,128)(2,1)} %constant.100.clone.select_hbm) | copy-start | bytes 3538948
  31.1 35.9 %copy-start.1 = (bf16[256,1024]{1,0:T(8,128)(2,1)S(1)}, bf16[256,1024]{1,0:T(8,128)(2,1)}, u32[]{:S(2)}) copy-start(bf16[256,1024]{1,0:T(8,128)(2,1)} %refs_0_) | copy-start | bytes 1572868
  31.1 8.7 %collective-permute-start.33 = (bf16[48,512]{1,0:T(8,128)(2,1)S(1)}, bf16[48,512]{1,0:T(8,128)(2,1)S(1)}, u32[]{:S(2)}, u32[]{:S(2)}) collective-permute-start(bf16[48,512]{1,0:T(8,128)(2,1)S(1)} %get-tuple-element.61), channel_id=1, source_target_pairs={{0,31},{1,24},{2,25},{3,26},{4,27},{5,28},{6,29},{7,30},{8,7},{9,0... | collective-permute-start | bytes 147464 | tf_op jit(solution)/shard_map/ppermute | solution.py:425
  32.9 7.5 %collective-permute-start.31 = (bf16[112,512]{1,0:T(8,128)(2,1)S(1)}, bf16[112,512]{1,0:T(8,128)(2,1)S(1)}, u32[]{:S(2)}, u32[]{:S(2)}) collective-permute-start(bf16[112,512]{1,0:T(8,128)(2,1)S(1)} %get-tuple-element.59), channel_id=1, source_target_pairs={{0,24},{8,0},{16,8},{24,16},{1,25},{9,1},{17,9},{25,17},{2,26},{10... | collective-permute-start | bytes 344072 | tf_op jit(solution)/shard_map/ppermute | solution.py:423
  34.3 9.5 %collective-permute-start.10 = (bf16[128,512]{1,0:T(8,128)(2,1)S(1)}, bf16[128,512]{1,0:T(8,128)(2,1)S(1)}, u32[]{:S(2)}, u32[]{:S(2)}) collective-permute-start(bf16[128,512]{1,0:T(8,128)(2,1)S(1)} %get-tuple-element.51), channel_id=1, source_target_pairs={{0,4},{1,5},{2,6},{3,7},{4,0},{5,1},{6,2},{7,3},{8,12},{9,13},{10,... | collective-permute-start | bytes 393224 | tf_op jit(solution)/shard_map/ppermute | solution.py:440
  35.9 4.8 %collective-permute-start.32 = (bf16[112,512]{1,0:T(8,128)(2,1)S(1)}, bf16[112,512]{1,0:T(8,128)(2,1)S(1)}, u32[]{:S(2)}, u32[]{:S(2)}) collective-permute-start(bf16[112,512]{1,0:T(8,128)(2,1)S(1)} %get-tuple-element.60), channel_id=1, source_target_pairs={{0,7},{1,0},{2,1},{3,2},{4,3},{5,4},{6,5},{7,6},{8,15},{9,8},{10,9... | collective-permute-start | bytes 344072 | tf_op jit(solution)/shard_map/ppermute | solution.py:424
  38.3 20.3 %collective-permute-start.16 = (bf16[3,256,256]{2,1,0:T(8,128)(2,1)S(1)}, bf16[3,256,256]{2,1,0:T(8,128)(2,1)S(1)}, u32[]{:S(2)}, u32[]{:S(2)}) collective-permute-start(bf16[3,256,256]{2,1,0:T(8,128)(2,1)S(1)} %shard_map.286.refs_1_), channel_id=1, source_target_pairs={{0,8},{1,17},{2,10},{3,19},{4,12},{5,21},{6,14},{7,23},{8,0},{9,25... | collective-permute-start | bytes 1179656 | tf_op jit(solution)/shard_map/ppermute | solution.py:450
  39.8 18.8 %collective-permute-start.24 = (bf16[3,256,256]{2,1,0:T(8,128)(2,1)S(1)}, bf16[3,256,256]{2,1,0:T(8,128)(2,1)S(1)}, u32[]{:S(2)}, u32[]{:S(2)}) collective-permute-start(bf16[3,256,256]{2,1,0:T(8,128)(2,1)S(1)} %shard_map.286.refs_1_), channel_id=1, source_target_pairs={{0,16},{1,9},{2,18},{3,11},{4,20},{5,13},{6,22},{7,15},{8,24},{9,1... | collective-permute-start | bytes 1179656 | tf_op jit(solution)/shard_map/ppermute | solution.py:450
  40.3 19.9 %collective-permute-start.27 = (bf16[3,256,256]{2,1,0:T(8,128)(2,1)S(1)}, bf16[3,256,256]{2,1,0:T(8,128)(2,1)S(1)}, u32[]{:S(2)}, u32[]{:S(2)}) collective-permute-start(bf16[3,256,256]{2,1,0:T(8,128)(2,1)S(1)} %shard_map.286.refs_1_), channel_id=1, source_target_pairs={{0,1},{1,0},{2,3},{3,2},{4,5},{5,4},{6,7},{7,6},{8,9},{9,8},{10,11... | collective-permute-start | bytes 1179656 | tf_op jit(solution)/shard_map/ppermute | solution.py:434
  40.7 20.3 %collective-permute-start.34 = (bf16[3,128,512]{2,1,0:T(8,128)(2,1)S(1)}, bf16[3,128,512]{2,1,0:T(8,128)(2,1)S(1)}, u32[]{:S(2)}, u32[]{:S(2)}) collective-permute-start(bf16[3,128,512]{2,1,0:T(8,128)(2,1)S(1)} %shard_map.288.refs_3_), channel_id=1, source_target_pairs={{0,8},{1,17},{2,10},{3,19},{4,12},{5,21},{6,14},{7,23},{8,0},{9,25... | collective-permute-start | bytes 1179656 | tf_op jit(solution)/shard_map/ppermute | solution.py:450
  43.7 5.8 %collective-permute-start.11 = (bf16[128,512]{1,0:T(8,128)(2,1)S(1)}, bf16[128,512]{1,0:T(8,128)(2,1)S(1)}, u32[]{:S(2)}, u32[]{:S(2)}) collective-permute-start(bf16[128,512]{1,0:T(8,128)(2,1)S(1)} %get-tuple-element.51), channel_id=1, source_target_pairs={{0,6},{1,7},{2,0},{3,1},{4,2},{5,3},{6,4},{7,5},{8,14},{9,15},{10,... | collective-permute-start | bytes 393224 | tf_op jit(solution)/shard_map/ppermute | solution.py:440
  49.5 7.1 %collective-permute-start.9 = (bf16[128,512]{1,0:T(8,128)(2,1)S(1)}, bf16[128,512]{1,0:T(8,128)(2,1)S(1)}, u32[]{:S(2)}, u32[]{:S(2)}) collective-permute-start(bf16[128,512]{1,0:T(8,128)(2,1)S(1)} %get-tuple-element.51), channel_id=1, source_target_pairs={{0,2},{1,3},{2,4},{3,5},{4,6},{5,7},{6,0},{7,1},{8,10},{9,11},{10,... | collective-permute-start | bytes 393224 | tf_op jit(solution)/shard_map/ppermute | solution.py:440
  56.6 10.4 %collective-permute-start.35 = (bf16[3,128,512]{2,1,0:T(8,128)(2,1)S(1)}, bf16[3,128,512]{2,1,0:T(8,128)(2,1)S(1)}, u32[]{:S(2)}, u32[]{:S(2)}) collective-permute-start(bf16[3,128,512]{2,1,0:T(8,128)(2,1)S(1)} %shard_map.288.refs_3_), channel_id=1, source_target_pairs={{0,16},{1,9},{2,18},{3,11},{4,20},{5,13},{6,22},{7,15},{8,24},{9,1... | collective-permute-start | bytes 1179656 | tf_op jit(solution)/shard_map/ppermute | solution.py:450
  58.6 8.4 %collective-permute-start.38 = (bf16[3,128,512]{2,1,0:T(8,128)(2,1)S(1)}, bf16[3,128,512]{2,1,0:T(8,128)(2,1)S(1)}, u32[]{:S(2)}, u32[]{:S(2)}) collective-permute-start(bf16[3,128,512]{2,1,0:T(8,128)(2,1)S(1)} %shard_map.288.refs_3_), channel_id=1, source_target_pairs={{0,1},{1,0},{2,3},{3,2},{4,5},{5,4},{6,7},{7,6},{8,9},{9,8},{10,11... | collective-permute-start | bytes 1179656 | tf_op jit(solution)/shard_map/ppermute | solution.py:434
  58.7 12.1 %collective-permute-start.12 = (bf16[3,128,512]{2,1,0:T(8,128)(2,1)S(1)}, bf16[3,128,512]{2,1,0:T(8,128)(2,1)S(1)}, u32[]{:S(2)}, u32[]{:S(2)}) collective-permute-start(bf16[3,128,512]{2,1,0:T(8,128)(2,1)S(1)} %shard_map.289.refs_3_), channel_id=1, source_target_pairs={{0,8},{1,17},{2,10},{3,19},{4,12},{5,21},{6,14},{7,23},{8,0},{9,25... | collective-permute-start | bytes 1179656 | tf_op jit(solution)/shard_map/ppermute | solution.py:450
  60.2 12.6 %collective-permute-start.17 = (bf16[3,128,512]{2,1,0:T(8,128)(2,1)S(1)}, bf16[3,128,512]{2,1,0:T(8,128)(2,1)S(1)}, u32[]{:S(2)}, u32[]{:S(2)}) collective-permute-start(bf16[3,128,512]{2,1,0:T(8,128)(2,1)S(1)} %shard_map.289.refs_3_), channel_id=1, source_target_pairs={{0,16},{1,9},{2,18},{3,11},{4,20},{5,13},{6,22},{7,15},{8,24},{9,1... | collective-permute-start | bytes 1179656 | tf_op jit(solution)/shard_map/ppermute | solution.py:450
  61.0 11.8 %collective-permute-start.20 = (bf16[3,128,512]{2,1,0:T(8,128)(2,1)S(1)}, bf16[3,128,512]{2,1,0:T(8,128)(2,1)S(1)}, u32[]{:S(2)}, u32[]{:S(2)}) collective-permute-start(bf16[3,128,512]{2,1,0:T(8,128)(2,1)S(1)} %shard_map.289.refs_3_), channel_id=1, source_target_pairs={{0,1},{1,0},{2,3},{3,2},{4,5},{5,4},{6,7},{7,6},{8,9},{9,8},{10,11... | collective-permute-start | bytes 1179656 | tf_op jit(solution)/shard_map/ppermute | solution.py:434
  67.0 12.0 %collective-permute-start.26 = (bf16[256,1024]{1,0:T(8,128)(2,1)S(1)}, bf16[256,1024]{1,0:T(8,128)(2,1)S(1)}, u32[]{:S(2)}, u32[]{:S(2)}) collective-permute-start(bf16[256,1024]{1,0:T(8,128)(2,1)S(1)} %copy-done.1), channel_id=1, source_target_pairs={{0,1},{1,0},{2,3},{3,2},{4,5},{5,4},{6,7},{7,6},{8,9},{9,8},{10,11... | collective-permute-start | bytes 1572872 | tf_op jit(solution)/shard_map/ppermute | solution.py:434
  67.0 10.0 %collective-permute-start.25 = (bf16[3,256,256]{2,1,0:T(8,128)(2,1)S(1)}, bf16[3,256,256]{2,1,0:T(8,128)(2,1)S(1)}, u32[]{:S(2)}, u32[]{:S(2)}) collective-permute-start(bf16[3,256,256]{2,1,0:T(8,128)(2,1)S(1)} %collective-permute-done.16.refs_2_), channel_id=1, source_target_pairs={{0,16},{1,9},{2,18},{3,11},{4,20},{5,13},{6,22},{7,15},{8,24},{9,1... | collective-permute-start | bytes 1179656 | tf_op jit(solution)/shard_map/ppermute | solution.py:450
  70.7 8.3 %collective-permute-start.37 = (bf16[128,2048]{1,0:T(8,128)(2,1)S(1)}, bf16[128,2048]{1,0:T(8,128)(2,1)S(1)}, u32[]{:S(2)}, u32[]{:S(2)}) collective-permute-start(bf16[128,2048]{1,0:T(8,128)(2,1)S(1)} %get-tuple-element.62.refs_2_), channel_id=1, source_target_pairs={{0,1},{1,0},{2,3},{3,2},{4,5},{5,4},{6,7},{7,6},{8,9},{9,8},{10,11... | collective-permute-start | bytes 1572872 | tf_op jit(solution)/shard_map/ppermute | solution.py:434
  72.8 4.2 %collective-permute-start.28 = (bf16[3,256,256]{2,1,0:T(8,128)(2,1)S(1)}, bf16[3,256,256]{2,1,0:T(8,128)(2,1)S(1)}, u32[]{:S(2)}, u32[]{:S(2)}) collective-permute-start(bf16[3,256,256]{2,1,0:T(8,128)(2,1)S(1)} %collective-permute-done.16.refs_2_), channel_id=1, source_target_pairs={{0,1},{1,0},{2,3},{3,2},{4,5},{5,4},{6,7},{7,6},{8,9},{9,8},{10,11... | collective-permute-start | bytes 1179656 | tf_op jit(solution)/shard_map/ppermute | solution.py:434
  72.8 5.6 %collective-permute-start.29 = (bf16[3,256,256]{2,1,0:T(8,128)(2,1)S(1)}, bf16[3,256,256]{2,1,0:T(8,128)(2,1)S(1)}, u32[]{:S(2)}, u32[]{:S(2)}) collective-permute-start(bf16[3,256,256]{2,1,0:T(8,128)(2,1)S(1)} %collective-permute-done.24.refs_3_), channel_id=1, source_target_pairs={{0,1},{1,0},{2,3},{3,2},{4,5},{5,4},{6,7},{7,6},{8,9},{9,8},{10,11... | collective-permute-start | bytes 1179656 | tf_op jit(solution)/shard_map/ppermute | solution.py:434
  77.1 8.4 %collective-permute-start.19 = (bf16[128,2048]{1,0:T(8,128)(2,1)S(1)}, bf16[128,2048]{1,0:T(8,128)(2,1)S(1)}, u32[]{:S(2)}, u32[]{:S(2)}) collective-permute-start(bf16[128,2048]{1,0:T(8,128)(2,1)S(1)} %get-tuple-element.57.refs_2_), channel_id=1, source_target_pairs={{0,1},{1,0},{2,3},{3,2},{4,5},{5,4},{6,7},{7,6},{8,9},{9,8},{10,11... | collective-permute-start | bytes 1572872 | tf_op jit(solution)/shard_map/ppermute | solution.py:434
  77.1 7.8 %collective-permute-start.36 = (bf16[3,128,512]{2,1,0:T(8,128)(2,1)S(1)}, bf16[3,128,512]{2,1,0:T(8,128)(2,1)S(1)}, u32[]{:S(2)}, u32[]{:S(2)}) collective-permute-start(bf16[3,128,512]{2,1,0:T(8,128)(2,1)S(1)} %collective-permute-done.34.refs_4_), channel_id=1, source_target_pairs={{0,16},{1,9},{2,18},{3,11},{4,20},{5,13},{6,22},{7,15},{8,24},{9,1... | collective-permute-start | bytes 1179656 | tf_op jit(solution)/shard_map/ppermute | solution.py:450
  78.5 6.3 %collective-permute-start.39 = (bf16[3,128,512]{2,1,0:T(8,128)(2,1)S(1)}, bf16[3,128,512]{2,1,0:T(8,128)(2,1)S(1)}, u32[]{:S(2)}, u32[]{:S(2)}) collective-permute-start(bf16[3,128,512]{2,1,0:T(8,128)(2,1)S(1)} %collective-permute-done.34.refs_4_), channel_id=1, source_target_pairs={{0,1},{1,0},{2,3},{3,2},{4,5},{5,4},{6,7},{7,6},{8,9},{9,8},{10,11... | collective-permute-start | bytes 1179656 | tf_op jit(solution)/shard_map/ppermute | solution.py:434
  79.0 6.4 %collective-permute-start.40 = (bf16[3,128,512]{2,1,0:T(8,128)(2,1)S(1)}, bf16[3,128,512]{2,1,0:T(8,128)(2,1)S(1)}, u32[]{:S(2)}, u32[]{:S(2)}) collective-permute-start(bf16[3,128,512]{2,1,0:T(8,128)(2,1)S(1)} %collective-permute-done.35.refs_5_), channel_id=1, source_target_pairs={{0,1},{1,0},{2,3},{3,2},{4,5},{5,4},{6,7},{7,6},{8,9},{9,8},{10,11... | collective-permute-start | bytes 1179656 | tf_op jit(solution)/shard_map/ppermute | solution.py:434
  79.0 10.0 %collective-permute-start.18 = (bf16[3,128,512]{2,1,0:T(8,128)(2,1)S(1)}, bf16[3,128,512]{2,1,0:T(8,128)(2,1)S(1)}, u32[]{:S(2)}, u32[]{:S(2)}) collective-permute-start(bf16[3,128,512]{2,1,0:T(8,128)(2,1)S(1)} %collective-permute-done.12.refs_4_), channel_id=1, source_target_pairs={{0,16},{1,9},{2,18},{3,11},{4,20},{5,13},{6,22},{7,15},{8,24},{9,1... | collective-permute-start | bytes 1179656 | tf_op jit(solution)/shard_map/ppermute | solution.py:450
  84.8 4.2 %collective-permute-start.21 = (bf16[3,128,512]{2,1,0:T(8,128)(2,1)S(1)}, bf16[3,128,512]{2,1,0:T(8,128)(2,1)S(1)}, u32[]{:S(2)}, u32[]{:S(2)}) collective-permute-start(bf16[3,128,512]{2,1,0:T(8,128)(2,1)S(1)} %collective-permute-done.12.refs_4_), channel_id=1, source_target_pairs={{0,1},{1,0},{2,3},{3,2},{4,5},{5,4},{6,7},{7,6},{8,9},{9,8},{10,11... | collective-permute-start | bytes 1179656 | tf_op jit(solution)/shard_map/ppermute | solution.py:434
  84.8 6.0 %collective-permute-start.30 = (bf16[3,256,256]{2,1,0:T(8,128)(2,1)S(1)}, bf16[3,256,256]{2,1,0:T(8,128)(2,1)S(1)}, u32[]{:S(2)}, u32[]{:S(2)}) collective-permute-start(bf16[3,256,256]{2,1,0:T(8,128)(2,1)S(1)} %collective-permute-done.25.refs_4_), channel_id=1, source_target_pairs={{0,1},{1,0},{2,3},{3,2},{4,5},{5,4},{6,7},{7,6},{8,9},{9,8},{10,11... | collective-permute-start | bytes 1179656 | tf_op jit(solution)/shard_map/ppermute | solution.py:434
  85.4 6.7 %collective-permute-start.41 = (bf16[3,128,512]{2,1,0:T(8,128)(2,1)S(1)}, bf16[3,128,512]{2,1,0:T(8,128)(2,1)S(1)}, u32[]{:S(2)}, u32[]{:S(2)}) collective-permute-start(bf16[3,128,512]{2,1,0:T(8,128)(2,1)S(1)} %collective-permute-done.36.refs_6_), channel_id=1, source_target_pairs={{0,1},{1,0},{2,3},{3,2},{4,5},{5,4},{6,7},{7,6},{8,9},{9,8},{10,11... | collective-permute-start | bytes 1179656 | tf_op jit(solution)/shard_map/ppermute | solution.py:434
  85.4 13.7 %collective-permute-start.22 = (bf16[3,128,512]{2,1,0:T(8,128)(2,1)S(1)}, bf16[3,128,512]{2,1,0:T(8,128)(2,1)S(1)}, u32[]{:S(2)}, u32[]{:S(2)}) collective-permute-start(bf16[3,128,512]{2,1,0:T(8,128)(2,1)S(1)} %collective-permute-done.17.refs_5_), channel_id=1, source_target_pairs={{0,1},{1,0},{2,3},{3,2},{4,5},{5,4},{6,7},{7,6},{8,9},{9,8},{10,11... | collective-permute-start | bytes 1179656 | tf_op jit(solution)/shard_map/ppermute | solution.py:434
  89.1 10.1 %collective-permute-start.23 = (bf16[3,128,512]{2,1,0:T(8,128)(2,1)S(1)}, bf16[3,128,512]{2,1,0:T(8,128)(2,1)S(1)}, u32[]{:S(2)}, u32[]{:S(2)}) collective-permute-start(bf16[3,128,512]{2,1,0:T(8,128)(2,1)S(1)} %collective-permute-done.18.refs_6_), channel_id=1, source_target_pairs={{0,1},{1,0},{2,3},{3,2},{4,5},{5,4},{6,7},{7,6},{8,9},{9,8},{10,11... | collective-permute-start | bytes 1179656 | tf_op jit(solution)/shard_map/ppermute | solution.py:434
  89.1 14.6 %collective-permute-start.15 = (bf16[48,512]{1,0:T(8,128)(2,1)S(1)}, bf16[48,512]{1,0:T(8,128)(2,1)S(1)}, u32[]{:S(2)}, u32[]{:S(2)}) collective-permute-start(bf16[48,512]{1,0:T(8,128)(2,1)S(1)} %get-tuple-element.54), channel_id=1, source_target_pairs={{0,9},{1,10},{2,11},{3,12},{4,13},{5,14},{6,15},{7,8},{8,17},{9,18... | collective-permute-start | bytes 147464 | tf_op jit(solution)/shard_map/ppermute | solution.py:425
  90.8 13.0 %collective-permute-start.13 = (bf16[112,512]{1,0:T(8,128)(2,1)S(1)}, bf16[112,512]{1,0:T(8,128)(2,1)S(1)}, u32[]{:S(2)}, u32[]{:S(2)}) collective-permute-start(bf16[112,512]{1,0:T(8,128)(2,1)S(1)} %get-tuple-element.52), channel_id=1, source_target_pairs={{0,8},{8,16},{16,24},{24,0},{1,9},{9,17},{17,25},{25,1},{2,10},{10... | collective-permute-start | bytes 344072 | tf_op jit(solution)/shard_map/ppermute | solution.py:423
  92.1 11.8 %collective-permute-start.14 = (bf16[112,512]{1,0:T(8,128)(2,1)S(1)}, bf16[112,512]{1,0:T(8,128)(2,1)S(1)}, u32[]{:S(2)}, u32[]{:S(2)}) collective-permute-start(bf16[112,512]{1,0:T(8,128)(2,1)S(1)} %get-tuple-element.53), channel_id=1, source_target_pairs={{0,1},{1,2},{2,3},{3,4},{4,5},{5,6},{6,7},{7,0},{8,9},{9,10},{10,1... | collective-permute-start | bytes 344072 | tf_op jit(solution)/shard_map/ppermute | solution.py:424
  102.2 5.6 %collective-permute-start.42 = (bf16[48,1024]{1,0:T(8,128)(2,1)S(1)}, bf16[48,1024]{1,0:T(8,128)(2,1)S(1)}, u32[]{:S(2)}, u32[]{:S(2)}) collective-permute-start(bf16[48,1024]{1,0:T(8,128)(2,1)S(1)} %get-tuple-element.65), channel_id=1, source_target_pairs={{0,8},{8,16},{16,24},{24,0},{1,9},{9,17},{17,25},{25,1},{2,10},{10... | collective-permute-start | bytes 294920 | tf_op jit(solution)/shard_map/ppermute | solution.py:423
  103.7 5.8 %collective-permute-start.43 = (bf16[48,1024]{1,0:T(8,128)(2,1)S(1)}, bf16[48,1024]{1,0:T(8,128)(2,1)S(1)}, u32[]{:S(2)}, u32[]{:S(2)}) collective-permute-start(bf16[48,1024]{1,0:T(8,128)(2,1)S(1)} %get-tuple-element.66), channel_id=1, source_target_pairs={{0,1},{1,2},{2,3},{3,4},{4,5},{5,6},{6,7},{7,0},{8,9},{9,10},{10,1... | collective-permute-start | bytes 294920 | tf_op jit(solution)/shard_map/ppermute | solution.py:424
  103.7 7.8 %collective-permute-start.44 = (bf16[48,1024]{1,0:T(8,128)(2,1)S(1)}, bf16[48,1024]{1,0:T(8,128)(2,1)S(1)}, u32[]{:S(2)}, u32[]{:S(2)}) collective-permute-start(bf16[48,1024]{1,0:T(8,128)(2,1)S(1)} %get-tuple-element.67), channel_id=1, source_target_pairs={{0,9},{1,10},{2,11},{3,12},{4,13},{5,14},{6,15},{7,8},{8,17},{9,18... | collective-permute-start | bytes 294920 | tf_op jit(solution)/shard_map/ppermute | solution.py:425
  (7 other events, 78.7 us)

commit v5 on v4

--- a/solution.py
+++ b/solution.py
@@ -168,34 +168,40 @@
     return jnp.broadcast_to(total, (8, total.shape[1])).astype(jnp.bfloat16)
 
 
-def quarters_kernel(at_ref, merge_ref, qkv_ref, out_ref, merge_part, score_part, value_part, sems):
-    corner = at_ref[0]
-    wide = out_ref.shape[1] // 4
-
-    def quarter(ref, first, columns):
-        start = pl.multiple_of(first + corner * columns, LANES)
-        return ref.at[:, pl.ds(start, columns)]
-
-    copies = fetch(
-        sems,
-        (quarter(merge_ref, 0, merge_part.shape[1]), merge_part),
-        (quarter(qkv_ref, 0, 2 * wide), score_part),
-        (quarter(qkv_ref, 8 * wide, wide), value_part.at[:, pl.ds(0, wide)]),
-        (quarter(out_ref, 0, wide), value_part.at[:, pl.ds(wide, wide)]),
-    )
-    for copy in copies:
+def block_sources(group, block, merge_ref, qkv_ref, out_ref):
+    rows, wide = out_ref.shape[0], out_ref.shape[1] // 2
+    if group == 0:
+        at_row = pl.multiple_of((block // 2) * rows, PACK)
+        at_column = pl.multiple_of((block % 2) * wide, LANES)
+        return [(merge_ref.at[pl.ds(at_row, rows), pl.ds(at_column, wide)], pl.ds(0, wide))]
+    if group == 1:
+        return [(qkv_ref.at[:, pl.ds(pl.multiple_of(block * wide, LANES), wide)], pl.ds(0, wide))]
+    half = wide // 2
+    return [
+        (qkv_ref.at[:, pl.ds(pl.multiple_of(4 * wide + block * half, LANES), half)], pl.ds(0, half)),
+        (out_ref.at[:, pl.ds(pl.multiple_of(block * half, LANES), half)], pl.ds(half, half)),
+    ]
+
+
+def quarters_kernel(at_ref, merge_ref, qkv_ref, out_ref, *refs):
+    parts, sems = refs[:3], refs[3]
+    pairs = []
+    for group, part in enumerate(parts):
+        for source, columns in block_sources(group, at_ref[0], merge_ref, qkv_ref, out_ref):
+            pairs.append((source, part.at[:, columns]))
+    for copy in fetch(sems, *pairs):
         copy.wait()
 
 
-def pack_kernel(counts, at_ref, x_hbm, ids_hbm, coarse_ids_hbm, fine_hbm, coarse_hbm, qkv_ref, out_ref, *refs):
-    outs, labels_ref, coarse_labels_ref, score_own, value_own = refs[:3], refs[3], refs[4], refs[5], refs[6]
-    x_ref, ids_ref, coarse_ids_ref, fine_ref, coarse_ref, sems = refs[7:]
+def pack_kernel(counts, at_ref, x_hbm, ids_hbm, coarse_ids_hbm, fine_hbm, coarse_hbm, *refs):
+    weights, (outs, (labels_ref, coarse_labels_ref, owns_ref)) = refs[:3], (refs[3:6], refs[6:9])
+    x_ref, ids_ref, coarse_ids_ref, fine_ref, coarse_ref, sems = refs[9:]
     edge = at_ref[1]
-    wide = out_ref.shape[1] // 4
-    pairs = [(qkv_ref.at[:, pl.ds(0, 8 * wide)], score_own)]
-    for number in range(4):
-        pairs.append((qkv_ref.at[:, pl.ds((8 + number) * wide, wide)], value_own.at[:, pl.ds(2 * number * wide, wide)]))
-        pairs.append((out_ref.at[:, pl.ds(number * wide, wide)], value_own.at[:, pl.ds((2 * number + 1) * wide, wide)]))
+    pairs = []
+    for group in range(3):
+        for block in range(4):
+            for source, columns in block_sources(group, block, *weights):
+                pairs.append((source, owns_ref.at[4 * group + block, :, columns]))
     copies = fetch(
         sems,
         (ids_hbm, ids_ref),
@@ -278,39 +284,49 @@
         first += height
 
 
-def join_kernel(*refs):
-    parts, (out_ref, sems) = refs[:-2], refs[-2:]
-    copies = fetch(sems, *[(part, out_ref.at[number]) for number, part in enumerate(parts)])
-    for copy in copies:
+def join_kernel(plans, *refs):
+    sems, outs = refs[-1], refs[-1 - len(plans) : -1]
+    pairs = []
+    for plan, out_ref in zip(plans, outs):
+        first = 0
+        for number in plan:
+            part = refs[number]
+            if len(part.shape) == 2:
+                pairs.append((part, out_ref.at[first]))
+                first += 1
+            else:
+                pairs.append((part, out_ref.at[pl.ds(first, part.shape[0])]))
+                first += part.shape[0]
+    for copy in fetch(sems, *pairs):
         copy.wait()
 
 
-def start_pieces(whole_ref, pieces, at_ref, sems):
+def start_pieces(whole_ref, sides, at_ref, sems):
     corner, side, here = at_ref[0], at_ref[2], at_ref[3]
-    stops, _, _, columns = whole_ref.shape
-    quarter = columns // 4
+    stops = whole_ref.shape[0]
     copies = []
-    for number, piece in enumerate(pieces):
-        other, kind = number // 5, number % 5
+
+    def put(source, stop, from_side, block):
+        rows, wide = source.shape
+        held = whole_ref.at[stop, from_side]
+        across = whole_ref.shape[3] // wide
+        at_row, at_column = (block // across) * rows, (block % across) * wide
+        target = held.at[pl.ds(pl.multiple_of(at_row, PACK), rows), pl.ds(pl.multiple_of(at_column, LANES), wide)]
+        copies.append(pltpu.make_async_copy(source, target, sems.at[len(copies)]))
+        copies[-1].start()
+
+    for other, (own, *stacks) in enumerate(sides):
         from_side = side ^ other
-        held = whole_ref.at[:, from_side]
-        mask = (None, 0, 1 + from_side, 2 - from_side, 3)[kind]
-        if mask is None:
-            pairs = [(piece, held.at[here])]
-        else:
-            start = pl.multiple_of((corner ^ mask) * quarter, LANES)
-            pairs = [
-                (piece.at[back - 1], held.at[lax.rem(here + (stops - back), stops), :, pl.ds(start, quarter)])
-                for back in range(1, stops)
-            ]
-        for source, target in pairs:
-            copies.append(pltpu.make_async_copy(source, target, sems.at[len(copies)]))
-            copies[-1].start()
+        for block in range(4):
+            put(own.at[block], here, from_side, block)
+        for stack, mask in zip(stacks, (0, 1 + from_side, 2 - from_side, 3)):
+            for back in range(1, stops):
+                put(stack.at[back - 1], lax.rem(here + (stops - back), stops), from_side, corner ^ mask)
     return copies
 
 
 def piece_copies(stops):
-    return 2 * (1 + 4 * (stops - 1))
+    return 2 * (4 + 4 * (stops - 1))
 
 
 def flat(whole_ref):
@@ -318,9 +334,13 @@
     return whole_ref[...].reshape(stops * sides * rows, columns)
 
 
-def merge_kernel(at_ref, select_hbm, *refs):
-    pieces, (y_ref, lat_ref, lon_ref, both_ref, out_ref) = refs[:10], refs[10:15]
-    select_ref, stage_ref, whole_ref, sems, piece_sems = refs[15:]
+def cuts(refs, plan):
+    return [[refs[number].at[pl.ds(first, count)] for number, first, count in side] for side in plan]
+
+
+def merge_kernel(count, plan, at_ref, select_hbm, *refs):
+    pieces, (y_ref, lat_ref, lon_ref, both_ref, out_ref) = cuts(refs[:count], plan), refs[count : count + 5]
+    select_ref, stage_ref, whole_ref, sems, piece_sems = refs[count + 5 :]
     loads = fetch(sems, (select_hbm, select_ref))
     copies = start_pieces(whole_ref, pieces, at_ref, piece_sems)
     fill(stage_ref, (y_ref, lat_ref, lon_ref, both_ref))
@@ -340,9 +360,10 @@
     out_ref[...] = dot(left, flat(whole_ref)).astype(jnp.bfloat16)
 
 
-def scores_kernel(heads, counts, at_ref, select_hbm, *refs):
-    pieces, (merged_ref, labels_ref, lat_ref, lon_ref, both_ref, expos_ref) = refs[:10], refs[10:16]
-    select_ref, whole_ref, packed_ref, sems, piece_sems = refs[16:]
+def scores_kernel(heads, counts, number, plan, at_ref, select_hbm, *refs):
+    pieces = cuts(refs[:number], plan)
+    merged_ref, labels_ref, lat_ref, lon_ref, both_ref, expos_ref = refs[number : number + 6]
+    select_ref, whole_ref, packed_ref, sems, piece_sems = refs[number + 6 :]
     copies = fetch(sems, (select_hbm, select_ref)) + start_pieces(whole_ref, pieces, at_ref, piece_sems)
     count, width = merged_ref.shape
     left = normalized(merged_ref[...].astype(jnp.float32))
@@ -360,9 +381,10 @@
             expos_ref[head * count : (head + 1) * count] = expos
 
 
-def close_kernel(heads, at_ref, pick_hbm, *refs):
-    pieces, (merged_ref, expos_ref, z_ref), packets = refs[:10], refs[10:13], refs[13:16]
-    pick_ref, whole_ref, values_ref, mixed_ref, sems, piece_sems = refs[16:]
+def close_kernel(heads, number, plan, at_ref, pick_hbm, *refs):
+    pieces, (merged_ref, expos_ref, z_ref) = cuts(refs[:number], plan), refs[number : number + 3]
+    packets, refs = refs[number + 3 : number + 6], refs[number + 6 :]
+    pick_ref, whole_ref, values_ref, mixed_ref, sems, piece_sems = refs
     copies = fetch(sems, (pick_hbm, pick_ref)) + start_pieces(whole_ref, pieces, at_ref, piece_sems)
     count, width = merged_ref.shape
     merged = merged_ref[...].astype(jnp.float32)
@@ -450,19 +472,25 @@
     return lax.ppermute(block, ("lat", "lon"), pairs)
 
 
-def joined_parts(far):
-    (near,) = call(
-        join_kernel,
-        [(len(far),) + far[0].shape],
-        [pltpu.SemaphoreType.DMA((len(far),))],
-        hbm=far,
-        hbm_outs=(0,),
-    )
-    return near
-
-
-def own_and_swapped(pieces):
-    return pieces + [exchange(piece, "lon", 1) for piece in pieces]
+def joined(*plans):
+    arrays = []
+    for plan in plans:
+        arrays += [array for array in plan if not any(array is seen for seen in arrays)]
+    numbers = [[next(n for n, seen in enumerate(arrays) if seen is array) for array in plan] for plan in plans]
+    shapes = [
+        (sum(1 if array.ndim == 2 else array.shape[0] for array in plan),) + plan[0].shape[-2:] for plan in plans
+    ]
+    return call(
+        lambda *refs: join_kernel(numbers, *refs),
+        shapes,
+        [pltpu.SemaphoreType.DMA((sum(len(plan) for plan in plans),))],
+        hbm=arrays,
+        hbm_outs=range(len(plans)),
+    )
+
+
+def swapped(pieces):
+    return [exchange(piece, "lon", 1) for piece in pieces]
 
 
 def after(value, *earlier):
@@ -499,7 +527,7 @@
     rows = second_out.shape[0]
     merge_part, score_part, value_part = call(
         quarters_kernel,
-        [(merge_weight.shape[0], wider // 4), (rows, wider // 2), (rows, wider // 2)],
+        [(rows, wider // 2)] * 3,
         [dma(4)],
         scalars=(at,),
         hbm=(merge_weight, second_qkv, second_out),
@@ -516,34 +544,29 @@
     fine = jnp.concatenate(picks(start, [LANES] * 3, cells) + [spreader(breadth, cells)])
     coarse = jnp.concatenate(picks(end, [LANES] * 3, coarse_cells) + [spreader(narrow, coarse_cells)])
     x = tokens.reshape(cells, width)
-    *packets, labels, coarse_labels, score_own, value_own = call(
+    *packets, labels, coarse_labels, owns = call(
         lambda *refs: pack_kernel(counts, *refs),
         [(count, width) for count in packet_rows]
-        + [(8, cells), (8, coarse_cells), (rows, 2 * wider), (rows, 2 * wider)],
+        + [(8, cells), (8, coarse_cells), (12, rows, wider // 2)],
         [
             bf16(cells, width),
             *[pltpu.VMEM((ids.shape[1], levels, ids.shape[2]), jnp.int32) for ids in (level_ids, coarse_ids)],
             bf16(*fine.shape),
             bf16(*coarse.shape),
-            dma(14),
+            dma(21),
         ],
         scalars=(after(at, merge_part),),
-        hbm=(x, *[ids.transpose(1, 0, 2) for ids in (level_ids, coarse_ids)], fine, coarse, second_qkv, second_out),
-        hbm_outs=(5, 6),
+        hbm=(x, *[ids.transpose(1, 0, 2) for ids in (level_ids, coarse_ids)], fine, coarse, merge_weight, second_qkv, second_out),
+        hbm_outs=(5,),
         pinned=True,
     )
     got = shifted(packets, -1)
-    nears, routes = [], []
-    for part in (merge_part, score_part, value_part):
-        near = joined_parts(far_parts(after(part, nears[-1]) if nears else part))
-        first, second = routed(near, 0), routed(near, 1)
-        nears.append(near)
-        routes.append([near, first, second, routed(first, 1)])
-    owns = after((merge_weight, score_own, value_own), routes[0][1])
-    merge_pieces, score_pieces, value_pieces = [
-        own_and_swapped([own] + route) for own, route in zip(owns, routes)
-    ]
-
+    far = stops - 1
+
+    (near1,) = joined(after(far_parts(merge_part), got))
+    first1 = routed(near1, 0)
+    far2 = far_parts(after(score_part, near1))
+    (other,) = swapped([after(owns, near1)])
     source, depth = replaced(cells, start)
     held = np.empty_like(order)
     held[order] = np.arange(cells)
@@ -552,7 +575,7 @@
         picks([inverse[part] for part in middle], packet_rows, cells)
         + picks([inverse[part] for part in start], packet_rows, cells)
     )
-    got_first = after(got, nears[0])
+    got_first = got
     y, *packets = call(
         lambda *refs: first_kernel(HEADS1, counts, *refs),
         [(cells, width)] + [(count, width) for count in packet_rows] * 2,
@@ -570,15 +593,36 @@
         hbm=(x, select, first_qkv, first_out, pick),
         vmem=(labels, *got_first),
     )
-    mid = shifted(packets[:3], -1)
-    back = shifted(after(packets[3:], routes[2][1]), 1)
+    (near2,) = joined(after(far2, first1, y, other))
+    first2 = routed(near2, 0)
+    far3 = far_parts(after(value_part, near2))
+    (join1,) = joined(after([near1, first1], near2))
+    second1 = routed(join1, 1)
+    (near3,) = joined(after(far3, first2, second1))
+    first3 = routed(near3, 0)
+    (join2,) = joined(after([near2, first2], near3))
+    second2 = routed(join2, 1)
+    mid = shifted(after(packets[:3], near3), -1)
+    last_first = after(first3, second2, mid)
+    (join3,) = joined([near3, last_first])
+    second3 = routed(join3, 1)
+    merge_pieces = (owns, join1, second1, other, *swapped(after((join1, second1), last_first)))
+    score_pieces = (owns, join2, second2, other, *swapped(after((join2, second2), last_first)))
+
+    def plan(group):
+        return [
+            [(own, 4 * group, 4), (own + 1, 0, far), (own + 1, far, far), (own + 2, 0, far), (own + 2, far, far)]
+            for own in (0, 3)
+        ]
+
+    merge_plan, score_plan, value_plan = plan(0), plan(1), plan(2)
 
     source, depth = replaced(cells, middle, held)
     fine = source.reshape(levels, low, 2, narrow, 2)
     patches = [fine[:, :, r, :, c].reshape(-1) for r, c in ((0, 0), (1, 0), (0, 1), (1, 1))]
     select = matrix(np.concatenate(patches), depth)
     (merged,) = call(
-        merge_kernel,
+        lambda *refs: merge_kernel(len(merge_pieces), merge_plan, *refs),
         [(coarse_cells, wider)],
         [
             bf16(*select.shape),
@@ -592,6 +636,7 @@
         vmem=(y, *mid),
     )
 
+    back = shifted(after(packets[3:], merged), 1)
     source, depth = replaced(cells, start, held)
     select = matrix(source, depth)
     (skip,) = call(
@@ -605,11 +650,11 @@
     source, depth = replaced(coarse_cells, end)
     select = matrix(source, depth)
     (expos,) = call(
-        lambda *refs: scores_kernel(HEADS2, counts, *refs),
+        lambda *refs: scores_kernel(HEADS2, counts, len(score_pieces), score_plan, *refs),
         [(HEADS2 * coarse_cells, coarse_cells)],
         [
             bf16(*select.shape),
-            bf16(stops, 2, *score_own.shape),
+            bf16(stops, 2, rows, 2 * wider),
             bf16(coarse_cells, 2 * wider),
             dma(1),
             dma(piece_copies(stops)),
@@ -618,13 +663,15 @@
         hbm=(select, *score_pieces),
         vmem=(merged, coarse_labels, *got),
     )
+    value_swapped = swapped([after(join3, last_first), after(second3, back, expos)])
+    value_pieces = (owns, join3, second3, other, *value_swapped)
     pick = jnp.concatenate(picks(end, end_rows, coarse_cells))
     z, *packets = call(
-        lambda *refs: close_kernel(HEADS2, *refs),
+        lambda *refs: close_kernel(HEADS2, len(value_pieces), value_plan, *refs),
         [(coarse_cells, wider)] + [(count, wider) for count in end_rows],
         [
             bf16(*pick.shape),
-            bf16(stops, 2, *value_own.shape),
+            bf16(stops, 2, rows, 2 * wider),
             bf16(coarse_cells, wider),
             bf16(coarse_cells, wider),
             dma(1),

time: 113 us -> 109 us (0.965)
  waiting for transfers between devices: 38.7 us -> 33.4 us
  Pallas kernels: 25.7 us -> 27.2 us
    ppermute x9 -> x6, waiting for transfers between devices: 20.8 us -> 2.32 us  [routed(): return lax.ppermute(block, ('lat', 'lon'), pairs)]
    ppermute x4, starting transfers between devices: 4.61 us -> 17.9 us  [shifted(): lax.ppermute(blocks[2], ('lat', 'lon'), [(i * lon + j, (i + step) % lat *...]
    ppermute x4, waiting for transfers between devices: 1.93 us -> 12.3 us  [shifted(): lax.ppermute(blocks[2], ('lat', 'lon'), [(i * lon + j, (i + step) % lat *...]
    ppermute x9 -> x6, starting transfers between devices: 12.4 us -> 4.46 us  [routed(): return lax.ppermute(block, ('lat', 'lon'), pairs)]
    ppermute x9, starting transfers between devices: 19.4 us -> 15.2 us  [far_parts(): lax.ppermute(part, 'lon', [(i, (i + 2 * back) % ranks) for i in range(ran...]
    ppermute x15 -> x7, waiting for transfers between devices: 0.04 us -> 3.01 us  [exchange(): lax.ppermute(block, axis, [(i, i ^ mask) for i in range(lax.axis_size(axi...]
    ppermute x4, waiting for transfers between devices: 1.99 us -> 4.14 us  [shifted(): lax.ppermute(blocks[0], 'lat', [(i, (i + step) % lat) for i in range(lat)])]
    pallas_call x11 -> x14, Pallas kernels: 25.7 us -> 27.2 us  [call(): pl.pallas_call(kernel, out_shape=[jax.ShapeDtypeStruct(shape, jnp.bfloat1...]
  transfers between devices with their start and end apart: 45 -> 34, of which waited for: 14 -> 12; matrix products, arithmetic and copies ran while one was open for 0% -> 0% of each run, Pallas kernels for 21% -> 15%
where the time goes in v5:
time: 109 us
  starting transfers between devices  46.2 us (42%)
  waiting for transfers between devices  33.4 us (31%)
  Pallas kernels  27.2 us (25%)
  local copies, waits for them, and re-layouts  1.14 us (1%)
    pallas_call x14, Pallas kernels, call(): pl.pallas_call(kernel, out_shape=[jax.ShapeDtypeStruct(shape, jnp.bfloat1...  27.2 us
    ppermute x4, starting transfers between devices, shifted(): lax.ppermute(blocks[2], ('lat', 'lon'), [(i * lon + j, (i + step) % lat *...  17.9 us
    ppermute x9, starting transfers between devices, far_parts(): lax.ppermute(part, 'lon', [(i, (i + 2 * back) % ranks) for i in range(ran...  15.2 us
    ppermute x4, waiting for transfers between devices, shifted(): lax.ppermute(blocks[2], ('lat', 'lon'), [(i * lon + j, (i + step) % lat *...  12.3 us
    ppermute x9, waiting for transfers between devices, far_parts(): lax.ppermute(part, 'lon', [(i, (i + 2 * back) % ranks) for i in range(ran...  10.4 us
    ppermute x4, starting transfers between devices, shifted(): lax.ppermute(blocks[0], 'lat', [(i, (i + step) % lat) for i in range(lat)])  5.02 us
    ppermute x6, starting transfers between devices, routed(): return lax.ppermute(block, ('lat', 'lon'), pairs)  4.46 us
    ppermute x4, waiting for transfers between devices, shifted(): lax.ppermute(blocks[0], 'lat', [(i, (i + step) % lat) for i in range(lat)])  4.14 us
  transfers between devices with their start and end apart: 34, of which 12 were waited for; matrix products, arithmetic and copies ran while one was open for 0% of the time, Pallas kernels for 15%

profile of v5, /device:TPU:0, one launch (start us, length us, event | category | flops | bytes accessed | tf_op | source)
XLA Modules:
  0.0 109.0 jit_solution(5833943809735692512)
XLA Ops:
  0.7 1.6 %shard_map.284 = (bf16[128,512]{1,0:T(8,128)(2,1)S(1)}, bf16[128,512]{1,0:T(8,128)(2,1)S(1)}, bf16[128,512]{1,0:T(8,128)(2,1)S(1)}) custom-call(s32[4]{0:T(128)S(1)} %pad_add_fusion.at_ref.refs_0_, bf16[256,1024]{1,0:T(8,128)(2,1)} %refs_6_.1, bf16[128,3072]{1,0:T(8,128)(2,1)} %refs_7_.1, bf16[128,1024]{1,0:T(8,128)(2,1)} %refs_8_.1), custom_call_target="tpu_custom_call" | custom-call | tf_op jit(solution)/shard_map/pallas_call | solution.py:429
  2.4 3.1 %shard_map.285 = (bf16[112,512]{1,0:T(8,128)(2,1)S(1)}, bf16[112,512]{1,0:T(8,128)(2,1)S(1)}, bf16[48,512]{1,0:T(8,128)(2,1)S(1)}, bf16[8,576]{1,0:T(8,128)(2,1)...) custom-call(s32[4]{0:T(128)S(1)} %pad_add_fusion.at_ref.refs_0_, bf16[576,512]{1,0:T(8,128)(2,1)} %bitcast.8, ...), custom_call_target="tpu_custom_call" | custom-call | tf_op jit(solution)/shard_map/pallas_call | solution.py:429
  5.4 6.4 %collective-permute-start.2 = (bf16[48,512]{1,0:T(8,128)(2,1)S(1)}, bf16[48,512]{1,0:T(8,128)(2,1)S(1)}, u32[]{:S(2)}, u32[]{:S(2)}) collective-permute-start(bf16[48,512]{1,0:T(8,128)(2,1)S(1)} %get-tuple-element.57), channel_id=1, source_target_pairs={{0,31},{1,24},{2,25},{3,26},{4,27},{5,28},{6,29},{7,30},{8,7},{9,0... | collective-permute-start | bytes 147464 | tf_op jit(solution)/shard_map/ppermute | solution.py:447
  11.9 1.0 collective-permute-start.4
  12.9 2.8 %collective-permute-start.5 = (bf16[128,512]{1,0:T(8,128)(2,1)S(1)}, bf16[128,512]{1,0:T(8,128)(2,1)S(1)}, u32[]{:S(2)}, u32[]{:S(2)}) collective-permute-start(bf16[128,512]{1,0:T(8,128)(2,1)S(1)} %get-tuple-element.52), channel_id=1, source_target_pairs={{0,6},{1,7},{2,0},{3,1},{4,2},{5,3},{6,4},{7,5},{8,14},{9,15},{10,... | collective-permute-start | bytes 393224 | tf_op jit(solution)/shard_map/ppermute | solution.py:462
  15.7 0.5 collective-permute-start
  16.4 4.1 %collective-permute-done.refs_6_.refs_10_ = bf16[112,512]{1,0:T(8,128)(2,1)S(1)} collective-permute-done((bf16[112,512]{1,0:T(8,128)(2,1)S(1)}, bf16[112,512]{1,0:T(8,128)(2,1)S(1)}, u32[]{:S(2)}, u32[]{:S(2)}) %collective-permute-start) | collective-permute-done | bytes 114720 | tf_op jit(solution)/shard_map/ppermute | solution.py:445
  20.5 1.2 %collective-permute-done.1.refs_7_.refs_11_ = bf16[112,512]{1,0:T(8,128)(2,1)S(1)} collective-permute-done((bf16[112,512]{1,0:T(8,128)(2,1)S(1)}, bf16[112,512]{1,0:T(8,128)(2,1)S(1)}, u32[]{:S(2)}, u32[]{:S(2)}) %collective-permute-start.1) | collective-permute-done | bytes 114720 | tf_op jit(solution)/shard_map/ppermute | solution.py:446
  21.7 1.3 %collective-permute-done.4.refs_1_ = bf16[128,512]{1,0:T(8,128)(2,1)S(1)} collective-permute-done((bf16[128,512]{1,0:T(8,128)(2,1)S(1)}, bf16[128,512]{1,0:T(8,128)(2,1)S(1)}, u32[]{:S(2)}, u32[]{:S(2)}) %collective-permute-start.4) | collective-permute-done | bytes 131104 | tf_op jit(solution)/shard_map/ppermute | solution.py:462
  23.0 0.5 shard_map.287.refs_0_
  23.5 0.7 collective-permute-start.10
  24.2 3.4 %collective-permute-start.7 = (bf16[128,512]{1,0:T(8,128)(2,1)S(1)}, bf16[128,512]{1,0:T(8,128)(2,1)S(1)}, u32[]{:S(2)}, u32[]{:S(2)}) collective-permute-start(bf16[128,512]{1,0:T(8,128)(2,1)S(1)} %get-tuple-element.67), channel_id=1, source_target_pairs={{0,2},{1,3},{2,4},{3,5},{4,6},{5,7},{6,0},{7,1},{8,10},{9,11},{10,... | collective-permute-start | bytes 393224 | tf_op jit(solution)/shard_map/ppermute | solution.py:462
  27.6 2.2 %collective-permute-start.8 = (bf16[128,512]{1,0:T(8,128)(2,1)S(1)}, bf16[128,512]{1,0:T(8,128)(2,1)S(1)}, u32[]{:S(2)}, u32[]{:S(2)}) collective-permute-start(bf16[128,512]{1,0:T(8,128)(2,1)S(1)} %get-tuple-element.67), channel_id=1, source_target_pairs={{0,4},{1,5},{2,6},{3,7},{4,0},{5,1},{6,2},{7,3},{8,12},{9,13},{10,... | collective-permute-start | bytes 393224 | tf_op jit(solution)/shard_map/ppermute | solution.py:462
  30.0 7.1 %shard_map.286 = (bf16[576,512]{1,0:T(8,128)(2,1)S(1)}, bf16[112,512]{1,0:T(8,128)(2,1)S(1)}, bf16[112,512]{1,0:T(8,128)(2,1)S(1)}, bf16[48,512]{1,0:T(8,128)(2,...) custom-call(bf16[576,512]{1,0:T(8,128)(2,1)S(1)} %bitcast.9, ...), custom_call_target="tpu_custom_call" | custom-call | tf_op jit(solution)/shard_map/pallas_call | solution.py:429
  37.2 2.1 %collective-permute-done.8.refs_1_ = bf16[128,512]{1,0:T(8,128)(2,1)S(1)} collective-permute-done((bf16[128,512]{1,0:T(8,128)(2,1)S(1)}, bf16[128,512]{1,0:T(8,128)(2,1)S(1)}, u32[]{:S(2)}, u32[]{:S(2)}) %collective-permute-start.8) | collective-permute-done | bytes 131104 | tf_op jit(solution)/shard_map/ppermute | solution.py:462
  39.3 0.5 shard_map.288.refs_0_
  40.2 1.2 %collective-permute-start.11 = (bf16[6,128,512]{2,1,0:T(8,128)(2,1)S(1)}, bf16[6,128,512]{2,1,0:T(8,128)(2,1)S(1)}, u32[]{:S(2)}, u32[]{:S(2)}) collective-permute-start(bf16[6,128,512]{2,1,0:T(8,128)(2,1)S(1)} %shard_map.289.refs_3_), channel_id=1, source_target_pairs={{0,16},{1,9},{2,18},{3,11},{4,20},{5,13},{6,22},{7,15},{8,24},{9,1... | collective-permute-start | bytes 2359304 | tf_op jit(solution)/shard_map/ppermute | solution.py:472
  41.5 3.2 %collective-permute-start.12 = (bf16[128,512]{1,0:T(8,128)(2,1)S(1)}, bf16[128,512]{1,0:T(8,128)(2,1)S(1)}, u32[]{:S(2)}, u32[]{:S(2)}) collective-permute-start(bf16[128,512]{1,0:T(8,128)(2,1)S(1)} %get-tuple-element.75), channel_id=1, source_target_pairs={{0,2},{1,3},{2,4},{3,5},{4,6},{5,7},{6,0},{7,1},{8,10},{9,11},{10,... | collective-permute-start | bytes 393224 | tf_op jit(solution)/shard_map/ppermute | solution.py:462
  44.7 0.8 collective-permute-start.13
  45.5 1.6 %collective-permute-start.14 = (bf16[128,512]{1,0:T(8,128)(2,1)S(1)}, bf16[128,512]{1,0:T(8,128)(2,1)S(1)}, u32[]{:S(2)}, u32[]{:S(2)}) collective-permute-start(bf16[128,512]{1,0:T(8,128)(2,1)S(1)} %get-tuple-element.75), channel_id=1, source_target_pairs={{0,6},{1,7},{2,0},{3,1},{4,2},{5,3},{6,4},{7,5},{8,14},{9,15},{10,... | collective-permute-start | bytes 393224 | tf_op jit(solution)/shard_map/ppermute | solution.py:462
  47.1 2.4 %collective-permute-done.12.refs_0_ = bf16[128,512]{1,0:T(8,128)(2,1)S(1)} collective-permute-done((bf16[128,512]{1,0:T(8,128)(2,1)S(1)}, bf16[128,512]{1,0:T(8,128)(2,1)S(1)}, u32[]{:S(2)}, u32[]{:S(2)}) %collective-permute-start.12) | collective-permute-done | bytes 131104 | tf_op jit(solution)/shard_map/ppermute | solution.py:462
  49.5 4.6 %collective-permute-done.13.refs_1_ = bf16[128,512]{1,0:T(8,128)(2,1)S(1)} collective-permute-done((bf16[128,512]{1,0:T(8,128)(2,1)S(1)}, bf16[128,512]{1,0:T(8,128)(2,1)S(1)}, u32[]{:S(2)}, u32[]{:S(2)}) %collective-permute-start.13) | collective-permute-done | bytes 131104 | tf_op jit(solution)/shard_map/ppermute | solution.py:462
  54.1 1.6 %collective-permute-done.11.refs_4_ = bf16[6,128,512]{2,1,0:T(8,128)(2,1)S(1)} collective-permute-done((bf16[6,128,512]{2,1,0:T(8,128)(2,1)S(1)}, bf16[6,128,512]{2,1,0:T(8,128)(2,1)S(1)}, u32[]{:S(2)}, u32[]{:S(2)}) %collective-permute-start.11) | collective-permute-done | bytes 786464 | tf_op jit(solution)/shard_map/ppermute | solution.py:472
  55.8 0.5 shard_map.290.refs_0_
  56.3 0.4 shard_map.291.refs_3_
  56.7 1.0 collective-permute-start.17
  57.7 1.0 collective-permute-start.16
  58.7 1.6 %collective-permute-start.18 = (bf16[112,512]{1,0:T(8,128)(2,1)S(1)}, bf16[112,512]{1,0:T(8,128)(2,1)S(1)}, u32[]{:S(2)}, u32[]{:S(2)}) collective-permute-start(bf16[112,512]{1,0:T(8,128)(2,1)S(1)} %get-tuple-element.84), channel_id=1, source_target_pairs={{0,24},{8,0},{16,8},{24,16},{1,25},{9,1},{17,9},{25,17},{2,26},{10... | collective-permute-start | bytes 344072 | tf_op jit(solution)/shard_map/ppermute | solution.py:445
  60.3 1.6 %collective-permute-start.19 = (bf16[112,512]{1,0:T(8,128)(2,1)S(1)}, bf16[112,512]{1,0:T(8,128)(2,1)S(1)}, u32[]{:S(2)}, u32[]{:S(2)}) collective-permute-start(bf16[112,512]{1,0:T(8,128)(2,1)S(1)} %get-tuple-element.85), channel_id=1, source_target_pairs={{0,7},{1,0},{2,1},{3,2},{4,3},{5,4},{6,5},{7,6},{8,15},{9,8},{10,9... | collective-permute-start | bytes 344072 | tf_op jit(solution)/shard_map/ppermute | solution.py:446
  61.8 2.9 %collective-permute-start.20 = (bf16[48,512]{1,0:T(8,128)(2,1)S(1)}, bf16[48,512]{1,0:T(8,128)(2,1)S(1)}, u32[]{:S(2)}, u32[]{:S(2)}) collective-permute-start(bf16[48,512]{1,0:T(8,128)(2,1)S(1)} %get-tuple-element.86), channel_id=1, source_target_pairs={{0,31},{1,24},{2,25},{3,26},{4,27},{5,28},{6,29},{7,30},{8,7},{9,0... | collective-permute-start | bytes 147464 | tf_op jit(solution)/shard_map/ppermute | solution.py:447
  64.8 10.6 %collective-permute-done.20.refs_11_ = bf16[48,512]{1,0:T(8,128)(2,1)S(1)} collective-permute-done((bf16[48,512]{1,0:T(8,128)(2,1)S(1)}, bf16[48,512]{1,0:T(8,128)(2,1)S(1)}, u32[]{:S(2)}, u32[]{:S(2)}) %collective-permute-start.20) | collective-permute-done | bytes 49184 | tf_op jit(solution)/shard_map/ppermute | solution.py:447
  75.4 0.5 collective-permute-start.22
  76.0 0.4 collective-permute-start.29
  76.8 1.2 %collective-permute-start.26 = (bf16[6,128,512]{2,1,0:T(8,128)(2,1)S(1)}, bf16[6,128,512]{2,1,0:T(8,128)(2,1)S(1)}, u32[]{:S(2)}, u32[]{:S(2)}) collective-permute-start(bf16[6,128,512]{2,1,0:T(8,128)(2,1)S(1)} %shard_map.294.refs_3_), channel_id=1, source_target_pairs={{0,16},{1,9},{2,18},{3,11},{4,20},{5,13},{6,22},{7,15},{8,24},{9,1... | collective-permute-start | bytes 2359304 | tf_op jit(solution)/shard_map/ppermute | solution.py:472
  78.1 0.7 collective-permute-done.22.refs_7_
  78.8 3.5 %shard_map.292.refs_8_ = bf16[144,1024]{1,0:T(8,128)(2,1)S(1)} custom-call(s32[4]{0:T(128)S(1)} %pad_add_fusion.at_ref.refs_0_, bf16[576,1024]{1,0:T(8,128)(2,1)S(1)} %copy-done.2, bf16[12,128,512]{2,1,0:T(8,128)(2,1)S(1)} %get-tuple-element.68.refs_2_, bf16[6,128,512]{2,1,0:T(8,128)(2,1)S(1)} %shard_map.289.refs_3_, ...), custom_call_target="tpu_custom_call" | custom-call | tf_op jit(solution)/shard_map/pallas_call | solution.py:429
  82.4 1.7 %collective-permute-start.23 = (bf16[112,512]{1,0:T(8,128)(2,1)S(1)}, bf16[112,512]{1,0:T(8,128)(2,1)S(1)}, u32[]{:S(2)}, u32[]{:S(2)}) collective-permute-start(bf16[112,512]{1,0:T(8,128)(2,1)S(1)} %get-tuple-element.90), channel_id=1, source_target_pairs={{0,8},{8,16},{16,24},{24,0},{1,9},{9,17},{17,25},{25,1},{2,10},{10... | collective-permute-start | bytes 344072 | tf_op jit(solution)/shard_map/ppermute | solution.py:445
  84.1 4.1 %collective-permute-start.25 = (bf16[48,512]{1,0:T(8,128)(2,1)S(1)}, bf16[48,512]{1,0:T(8,128)(2,1)S(1)}, u32[]{:S(2)}, u32[]{:S(2)}) collective-permute-start(bf16[48,512]{1,0:T(8,128)(2,1)S(1)} %get-tuple-element.92), channel_id=1, source_target_pairs={{0,9},{1,10},{2,11},{3,12},{4,13},{5,14},{6,15},{7,8},{8,17},{9,18... | collective-permute-start | bytes 147464 | tf_op jit(solution)/shard_map/ppermute | solution.py:447
  88.2 3.5 %shard_map.295.refs_9_ = bf16[2304,144]{1,0:T(8,128)(2,1)S(1)} custom-call(s32[4]{0:T(128)S(1)} %pad_add_fusion.at_ref.refs_0_, bf16[144,640]{1,0:T(8,128)(2,1)S(1)} %copy-done.5, bf16[12,128,512]{2,1,0:T(8,128)(2,1)S(1)} %get-tuple-element.68.refs_2_, bf16[6,128,512]{2,1,0:T(8,128)(2,1)S(1)} %shard_map.291.refs_3_, ...), custom_call_target="tpu_custom_call" | custom-call | tf_op jit(solution)/shard_map/pallas_call | solution.py:429
  91.7 0.7 collective-permute-done.26.refs_4_
  92.5 2.3 %collective-permute-done.30.refs_7_ = bf16[6,128,512]{2,1,0:T(8,128)(2,1)S(1)} collective-permute-done((bf16[6,128,512]{2,1,0:T(8,128)(2,1)S(1)}, bf16[6,128,512]{2,1,0:T(8,128)(2,1)S(1)}, u32[]{:S(2)}, u32[]{:S(2)}) %collective-permute-start.30) | collective-permute-done | bytes 786464 | tf_op jit(solution)/shard_map/ppermute | solution.py:456
  94.8 3.1 %shard_map.296 = (bf16[144,1024]{1,0:T(8,128)(2,1)S(1)}, bf16[48,1024]{1,0:T(8,128)(2,1)S(1)}, bf16[48,1024]{1,0:T(8,128)(2,1)S(1)}, bf16[48,1024]{1,0:T(8,128)(2,1)S(1)}) custom-call(s32[4]{0:T(128)S(1)} %pad_add_fusion.at_ref.refs_0_, bf16[144,144]{1,0:T(8,128)(2,1)S(1)} %copy-done.8, bf16[12,128,512]{2,1,0:T(8,128)(2,1)S(1)} %get-tuple-element.68.refs_2_, ...), custom_call_target="tpu_custom_call" | custom-call | tf_op jit(solution)/shard_map/pallas_call | solution.py:429
  97.9 1.2 %collective-permute-start.31 = (bf16[48,1024]{1,0:T(8,128)(2,1)S(1)}, bf16[48,1024]{1,0:T(8,128)(2,1)S(1)}, u32[]{:S(2)}, u32[]{:S(2)}) collective-permute-start(bf16[48,1024]{1,0:T(8,128)(2,1)S(1)} %get-tuple-element.99), channel_id=1, source_target_pairs={{0,8},{8,16},{16,24},{24,0},{1,9},{9,17},{17,25},{25,1},{2,10},{10... | collective-permute-start | bytes 294920 | tf_op jit(solution)/shard_map/ppermute | solution.py:445
  99.1 4.5 %collective-permute-start.33 = (bf16[48,1024]{1,0:T(8,128)(2,1)S(1)}, bf16[48,1024]{1,0:T(8,128)(2,1)S(1)}, u32[]{:S(2)}, u32[]{:S(2)}) collective-permute-start(bf16[48,1024]{1,0:T(8,128)(2,1)S(1)} %get-tuple-element.101), channel_id=1, source_target_pairs={{0,9},{1,10},{2,11},{3,12},{4,13},{5,14},{6,15},{7,8},{8,17},{9,18... | collective-permute-start | bytes 294920 | tf_op jit(solution)/shard_map/ppermute | solution.py:447
  103.6 1.9 %shard_map.293 = bf16[576,512]{1,0:T(8,128)(2,1)} custom-call(bf16[576,1024]{1,0:T(8,128)(2,1)S(1)} %copy-done.3, bf16[576,512]{1,0:T(8,128)(2,1)S(1)} %get-tuple-element.58.refs_8_.own_ref, bf16[112,512]{1,0:T(8,128)(2,1)S(1)} %collective-permute-done.23.lat_ref, bf16[112,512]{1,0:T(8,128)(2,1)S(1)} %collective-permute-done.24.lon_ref, ...), custom_call_target="tpu_custom_call" | custom-call | tf_op jit(solution)/shard_map/pallas_call | solution.py:429
  105.6 1.7 %collective-permute-done.33.both_ref = bf16[48,1024]{1,0:T(8,128)(2,1)S(1)} collective-permute-done((bf16[48,1024]{1,0:T(8,128)(2,1)S(1)}, bf16[48,1024]{1,0:T(8,128)(2,1)S(1)}, u32[]{:S(2)}, u32[]{:S(2)}) %collective-permute-start.33) | collective-permute-done | bytes 98336 | tf_op jit(solution)/shard_map/ppermute | solution.py:447
  107.3 0.6 shard_map.297
  108.0 1.0 copy.32
  (55 shorter events, 1.7 us)
Async XLA Ops:
  0.7 29.3 %copy-start.6 = (bf16[544,576]{1,0:T(8,128)(2,1)S(1)}, bf16[544,576]{1,0:T(8,128)(2,1)}, u32[]{:S(2)}) copy-start(bf16[544,576]{1,0:T(8,128)(2,1)} %constant.107.refs_4_) | copy-start | bytes 1880068
  0.7 29.3 %copy-start.7 = (bf16[512,512]{1,0:T(8,128)(2,1)S(1)}, bf16[512,512]{1,0:T(8,128)(2,1)}, u32[]{:S(2)}) copy-start(bf16[512,512]{1,0:T(8,128)(2,1)} %refs_3_.1) | copy-start | bytes 1572868
  2.3 27.7 %copy-start = (bf16[2,12,24,512]{3,2,1,0:T(8,128)(2,1)S(1)}, bf16[2,12,24,512]{3,2,1,0:T(8,128)(2,1)}, u32[]{:S(2)}) copy-start(bf16[2,12,24,512]{3,2,1,0:T(8,128)(2,1)} %param.29) | copy-start | bytes 1769476
  2.3 27.7 %copy-start.1 = (bf16[512,1536]{1,0:T(8,128)(2,1)S(1)}, bf16[512,1536]{1,0:T(8,128)(2,1)}, u32[]{:S(2)}) copy-start(bf16[512,1536]{1,0:T(8,128)(2,1)} %refs_2_.1) | copy-start | bytes 4718596
  2.4 27.7 %copy-start.4 = (bf16[576,1024]{1,0:T(8,128)(2,1)S(1)}, bf16[576,1024]{1,0:T(8,128)(2,1)}, u32[]{:S(2)}) copy-start(bf16[576,1024]{1,0:T(8,128)(2,1)} %constant.93.clone.refs_1_) | copy-start | bytes 3538948
  5.4 10.8 %collective-permute-start.2 = (bf16[48,512]{1,0:T(8,128)(2,1)S(1)}, bf16[48,512]{1,0:T(8,128)(2,1)S(1)}, u32[]{:S(2)}, u32[]{:S(2)}) collective-permute-start(bf16[48,512]{1,0:T(8,128)(2,1)S(1)} %get-tuple-element.57), channel_id=1, source_target_pairs={{0,31},{1,24},{2,25},{3,26},{4,27},{5,28},{6,29},{7,30},{8,7},{9,0... | collective-permute-start | bytes 147464 | tf_op jit(solution)/shard_map/ppermute | solution.py:447
  11.9 9.9 %collective-permute-start.3 = (bf16[128,512]{1,0:T(8,128)(2,1)S(1)}, bf16[128,512]{1,0:T(8,128)(2,1)S(1)}, u32[]{:S(2)}, u32[]{:S(2)}) collective-permute-start(bf16[128,512]{1,0:T(8,128)(2,1)S(1)} %get-tuple-element.52), channel_id=1, source_target_pairs={{0,2},{1,3},{2,4},{3,5},{4,6},{5,7},{6,0},{7,1},{8,10},{9,11},{10,... | collective-permute-start | bytes 393224 | tf_op jit(solution)/shard_map/ppermute | solution.py:462
  11.9 11.1 %collective-permute-start.4 = (bf16[128,512]{1,0:T(8,128)(2,1)S(1)}, bf16[128,512]{1,0:T(8,128)(2,1)S(1)}, u32[]{:S(2)}, u32[]{:S(2)}) collective-permute-start(bf16[128,512]{1,0:T(8,128)(2,1)S(1)} %get-tuple-element.52), channel_id=1, source_target_pairs={{0,4},{1,5},{2,6},{3,7},{4,0},{5,1},{6,2},{7,3},{8,12},{9,13},{10,... | collective-permute-start | bytes 393224 | tf_op jit(solution)/shard_map/ppermute | solution.py:462
  12.9 10.1 %collective-permute-start.5 = (bf16[128,512]{1,0:T(8,128)(2,1)S(1)}, bf16[128,512]{1,0:T(8,128)(2,1)S(1)}, u32[]{:S(2)}, u32[]{:S(2)}) collective-permute-start(bf16[128,512]{1,0:T(8,128)(2,1)S(1)} %get-tuple-element.52), channel_id=1, source_target_pairs={{0,6},{1,7},{2,0},{3,1},{4,2},{5,3},{6,4},{7,5},{8,14},{9,15},{10,... | collective-permute-start | bytes 393224 | tf_op jit(solution)/shard_map/ppermute | solution.py:462
  15.7 4.8 %collective-permute-start = (bf16[112,512]{1,0:T(8,128)(2,1)S(1)}, bf16[112,512]{1,0:T(8,128)(2,1)S(1)}, u32[]{:S(2)}, u32[]{:S(2)}) collective-permute-start(bf16[112,512]{1,0:T(8,128)(2,1)S(1)} %get-tuple-element.55), channel_id=1, source_target_pairs={{0,24},{8,0},{16,8},{24,16},{1,25},{9,1},{17,9},{25,17},{2,26},{10... | collective-permute-start | bytes 344072 | tf_op jit(solution)/shard_map/ppermute | solution.py:445
  16.2 5.5 %collective-permute-start.1 = (bf16[112,512]{1,0:T(8,128)(2,1)S(1)}, bf16[112,512]{1,0:T(8,128)(2,1)S(1)}, u32[]{:S(2)}, u32[]{:S(2)}) collective-permute-start(bf16[112,512]{1,0:T(8,128)(2,1)S(1)} %get-tuple-element.56), channel_id=1, source_target_pairs={{0,7},{1,0},{2,1},{3,2},{4,3},{5,4},{6,5},{7,6},{8,15},{9,8},{10,9... | collective-permute-start | bytes 344072 | tf_op jit(solution)/shard_map/ppermute | solution.py:446
  23.5 15.7 %collective-permute-start.10 = (bf16[12,128,512]{2,1,0:T(8,128)(2,1)S(1)}, bf16[12,128,512]{2,1,0:T(8,128)(2,1)S(1)}, u32[]{:S(2)}, u32[]{:S(2)}) collective-permute-start(bf16[12,128,512]{2,1,0:T(8,128)(2,1)S(1)} %get-tuple-element.68.refs_2_), channel_id=1, source_target_pairs={{0,1},{1,0},{2,3},{3,2},{4,5},{5,4},{6,7},{7,6},{8,9},{9,8},{10,11... | collective-permute-start | bytes 4718600 | tf_op jit(solution)/shard_map/ppermute | solution.py:456
  24.2 15.1 %collective-permute-start.6 = (bf16[3,128,512]{2,1,0:T(8,128)(2,1)S(1)}, bf16[3,128,512]{2,1,0:T(8,128)(2,1)S(1)}, u32[]{:S(2)}, u32[]{:S(2)}) collective-permute-start(bf16[3,128,512]{2,1,0:T(8,128)(2,1)S(1)} %shard_map.287.refs_0_), channel_id=1, source_target_pairs={{0,8},{1,17},{2,10},{3,19},{4,12},{5,21},{6,14},{7,23},{8,0},{9,25... | collective-permute-start | bytes 1179656 | tf_op jit(solution)/shard_map/ppermute | solution.py:472
  24.2 13.0 %collective-permute-start.7 = (bf16[128,512]{1,0:T(8,128)(2,1)S(1)}, bf16[128,512]{1,0:T(8,128)(2,1)S(1)}, u32[]{:S(2)}, u32[]{:S(2)}) collective-permute-start(bf16[128,512]{1,0:T(8,128)(2,1)S(1)} %get-tuple-element.67), channel_id=1, source_target_pairs={{0,2},{1,3},{2,4},{3,5},{4,6},{5,7},{6,0},{7,1},{8,10},{9,11},{10,... | collective-permute-start | bytes 393224 | tf_op jit(solution)/shard_map/ppermute | solution.py:462
  27.6 11.6 %collective-permute-start.8 = (bf16[128,512]{1,0:T(8,128)(2,1)S(1)}, bf16[128,512]{1,0:T(8,128)(2,1)S(1)}, u32[]{:S(2)}, u32[]{:S(2)}) collective-permute-start(bf16[128,512]{1,0:T(8,128)(2,1)S(1)} %get-tuple-element.67), channel_id=1, source_target_pairs={{0,4},{1,5},{2,6},{3,7},{4,0},{5,1},{6,2},{7,3},{8,12},{9,13},{10,... | collective-permute-start | bytes 393224 | tf_op jit(solution)/shard_map/ppermute | solution.py:462
  29.9 9.4 %collective-permute-start.9 = (bf16[128,512]{1,0:T(8,128)(2,1)S(1)}, bf16[128,512]{1,0:T(8,128)(2,1)S(1)}, u32[]{:S(2)}, u32[]{:S(2)}) collective-permute-start(bf16[128,512]{1,0:T(8,128)(2,1)S(1)} %get-tuple-element.67), channel_id=1, source_target_pairs={{0,6},{1,7},{2,0},{3,1},{4,2},{5,3},{6,4},{7,5},{8,14},{9,15},{10,... | collective-permute-start | bytes 393224 | tf_op jit(solution)/shard_map/ppermute | solution.py:462
  40.2 15.5 %collective-permute-start.11 = (bf16[6,128,512]{2,1,0:T(8,128)(2,1)S(1)}, bf16[6,128,512]{2,1,0:T(8,128)(2,1)S(1)}, u32[]{:S(2)}, u32[]{:S(2)}) collective-permute-start(bf16[6,128,512]{2,1,0:T(8,128)(2,1)S(1)} %shard_map.289.refs_3_), channel_id=1, source_target_pairs={{0,16},{1,9},{2,18},{3,11},{4,20},{5,13},{6,22},{7,15},{8,24},{9,1... | collective-permute-start | bytes 2359304 | tf_op jit(solution)/shard_map/ppermute | solution.py:472
  41.4 12.8 %collective-permute-start.15 = (bf16[3,128,512]{2,1,0:T(8,128)(2,1)S(1)}, bf16[3,128,512]{2,1,0:T(8,128)(2,1)S(1)}, u32[]{:S(2)}, u32[]{:S(2)}) collective-permute-start(bf16[3,128,512]{2,1,0:T(8,128)(2,1)S(1)} %shard_map.288.refs_0_), channel_id=1, source_target_pairs={{0,8},{1,17},{2,10},{3,19},{4,12},{5,21},{6,14},{7,23},{8,0},{9,25... | collective-permute-start | bytes 1179656 | tf_op jit(solution)/shard_map/ppermute | solution.py:472
  41.5 8.0 %collective-permute-start.12 = (bf16[128,512]{1,0:T(8,128)(2,1)S(1)}, bf16[128,512]{1,0:T(8,128)(2,1)S(1)}, u32[]{:S(2)}, u32[]{:S(2)}) collective-permute-start(bf16[128,512]{1,0:T(8,128)(2,1)S(1)} %get-tuple-element.75), channel_id=1, source_target_pairs={{0,2},{1,3},{2,4},{3,5},{4,6},{5,7},{6,0},{7,1},{8,10},{9,11},{10,... | collective-permute-start | bytes 393224 | tf_op jit(solution)/shard_map/ppermute | solution.py:462
  44.7 9.4 %collective-permute-start.13 = (bf16[128,512]{1,0:T(8,128)(2,1)S(1)}, bf16[128,512]{1,0:T(8,128)(2,1)S(1)}, u32[]{:S(2)}, u32[]{:S(2)}) collective-permute-start(bf16[128,512]{1,0:T(8,128)(2,1)S(1)} %get-tuple-element.75), channel_id=1, source_target_pairs={{0,4},{1,5},{2,6},{3,7},{4,0},{5,1},{6,2},{7,3},{8,12},{9,13},{10,... | collective-permute-start | bytes 393224 | tf_op jit(solution)/shard_map/ppermute | solution.py:462
  45.5 8.6 %collective-permute-start.14 = (bf16[128,512]{1,0:T(8,128)(2,1)S(1)}, bf16[128,512]{1,0:T(8,128)(2,1)S(1)}, u32[]{:S(2)}, u32[]{:S(2)}) collective-permute-start(bf16[128,512]{1,0:T(8,128)(2,1)S(1)} %get-tuple-element.75), channel_id=1, source_target_pairs={{0,6},{1,7},{2,0},{3,1},{4,2},{5,3},{6,4},{7,5},{8,14},{9,15},{10,... | collective-permute-start | bytes 393224 | tf_op jit(solution)/shard_map/ppermute | solution.py:462
  56.7 22.1 %copy-start.2 = (bf16[576,1024]{1,0:T(8,128)(2,1)S(1)}, bf16[576,1024]{1,0:T(8,128)(2,1)}, u32[]{:S(2)}) copy-start(bf16[576,1024]{1,0:T(8,128)(2,1)} %constant.100.clone.refs_1_) | copy-start | bytes 3538948
  56.7 18.6 %collective-permute-start.17 = (bf16[6,128,512]{2,1,0:T(8,128)(2,1)S(1)}, bf16[6,128,512]{2,1,0:T(8,128)(2,1)S(1)}, u32[]{:S(2)}, u32[]{:S(2)}) collective-permute-start(bf16[6,128,512]{2,1,0:T(8,128)(2,1)S(1)} %shard_map.291.refs_3_), channel_id=1, source_target_pairs={{0,16},{1,9},{2,18},{3,11},{4,20},{5,13},{6,22},{7,15},{8,24},{9,1... | collective-permute-start | bytes 2359304 | tf_op jit(solution)/shard_map/ppermute | solution.py:472
  57.7 17.6 %collective-permute-start.16 = (bf16[3,128,512]{2,1,0:T(8,128)(2,1)S(1)}, bf16[3,128,512]{2,1,0:T(8,128)(2,1)S(1)}, u32[]{:S(2)}, u32[]{:S(2)}) collective-permute-start(bf16[3,128,512]{2,1,0:T(8,128)(2,1)S(1)} %shard_map.290.refs_0_), channel_id=1, source_target_pairs={{0,8},{1,17},{2,10},{3,19},{4,12},{5,21},{6,14},{7,23},{8,0},{9,25... | collective-permute-start | bytes 1179656 | tf_op jit(solution)/shard_map/ppermute | solution.py:472
  58.7 16.6 %collective-permute-start.18 = (bf16[112,512]{1,0:T(8,128)(2,1)S(1)}, bf16[112,512]{1,0:T(8,128)(2,1)S(1)}, u32[]{:S(2)}, u32[]{:S(2)}) collective-permute-start(bf16[112,512]{1,0:T(8,128)(2,1)S(1)} %get-tuple-element.84), channel_id=1, source_target_pairs={{0,24},{8,0},{16,8},{24,16},{1,25},{9,1},{17,9},{25,17},{2,26},{10... | collective-permute-start | bytes 344072 | tf_op jit(solution)/shard_map/ppermute | solution.py:445
  60.3 15.1 %collective-permute-start.19 = (bf16[112,512]{1,0:T(8,128)(2,1)S(1)}, bf16[112,512]{1,0:T(8,128)(2,1)S(1)}, u32[]{:S(2)}, u32[]{:S(2)}) collective-permute-start(bf16[112,512]{1,0:T(8,128)(2,1)S(1)} %get-tuple-element.85), channel_id=1, source_target_pairs={{0,7},{1,0},{2,1},{3,2},{4,3},{5,4},{6,5},{7,6},{8,15},{9,8},{10,9... | collective-permute-start | bytes 344072 | tf_op jit(solution)/shard_map/ppermute | solution.py:446
  61.8 13.5 %collective-permute-start.20 = (bf16[48,512]{1,0:T(8,128)(2,1)S(1)}, bf16[48,512]{1,0:T(8,128)(2,1)S(1)}, u32[]{:S(2)}, u32[]{:S(2)}) collective-permute-start(bf16[48,512]{1,0:T(8,128)(2,1)S(1)} %get-tuple-element.86), channel_id=1, source_target_pairs={{0,31},{1,24},{2,25},{3,26},{4,27},{5,28},{6,29},{7,30},{8,7},{9,0... | collective-permute-start | bytes 147464 | tf_op jit(solution)/shard_map/ppermute | solution.py:447
  75.3 2.7 %collective-permute-start.21 = (bf16[6,128,512]{2,1,0:T(8,128)(2,1)S(1)}, bf16[6,128,512]{2,1,0:T(8,128)(2,1)S(1)}, u32[]{:S(2)}, u32[]{:S(2)}) collective-permute-start(bf16[6,128,512]{2,1,0:T(8,128)(2,1)S(1)} %shard_map.289.refs_3_), channel_id=1, source_target_pairs={{0,1},{1,0},{2,3},{3,2},{4,5},{5,4},{6,7},{7,6},{8,9},{9,8},{10,11... | collective-permute-start | bytes 2359304 | tf_op jit(solution)/shard_map/ppermute | solution.py:456
  75.4 3.4 %collective-permute-start.22 = (bf16[6,128,512]{2,1,0:T(8,128)(2,1)S(1)}, bf16[6,128,512]{2,1,0:T(8,128)(2,1)S(1)}, u32[]{:S(2)}, u32[]{:S(2)}) collective-permute-start(bf16[6,128,512]{2,1,0:T(8,128)(2,1)S(1)} %collective-permute-done.11.refs_4_), channel_id=1, source_target_pairs={{0,1},{1,0},{2,3},{3,2},{4,5},{5,4},{6,7},{7,6},{8,9},{9,8},{10,11... | collective-permute-start | bytes 2359304 | tf_op jit(solution)/shard_map/ppermute | solution.py:456
  75.9 8.2 %collective-permute-start.28 = (bf16[6,128,512]{2,1,0:T(8,128)(2,1)S(1)}, bf16[6,128,512]{2,1,0:T(8,128)(2,1)S(1)}, u32[]{:S(2)}, u32[]{:S(2)}) collective-permute-start(bf16[6,128,512]{2,1,0:T(8,128)(2,1)S(1)} %shard_map.291.refs_3_), channel_id=1, source_target_pairs={{0,1},{1,0},{2,3},{3,2},{4,5},{5,4},{6,7},{7,6},{8,9},{9,8},{10,11... | collective-permute-start | bytes 2359304 | tf_op jit(solution)/shard_map/ppermute | solution.py:456
  76.0 12.2 %collective-permute-start.29 = (bf16[6,128,512]{2,1,0:T(8,128)(2,1)S(1)}, bf16[6,128,512]{2,1,0:T(8,128)(2,1)S(1)}, u32[]{:S(2)}, u32[]{:S(2)}) collective-permute-start(bf16[6,128,512]{2,1,0:T(8,128)(2,1)S(1)} %collective-permute-done.17.refs_4_), channel_id=1, source_target_pairs={{0,1},{1,0},{2,3},{3,2},{4,5},{5,4},{6,7},{7,6},{8,9},{9,8},{10,11... | collective-permute-start | bytes 2359304 | tf_op jit(solution)/shard_map/ppermute | solution.py:456
  76.8 11.3 %copy-start.5 = (bf16[144,640]{1,0:T(8,128)(2,1)S(1)}, bf16[144,640]{1,0:T(8,128)(2,1)}, u32[]{:S(2)}) copy-start(bf16[144,640]{1,0:T(8,128)(2,1)} %constant.102.clone.refs_1_.select_hbm) | copy-start | bytes 552964
  76.8 15.6 %collective-permute-start.26 = (bf16[6,128,512]{2,1,0:T(8,128)(2,1)S(1)}, bf16[6,128,512]{2,1,0:T(8,128)(2,1)S(1)}, u32[]{:S(2)}, u32[]{:S(2)}) collective-permute-start(bf16[6,128,512]{2,1,0:T(8,128)(2,1)S(1)} %shard_map.294.refs_3_), channel_id=1, source_target_pairs={{0,16},{1,9},{2,18},{3,11},{4,20},{5,13},{6,22},{7,15},{8,24},{9,1... | collective-permute-start | bytes 2359304 | tf_op jit(solution)/shard_map/ppermute | solution.py:472
  82.4 10.0 %collective-permute-start.23 = (bf16[112,512]{1,0:T(8,128)(2,1)S(1)}, bf16[112,512]{1,0:T(8,128)(2,1)S(1)}, u32[]{:S(2)}, u32[]{:S(2)}) collective-permute-start(bf16[112,512]{1,0:T(8,128)(2,1)S(1)} %get-tuple-element.90), channel_id=1, source_target_pairs={{0,8},{8,16},{16,24},{24,0},{1,9},{9,17},{17,25},{25,1},{2,10},{10... | collective-permute-start | bytes 344072 | tf_op jit(solution)/shard_map/ppermute | solution.py:445
  84.1 8.3 %collective-permute-start.24 = (bf16[112,512]{1,0:T(8,128)(2,1)S(1)}, bf16[112,512]{1,0:T(8,128)(2,1)S(1)}, u32[]{:S(2)}, u32[]{:S(2)}) collective-permute-start(bf16[112,512]{1,0:T(8,128)(2,1)S(1)} %get-tuple-element.91), channel_id=1, source_target_pairs={{0,1},{1,2},{2,3},{3,4},{4,5},{5,6},{6,7},{7,0},{8,9},{9,10},{10,1... | collective-permute-start | bytes 344072 | tf_op jit(solution)/shard_map/ppermute | solution.py:446
  84.1 8.3 %collective-permute-start.25 = (bf16[48,512]{1,0:T(8,128)(2,1)S(1)}, bf16[48,512]{1,0:T(8,128)(2,1)S(1)}, u32[]{:S(2)}, u32[]{:S(2)}) collective-permute-start(bf16[48,512]{1,0:T(8,128)(2,1)S(1)} %get-tuple-element.92), channel_id=1, source_target_pairs={{0,9},{1,10},{2,11},{3,12},{4,13},{5,14},{6,15},{7,8},{8,17},{9,18... | collective-permute-start | bytes 147464 | tf_op jit(solution)/shard_map/ppermute | solution.py:447
  88.2 4.3 %collective-permute-start.27 = (bf16[6,128,512]{2,1,0:T(8,128)(2,1)S(1)}, bf16[6,128,512]{2,1,0:T(8,128)(2,1)S(1)}, u32[]{:S(2)}, u32[]{:S(2)}) collective-permute-start(bf16[6,128,512]{2,1,0:T(8,128)(2,1)S(1)} %shard_map.294.refs_3_), channel_id=1, source_target_pairs={{0,1},{1,0},{2,3},{3,2},{4,5},{5,4},{6,7},{7,6},{8,9},{9,8},{10,11... | collective-permute-start | bytes 2359304 | tf_op jit(solution)/shard_map/ppermute | solution.py:456
  88.2 6.6 %copy-start.8 = (bf16[144,144]{1,0:T(8,128)(2,1)S(1)}, bf16[144,144]{1,0:T(8,128)(2,1)}, u32[]{:S(2)}) copy-start(bf16[144,144]{1,0:T(8,128)(2,1)} %constant.112.refs_1_) | copy-start | bytes 124420
  91.7 11.9 %copy-start.3 = (bf16[576,1024]{1,0:T(8,128)(2,1)S(1)}, bf16[576,1024]{1,0:T(8,128)(2,1)}, u32[]{:S(2)}) copy-start(bf16[576,1024]{1,0:T(8,128)(2,1)} %constant.101.clone.select_hbm) | copy-start | bytes 3538948
  92.4 2.4 %collective-permute-start.30 = (bf16[6,128,512]{2,1,0:T(8,128)(2,1)S(1)}, bf16[6,128,512]{2,1,0:T(8,128)(2,1)S(1)}, u32[]{:S(2)}, u32[]{:S(2)}) collective-permute-start(bf16[6,128,512]{2,1,0:T(8,128)(2,1)S(1)} %collective-permute-done.26.refs_4_), channel_id=1, source_target_pairs={{0,1},{1,0},{2,3},{3,2},{4,5},{5,4},{6,7},{7,6},{8,9},{9,8},{10,11... | collective-permute-start | bytes 2359304 | tf_op jit(solution)/shard_map/ppermute | solution.py:456
  97.9 7.7 %collective-permute-start.31 = (bf16[48,1024]{1,0:T(8,128)(2,1)S(1)}, bf16[48,1024]{1,0:T(8,128)(2,1)S(1)}, u32[]{:S(2)}, u32[]{:S(2)}) collective-permute-start(bf16[48,1024]{1,0:T(8,128)(2,1)S(1)} %get-tuple-element.99), channel_id=1, source_target_pairs={{0,8},{8,16},{16,24},{24,0},{1,9},{9,17},{17,25},{25,1},{2,10},{10... | collective-permute-start | bytes 294920 | tf_op jit(solution)/shard_map/ppermute | solution.py:445
  99.0 6.5 %collective-permute-start.32 = (bf16[48,1024]{1,0:T(8,128)(2,1)S(1)}, bf16[48,1024]{1,0:T(8,128)(2,1)S(1)}, u32[]{:S(2)}, u32[]{:S(2)}) collective-permute-start(bf16[48,1024]{1,0:T(8,128)(2,1)S(1)} %get-tuple-element.100), channel_id=1, source_target_pairs={{0,1},{1,2},{2,3},{3,4},{4,5},{5,6},{6,7},{7,0},{8,9},{9,10},{10,1... | collective-permute-start | bytes 294920 | tf_op jit(solution)/shard_map/ppermute | solution.py:446
  99.1 8.1 %collective-permute-start.33 = (bf16[48,1024]{1,0:T(8,128)(2,1)S(1)}, bf16[48,1024]{1,0:T(8,128)(2,1)S(1)}, u32[]{:S(2)}, u32[]{:S(2)}) collective-permute-start(bf16[48,1024]{1,0:T(8,128)(2,1)S(1)} %get-tuple-element.101), channel_id=1, source_target_pairs={{0,9},{1,10},{2,11},{3,12},{4,13},{5,14},{6,15},{7,8},{8,17},{9,18... | collective-permute-start | bytes 294920 | tf_op jit(solution)/shard_map/ppermute | solution.py:447

commit v6 on v5

--- a/solution.py
+++ b/solution.py
@@ -183,22 +183,14 @@
     ]
 
 
-def quarters_kernel(at_ref, merge_ref, qkv_ref, out_ref, *refs):
-    parts, sems = refs[:3], refs[3]
+def pack_kernel(counts, at_ref, x_hbm, ids_hbm, coarse_ids_hbm, fine_hbm, coarse_hbm, *refs):
+    weights, outs, labels_ref, coarse_labels_ref, owns_ref, parts = refs[:3], refs[3:6], *refs[6:9], refs[9:12]
+    x_ref, ids_ref, coarse_ids_ref, fine_ref, coarse_ref, sems = refs[12:]
+    edge = at_ref[1]
     pairs = []
     for group, part in enumerate(parts):
-        for source, columns in block_sources(group, at_ref[0], merge_ref, qkv_ref, out_ref):
+        for source, columns in block_sources(group, at_ref[0], *weights):
             pairs.append((source, part.at[:, columns]))
-    for copy in fetch(sems, *pairs):
-        copy.wait()
-
-
-def pack_kernel(counts, at_ref, x_hbm, ids_hbm, coarse_ids_hbm, fine_hbm, coarse_hbm, *refs):
-    weights, (outs, (labels_ref, coarse_labels_ref, owns_ref)) = refs[:3], (refs[3:6], refs[6:9])
-    x_ref, ids_ref, coarse_ids_ref, fine_ref, coarse_ref, sems = refs[9:]
-    edge = at_ref[1]
-    pairs = []
-    for group in range(3):
         for block in range(4):
             for source, columns in block_sources(group, block, *weights):
                 pairs.append((source, owns_ref.at[4 * group + block, :, columns]))
@@ -525,18 +517,9 @@
     order = window_order(levels, height, breadth)
     inverse = np.argsort(order)
     rows = second_out.shape[0]
-    merge_part, score_part, value_part = call(
-        quarters_kernel,
-        [(rows, wider // 2)] * 3,
-        [dma(4)],
-        scalars=(at,),
-        hbm=(merge_weight, second_qkv, second_out),
-        hbm_outs=(0, 1, 2),
-        pinned=True,
-    )
-
-    def picks(parts, rows, columns):
-        return [matrix(part, columns, count) for part, count in zip(parts, rows)]
+
+    def picks(parts, counts, columns):
+        return [matrix(part, columns, count) for part, count in zip(parts, counts)]
 
     def spreader(columns, count):
         return matrix(np.arange(count) % columns, up(columns, PACK)).T
@@ -544,20 +527,21 @@
     fine = jnp.concatenate(picks(start, [LANES] * 3, cells) + [spreader(breadth, cells)])
     coarse = jnp.concatenate(picks(end, [LANES] * 3, coarse_cells) + [spreader(narrow, coarse_cells)])
     x = tokens.reshape(cells, width)
-    *packets, labels, coarse_labels, owns = call(
+    *packets, labels, coarse_labels, owns, merge_part, score_part, value_part = call(
         lambda *refs: pack_kernel(counts, *refs),
         [(count, width) for count in packet_rows]
-        + [(8, cells), (8, coarse_cells), (12, rows, wider // 2)],
+        + [(8, cells), (8, coarse_cells), (12, rows, wider // 2)]
+        + [(rows, wider // 2)] * 3,
         [
             bf16(cells, width),
             *[pltpu.VMEM((ids.shape[1], levels, ids.shape[2]), jnp.int32) for ids in (level_ids, coarse_ids)],
             bf16(*fine.shape),
             bf16(*coarse.shape),
-            dma(21),
+            dma(25),
         ],
-        scalars=(after(at, merge_part),),
+        scalars=(at,),
         hbm=(x, *[ids.transpose(1, 0, 2) for ids in (level_ids, coarse_ids)], fine, coarse, merge_weight, second_qkv, second_out),
-        hbm_outs=(5,),
+        hbm_outs=(5, 6, 7, 8),
         pinned=True,
     )
     got = shifted(packets, -1)

time: 109 us -> 107 us (0.982)
  waiting for transfers between devices: 33.4 us -> 29.7 us
  local copies, waits for them, and re-layouts: 1.14 us -> 3.26 us
  Pallas kernels: 27.2 us -> 25.6 us
  starting transfers between devices: 46.2 us -> 47.4 us
    ppermute x6, starting transfers between devices: 4.46 us -> 7.19 us  [routed(): return lax.ppermute(block, ('lat', 'lon'), pairs)]
    unnamed x19, local copies, waits for them, and re-layouts: 1.07 us -> 3.19 us
    ppermute x9, waiting for transfers between devices: 10.4 us -> 8.81 us  [far_parts(): lax.ppermute(part, 'lon', [(i, (i + 2 * back) % ranks) for i in range(ran...]
    pallas_call x14 -> x13, Pallas kernels: 27.2 us -> 25.6 us  [call(): pl.pallas_call(kernel, out_shape=[jax.ShapeDtypeStruct(shape, jnp.bfloat1...]
    ppermute x9, starting transfers between devices: 15.2 us -> 13.8 us  [far_parts(): lax.ppermute(part, 'lon', [(i, (i + 2 * back) % ranks) for i in range(ran...]
    ppermute x6, waiting for transfers between devices: 2.32 us -> 1.23 us  [routed(): return lax.ppermute(block, ('lat', 'lon'), pairs)]
  transfers between devices with their start and end apart: 34 -> 34, of which waited for: 12 -> 10; matrix products, arithmetic and copies ran while one was open for 0% -> 0% of each run, Pallas kernels for 15% -> 15%
where the time goes in v6:
time: 107 us
  starting transfers between devices  47.4 us (44%)
  waiting for transfers between devices  29.7 us (28%)
  Pallas kernels  25.6 us (24%)
  local copies, waits for them, and re-layouts  3.26 us (3%)
    pallas_call x13, Pallas kernels, call(): pl.pallas_call(kernel, out_shape=[jax.ShapeDtypeStruct(shape, jnp.bfloat1...  25.6 us
    ppermute x4, starting transfers between devices, shifted(): lax.ppermute(blocks[2], ('lat', 'lon'), [(i * lon + j, (i + step) % lat *...  17.9 us
    ppermute x9, starting transfers between devices, far_parts(): lax.ppermute(part, 'lon', [(i, (i + 2 * back) % ranks) for i in range(ran...  13.8 us
    ppermute x4, waiting for transfers between devices, shifted(): lax.ppermute(blocks[2], ('lat', 'lon'), [(i * lon + j, (i + step) % lat *...  11.9 us
    ppermute x9, waiting for transfers between devices, far_parts(): lax.ppermute(part, 'lon', [(i, (i + 2 * back) % ranks) for i in range(ran...  8.81 us
    ppermute x6, starting transfers between devices, routed(): return lax.ppermute(block, ('lat', 'lon'), pairs)  7.19 us
    ppermute x4, starting transfers between devices, shifted(): lax.ppermute(blocks[0], 'lat', [(i, (i + step) % lat) for i in range(lat)])  4.47 us
    ppermute x4, waiting for transfers between devices, shifted(): lax.ppermute(blocks[0], 'lat', [(i, (i + step) % lat) for i in range(lat)])  4.14 us
  transfers between devices with their start and end apart: 34, of which 10 were waited for; matrix products, arithmetic and copies ran while one was open for 0% of the time, Pallas kernels for 15%

profile of v6, /device:TPU:0, one launch (start us, length us, event | category | flops | bytes accessed | tf_op | source)
XLA Modules:
  0.0 107.0 jit_solution(18031438595217602264)
XLA Ops:
  0.7 3.1 %shard_map.284 = (bf16[112,512]{1,0:T(8,128)(2,1)S(1)}, bf16[112,512]{1,0:T(8,128)(2,1)S(1)}, bf16[48,512]{1,0:T(8,128)(2,1)S(1)}, bf16[8,576]{1,0:T(8,128)(2,1)...) custom-call(s32[4]{0:T(128)S(1)} %pad_add_fusion.refs_0_, ...), custom_call_target="tpu_custom_call" | custom-call | tf_op jit(solution)/shard_map/pallas_call | solution.py:421
  3.8 6.4 %collective-permute-start.2 = (bf16[48,512]{1,0:T(8,128)(2,1)S(1)}, bf16[48,512]{1,0:T(8,128)(2,1)S(1)}, u32[]{:S(2)}, u32[]{:S(2)}) collective-permute-start(bf16[48,512]{1,0:T(8,128)(2,1)S(1)} %get-tuple-element.54), channel_id=1, source_target_pairs={{0,31},{1,24},{2,25},{3,26},{4,27},{5,28},{6,29},{7,30},{8,7},{9,0... | collective-permute-start | bytes 147464 | tf_op jit(solution)/shard_map/ppermute | solution.py:439
  10.3 1.0 collective-permute-start.4
  11.3 2.8 %collective-permute-start.5 = (bf16[128,512]{1,0:T(8,128)(2,1)S(1)}, bf16[128,512]{1,0:T(8,128)(2,1)S(1)}, u32[]{:S(2)}, u32[]{:S(2)}) collective-permute-start(bf16[128,512]{1,0:T(8,128)(2,1)S(1)} %get-tuple-element.60), channel_id=1, source_target_pairs={{0,6},{1,7},{2,0},{3,1},{4,2},{5,3},{6,4},{7,5},{8,14},{9,15},{10,... | collective-permute-start | bytes 393224 | tf_op jit(solution)/shard_map/ppermute | solution.py:454
  14.1 0.5 collective-permute-start
  14.8 4.1 %collective-permute-done.refs_6_.refs_10_ = bf16[112,512]{1,0:T(8,128)(2,1)S(1)} collective-permute-done((bf16[112,512]{1,0:T(8,128)(2,1)S(1)}, bf16[112,512]{1,0:T(8,128)(2,1)S(1)}, u32[]{:S(2)}, u32[]{:S(2)}) %collective-permute-start) | collective-permute-done | bytes 114720 | tf_op jit(solution)/shard_map/ppermute | solution.py:437
  18.9 1.2 %collective-permute-done.1.refs_7_.refs_11_ = bf16[112,512]{1,0:T(8,128)(2,1)S(1)} collective-permute-done((bf16[112,512]{1,0:T(8,128)(2,1)S(1)}, bf16[112,512]{1,0:T(8,128)(2,1)S(1)}, u32[]{:S(2)}, u32[]{:S(2)}) %collective-permute-start.1) | collective-permute-done | bytes 114720 | tf_op jit(solution)/shard_map/ppermute | solution.py:438
  20.1 1.3 %collective-permute-done.4.refs_1_ = bf16[128,512]{1,0:T(8,128)(2,1)S(1)} collective-permute-done((bf16[128,512]{1,0:T(8,128)(2,1)S(1)}, bf16[128,512]{1,0:T(8,128)(2,1)S(1)}, u32[]{:S(2)}, u32[]{:S(2)}) %collective-permute-start.4) | collective-permute-done | bytes 131104 | tf_op jit(solution)/shard_map/ppermute | solution.py:454
  21.4 0.5 shard_map.286.refs_0_
  21.9 0.7 collective-permute-start.10
  22.6 3.4 %collective-permute-start.7 = (bf16[128,512]{1,0:T(8,128)(2,1)S(1)}, bf16[128,512]{1,0:T(8,128)(2,1)S(1)}, u32[]{:S(2)}, u32[]{:S(2)}) collective-permute-start(bf16[128,512]{1,0:T(8,128)(2,1)S(1)} %get-tuple-element.65), channel_id=1, source_target_pairs={{0,2},{1,3},{2,4},{3,5},{4,6},{5,7},{6,0},{7,1},{8,10},{9,11},{10,... | collective-permute-start | bytes 393224 | tf_op jit(solution)/shard_map/ppermute | solution.py:454
  26.0 2.2 %collective-permute-start.8 = (bf16[128,512]{1,0:T(8,128)(2,1)S(1)}, bf16[128,512]{1,0:T(8,128)(2,1)S(1)}, u32[]{:S(2)}, u32[]{:S(2)}) collective-permute-start(bf16[128,512]{1,0:T(8,128)(2,1)S(1)} %get-tuple-element.65), channel_id=1, source_target_pairs={{0,4},{1,5},{2,6},{3,7},{4,0},{5,1},{6,2},{7,3},{8,12},{9,13},{10,... | collective-permute-start | bytes 393224 | tf_op jit(solution)/shard_map/ppermute | solution.py:454
  28.4 1.1 %copy-done.6 = bf16[544,576]{1,0:T(8,128)(2,1)S(1)} copy-done((bf16[544,576]{1,0:T(8,128)(2,1)S(1)}, bf16[544,576]{1,0:T(8,128)(2,1)}, u32[]{:S(2)}) %copy-start.6) | copy-done | bytes 626712
  29.5 1.0 copy-done.7
  30.6 7.1 %shard_map.285 = (bf16[576,512]{1,0:T(8,128)(2,1)S(1)}, bf16[112,512]{1,0:T(8,128)(2,1)S(1)}, bf16[112,512]{1,0:T(8,128)(2,1)S(1)}, bf16[48,512]{1,0:T(8,128)(2,...) custom-call(bf16[576,512]{1,0:T(8,128)(2,1)S(1)} %bitcast.9, ...), custom_call_target="tpu_custom_call" | custom-call | tf_op jit(solution)/shard_map/pallas_call | solution.py:421
  37.8 0.5 shard_map.287.refs_0_
  38.7 1.1 %collective-permute-start.11 = (bf16[6,128,512]{2,1,0:T(8,128)(2,1)S(1)}, bf16[6,128,512]{2,1,0:T(8,128)(2,1)S(1)}, u32[]{:S(2)}, u32[]{:S(2)}) collective-permute-start(bf16[6,128,512]{2,1,0:T(8,128)(2,1)S(1)} %shard_map.288.refs_3_), channel_id=1, source_target_pairs={{0,16},{1,9},{2,18},{3,11},{4,20},{5,13},{6,22},{7,15},{8,24},{9,1... | collective-permute-start | bytes 2359304 | tf_op jit(solution)/shard_map/ppermute | solution.py:464
  39.8 1.5 %collective-permute-start.15 = (bf16[3,128,512]{2,1,0:T(8,128)(2,1)S(1)}, bf16[3,128,512]{2,1,0:T(8,128)(2,1)S(1)}, u32[]{:S(2)}, u32[]{:S(2)}) collective-permute-start(bf16[3,128,512]{2,1,0:T(8,128)(2,1)S(1)} %shard_map.287.refs_0_), channel_id=1, source_target_pairs={{0,8},{1,17},{2,10},{3,19},{4,12},{5,21},{6,14},{7,23},{8,0},{9,25... | collective-permute-start | bytes 1179656 | tf_op jit(solution)/shard_map/ppermute | solution.py:464
  41.3 1.8 %collective-permute-start.12 = (bf16[128,512]{1,0:T(8,128)(2,1)S(1)}, bf16[128,512]{1,0:T(8,128)(2,1)S(1)}, u32[]{:S(2)}, u32[]{:S(2)}) collective-permute-start(bf16[128,512]{1,0:T(8,128)(2,1)S(1)} %get-tuple-element.73), channel_id=1, source_target_pairs={{0,2},{1,3},{2,4},{3,5},{4,6},{5,7},{6,0},{7,1},{8,10},{9,11},{10,... | collective-permute-start | bytes 393224 | tf_op jit(solution)/shard_map/ppermute | solution.py:454
  43.1 0.8 collective-permute-start.13
  43.9 1.6 %collective-permute-start.14 = (bf16[128,512]{1,0:T(8,128)(2,1)S(1)}, bf16[128,512]{1,0:T(8,128)(2,1)S(1)}, u32[]{:S(2)}, u32[]{:S(2)}) collective-permute-start(bf16[128,512]{1,0:T(8,128)(2,1)S(1)} %get-tuple-element.73), channel_id=1, source_target_pairs={{0,6},{1,7},{2,0},{3,1},{4,2},{5,3},{6,4},{7,5},{8,14},{9,15},{10,... | collective-permute-start | bytes 393224 | tf_op jit(solution)/shard_map/ppermute | solution.py:454
  45.5 4.0 %collective-permute-done.12.refs_0_ = bf16[128,512]{1,0:T(8,128)(2,1)S(1)} collective-permute-done((bf16[128,512]{1,0:T(8,128)(2,1)S(1)}, bf16[128,512]{1,0:T(8,128)(2,1)S(1)}, u32[]{:S(2)}, u32[]{:S(2)}) %collective-permute-start.12) | collective-permute-done | bytes 131104 | tf_op jit(solution)/shard_map/ppermute | solution.py:454
  49.5 3.5 %collective-permute-done.13.refs_1_ = bf16[128,512]{1,0:T(8,128)(2,1)S(1)} collective-permute-done((bf16[128,512]{1,0:T(8,128)(2,1)S(1)}, bf16[128,512]{1,0:T(8,128)(2,1)S(1)}, u32[]{:S(2)}, u32[]{:S(2)}) %collective-permute-start.13) | collective-permute-done | bytes 131104 | tf_op jit(solution)/shard_map/ppermute | solution.py:454
  53.0 1.2 %collective-permute-done.11.refs_4_ = bf16[6,128,512]{2,1,0:T(8,128)(2,1)S(1)} collective-permute-done((bf16[6,128,512]{2,1,0:T(8,128)(2,1)S(1)}, bf16[6,128,512]{2,1,0:T(8,128)(2,1)S(1)}, u32[]{:S(2)}, u32[]{:S(2)}) %collective-permute-start.11) | collective-permute-done | bytes 786464 | tf_op jit(solution)/shard_map/ppermute | solution.py:464
  54.2 0.5 shard_map.289.refs_0_
  54.8 0.4 shard_map.290.refs_3_
  55.2 1.3 %collective-permute-start.17 = (bf16[6,128,512]{2,1,0:T(8,128)(2,1)S(1)}, bf16[6,128,512]{2,1,0:T(8,128)(2,1)S(1)}, u32[]{:S(2)}, u32[]{:S(2)}) collective-permute-start(bf16[6,128,512]{2,1,0:T(8,128)(2,1)S(1)} %shard_map.290.refs_3_), channel_id=1, source_target_pairs={{0,16},{1,9},{2,18},{3,11},{4,20},{5,13},{6,22},{7,15},{8,24},{9,1... | collective-permute-start | bytes 2359304 | tf_op jit(solution)/shard_map/ppermute | solution.py:464
  56.5 1.7 %collective-permute-start.16 = (bf16[3,128,512]{2,1,0:T(8,128)(2,1)S(1)}, bf16[3,128,512]{2,1,0:T(8,128)(2,1)S(1)}, u32[]{:S(2)}, u32[]{:S(2)}) collective-permute-start(bf16[3,128,512]{2,1,0:T(8,128)(2,1)S(1)} %shard_map.289.refs_0_), channel_id=1, source_target_pairs={{0,8},{1,17},{2,10},{3,19},{4,12},{5,21},{6,14},{7,23},{8,0},{9,25... | collective-permute-start | bytes 1179656 | tf_op jit(solution)/shard_map/ppermute | solution.py:464
  58.2 0.5 collective-permute-start.18
  58.7 1.5 %collective-permute-start.19 = (bf16[112,512]{1,0:T(8,128)(2,1)S(1)}, bf16[112,512]{1,0:T(8,128)(2,1)S(1)}, u32[]{:S(2)}, u32[]{:S(2)}) collective-permute-start(bf16[112,512]{1,0:T(8,128)(2,1)S(1)} %get-tuple-element.83), channel_id=1, source_target_pairs={{0,7},{1,0},{2,1},{3,2},{4,3},{5,4},{6,5},{7,6},{8,15},{9,8},{10,9... | collective-permute-start | bytes 344072 | tf_op jit(solution)/shard_map/ppermute | solution.py:438
  60.2 2.9 %collective-permute-start.20 = (bf16[48,512]{1,0:T(8,128)(2,1)S(1)}, bf16[48,512]{1,0:T(8,128)(2,1)S(1)}, u32[]{:S(2)}, u32[]{:S(2)}) collective-permute-start(bf16[48,512]{1,0:T(8,128)(2,1)S(1)} %get-tuple-element.84), channel_id=1, source_target_pairs={{0,31},{1,24},{2,25},{3,26},{4,27},{5,28},{6,29},{7,30},{8,7},{9,0... | collective-permute-start | bytes 147464 | tf_op jit(solution)/shard_map/ppermute | solution.py:439
  63.2 10.6 %collective-permute-done.20.refs_11_ = bf16[48,512]{1,0:T(8,128)(2,1)S(1)} collective-permute-done((bf16[48,512]{1,0:T(8,128)(2,1)S(1)}, bf16[48,512]{1,0:T(8,128)(2,1)S(1)}, u32[]{:S(2)}, u32[]{:S(2)}) %collective-permute-start.20) | collective-permute-done | bytes 49184 | tf_op jit(solution)/shard_map/ppermute | solution.py:439
  73.9 0.5 collective-permute-start.22
  74.5 0.4 collective-permute-start.29
  75.3 1.6 %collective-permute-start.26 = (bf16[6,128,512]{2,1,0:T(8,128)(2,1)S(1)}, bf16[6,128,512]{2,1,0:T(8,128)(2,1)S(1)}, u32[]{:S(2)}, u32[]{:S(2)}) collective-permute-start(bf16[6,128,512]{2,1,0:T(8,128)(2,1)S(1)} %shard_map.293.refs_3_), channel_id=1, source_target_pairs={{0,16},{1,9},{2,18},{3,11},{4,20},{5,13},{6,22},{7,15},{8,24},{9,1... | collective-permute-start | bytes 2359304 | tf_op jit(solution)/shard_map/ppermute | solution.py:464
  77.3 3.5 %shard_map.291.refs_8_ = bf16[144,1024]{1,0:T(8,128)(2,1)S(1)} custom-call(s32[4]{0:T(128)S(1)} %pad_add_fusion.refs_0_, bf16[576,1024]{1,0:T(8,128)(2,1)S(1)} %copy-done.2, bf16[12,128,512]{2,1,0:T(8,128)(2,1)S(1)} %get-tuple-element.66.refs_2_, bf16[6,128,512]{2,1,0:T(8,128)(2,1)S(1)} %shard_map.288.refs_3_, ...), custom_call_target="tpu_custom_call" | custom-call | tf_op jit(solution)/shard_map/pallas_call | solution.py:421
  80.8 1.7 %collective-permute-start.23 = (bf16[112,512]{1,0:T(8,128)(2,1)S(1)}, bf16[112,512]{1,0:T(8,128)(2,1)S(1)}, u32[]{:S(2)}, u32[]{:S(2)}) collective-permute-start(bf16[112,512]{1,0:T(8,128)(2,1)S(1)} %get-tuple-element.88), channel_id=1, source_target_pairs={{0,8},{8,16},{16,24},{24,0},{1,9},{9,17},{17,25},{25,1},{2,10},{10... | collective-permute-start | bytes 344072 | tf_op jit(solution)/shard_map/ppermute | solution.py:437
  82.6 4.0 %collective-permute-start.25 = (bf16[48,512]{1,0:T(8,128)(2,1)S(1)}, bf16[48,512]{1,0:T(8,128)(2,1)S(1)}, u32[]{:S(2)}, u32[]{:S(2)}) collective-permute-start(bf16[48,512]{1,0:T(8,128)(2,1)S(1)} %get-tuple-element.90), channel_id=1, source_target_pairs={{0,9},{1,10},{2,11},{3,12},{4,13},{5,14},{6,15},{7,8},{8,17},{9,18... | collective-permute-start | bytes 147464 | tf_op jit(solution)/shard_map/ppermute | solution.py:439
  86.6 3.5 %shard_map.294.refs_9_ = bf16[2304,144]{1,0:T(8,128)(2,1)S(1)} custom-call(s32[4]{0:T(128)S(1)} %pad_add_fusion.refs_0_, bf16[144,640]{1,0:T(8,128)(2,1)S(1)} %copy-done.5, bf16[12,128,512]{2,1,0:T(8,128)(2,1)S(1)} %get-tuple-element.66.refs_2_, bf16[6,128,512]{2,1,0:T(8,128)(2,1)S(1)} %shard_map.290.refs_3_, ...), custom_call_target="tpu_custom_call" | custom-call | tf_op jit(solution)/shard_map/pallas_call | solution.py:421
  90.2 0.6 collective-permute-start.30
  90.8 1.9 %collective-permute-done.30.refs_7_ = bf16[6,128,512]{2,1,0:T(8,128)(2,1)S(1)} collective-permute-done((bf16[6,128,512]{2,1,0:T(8,128)(2,1)S(1)}, bf16[6,128,512]{2,1,0:T(8,128)(2,1)S(1)}, u32[]{:S(2)}, u32[]{:S(2)}) %collective-permute-start.30) | collective-permute-done | bytes 786464 | tf_op jit(solution)/shard_map/ppermute | solution.py:448
  92.7 3.1 %shard_map.295 = (bf16[144,1024]{1,0:T(8,128)(2,1)S(1)}, bf16[48,1024]{1,0:T(8,128)(2,1)S(1)}, bf16[48,1024]{1,0:T(8,128)(2,1)S(1)}, bf16[48,1024]{1,0:T(8,128)(2,1)S(1)}) custom-call(s32[4]{0:T(128)S(1)} %pad_add_fusion.refs_0_, bf16[144,144]{1,0:T(8,128)(2,1)S(1)} %copy-done.8, bf16[12,128,512]{2,1,0:T(8,128)(2,1)S(1)} %get-tuple-element.66.refs_2_, ...), custom_call_target="tpu_custom_call" | custom-call | tf_op jit(solution)/shard_map/pallas_call | solution.py:421
  95.8 1.7 %collective-permute-start.31 = (bf16[48,1024]{1,0:T(8,128)(2,1)S(1)}, bf16[48,1024]{1,0:T(8,128)(2,1)S(1)}, u32[]{:S(2)}, u32[]{:S(2)}) collective-permute-start(bf16[48,1024]{1,0:T(8,128)(2,1)S(1)} %get-tuple-element.97), channel_id=1, source_target_pairs={{0,8},{8,16},{16,24},{24,0},{1,9},{9,17},{17,25},{25,1},{2,10},{10... | collective-permute-start | bytes 294920 | tf_op jit(solution)/shard_map/ppermute | solution.py:437
  97.5 4.5 %collective-permute-start.33 = (bf16[48,1024]{1,0:T(8,128)(2,1)S(1)}, bf16[48,1024]{1,0:T(8,128)(2,1)S(1)}, u32[]{:S(2)}, u32[]{:S(2)}) collective-permute-start(bf16[48,1024]{1,0:T(8,128)(2,1)S(1)} %get-tuple-element.99), channel_id=1, source_target_pairs={{0,9},{1,10},{2,11},{3,12},{4,13},{5,14},{6,15},{7,8},{8,17},{9,18... | collective-permute-start | bytes 294920 | tf_op jit(solution)/shard_map/ppermute | solution.py:439
  102.0 1.9 %shard_map.292 = bf16[576,512]{1,0:T(8,128)(2,1)} custom-call(bf16[576,1024]{1,0:T(8,128)(2,1)S(1)} %copy-done.3, bf16[576,512]{1,0:T(8,128)(2,1)S(1)} %get-tuple-element.55.refs_8_.own_ref, bf16[112,512]{1,0:T(8,128)(2,1)S(1)} %collective-permute-done.23.lat_ref, bf16[112,512]{1,0:T(8,128)(2,1)S(1)} %collective-permute-done.24.lon_ref, ...), custom_call_target="tpu_custom_call" | custom-call | tf_op jit(solution)/shard_map/pallas_call | solution.py:421
  104.0 1.3 %collective-permute-done.33.both_ref = bf16[48,1024]{1,0:T(8,128)(2,1)S(1)} collective-permute-done((bf16[48,1024]{1,0:T(8,128)(2,1)S(1)}, bf16[48,1024]{1,0:T(8,128)(2,1)S(1)}, u32[]{:S(2)}, u32[]{:S(2)}) %collective-permute-start.33) | collective-permute-done | bytes 98336 | tf_op jit(solution)/shard_map/ppermute | solution.py:439
  105.3 0.6 shard_map.296
  106.0 1.0 copy.32
  (54 shorter events, 1.9 us)
Async XLA Ops:
  0.7 27.7 %copy-start = (bf16[2,12,24,512]{3,2,1,0:T(8,128)(2,1)S(1)}, bf16[2,12,24,512]{3,2,1,0:T(8,128)(2,1)}, u32[]{:S(2)}) copy-start(bf16[2,12,24,512]{3,2,1,0:T(8,128)(2,1)} %param.29) | copy-start | bytes 1769476
  0.7 27.7 %copy-start.1 = (bf16[512,1536]{1,0:T(8,128)(2,1)S(1)}, bf16[512,1536]{1,0:T(8,128)(2,1)}, u32[]{:S(2)}) copy-start(bf16[512,1536]{1,0:T(8,128)(2,1)} %refs_2_.1) | copy-start | bytes 4718596
  0.7 27.7 %copy-start.4 = (bf16[576,1024]{1,0:T(8,128)(2,1)S(1)}, bf16[576,1024]{1,0:T(8,128)(2,1)}, u32[]{:S(2)}) copy-start(bf16[576,1024]{1,0:T(8,128)(2,1)} %constant.93.clone.refs_1_) | copy-start | bytes 3538948
  3.8 10.8 %collective-permute-start.2 = (bf16[48,512]{1,0:T(8,128)(2,1)S(1)}, bf16[48,512]{1,0:T(8,128)(2,1)S(1)}, u32[]{:S(2)}, u32[]{:S(2)}) collective-permute-start(bf16[48,512]{1,0:T(8,128)(2,1)S(1)} %get-tuple-element.54), channel_id=1, source_target_pairs={{0,31},{1,24},{2,25},{3,26},{4,27},{5,28},{6,29},{7,30},{8,7},{9,0... | collective-permute-start | bytes 147464 | tf_op jit(solution)/shard_map/ppermute | solution.py:439
  10.3 9.9 %collective-permute-start.3 = (bf16[128,512]{1,0:T(8,128)(2,1)S(1)}, bf16[128,512]{1,0:T(8,128)(2,1)S(1)}, u32[]{:S(2)}, u32[]{:S(2)}) collective-permute-start(bf16[128,512]{1,0:T(8,128)(2,1)S(1)} %get-tuple-element.60), channel_id=1, source_target_pairs={{0,2},{1,3},{2,4},{3,5},{4,6},{5,7},{6,0},{7,1},{8,10},{9,11},{10,... | collective-permute-start | bytes 393224 | tf_op jit(solution)/shard_map/ppermute | solution.py:454
  10.3 11.1 %collective-permute-start.4 = (bf16[128,512]{1,0:T(8,128)(2,1)S(1)}, bf16[128,512]{1,0:T(8,128)(2,1)S(1)}, u32[]{:S(2)}, u32[]{:S(2)}) collective-permute-start(bf16[128,512]{1,0:T(8,128)(2,1)S(1)} %get-tuple-element.60), channel_id=1, source_target_pairs={{0,4},{1,5},{2,6},{3,7},{4,0},{5,1},{6,2},{7,3},{8,12},{9,13},{10,... | collective-permute-start | bytes 393224 | tf_op jit(solution)/shard_map/ppermute | solution.py:454
  11.3 10.1 %collective-permute-start.5 = (bf16[128,512]{1,0:T(8,128)(2,1)S(1)}, bf16[128,512]{1,0:T(8,128)(2,1)S(1)}, u32[]{:S(2)}, u32[]{:S(2)}) collective-permute-start(bf16[128,512]{1,0:T(8,128)(2,1)S(1)} %get-tuple-element.60), channel_id=1, source_target_pairs={{0,6},{1,7},{2,0},{3,1},{4,2},{5,3},{6,4},{7,5},{8,14},{9,15},{10,... | collective-permute-start | bytes 393224 | tf_op jit(solution)/shard_map/ppermute | solution.py:454
  14.1 4.8 %collective-permute-start = (bf16[112,512]{1,0:T(8,128)(2,1)S(1)}, bf16[112,512]{1,0:T(8,128)(2,1)S(1)}, u32[]{:S(2)}, u32[]{:S(2)}) collective-permute-start(bf16[112,512]{1,0:T(8,128)(2,1)S(1)} %get-tuple-element.52), channel_id=1, source_target_pairs={{0,24},{8,0},{16,8},{24,16},{1,25},{9,1},{17,9},{25,17},{2,26},{10... | collective-permute-start | bytes 344072 | tf_op jit(solution)/shard_map/ppermute | solution.py:437
  14.6 5.5 %collective-permute-start.1 = (bf16[112,512]{1,0:T(8,128)(2,1)S(1)}, bf16[112,512]{1,0:T(8,128)(2,1)S(1)}, u32[]{:S(2)}, u32[]{:S(2)}) collective-permute-start(bf16[112,512]{1,0:T(8,128)(2,1)S(1)} %get-tuple-element.53), channel_id=1, source_target_pairs={{0,7},{1,0},{2,1},{3,2},{4,3},{5,4},{6,5},{7,6},{8,15},{9,8},{10,9... | collective-permute-start | bytes 344072 | tf_op jit(solution)/shard_map/ppermute | solution.py:438
  21.9 15.8 %collective-permute-start.10 = (bf16[12,128,512]{2,1,0:T(8,128)(2,1)S(1)}, bf16[12,128,512]{2,1,0:T(8,128)(2,1)S(1)}, u32[]{:S(2)}, u32[]{:S(2)}) collective-permute-start(bf16[12,128,512]{2,1,0:T(8,128)(2,1)S(1)} %get-tuple-element.66.refs_2_), channel_id=1, source_target_pairs={{0,1},{1,0},{2,3},{3,2},{4,5},{5,4},{6,7},{7,6},{8,9},{9,8},{10,11... | collective-permute-start | bytes 4718600 | tf_op jit(solution)/shard_map/ppermute | solution.py:448
  22.6 15.1 %collective-permute-start.6 = (bf16[3,128,512]{2,1,0:T(8,128)(2,1)S(1)}, bf16[3,128,512]{2,1,0:T(8,128)(2,1)S(1)}, u32[]{:S(2)}, u32[]{:S(2)}) collective-permute-start(bf16[3,128,512]{2,1,0:T(8,128)(2,1)S(1)} %shard_map.286.refs_0_), channel_id=1, source_target_pairs={{0,8},{1,17},{2,10},{3,19},{4,12},{5,21},{6,14},{7,23},{8,0},{9,25... | collective-permute-start | bytes 1179656 | tf_op jit(solution)/shard_map/ppermute | solution.py:464
  22.6 15.1 %collective-permute-start.7 = (bf16[128,512]{1,0:T(8,128)(2,1)S(1)}, bf16[128,512]{1,0:T(8,128)(2,1)S(1)}, u32[]{:S(2)}, u32[]{:S(2)}) collective-permute-start(bf16[128,512]{1,0:T(8,128)(2,1)S(1)} %get-tuple-element.65), channel_id=1, source_target_pairs={{0,2},{1,3},{2,4},{3,5},{4,6},{5,7},{6,0},{7,1},{8,10},{9,11},{10,... | collective-permute-start | bytes 393224 | tf_op jit(solution)/shard_map/ppermute | solution.py:454
  26.0 11.7 %collective-permute-start.8 = (bf16[128,512]{1,0:T(8,128)(2,1)S(1)}, bf16[128,512]{1,0:T(8,128)(2,1)S(1)}, u32[]{:S(2)}, u32[]{:S(2)}) collective-permute-start(bf16[128,512]{1,0:T(8,128)(2,1)S(1)} %get-tuple-element.65), channel_id=1, source_target_pairs={{0,4},{1,5},{2,6},{3,7},{4,0},{5,1},{6,2},{7,3},{8,12},{9,13},{10,... | collective-permute-start | bytes 393224 | tf_op jit(solution)/shard_map/ppermute | solution.py:454
  28.3 9.4 %collective-permute-start.9 = (bf16[128,512]{1,0:T(8,128)(2,1)S(1)}, bf16[128,512]{1,0:T(8,128)(2,1)S(1)}, u32[]{:S(2)}, u32[]{:S(2)}) collective-permute-start(bf16[128,512]{1,0:T(8,128)(2,1)S(1)} %get-tuple-element.65), channel_id=1, source_target_pairs={{0,6},{1,7},{2,0},{3,1},{4,2},{5,3},{6,4},{7,5},{8,14},{9,15},{10,... | collective-permute-start | bytes 393224 | tf_op jit(solution)/shard_map/ppermute | solution.py:454
  28.4 1.1 %copy-start.6 = (bf16[544,576]{1,0:T(8,128)(2,1)S(1)}, bf16[544,576]{1,0:T(8,128)(2,1)}, u32[]{:S(2)}) copy-start(bf16[544,576]{1,0:T(8,128)(2,1)} %constant.107.refs_4_) | copy-start | bytes 1880068
  29.5 1.0 copy-start.7
  38.7 15.5 %collective-permute-start.11 = (bf16[6,128,512]{2,1,0:T(8,128)(2,1)S(1)}, bf16[6,128,512]{2,1,0:T(8,128)(2,1)S(1)}, u32[]{:S(2)}, u32[]{:S(2)}) collective-permute-start(bf16[6,128,512]{2,1,0:T(8,128)(2,1)S(1)} %shard_map.288.refs_3_), channel_id=1, source_target_pairs={{0,16},{1,9},{2,18},{3,11},{4,20},{5,13},{6,22},{7,15},{8,24},{9,1... | collective-permute-start | bytes 2359304 | tf_op jit(solution)/shard_map/ppermute | solution.py:464
  39.8 13.2 %collective-permute-start.15 = (bf16[3,128,512]{2,1,0:T(8,128)(2,1)S(1)}, bf16[3,128,512]{2,1,0:T(8,128)(2,1)S(1)}, u32[]{:S(2)}, u32[]{:S(2)}) collective-permute-start(bf16[3,128,512]{2,1,0:T(8,128)(2,1)S(1)} %shard_map.287.refs_0_), channel_id=1, source_target_pairs={{0,8},{1,17},{2,10},{3,19},{4,12},{5,21},{6,14},{7,23},{8,0},{9,25... | collective-permute-start | bytes 1179656 | tf_op jit(solution)/shard_map/ppermute | solution.py:464
  41.3 8.2 %collective-permute-start.12 = (bf16[128,512]{1,0:T(8,128)(2,1)S(1)}, bf16[128,512]{1,0:T(8,128)(2,1)S(1)}, u32[]{:S(2)}, u32[]{:S(2)}) collective-permute-start(bf16[128,512]{1,0:T(8,128)(2,1)S(1)} %get-tuple-element.73), channel_id=1, source_target_pairs={{0,2},{1,3},{2,4},{3,5},{4,6},{5,7},{6,0},{7,1},{8,10},{9,11},{10,... | collective-permute-start | bytes 393224 | tf_op jit(solution)/shard_map/ppermute | solution.py:454
  43.1 9.9 %collective-permute-start.13 = (bf16[128,512]{1,0:T(8,128)(2,1)S(1)}, bf16[128,512]{1,0:T(8,128)(2,1)S(1)}, u32[]{:S(2)}, u32[]{:S(2)}) collective-permute-start(bf16[128,512]{1,0:T(8,128)(2,1)S(1)} %get-tuple-element.73), channel_id=1, source_target_pairs={{0,4},{1,5},{2,6},{3,7},{4,0},{5,1},{6,2},{7,3},{8,12},{9,13},{10,... | collective-permute-start | bytes 393224 | tf_op jit(solution)/shard_map/ppermute | solution.py:454
  43.9 9.1 %collective-permute-start.14 = (bf16[128,512]{1,0:T(8,128)(2,1)S(1)}, bf16[128,512]{1,0:T(8,128)(2,1)S(1)}, u32[]{:S(2)}, u32[]{:S(2)}) collective-permute-start(bf16[128,512]{1,0:T(8,128)(2,1)S(1)} %get-tuple-element.73), channel_id=1, source_target_pairs={{0,6},{1,7},{2,0},{3,1},{4,2},{5,3},{6,4},{7,5},{8,14},{9,15},{10,... | collective-permute-start | bytes 393224 | tf_op jit(solution)/shard_map/ppermute | solution.py:454
  55.2 22.1 %copy-start.2 = (bf16[576,1024]{1,0:T(8,128)(2,1)S(1)}, bf16[576,1024]{1,0:T(8,128)(2,1)}, u32[]{:S(2)}) copy-start(bf16[576,1024]{1,0:T(8,128)(2,1)} %constant.100.clone.refs_1_) | copy-start | bytes 3538948
  55.2 18.6 %collective-permute-start.17 = (bf16[6,128,512]{2,1,0:T(8,128)(2,1)S(1)}, bf16[6,128,512]{2,1,0:T(8,128)(2,1)S(1)}, u32[]{:S(2)}, u32[]{:S(2)}) collective-permute-start(bf16[6,128,512]{2,1,0:T(8,128)(2,1)S(1)} %shard_map.290.refs_3_), channel_id=1, source_target_pairs={{0,16},{1,9},{2,18},{3,11},{4,20},{5,13},{6,22},{7,15},{8,24},{9,1... | collective-permute-start | bytes 2359304 | tf_op jit(solution)/shard_map/ppermute | solution.py:464
  56.5 17.3 %collective-permute-start.16 = (bf16[3,128,512]{2,1,0:T(8,128)(2,1)S(1)}, bf16[3,128,512]{2,1,0:T(8,128)(2,1)S(1)}, u32[]{:S(2)}, u32[]{:S(2)}) collective-permute-start(bf16[3,128,512]{2,1,0:T(8,128)(2,1)S(1)} %shard_map.289.refs_0_), channel_id=1, source_target_pairs={{0,8},{1,17},{2,10},{3,19},{4,12},{5,21},{6,14},{7,23},{8,0},{9,25... | collective-permute-start | bytes 1179656 | tf_op jit(solution)/shard_map/ppermute | solution.py:464
  58.2 15.6 %collective-permute-start.18 = (bf16[112,512]{1,0:T(8,128)(2,1)S(1)}, bf16[112,512]{1,0:T(8,128)(2,1)S(1)}, u32[]{:S(2)}, u32[]{:S(2)}) collective-permute-start(bf16[112,512]{1,0:T(8,128)(2,1)S(1)} %get-tuple-element.82), channel_id=1, source_target_pairs={{0,24},{8,0},{16,8},{24,16},{1,25},{9,1},{17,9},{25,17},{2,26},{10... | collective-permute-start | bytes 344072 | tf_op jit(solution)/shard_map/ppermute | solution.py:437
  58.7 15.1 %collective-permute-start.19 = (bf16[112,512]{1,0:T(8,128)(2,1)S(1)}, bf16[112,512]{1,0:T(8,128)(2,1)S(1)}, u32[]{:S(2)}, u32[]{:S(2)}) collective-permute-start(bf16[112,512]{1,0:T(8,128)(2,1)S(1)} %get-tuple-element.83), channel_id=1, source_target_pairs={{0,7},{1,0},{2,1},{3,2},{4,3},{5,4},{6,5},{7,6},{8,15},{9,8},{10,9... | collective-permute-start | bytes 344072 | tf_op jit(solution)/shard_map/ppermute | solution.py:438
  60.2 13.5 %collective-permute-start.20 = (bf16[48,512]{1,0:T(8,128)(2,1)S(1)}, bf16[48,512]{1,0:T(8,128)(2,1)S(1)}, u32[]{:S(2)}, u32[]{:S(2)}) collective-permute-start(bf16[48,512]{1,0:T(8,128)(2,1)S(1)} %get-tuple-element.84), channel_id=1, source_target_pairs={{0,31},{1,24},{2,25},{3,26},{4,27},{5,28},{6,29},{7,30},{8,7},{9,0... | collective-permute-start | bytes 147464 | tf_op jit(solution)/shard_map/ppermute | solution.py:439
  73.8 3.1 %collective-permute-start.21 = (bf16[6,128,512]{2,1,0:T(8,128)(2,1)S(1)}, bf16[6,128,512]{2,1,0:T(8,128)(2,1)S(1)}, u32[]{:S(2)}, u32[]{:S(2)}) collective-permute-start(bf16[6,128,512]{2,1,0:T(8,128)(2,1)S(1)} %shard_map.288.refs_3_), channel_id=1, source_target_pairs={{0,1},{1,0},{2,3},{3,2},{4,5},{5,4},{6,7},{7,6},{8,9},{9,8},{10,11... | collective-permute-start | bytes 2359304 | tf_op jit(solution)/shard_map/ppermute | solution.py:448
  73.9 3.4 %collective-permute-start.22 = (bf16[6,128,512]{2,1,0:T(8,128)(2,1)S(1)}, bf16[6,128,512]{2,1,0:T(8,128)(2,1)S(1)}, u32[]{:S(2)}, u32[]{:S(2)}) collective-permute-start(bf16[6,128,512]{2,1,0:T(8,128)(2,1)S(1)} %collective-permute-done.11.refs_4_), channel_id=1, source_target_pairs={{0,1},{1,0},{2,3},{3,2},{4,5},{5,4},{6,7},{7,6},{8,9},{9,8},{10,11... | collective-permute-start | bytes 2359304 | tf_op jit(solution)/shard_map/ppermute | solution.py:448
  74.4 8.2 %collective-permute-start.28 = (bf16[6,128,512]{2,1,0:T(8,128)(2,1)S(1)}, bf16[6,128,512]{2,1,0:T(8,128)(2,1)S(1)}, u32[]{:S(2)}, u32[]{:S(2)}) collective-permute-start(bf16[6,128,512]{2,1,0:T(8,128)(2,1)S(1)} %shard_map.290.refs_3_), channel_id=1, source_target_pairs={{0,1},{1,0},{2,3},{3,2},{4,5},{5,4},{6,7},{7,6},{8,9},{9,8},{10,11... | collective-permute-start | bytes 2359304 | tf_op jit(solution)/shard_map/ppermute | solution.py:448
  74.5 12.1 %collective-permute-start.29 = (bf16[6,128,512]{2,1,0:T(8,128)(2,1)S(1)}, bf16[6,128,512]{2,1,0:T(8,128)(2,1)S(1)}, u32[]{:S(2)}, u32[]{:S(2)}) collective-permute-start(bf16[6,128,512]{2,1,0:T(8,128)(2,1)S(1)} %collective-permute-done.17.refs_4_), channel_id=1, source_target_pairs={{0,1},{1,0},{2,3},{3,2},{4,5},{5,4},{6,7},{7,6},{8,9},{9,8},{10,11... | collective-permute-start | bytes 2359304 | tf_op jit(solution)/shard_map/ppermute | solution.py:448
  75.3 11.3 %copy-start.5 = (bf16[144,640]{1,0:T(8,128)(2,1)S(1)}, bf16[144,640]{1,0:T(8,128)(2,1)}, u32[]{:S(2)}) copy-start(bf16[144,640]{1,0:T(8,128)(2,1)} %constant.102.clone.refs_1_.select_hbm) | copy-start | bytes 552964
  75.3 14.8 %collective-permute-start.26 = (bf16[6,128,512]{2,1,0:T(8,128)(2,1)S(1)}, bf16[6,128,512]{2,1,0:T(8,128)(2,1)S(1)}, u32[]{:S(2)}, u32[]{:S(2)}) collective-permute-start(bf16[6,128,512]{2,1,0:T(8,128)(2,1)S(1)} %shard_map.293.refs_3_), channel_id=1, source_target_pairs={{0,16},{1,9},{2,18},{3,11},{4,20},{5,13},{6,22},{7,15},{8,24},{9,1... | collective-permute-start | bytes 2359304 | tf_op jit(solution)/shard_map/ppermute | solution.py:464
  80.8 9.3 %collective-permute-start.23 = (bf16[112,512]{1,0:T(8,128)(2,1)S(1)}, bf16[112,512]{1,0:T(8,128)(2,1)S(1)}, u32[]{:S(2)}, u32[]{:S(2)}) collective-permute-start(bf16[112,512]{1,0:T(8,128)(2,1)S(1)} %get-tuple-element.88), channel_id=1, source_target_pairs={{0,8},{8,16},{16,24},{24,0},{1,9},{9,17},{17,25},{25,1},{2,10},{10... | collective-permute-start | bytes 344072 | tf_op jit(solution)/shard_map/ppermute | solution.py:437
  82.6 7.6 %collective-permute-start.24 = (bf16[112,512]{1,0:T(8,128)(2,1)S(1)}, bf16[112,512]{1,0:T(8,128)(2,1)S(1)}, u32[]{:S(2)}, u32[]{:S(2)}) collective-permute-start(bf16[112,512]{1,0:T(8,128)(2,1)S(1)} %get-tuple-element.89), channel_id=1, source_target_pairs={{0,1},{1,2},{2,3},{3,4},{4,5},{5,6},{6,7},{7,0},{8,9},{9,10},{10,1... | collective-permute-start | bytes 344072 | tf_op jit(solution)/shard_map/ppermute | solution.py:438
  82.6 7.6 %collective-permute-start.25 = (bf16[48,512]{1,0:T(8,128)(2,1)S(1)}, bf16[48,512]{1,0:T(8,128)(2,1)S(1)}, u32[]{:S(2)}, u32[]{:S(2)}) collective-permute-start(bf16[48,512]{1,0:T(8,128)(2,1)S(1)} %get-tuple-element.90), channel_id=1, source_target_pairs={{0,9},{1,10},{2,11},{3,12},{4,13},{5,14},{6,15},{7,8},{8,17},{9,18... | collective-permute-start | bytes 147464 | tf_op jit(solution)/shard_map/ppermute | solution.py:439
  86.6 4.2 %collective-permute-start.27 = (bf16[6,128,512]{2,1,0:T(8,128)(2,1)S(1)}, bf16[6,128,512]{2,1,0:T(8,128)(2,1)S(1)}, u32[]{:S(2)}, u32[]{:S(2)}) collective-permute-start(bf16[6,128,512]{2,1,0:T(8,128)(2,1)S(1)} %shard_map.293.refs_3_), channel_id=1, source_target_pairs={{0,1},{1,0},{2,3},{3,2},{4,5},{5,4},{6,7},{7,6},{8,9},{9,8},{10,11... | collective-permute-start | bytes 2359304 | tf_op jit(solution)/shard_map/ppermute | solution.py:448
  86.6 6.1 %copy-start.8 = (bf16[144,144]{1,0:T(8,128)(2,1)S(1)}, bf16[144,144]{1,0:T(8,128)(2,1)}, u32[]{:S(2)}) copy-start(bf16[144,144]{1,0:T(8,128)(2,1)} %constant.112.refs_1_) | copy-start | bytes 124420
  90.1 11.9 %copy-start.3 = (bf16[576,1024]{1,0:T(8,128)(2,1)S(1)}, bf16[576,1024]{1,0:T(8,128)(2,1)}, u32[]{:S(2)}) copy-start(bf16[576,1024]{1,0:T(8,128)(2,1)} %constant.101.clone.select_hbm) | copy-start | bytes 3538948
  90.2 2.5 %collective-permute-start.30 = (bf16[6,128,512]{2,1,0:T(8,128)(2,1)S(1)}, bf16[6,128,512]{2,1,0:T(8,128)(2,1)S(1)}, u32[]{:S(2)}, u32[]{:S(2)}) collective-permute-start(bf16[6,128,512]{2,1,0:T(8,128)(2,1)S(1)} %collective-permute-done.26.refs_4_), channel_id=1, source_target_pairs={{0,1},{1,0},{2,3},{3,2},{4,5},{5,4},{6,7},{7,6},{8,9},{9,8},{10,11... | collective-permute-start | bytes 2359304 | tf_op jit(solution)/shard_map/ppermute | solution.py:448
  95.8 8.2 %collective-permute-start.31 = (bf16[48,1024]{1,0:T(8,128)(2,1)S(1)}, bf16[48,1024]{1,0:T(8,128)(2,1)S(1)}, u32[]{:S(2)}, u32[]{:S(2)}) collective-permute-start(bf16[48,1024]{1,0:T(8,128)(2,1)S(1)} %get-tuple-element.97), channel_id=1, source_target_pairs={{0,8},{8,16},{16,24},{24,0},{1,9},{9,17},{17,25},{25,1},{2,10},{10... | collective-permute-start | bytes 294920 | tf_op jit(solution)/shard_map/ppermute | solution.py:437
  97.5 6.5 %collective-permute-start.32 = (bf16[48,1024]{1,0:T(8,128)(2,1)S(1)}, bf16[48,1024]{1,0:T(8,128)(2,1)S(1)}, u32[]{:S(2)}, u32[]{:S(2)}) collective-permute-start(bf16[48,1024]{1,0:T(8,128)(2,1)S(1)} %get-tuple-element.98), channel_id=1, source_target_pairs={{0,1},{1,2},{2,3},{3,4},{4,5},{5,6},{6,7},{7,0},{8,9},{9,10},{10,1... | collective-permute-start | bytes 294920 | tf_op jit(solution)/shard_map/ppermute | solution.py:438
  97.5 7.7 %collective-permute-start.33 = (bf16[48,1024]{1,0:T(8,128)(2,1)S(1)}, bf16[48,1024]{1,0:T(8,128)(2,1)S(1)}, u32[]{:S(2)}, u32[]{:S(2)}) collective-permute-start(bf16[48,1024]{1,0:T(8,128)(2,1)S(1)} %get-tuple-element.99), channel_id=1, source_target_pairs={{0,9},{1,10},{2,11},{3,12},{4,13},{5,14},{6,15},{7,8},{8,17},{9,18... | collective-permute-start | bytes 294920 | tf_op jit(solution)/shard_map/ppermute | solution.py:439

commit v7 on v6

--- a/solution.py
+++ b/solution.py
@@ -330,16 +330,19 @@
     return [[refs[number].at[pl.ds(first, count)] for number, first, count in side] for side in plan]
 
 
-def merge_kernel(count, plan, at_ref, select_hbm, *refs):
-    pieces, (y_ref, lat_ref, lon_ref, both_ref, out_ref) = cuts(refs[:count], plan), refs[count : count + 5]
-    select_ref, stage_ref, whole_ref, sems, piece_sems = refs[count + 5 :]
-    loads = fetch(sems, (select_hbm, select_ref))
-    copies = start_pieces(whole_ref, pieces, at_ref, piece_sems)
+def merge_kernel(heads, counts, number, plans, at_ref, select_hbm, coarse_select_hbm, *refs):
+    pieces, refs = refs[:number], refs[number:]
+    (y_ref, lat_ref, lon_ref, both_ref), labels_ref, packets = refs[:4], refs[4], refs[5:8]
+    merged_ref, expos_ref, select_ref, coarse_select_ref, stage_ref = refs[8:13]
+    merge_ref, score_ref, packed_ref, sems, merge_sems, score_sems = refs[13:]
+    loads = fetch(sems, (select_hbm, select_ref), (coarse_select_hbm, coarse_select_ref))
+    merge_copies = start_pieces(merge_ref, cuts(pieces, plans[0]), at_ref, merge_sems)
+    score_copies = start_pieces(score_ref, cuts(pieces, plans[1]), at_ref, score_sems)
     fill(stage_ref, (y_ref, lat_ref, lon_ref, both_ref))
-    cells = out_ref.shape[0]
+    count, width = merged_ref.shape
     loads[0].wait()
     patches = [
-        dot(select_ref[first : first + cells], stage_ref[...]) for first in range(0, select_ref.shape[0], cells)
+        dot(select_ref[first : first + count], stage_ref[...]) for first in range(0, select_ref.shape[0], count)
     ]
     total = 1.0 / (len(patches) * y_ref.shape[1])
     center = sum(jnp.sum(patch, axis=-1, keepdims=True) for patch in patches) * total
@@ -347,24 +350,17 @@
     spread = sum(jnp.sum(patch * patch, axis=-1, keepdims=True) for patch in moved) * total
     scale = lax.rsqrt(spread + EPSILON)
     left = jnp.concatenate([(patch * scale).astype(jnp.bfloat16) for patch in moved], axis=1)
-    for copy in copies:
+    wide = wide_labels(labels_ref, packets, counts, 1)
+    loads[1].wait()
+    bias = label_bias(wide, coarse_select_ref[...])
+    for copy in merge_copies:
         copy.wait()
-    out_ref[...] = dot(left, flat(whole_ref)).astype(jnp.bfloat16)
-
-
-def scores_kernel(heads, counts, number, plan, at_ref, select_hbm, *refs):
-    pieces = cuts(refs[:number], plan)
-    merged_ref, labels_ref, lat_ref, lon_ref, both_ref, expos_ref = refs[number : number + 6]
-    select_ref, whole_ref, packed_ref, sems, piece_sems = refs[number + 6 :]
-    copies = fetch(sems, (select_hbm, select_ref)) + start_pieces(whole_ref, pieces, at_ref, piece_sems)
-    count, width = merged_ref.shape
-    left = normalized(merged_ref[...].astype(jnp.float32))
-    wide = wide_labels(labels_ref, (lat_ref, lon_ref, both_ref), counts, 1)
-    copies[0].wait()
-    bias = label_bias(wide, select_ref[...])
-    for copy in copies[1:]:
+    merged = dot(left, flat(merge_ref)).astype(jnp.bfloat16)
+    merged_ref[...] = merged
+    left = normalized(merged.astype(jnp.float32))
+    for copy in score_copies:
         copy.wait()
-    packed_ref[...] = dot(left, flat(whole_ref)).astype(jnp.bfloat16)
+    packed_ref[...] = dot(left, flat(score_ref)).astype(jnp.bfloat16)
     for start, members in lane_heads(width, heads):
         queries = packed_ref[:, start : start + LANES]
         keys = packed_ref[:, width + start : width + start + LANES]
@@ -590,37 +586,44 @@
     last_first = after(first3, second2, mid)
     (join3,) = joined([near3, last_first])
     second3 = routed(join3, 1)
-    merge_pieces = (owns, join1, second1, other, *swapped(after((join1, second1), last_first)))
-    score_pieces = (owns, join2, second2, other, *swapped(after((join2, second2), last_first)))
-
-    def plan(group):
+    early_pieces = (owns, join1, second1, other, *swapped(after((join1, second1), near3)))
+    early_pieces += (join2, second2, *swapped(after((join2, second2), last_first)))
+
+    def plan(group, *rest):
         return [
-            [(own, 4 * group, 4), (own + 1, 0, far), (own + 1, far, far), (own + 2, 0, far), (own + 2, far, far)]
-            for own in (0, 3)
+            [(own, 4 * group, 4), (n, 0, far), (n, far, far), (n + 1, 0, far), (n + 1, far, far)]
+            for own, n in zip((0, 3), rest)
         ]
 
-    merge_plan, score_plan, value_plan = plan(0), plan(1), plan(2)
+    early_plans, value_plan = (plan(0, 1, 4), plan(1, 6, 8)), plan(2, 1, 4)
 
     source, depth = replaced(cells, middle, held)
     fine = source.reshape(levels, low, 2, narrow, 2)
     patches = [fine[:, :, r, :, c].reshape(-1) for r, c in ((0, 0), (1, 0), (0, 1), (1, 1))]
     select = matrix(np.concatenate(patches), depth)
-    (merged,) = call(
-        lambda *refs: merge_kernel(len(merge_pieces), merge_plan, *refs),
-        [(coarse_cells, wider)],
+    fine_depth = depth
+    source, depth = replaced(coarse_cells, end)
+    coarse_select = matrix(source, depth)
+    merged, expos = call(
+        lambda *refs: merge_kernel(HEADS2, counts, len(early_pieces), early_plans, *refs),
+        [(coarse_cells, wider), (HEADS2 * coarse_cells, coarse_cells)],
         [
             bf16(*select.shape),
-            bf16(depth, width),
+            bf16(*coarse_select.shape),
+            bf16(fine_depth, width),
             bf16(stops, 2, *merge_weight.shape),
-            dma(1),
+            bf16(stops, 2, rows, 2 * wider),
+            bf16(coarse_cells, 2 * wider),
+            dma(2),
+            dma(piece_copies(stops)),
             dma(piece_copies(stops)),
         ],
         scalars=(at,),
-        hbm=(select, *merge_pieces),
-        vmem=(y, *mid),
-    )
-
-    back = shifted(after(packets[3:], merged), 1)
+        hbm=(select, coarse_select, *early_pieces),
+        vmem=(y, *mid, coarse_labels, *got),
+    )
+
+    back = shifted(after(packets[3:], last_first), 1)
     source, depth = replaced(cells, start, held)
     select = matrix(source, depth)
     (skip,) = call(
@@ -633,20 +636,6 @@
 
     source, depth = replaced(coarse_cells, end)
     select = matrix(source, depth)
-    (expos,) = call(
-        lambda *refs: scores_kernel(HEADS2, counts, len(score_pieces), score_plan, *refs),
-        [(HEADS2 * coarse_cells, coarse_cells)],
-        [
-            bf16(*select.shape),
-            bf16(stops, 2, rows, 2 * wider),
-            bf16(coarse_cells, 2 * wider),
-            dma(1),
-            dma(piece_copies(stops)),
-        ],
-        scalars=(at,),
-        hbm=(select, *score_pieces),
-        vmem=(merged, coarse_labels, *got),
-    )
     value_swapped = swapped([after(join3, last_first), after(second3, back, expos)])
     value_pieces = (owns, join3, second3, other, *value_swapped)
     pick = jnp.concatenate(picks(end, end_rows, coarse_cells))

time: 107 us -> 107 us (level)
    ppermute x4, starting transfers between devices: 4.47 us -> 2.69 us  [shifted(): lax.ppermute(blocks[0], 'lat', [(i, (i + step) % lat) for i in range(lat)])]
    pallas_call x13 -> x12, Pallas kernels: 25.6 us -> 25.2 us  [call(): pl.pallas_call(kernel, out_shape=[jax.ShapeDtypeStruct(shape, jnp.bfloat1...]
  transfers between devices with their start and end apart: 34 -> 34, of which waited for: 10 -> 11; matrix products, arithmetic and copies ran while one was open for 0% -> 0% of each run, Pallas kernels for 15% -> 15%
where the time goes in v7:
time: 107 us
  starting transfers between devices  46.9 us (44%)
  waiting for transfers between devices  30.6 us (29%)
  Pallas kernels  25.2 us (24%)
  local copies, waits for them, and re-layouts  3.26 us (3%)
    pallas_call x12, Pallas kernels, call(): pl.pallas_call(kernel, out_shape=[jax.ShapeDtypeStruct(shape, jnp.bfloat1...  25.2 us
    ppermute x4, starting transfers between devices, shifted(): lax.ppermute(blocks[2], ('lat', 'lon'), [(i * lon + j, (i + step) % lat *...  18.6 us
    ppermute x9, starting transfers between devices, far_parts(): lax.ppermute(part, 'lon', [(i, (i + 2 * back) % ranks) for i in range(ran...  13.8 us
    ppermute x4, waiting for transfers between devices, shifted(): lax.ppermute(blocks[2], ('lat', 'lon'), [(i * lon + j, (i + step) % lat *...  11.9 us
    ppermute x9, waiting for transfers between devices, far_parts(): lax.ppermute(part, 'lon', [(i, (i + 2 * back) % ranks) for i in range(ran...  8.81 us
    ppermute x6, starting transfers between devices, routed(): return lax.ppermute(block, ('lat', 'lon'), pairs)  7.19 us
    ppermute x4, waiting for transfers between devices, shifted(): lax.ppermute(blocks[0], 'lat', [(i, (i + step) % lat) for i in range(lat)])  4.14 us
    unnamed x19, local copies, waits for them, and re-layouts  3.19 us
  transfers between devices with their start and end apart: 34, of which 11 were waited for; matrix products, arithmetic and copies ran while one was open for 0% of the time, Pallas kernels for 15%

profile of v7, /device:TPU:0, one launch (start us, length us, event | category | flops | bytes accessed | tf_op | source)
XLA Modules:
  0.0 106.9 jit_solution(15223013509091946903)
XLA Ops:
  0.7 3.1 %shard_map.293 = (bf16[112,512]{1,0:T(8,128)(2,1)S(1)}, bf16[112,512]{1,0:T(8,128)(2,1)S(1)}, bf16[48,512]{1,0:T(8,128)(2,1)S(1)}, bf16[8,576]{1,0:T(8,128)(2,1)...) custom-call(s32[4]{0:T(128)S(1)} %pad_add_fusion.refs_0_, ...), custom_call_target="tpu_custom_call" | custom-call | tf_op jit(solution)/shard_map/pallas_call | solution.py:417
  3.8 6.4 %collective-permute-start.2 = (bf16[48,512]{1,0:T(8,128)(2,1)S(1)}, bf16[48,512]{1,0:T(8,128)(2,1)S(1)}, u32[]{:S(2)}, u32[]{:S(2)}) collective-permute-start(bf16[48,512]{1,0:T(8,128)(2,1)S(1)} %get-tuple-element.56), channel_id=1, source_target_pairs={{0,31},{1,24},{2,25},{3,26},{4,27},{5,28},{6,29},{7,30},{8,7},{9,0... | collective-permute-start | bytes 147464 | tf_op jit(solution)/shard_map/ppermute | solution.py:435
  10.3 1.0 collective-permute-start.4
  11.3 2.8 %collective-permute-start.5 = (bf16[128,512]{1,0:T(8,128)(2,1)S(1)}, bf16[128,512]{1,0:T(8,128)(2,1)S(1)}, u32[]{:S(2)}, u32[]{:S(2)}) collective-permute-start(bf16[128,512]{1,0:T(8,128)(2,1)S(1)} %get-tuple-element.63), channel_id=1, source_target_pairs={{0,6},{1,7},{2,0},{3,1},{4,2},{5,3},{6,4},{7,5},{8,14},{9,15},{10,... | collective-permute-start | bytes 393224 | tf_op jit(solution)/shard_map/ppermute | solution.py:450
  14.1 0.5 collective-permute-start
  14.8 4.1 %collective-permute-done.refs_6_.refs_18_ = bf16[112,512]{1,0:T(8,128)(2,1)S(1)} collective-permute-done((bf16[112,512]{1,0:T(8,128)(2,1)S(1)}, bf16[112,512]{1,0:T(8,128)(2,1)S(1)}, u32[]{:S(2)}, u32[]{:S(2)}) %collective-permute-start) | collective-permute-done | bytes 114720 | tf_op jit(solution)/shard_map/ppermute | solution.py:433
  18.9 1.2 %collective-permute-done.1.refs_7_.refs_19_ = bf16[112,512]{1,0:T(8,128)(2,1)S(1)} collective-permute-done((bf16[112,512]{1,0:T(8,128)(2,1)S(1)}, bf16[112,512]{1,0:T(8,128)(2,1)S(1)}, u32[]{:S(2)}, u32[]{:S(2)}) %collective-permute-start.1) | collective-permute-done | bytes 114720 | tf_op jit(solution)/shard_map/ppermute | solution.py:434
  20.1 1.3 %collective-permute-done.4.refs_1_ = bf16[128,512]{1,0:T(8,128)(2,1)S(1)} collective-permute-done((bf16[128,512]{1,0:T(8,128)(2,1)S(1)}, bf16[128,512]{1,0:T(8,128)(2,1)S(1)}, u32[]{:S(2)}, u32[]{:S(2)}) %collective-permute-start.4) | collective-permute-done | bytes 131104 | tf_op jit(solution)/shard_map/ppermute | solution.py:450
  21.4 0.5 shard_map.295.refs_0_
  21.9 0.7 collective-permute-start.10
  22.6 3.4 %collective-permute-start.6 = (bf16[128,512]{1,0:T(8,128)(2,1)S(1)}, bf16[128,512]{1,0:T(8,128)(2,1)S(1)}, u32[]{:S(2)}, u32[]{:S(2)}) collective-permute-start(bf16[128,512]{1,0:T(8,128)(2,1)S(1)} %get-tuple-element.67), channel_id=1, source_target_pairs={{0,2},{1,3},{2,4},{3,5},{4,6},{5,7},{6,0},{7,1},{8,10},{9,11},{10,... | collective-permute-start | bytes 393224 | tf_op jit(solution)/shard_map/ppermute | solution.py:450
  26.0 2.2 %collective-permute-start.7 = (bf16[128,512]{1,0:T(8,128)(2,1)S(1)}, bf16[128,512]{1,0:T(8,128)(2,1)S(1)}, u32[]{:S(2)}, u32[]{:S(2)}) collective-permute-start(bf16[128,512]{1,0:T(8,128)(2,1)S(1)} %get-tuple-element.67), channel_id=1, source_target_pairs={{0,4},{1,5},{2,6},{3,7},{4,0},{5,1},{6,2},{7,3},{8,12},{9,13},{10,... | collective-permute-start | bytes 393224 | tf_op jit(solution)/shard_map/ppermute | solution.py:450
  28.4 1.1 %copy-done.6 = bf16[544,576]{1,0:T(8,128)(2,1)S(1)} copy-done((bf16[544,576]{1,0:T(8,128)(2,1)S(1)}, bf16[544,576]{1,0:T(8,128)(2,1)}, u32[]{:S(2)}) %copy-start.6) | copy-done | bytes 626712
  29.5 1.0 copy-done.7
  30.6 7.1 %shard_map.294 = (bf16[576,512]{1,0:T(8,128)(2,1)S(1)}, bf16[112,512]{1,0:T(8,128)(2,1)S(1)}, bf16[112,512]{1,0:T(8,128)(2,1)S(1)}, bf16[48,512]{1,0:T(8,128)(2,...) custom-call(bf16[576,512]{1,0:T(8,128)(2,1)S(1)} %bitcast.9, ...), custom_call_target="tpu_custom_call" | custom-call | tf_op jit(solution)/shard_map/pallas_call | solution.py:417
  37.8 0.5 shard_map.296.refs_0_
  38.3 0.4 shard_map.297.refs_4_
  38.7 1.2 %collective-permute-start.15 = (bf16[6,128,512]{2,1,0:T(8,128)(2,1)S(1)}, bf16[6,128,512]{2,1,0:T(8,128)(2,1)S(1)}, u32[]{:S(2)}, u32[]{:S(2)}) collective-permute-start(bf16[6,128,512]{2,1,0:T(8,128)(2,1)S(1)} %shard_map.297.refs_4_), channel_id=1, source_target_pairs={{0,16},{1,9},{2,18},{3,11},{4,20},{5,13},{6,22},{7,15},{8,24},{9,1... | collective-permute-start | bytes 2359304 | tf_op jit(solution)/shard_map/ppermute | solution.py:460
  39.9 1.4 %collective-permute-start.14 = (bf16[3,128,512]{2,1,0:T(8,128)(2,1)S(1)}, bf16[3,128,512]{2,1,0:T(8,128)(2,1)S(1)}, u32[]{:S(2)}, u32[]{:S(2)}) collective-permute-start(bf16[3,128,512]{2,1,0:T(8,128)(2,1)S(1)} %shard_map.296.refs_0_), channel_id=1, source_target_pairs={{0,8},{1,17},{2,10},{3,19},{4,12},{5,21},{6,14},{7,23},{8,0},{9,25... | collective-permute-start | bytes 1179656 | tf_op jit(solution)/shard_map/ppermute | solution.py:460
  41.3 1.8 %collective-permute-start.11 = (bf16[128,512]{1,0:T(8,128)(2,1)S(1)}, bf16[128,512]{1,0:T(8,128)(2,1)S(1)}, u32[]{:S(2)}, u32[]{:S(2)}) collective-permute-start(bf16[128,512]{1,0:T(8,128)(2,1)S(1)} %get-tuple-element.73), channel_id=1, source_target_pairs={{0,2},{1,3},{2,4},{3,5},{4,6},{5,7},{6,0},{7,1},{8,10},{9,11},{10,... | collective-permute-start | bytes 393224 | tf_op jit(solution)/shard_map/ppermute | solution.py:450
  43.1 0.8 collective-permute-start.12
  43.9 1.6 %collective-permute-start.13 = (bf16[128,512]{1,0:T(8,128)(2,1)S(1)}, bf16[128,512]{1,0:T(8,128)(2,1)S(1)}, u32[]{:S(2)}, u32[]{:S(2)}) collective-permute-start(bf16[128,512]{1,0:T(8,128)(2,1)S(1)} %get-tuple-element.73), channel_id=1, source_target_pairs={{0,6},{1,7},{2,0},{3,1},{4,2},{5,3},{6,4},{7,5},{8,14},{9,15},{10,... | collective-permute-start | bytes 393224 | tf_op jit(solution)/shard_map/ppermute | solution.py:450
  45.5 4.0 %collective-permute-done.11.refs_0_ = bf16[128,512]{1,0:T(8,128)(2,1)S(1)} collective-permute-done((bf16[128,512]{1,0:T(8,128)(2,1)S(1)}, bf16[128,512]{1,0:T(8,128)(2,1)S(1)}, u32[]{:S(2)}, u32[]{:S(2)}) %collective-permute-start.11) | collective-permute-done | bytes 131104 | tf_op jit(solution)/shard_map/ppermute | solution.py:450
  49.5 3.5 %collective-permute-done.12.refs_1_ = bf16[128,512]{1,0:T(8,128)(2,1)S(1)} collective-permute-done((bf16[128,512]{1,0:T(8,128)(2,1)S(1)}, bf16[128,512]{1,0:T(8,128)(2,1)S(1)}, u32[]{:S(2)}, u32[]{:S(2)}) %collective-permute-start.12) | collective-permute-done | bytes 131104 | tf_op jit(solution)/shard_map/ppermute | solution.py:450
  53.0 1.2 %collective-permute-done.15.refs_5_ = bf16[6,128,512]{2,1,0:T(8,128)(2,1)S(1)} collective-permute-done((bf16[6,128,512]{2,1,0:T(8,128)(2,1)S(1)}, bf16[6,128,512]{2,1,0:T(8,128)(2,1)S(1)}, u32[]{:S(2)}, u32[]{:S(2)}) %collective-permute-start.15) | collective-permute-done | bytes 786464 | tf_op jit(solution)/shard_map/ppermute | solution.py:460
  54.2 0.5 shard_map.298.refs_0_
  55.2 1.4 %collective-permute-start.17 = (bf16[6,128,512]{2,1,0:T(8,128)(2,1)S(1)}, bf16[6,128,512]{2,1,0:T(8,128)(2,1)S(1)}, u32[]{:S(2)}, u32[]{:S(2)}) collective-permute-start(bf16[6,128,512]{2,1,0:T(8,128)(2,1)S(1)} %shard_map.299.refs_9_), channel_id=1, source_target_pairs={{0,16},{1,9},{2,18},{3,11},{4,20},{5,13},{6,22},{7,15},{8,24},{9,1... | collective-permute-start | bytes 2359304 | tf_op jit(solution)/shard_map/ppermute | solution.py:460
  56.6 1.7 %collective-permute-start.16 = (bf16[3,128,512]{2,1,0:T(8,128)(2,1)S(1)}, bf16[3,128,512]{2,1,0:T(8,128)(2,1)S(1)}, u32[]{:S(2)}, u32[]{:S(2)}) collective-permute-start(bf16[3,128,512]{2,1,0:T(8,128)(2,1)S(1)} %shard_map.298.refs_0_), channel_id=1, source_target_pairs={{0,8},{1,17},{2,10},{3,19},{4,12},{5,21},{6,14},{7,23},{8,0},{9,25... | collective-permute-start | bytes 1179656 | tf_op jit(solution)/shard_map/ppermute | solution.py:460
  58.2 0.5 collective-permute-start.18
  58.7 1.5 %collective-permute-start.19 = (bf16[112,512]{1,0:T(8,128)(2,1)S(1)}, bf16[112,512]{1,0:T(8,128)(2,1)S(1)}, u32[]{:S(2)}, u32[]{:S(2)}) collective-permute-start(bf16[112,512]{1,0:T(8,128)(2,1)S(1)} %get-tuple-element.85), channel_id=1, source_target_pairs={{0,7},{1,0},{2,1},{3,2},{4,3},{5,4},{6,5},{7,6},{8,15},{9,8},{10,9... | collective-permute-start | bytes 344072 | tf_op jit(solution)/shard_map/ppermute | solution.py:434
  60.3 2.9 %collective-permute-start.20 = (bf16[48,512]{1,0:T(8,128)(2,1)S(1)}, bf16[48,512]{1,0:T(8,128)(2,1)S(1)}, u32[]{:S(2)}, u32[]{:S(2)}) collective-permute-start(bf16[48,512]{1,0:T(8,128)(2,1)S(1)} %get-tuple-element.86), channel_id=1, source_target_pairs={{0,31},{1,24},{2,25},{3,26},{4,27},{5,28},{6,29},{7,30},{8,7},{9,0... | collective-permute-start | bytes 147464 | tf_op jit(solution)/shard_map/ppermute | solution.py:435
  63.2 10.6 %collective-permute-done.20.refs_16_ = bf16[48,512]{1,0:T(8,128)(2,1)S(1)} collective-permute-done((bf16[48,512]{1,0:T(8,128)(2,1)S(1)}, bf16[48,512]{1,0:T(8,128)(2,1)S(1)}, u32[]{:S(2)}, u32[]{:S(2)}) %collective-permute-start.20) | collective-permute-done | bytes 49184 | tf_op jit(solution)/shard_map/ppermute | solution.py:435
  73.8 0.5 collective-permute-start.27
  74.4 0.5 collective-permute-start.29
  75.3 1.6 %collective-permute-start.24 = (bf16[6,128,512]{2,1,0:T(8,128)(2,1)S(1)}, bf16[6,128,512]{2,1,0:T(8,128)(2,1)S(1)}, u32[]{:S(2)}, u32[]{:S(2)}) collective-permute-start(bf16[6,128,512]{2,1,0:T(8,128)(2,1)S(1)} %shard_map.301.refs_3_), channel_id=1, source_target_pairs={{0,16},{1,9},{2,18},{3,11},{4,20},{5,13},{6,22},{7,15},{8,24},{9,1... | collective-permute-start | bytes 2359304 | tf_op jit(solution)/shard_map/ppermute | solution.py:460
  76.9 1.2 %collective-permute-start.21 = (bf16[112,512]{1,0:T(8,128)(2,1)S(1)}, bf16[112,512]{1,0:T(8,128)(2,1)S(1)}, u32[]{:S(2)}, u32[]{:S(2)}) collective-permute-start(bf16[112,512]{1,0:T(8,128)(2,1)S(1)} %get-tuple-element.88), channel_id=1, source_target_pairs={{0,8},{8,16},{16,24},{24,0},{1,9},{9,17},{17,25},{25,1},{2,10},{10... | collective-permute-start | bytes 344072 | tf_op jit(solution)/shard_map/ppermute | solution.py:433
  78.3 3.6 %collective-permute-start.23 = (bf16[48,512]{1,0:T(8,128)(2,1)S(1)}, bf16[48,512]{1,0:T(8,128)(2,1)S(1)}, u32[]{:S(2)}, u32[]{:S(2)}) collective-permute-start(bf16[48,512]{1,0:T(8,128)(2,1)S(1)} %get-tuple-element.90), channel_id=1, source_target_pairs={{0,9},{1,10},{2,11},{3,12},{4,13},{5,14},{6,15},{7,8},{8,17},{9,18... | collective-permute-start | bytes 147464 | tf_op jit(solution)/shard_map/ppermute | solution.py:435
  82.2 6.6 %shard_map.302 = (bf16[144,1024]{1,0:T(8,128)(2,1)S(1)}, bf16[2304,144]{1,0:T(8,128)(2,1)S(1)}) custom-call(s32[4]{0:T(128)S(1)} %pad_add_fusion.refs_0_, bf16[576,1024]{1,0:T(8,128)(2,1)S(1)} %copy-done.3, bf16[144,640]{1,0:T(8,128)(2,1)S(1)} %copy-done.5, bf16[12,128,512]{2,1,0:T(8,128)(2,1)S(1)} %get-tuple-element.69.refs_3_.refs_2_, ...), custom_call_target="tpu_custom_call" | custom-call | tf_op jit(solution)/shard_map/pallas_call | solution.py:417
  88.9 1.0 collective-permute-done.24.refs_4_
  89.9 0.9 collective-permute-start.30
  90.8 1.9 %collective-permute-done.30.refs_7_ = bf16[6,128,512]{2,1,0:T(8,128)(2,1)S(1)} collective-permute-done((bf16[6,128,512]{2,1,0:T(8,128)(2,1)S(1)}, bf16[6,128,512]{2,1,0:T(8,128)(2,1)S(1)}, u32[]{:S(2)}, u32[]{:S(2)}) %collective-permute-start.30) | collective-permute-done | bytes 786464 | tf_op jit(solution)/shard_map/ppermute | solution.py:444
  92.7 3.1 %shard_map.303 = (bf16[144,1024]{1,0:T(8,128)(2,1)S(1)}, bf16[48,1024]{1,0:T(8,128)(2,1)S(1)}, bf16[48,1024]{1,0:T(8,128)(2,1)S(1)}, bf16[48,1024]{1,0:T(8,128)(2,1)S(1)}) custom-call(s32[4]{0:T(128)S(1)} %pad_add_fusion.refs_0_, bf16[144,144]{1,0:T(8,128)(2,1)S(1)} %copy-done.8, bf16[12,128,512]{2,1,0:T(8,128)(2,1)S(1)} %get-tuple-element.69.refs_3_.refs_2_, ...), custom_call_target="tpu_custom_call" | custom-call | tf_op jit(solution)/shard_map/pallas_call | solution.py:417
  95.8 0.5 collective-permute-start.31
  96.3 5.7 %collective-permute-start.33 = (bf16[48,1024]{1,0:T(8,128)(2,1)S(1)}, bf16[48,1024]{1,0:T(8,128)(2,1)S(1)}, u32[]{:S(2)}, u32[]{:S(2)}) collective-permute-start(bf16[48,1024]{1,0:T(8,128)(2,1)S(1)} %get-tuple-element.103), channel_id=1, source_target_pairs={{0,9},{1,10},{2,11},{3,12},{4,13},{5,14},{6,15},{7,8},{8,17},{9,18... | collective-permute-start | bytes 294920 | tf_op jit(solution)/shard_map/ppermute | solution.py:435
  102.0 1.9 %shard_map.300 = bf16[576,512]{1,0:T(8,128)(2,1)} custom-call(bf16[576,1024]{1,0:T(8,128)(2,1)S(1)} %copy-done.2, bf16[576,512]{1,0:T(8,128)(2,1)S(1)} %get-tuple-element.57.own_ref.refs_13_, bf16[112,512]{1,0:T(8,128)(2,1)S(1)} %collective-permute-done.21.lat_ref, bf16[112,512]{1,0:T(8,128)(2,1)S(1)} %collective-permute-done.22.lon_ref, ...), custom_call_target="tpu_custom_call" | custom-call | tf_op jit(solution)/shard_map/pallas_call | solution.py:417
  103.9 1.3 %collective-permute-done.33.both_ref = bf16[48,1024]{1,0:T(8,128)(2,1)S(1)} collective-permute-done((bf16[48,1024]{1,0:T(8,128)(2,1)S(1)}, bf16[48,1024]{1,0:T(8,128)(2,1)S(1)}, u32[]{:S(2)}, u32[]{:S(2)}) %collective-permute-start.33) | collective-permute-done | bytes 98336 | tf_op jit(solution)/shard_map/ppermute | solution.py:435
  105.2 0.6 shard_map.304
  105.9 1.0 copy.33
  (53 shorter events, 2.0 us)
Async XLA Ops:
  0.7 27.7 %copy-start = (bf16[2,12,24,512]{3,2,1,0:T(8,128)(2,1)S(1)}, bf16[2,12,24,512]{3,2,1,0:T(8,128)(2,1)}, u32[]{:S(2)}) copy-start(bf16[2,12,24,512]{3,2,1,0:T(8,128)(2,1)} %param.30) | copy-start | bytes 1769476
  0.7 27.7 %copy-start.1 = (bf16[512,1536]{1,0:T(8,128)(2,1)S(1)}, bf16[512,1536]{1,0:T(8,128)(2,1)}, u32[]{:S(2)}) copy-start(bf16[512,1536]{1,0:T(8,128)(2,1)} %refs_2_.2) | copy-start | bytes 4718596
  0.7 27.7 %copy-start.4 = (bf16[576,1024]{1,0:T(8,128)(2,1)S(1)}, bf16[576,1024]{1,0:T(8,128)(2,1)}, u32[]{:S(2)}) copy-start(bf16[576,1024]{1,0:T(8,128)(2,1)} %constant.93.clone.refs_1_) | copy-start | bytes 3538948
  3.8 10.8 %collective-permute-start.2 = (bf16[48,512]{1,0:T(8,128)(2,1)S(1)}, bf16[48,512]{1,0:T(8,128)(2,1)S(1)}, u32[]{:S(2)}, u32[]{:S(2)}) collective-permute-start(bf16[48,512]{1,0:T(8,128)(2,1)S(1)} %get-tuple-element.56), channel_id=1, source_target_pairs={{0,31},{1,24},{2,25},{3,26},{4,27},{5,28},{6,29},{7,30},{8,7},{9,0... | collective-permute-start | bytes 147464 | tf_op jit(solution)/shard_map/ppermute | solution.py:435
  10.3 9.9 %collective-permute-start.3 = (bf16[128,512]{1,0:T(8,128)(2,1)S(1)}, bf16[128,512]{1,0:T(8,128)(2,1)S(1)}, u32[]{:S(2)}, u32[]{:S(2)}) collective-permute-start(bf16[128,512]{1,0:T(8,128)(2,1)S(1)} %get-tuple-element.63), channel_id=1, source_target_pairs={{0,2},{1,3},{2,4},{3,5},{4,6},{5,7},{6,0},{7,1},{8,10},{9,11},{10,... | collective-permute-start | bytes 393224 | tf_op jit(solution)/shard_map/ppermute | solution.py:450
  10.3 11.1 %collective-permute-start.4 = (bf16[128,512]{1,0:T(8,128)(2,1)S(1)}, bf16[128,512]{1,0:T(8,128)(2,1)S(1)}, u32[]{:S(2)}, u32[]{:S(2)}) collective-permute-start(bf16[128,512]{1,0:T(8,128)(2,1)S(1)} %get-tuple-element.63), channel_id=1, source_target_pairs={{0,4},{1,5},{2,6},{3,7},{4,0},{5,1},{6,2},{7,3},{8,12},{9,13},{10,... | collective-permute-start | bytes 393224 | tf_op jit(solution)/shard_map/ppermute | solution.py:450
  11.3 10.1 %collective-permute-start.5 = (bf16[128,512]{1,0:T(8,128)(2,1)S(1)}, bf16[128,512]{1,0:T(8,128)(2,1)S(1)}, u32[]{:S(2)}, u32[]{:S(2)}) collective-permute-start(bf16[128,512]{1,0:T(8,128)(2,1)S(1)} %get-tuple-element.63), channel_id=1, source_target_pairs={{0,6},{1,7},{2,0},{3,1},{4,2},{5,3},{6,4},{7,5},{8,14},{9,15},{10,... | collective-permute-start | bytes 393224 | tf_op jit(solution)/shard_map/ppermute | solution.py:450
  14.1 4.8 %collective-permute-start = (bf16[112,512]{1,0:T(8,128)(2,1)S(1)}, bf16[112,512]{1,0:T(8,128)(2,1)S(1)}, u32[]{:S(2)}, u32[]{:S(2)}) collective-permute-start(bf16[112,512]{1,0:T(8,128)(2,1)S(1)} %get-tuple-element.54), channel_id=1, source_target_pairs={{0,24},{8,0},{16,8},{24,16},{1,25},{9,1},{17,9},{25,17},{2,26},{10... | collective-permute-start | bytes 344072 | tf_op jit(solution)/shard_map/ppermute | solution.py:433
  14.6 5.5 %collective-permute-start.1 = (bf16[112,512]{1,0:T(8,128)(2,1)S(1)}, bf16[112,512]{1,0:T(8,128)(2,1)S(1)}, u32[]{:S(2)}, u32[]{:S(2)}) collective-permute-start(bf16[112,512]{1,0:T(8,128)(2,1)S(1)} %get-tuple-element.55), channel_id=1, source_target_pairs={{0,7},{1,0},{2,1},{3,2},{4,3},{5,4},{6,5},{7,6},{8,15},{9,8},{10,9... | collective-permute-start | bytes 344072 | tf_op jit(solution)/shard_map/ppermute | solution.py:434
  21.9 15.8 %collective-permute-start.10 = (bf16[12,128,512]{2,1,0:T(8,128)(2,1)S(1)}, bf16[12,128,512]{2,1,0:T(8,128)(2,1)S(1)}, u32[]{:S(2)}, u32[]{:S(2)}) collective-permute-start(bf16[12,128,512]{2,1,0:T(8,128)(2,1)S(1)} %get-tuple-element.69.refs_3_.refs_2_), channel_id=1, source_target_pairs={{0,1},{1,0},{2,3},{3,2},{4,5},{5,4},{6,7},{7,6},{8,9},{9,8},{10,11... | collective-permute-start | bytes 4718600 | tf_op jit(solution)/shard_map/ppermute | solution.py:444
  22.6 15.1 %collective-permute-start.9 = (bf16[3,128,512]{2,1,0:T(8,128)(2,1)S(1)}, bf16[3,128,512]{2,1,0:T(8,128)(2,1)S(1)}, u32[]{:S(2)}, u32[]{:S(2)}) collective-permute-start(bf16[3,128,512]{2,1,0:T(8,128)(2,1)S(1)} %shard_map.295.refs_0_), channel_id=1, source_target_pairs={{0,8},{1,17},{2,10},{3,19},{4,12},{5,21},{6,14},{7,23},{8,0},{9,25... | collective-permute-start | bytes 1179656 | tf_op jit(solution)/shard_map/ppermute | solution.py:460
  22.6 15.1 %collective-permute-start.6 = (bf16[128,512]{1,0:T(8,128)(2,1)S(1)}, bf16[128,512]{1,0:T(8,128)(2,1)S(1)}, u32[]{:S(2)}, u32[]{:S(2)}) collective-permute-start(bf16[128,512]{1,0:T(8,128)(2,1)S(1)} %get-tuple-element.67), channel_id=1, source_target_pairs={{0,2},{1,3},{2,4},{3,5},{4,6},{5,7},{6,0},{7,1},{8,10},{9,11},{10,... | collective-permute-start | bytes 393224 | tf_op jit(solution)/shard_map/ppermute | solution.py:450
  26.0 11.7 %collective-permute-start.7 = (bf16[128,512]{1,0:T(8,128)(2,1)S(1)}, bf16[128,512]{1,0:T(8,128)(2,1)S(1)}, u32[]{:S(2)}, u32[]{:S(2)}) collective-permute-start(bf16[128,512]{1,0:T(8,128)(2,1)S(1)} %get-tuple-element.67), channel_id=1, source_target_pairs={{0,4},{1,5},{2,6},{3,7},{4,0},{5,1},{6,2},{7,3},{8,12},{9,13},{10,... | collective-permute-start | bytes 393224 | tf_op jit(solution)/shard_map/ppermute | solution.py:450
  28.3 9.4 %collective-permute-start.8 = (bf16[128,512]{1,0:T(8,128)(2,1)S(1)}, bf16[128,512]{1,0:T(8,128)(2,1)S(1)}, u32[]{:S(2)}, u32[]{:S(2)}) collective-permute-start(bf16[128,512]{1,0:T(8,128)(2,1)S(1)} %get-tuple-element.67), channel_id=1, source_target_pairs={{0,6},{1,7},{2,0},{3,1},{4,2},{5,3},{6,4},{7,5},{8,14},{9,15},{10,... | collective-permute-start | bytes 393224 | tf_op jit(solution)/shard_map/ppermute | solution.py:450
  28.4 1.1 %copy-start.6 = (bf16[544,576]{1,0:T(8,128)(2,1)S(1)}, bf16[544,576]{1,0:T(8,128)(2,1)}, u32[]{:S(2)}) copy-start(bf16[544,576]{1,0:T(8,128)(2,1)} %constant.107.refs_4_) | copy-start | bytes 1880068
  29.5 1.0 copy-start.7
  38.7 15.5 %collective-permute-start.15 = (bf16[6,128,512]{2,1,0:T(8,128)(2,1)S(1)}, bf16[6,128,512]{2,1,0:T(8,128)(2,1)S(1)}, u32[]{:S(2)}, u32[]{:S(2)}) collective-permute-start(bf16[6,128,512]{2,1,0:T(8,128)(2,1)S(1)} %shard_map.297.refs_4_), channel_id=1, source_target_pairs={{0,16},{1,9},{2,18},{3,11},{4,20},{5,13},{6,22},{7,15},{8,24},{9,1... | collective-permute-start | bytes 2359304 | tf_op jit(solution)/shard_map/ppermute | solution.py:460
  39.9 13.2 %collective-permute-start.14 = (bf16[3,128,512]{2,1,0:T(8,128)(2,1)S(1)}, bf16[3,128,512]{2,1,0:T(8,128)(2,1)S(1)}, u32[]{:S(2)}, u32[]{:S(2)}) collective-permute-start(bf16[3,128,512]{2,1,0:T(8,128)(2,1)S(1)} %shard_map.296.refs_0_), channel_id=1, source_target_pairs={{0,8},{1,17},{2,10},{3,19},{4,12},{5,21},{6,14},{7,23},{8,0},{9,25... | collective-permute-start | bytes 1179656 | tf_op jit(solution)/shard_map/ppermute | solution.py:460
  41.3 8.2 %collective-permute-start.11 = (bf16[128,512]{1,0:T(8,128)(2,1)S(1)}, bf16[128,512]{1,0:T(8,128)(2,1)S(1)}, u32[]{:S(2)}, u32[]{:S(2)}) collective-permute-start(bf16[128,512]{1,0:T(8,128)(2,1)S(1)} %get-tuple-element.73), channel_id=1, source_target_pairs={{0,2},{1,3},{2,4},{3,5},{4,6},{5,7},{6,0},{7,1},{8,10},{9,11},{10,... | collective-permute-start | bytes 393224 | tf_op jit(solution)/shard_map/ppermute | solution.py:450
  43.1 9.9 %collective-permute-start.12 = (bf16[128,512]{1,0:T(8,128)(2,1)S(1)}, bf16[128,512]{1,0:T(8,128)(2,1)S(1)}, u32[]{:S(2)}, u32[]{:S(2)}) collective-permute-start(bf16[128,512]{1,0:T(8,128)(2,1)S(1)} %get-tuple-element.73), channel_id=1, source_target_pairs={{0,4},{1,5},{2,6},{3,7},{4,0},{5,1},{6,2},{7,3},{8,12},{9,13},{10,... | collective-permute-start | bytes 393224 | tf_op jit(solution)/shard_map/ppermute | solution.py:450
  43.9 9.1 %collective-permute-start.13 = (bf16[128,512]{1,0:T(8,128)(2,1)S(1)}, bf16[128,512]{1,0:T(8,128)(2,1)S(1)}, u32[]{:S(2)}, u32[]{:S(2)}) collective-permute-start(bf16[128,512]{1,0:T(8,128)(2,1)S(1)} %get-tuple-element.73), channel_id=1, source_target_pairs={{0,6},{1,7},{2,0},{3,1},{4,2},{5,3},{6,4},{7,5},{8,14},{9,15},{10,... | collective-permute-start | bytes 393224 | tf_op jit(solution)/shard_map/ppermute | solution.py:450
  55.2 27.0 %copy-start.3 = (bf16[576,1024]{1,0:T(8,128)(2,1)S(1)}, bf16[576,1024]{1,0:T(8,128)(2,1)}, u32[]{:S(2)}) copy-start(bf16[576,1024]{1,0:T(8,128)(2,1)} %constant.100.clone.refs_1_) | copy-start | bytes 3538948
  55.2 27.0 %copy-start.5 = (bf16[144,640]{1,0:T(8,128)(2,1)S(1)}, bf16[144,640]{1,0:T(8,128)(2,1)}, u32[]{:S(2)}) copy-start(bf16[144,640]{1,0:T(8,128)(2,1)} %constant.101.clone.refs_2_.select_hbm) | copy-start | bytes 552964
  55.2 19.1 %collective-permute-start.17 = (bf16[6,128,512]{2,1,0:T(8,128)(2,1)S(1)}, bf16[6,128,512]{2,1,0:T(8,128)(2,1)S(1)}, u32[]{:S(2)}, u32[]{:S(2)}) collective-permute-start(bf16[6,128,512]{2,1,0:T(8,128)(2,1)S(1)} %shard_map.299.refs_9_), channel_id=1, source_target_pairs={{0,16},{1,9},{2,18},{3,11},{4,20},{5,13},{6,22},{7,15},{8,24},{9,1... | collective-permute-start | bytes 2359304 | tf_op jit(solution)/shard_map/ppermute | solution.py:460
  56.6 17.8 %collective-permute-start.16 = (bf16[3,128,512]{2,1,0:T(8,128)(2,1)S(1)}, bf16[3,128,512]{2,1,0:T(8,128)(2,1)S(1)}, u32[]{:S(2)}, u32[]{:S(2)}) collective-permute-start(bf16[3,128,512]{2,1,0:T(8,128)(2,1)S(1)} %shard_map.298.refs_0_), channel_id=1, source_target_pairs={{0,8},{1,17},{2,10},{3,19},{4,12},{5,21},{6,14},{7,23},{8,0},{9,25... | collective-permute-start | bytes 1179656 | tf_op jit(solution)/shard_map/ppermute | solution.py:460
  58.2 15.6 %collective-permute-start.18 = (bf16[112,512]{1,0:T(8,128)(2,1)S(1)}, bf16[112,512]{1,0:T(8,128)(2,1)S(1)}, u32[]{:S(2)}, u32[]{:S(2)}) collective-permute-start(bf16[112,512]{1,0:T(8,128)(2,1)S(1)} %get-tuple-element.84), channel_id=1, source_target_pairs={{0,24},{8,0},{16,8},{24,16},{1,25},{9,1},{17,9},{25,17},{2,26},{10... | collective-permute-start | bytes 344072 | tf_op jit(solution)/shard_map/ppermute | solution.py:433
  58.7 15.6 %collective-permute-start.19 = (bf16[112,512]{1,0:T(8,128)(2,1)S(1)}, bf16[112,512]{1,0:T(8,128)(2,1)S(1)}, u32[]{:S(2)}, u32[]{:S(2)}) collective-permute-start(bf16[112,512]{1,0:T(8,128)(2,1)S(1)} %get-tuple-element.85), channel_id=1, source_target_pairs={{0,7},{1,0},{2,1},{3,2},{4,3},{5,4},{6,5},{7,6},{8,15},{9,8},{10,9... | collective-permute-start | bytes 344072 | tf_op jit(solution)/shard_map/ppermute | solution.py:434
  60.3 13.5 %collective-permute-start.20 = (bf16[48,512]{1,0:T(8,128)(2,1)S(1)}, bf16[48,512]{1,0:T(8,128)(2,1)S(1)}, u32[]{:S(2)}, u32[]{:S(2)}) collective-permute-start(bf16[48,512]{1,0:T(8,128)(2,1)S(1)} %get-tuple-element.86), channel_id=1, source_target_pairs={{0,31},{1,24},{2,25},{3,26},{4,27},{5,28},{6,29},{7,30},{8,7},{9,0... | collective-permute-start | bytes 147464 | tf_op jit(solution)/shard_map/ppermute | solution.py:435
  73.8 3.1 %collective-permute-start.26 = (bf16[6,128,512]{2,1,0:T(8,128)(2,1)S(1)}, bf16[6,128,512]{2,1,0:T(8,128)(2,1)S(1)}, u32[]{:S(2)}, u32[]{:S(2)}) collective-permute-start(bf16[6,128,512]{2,1,0:T(8,128)(2,1)S(1)} %shard_map.297.refs_4_), channel_id=1, source_target_pairs={{0,1},{1,0},{2,3},{3,2},{4,5},{5,4},{6,7},{7,6},{8,9},{9,8},{10,11... | collective-permute-start | bytes 2359304 | tf_op jit(solution)/shard_map/ppermute | solution.py:444
  73.8 4.2 %collective-permute-start.27 = (bf16[6,128,512]{2,1,0:T(8,128)(2,1)S(1)}, bf16[6,128,512]{2,1,0:T(8,128)(2,1)S(1)}, u32[]{:S(2)}, u32[]{:S(2)}) collective-permute-start(bf16[6,128,512]{2,1,0:T(8,128)(2,1)S(1)} %collective-permute-done.15.refs_5_), channel_id=1, source_target_pairs={{0,1},{1,0},{2,3},{3,2},{4,5},{5,4},{6,7},{7,6},{8,9},{9,8},{10,11... | collective-permute-start | bytes 2359304 | tf_op jit(solution)/shard_map/ppermute | solution.py:444
  74.3 4.0 %collective-permute-start.28 = (bf16[6,128,512]{2,1,0:T(8,128)(2,1)S(1)}, bf16[6,128,512]{2,1,0:T(8,128)(2,1)S(1)}, u32[]{:S(2)}, u32[]{:S(2)}) collective-permute-start(bf16[6,128,512]{2,1,0:T(8,128)(2,1)S(1)} %shard_map.299.refs_9_), channel_id=1, source_target_pairs={{0,1},{1,0},{2,3},{3,2},{4,5},{5,4},{6,7},{7,6},{8,9},{9,8},{10,11... | collective-permute-start | bytes 2359304 | tf_op jit(solution)/shard_map/ppermute | solution.py:444
  74.4 7.5 %collective-permute-start.29 = (bf16[6,128,512]{2,1,0:T(8,128)(2,1)S(1)}, bf16[6,128,512]{2,1,0:T(8,128)(2,1)S(1)}, u32[]{:S(2)}, u32[]{:S(2)}) collective-permute-start(bf16[6,128,512]{2,1,0:T(8,128)(2,1)S(1)} %collective-permute-done.17.refs_10_), channel_id=1, source_target_pairs={{0,1},{1,0},{2,3},{3,2},{4,5},{5,4},{6,7},{7,6},{8,9},{9,8},{10,11... | collective-permute-start | bytes 2359304 | tf_op jit(solution)/shard_map/ppermute | solution.py:444
  75.3 14.6 %collective-permute-start.24 = (bf16[6,128,512]{2,1,0:T(8,128)(2,1)S(1)}, bf16[6,128,512]{2,1,0:T(8,128)(2,1)S(1)}, u32[]{:S(2)}, u32[]{:S(2)}) collective-permute-start(bf16[6,128,512]{2,1,0:T(8,128)(2,1)S(1)} %shard_map.301.refs_3_), channel_id=1, source_target_pairs={{0,16},{1,9},{2,18},{3,11},{4,20},{5,13},{6,22},{7,15},{8,24},{9,1... | collective-permute-start | bytes 2359304 | tf_op jit(solution)/shard_map/ppermute | solution.py:460
  76.9 12.0 %collective-permute-start.21 = (bf16[112,512]{1,0:T(8,128)(2,1)S(1)}, bf16[112,512]{1,0:T(8,128)(2,1)S(1)}, u32[]{:S(2)}, u32[]{:S(2)}) collective-permute-start(bf16[112,512]{1,0:T(8,128)(2,1)S(1)} %get-tuple-element.88), channel_id=1, source_target_pairs={{0,8},{8,16},{16,24},{24,0},{1,9},{9,17},{17,25},{25,1},{2,10},{10... | collective-permute-start | bytes 344072 | tf_op jit(solution)/shard_map/ppermute | solution.py:433
  78.0 10.8 %collective-permute-start.22 = (bf16[112,512]{1,0:T(8,128)(2,1)S(1)}, bf16[112,512]{1,0:T(8,128)(2,1)S(1)}, u32[]{:S(2)}, u32[]{:S(2)}) collective-permute-start(bf16[112,512]{1,0:T(8,128)(2,1)S(1)} %get-tuple-element.89), channel_id=1, source_target_pairs={{0,1},{1,2},{2,3},{3,4},{4,5},{5,6},{6,7},{7,0},{8,9},{9,10},{10,1... | collective-permute-start | bytes 344072 | tf_op jit(solution)/shard_map/ppermute | solution.py:434
  78.3 10.5 %collective-permute-start.23 = (bf16[48,512]{1,0:T(8,128)(2,1)S(1)}, bf16[48,512]{1,0:T(8,128)(2,1)S(1)}, u32[]{:S(2)}, u32[]{:S(2)}) collective-permute-start(bf16[48,512]{1,0:T(8,128)(2,1)S(1)} %get-tuple-element.90), channel_id=1, source_target_pairs={{0,9},{1,10},{2,11},{3,12},{4,13},{5,14},{6,15},{7,8},{8,17},{9,18... | collective-permute-start | bytes 147464 | tf_op jit(solution)/shard_map/ppermute | solution.py:435
  81.9 8.9 %collective-permute-start.25 = (bf16[6,128,512]{2,1,0:T(8,128)(2,1)S(1)}, bf16[6,128,512]{2,1,0:T(8,128)(2,1)S(1)}, u32[]{:S(2)}, u32[]{:S(2)}) collective-permute-start(bf16[6,128,512]{2,1,0:T(8,128)(2,1)S(1)} %shard_map.301.refs_3_), channel_id=1, source_target_pairs={{0,1},{1,0},{2,3},{3,2},{4,5},{5,4},{6,7},{7,6},{8,9},{9,8},{10,11... | collective-permute-start | bytes 2359304 | tf_op jit(solution)/shard_map/ppermute | solution.py:444
  82.2 10.5 %copy-start.8 = (bf16[144,144]{1,0:T(8,128)(2,1)S(1)}, bf16[144,144]{1,0:T(8,128)(2,1)}, u32[]{:S(2)}) copy-start(bf16[144,144]{1,0:T(8,128)(2,1)} %constant.112.refs_1_) | copy-start | bytes 124420
  89.9 2.8 %collective-permute-start.30 = (bf16[6,128,512]{2,1,0:T(8,128)(2,1)S(1)}, bf16[6,128,512]{2,1,0:T(8,128)(2,1)S(1)}, u32[]{:S(2)}, u32[]{:S(2)}) collective-permute-start(bf16[6,128,512]{2,1,0:T(8,128)(2,1)S(1)} %collective-permute-done.24.refs_4_), channel_id=1, source_target_pairs={{0,1},{1,0},{2,3},{3,2},{4,5},{5,4},{6,7},{7,6},{8,9},{9,8},{10,11... | collective-permute-start | bytes 2359304 | tf_op jit(solution)/shard_map/ppermute | solution.py:444
  92.7 9.3 %copy-start.2 = (bf16[576,1024]{1,0:T(8,128)(2,1)S(1)}, bf16[576,1024]{1,0:T(8,128)(2,1)}, u32[]{:S(2)}) copy-start(bf16[576,1024]{1,0:T(8,128)(2,1)} %constant.102.clone.select_hbm) | copy-start | bytes 3538948
  95.8 8.1 %collective-permute-start.31 = (bf16[48,1024]{1,0:T(8,128)(2,1)S(1)}, bf16[48,1024]{1,0:T(8,128)(2,1)S(1)}, u32[]{:S(2)}, u32[]{:S(2)}) collective-permute-start(bf16[48,1024]{1,0:T(8,128)(2,1)S(1)} %get-tuple-element.101), channel_id=1, source_target_pairs={{0,8},{8,16},{16,24},{24,0},{1,9},{9,17},{17,25},{25,1},{2,10},{10... | collective-permute-start | bytes 294920 | tf_op jit(solution)/shard_map/ppermute | solution.py:433
  96.2 7.6 %collective-permute-start.32 = (bf16[48,1024]{1,0:T(8,128)(2,1)S(1)}, bf16[48,1024]{1,0:T(8,128)(2,1)S(1)}, u32[]{:S(2)}, u32[]{:S(2)}) collective-permute-start(bf16[48,1024]{1,0:T(8,128)(2,1)S(1)} %get-tuple-element.102), channel_id=1, source_target_pairs={{0,1},{1,2},{2,3},{3,4},{4,5},{5,6},{6,7},{7,0},{8,9},{9,10},{10,1... | collective-permute-start | bytes 294920 | tf_op jit(solution)/shard_map/ppermute | solution.py:434
  96.3 8.9 %collective-permute-start.33 = (bf16[48,1024]{1,0:T(8,128)(2,1)S(1)}, bf16[48,1024]{1,0:T(8,128)(2,1)S(1)}, u32[]{:S(2)}, u32[]{:S(2)}) collective-permute-start(bf16[48,1024]{1,0:T(8,128)(2,1)S(1)} %get-tuple-element.103), channel_id=1, source_target_pairs={{0,9},{1,10},{2,11},{3,12},{4,13},{5,14},{6,15},{7,8},{8,17},{9,18... | collective-permute-start | bytes 294920 | tf_op jit(solution)/shard_map/ppermute | solution.py:435

commit v8 on v7

--- a/solution.py
+++ b/solution.py
@@ -410,9 +410,11 @@
     out_ref[...] = dot(select_ref[...], stage_ref[...]).astype(out_ref.dtype)
 
 
-def call(kernel, outs, scratch, scalars=(), hbm=(), vmem=(), hbm_outs=(), pinned=False):
-    if pinned:
-        hbm = [pltpu.with_memory_space_constraint(array, pltpu.HBM) for array in hbm]
+def call(kernel, outs, scratch, scalars=(), hbm=(), vmem=(), hbm_outs=(), pinned=()):
+    hbm = [
+        pltpu.with_memory_space_constraint(array, pltpu.HBM) if number in pinned else array
+        for number, array in enumerate(hbm)
+    ]
     spaces = [pltpu.SMEM] * len(scalars) + [pltpu.HBM] * len(hbm) + [pltpu.VMEM] * len(vmem)
     return pl.pallas_call(
         kernel,
@@ -538,7 +540,7 @@
         scalars=(at,),
         hbm=(x, *[ids.transpose(1, 0, 2) for ids in (level_ids, coarse_ids)], fine, coarse, merge_weight, second_qkv, second_out),
         hbm_outs=(5, 6, 7, 8),
-        pinned=True,
+        pinned=range(8),
     )
     got = shifted(packets, -1)
     far = stops - 1
@@ -571,6 +573,7 @@
             dma(5),
         ],
         hbm=(x, select, first_qkv, first_out, pick),
+        pinned=(3, 4),
         vmem=(labels, *got_first),
     )
     (near2,) = joined(after(far2, first1, y, other))

time: 107 us -> 107 us (level)
  waiting for transfers between devices: 30.6 us -> 34.9 us
  local copies, waits for them, and re-layouts: 3.26 us -> 1.12 us
  starting transfers between devices: 46.9 us -> 45.4 us
    ppermute x6, starting transfers between devices: 7.19 us -> 4.46 us  [routed(): return lax.ppermute(block, ('lat', 'lon'), pairs)]
    unnamed x19 -> x15, local copies, waits for them, and re-layouts: 3.19 us -> 1.05 us
    ppermute x9, waiting for transfers between devices: 8.81 us -> 10.7 us  [far_parts(): lax.ppermute(part, 'lon', [(i, (i + 2 * back) % ranks) for i in range(ran...]
    ppermute x9, starting transfers between devices: 13.8 us -> 15.2 us  [far_parts(): lax.ppermute(part, 'lon', [(i, (i + 2 * back) % ranks) for i in range(ran...]
    ppermute x6, waiting for transfers between devices: 2.27 us -> 3.63 us  [routed(): return lax.ppermute(block, ('lat', 'lon'), pairs)]
  transfers between devices with their start and end apart: 34 -> 34, of which waited for: 11 -> 12; matrix products, arithmetic and copies ran while one was open for 0% -> 0% of each run, Pallas kernels for 15% -> 15%
where the time goes in v8:
time: 107 us
  starting transfers between devices  45.4 us (42%)
  waiting for transfers between devices  34.9 us (33%)
  Pallas kernels  24.9 us (23%)
  local copies, waits for them, and re-layouts  1.12 us (1%)
    pallas_call x12, Pallas kernels, call(): pl.pallas_call(kernel, out_shape=[jax.ShapeDtypeStruct(shape, jnp.bfloat1...  24.9 us
    ppermute x4, starting transfers between devices, shifted(): lax.ppermute(blocks[2], ('lat', 'lon'), [(i * lon + j, (i + step) % lat *...  18.5 us
    ppermute x9, starting transfers between devices, far_parts(): lax.ppermute(part, 'lon', [(i, (i + 2 * back) % ranks) for i in range(ran...  15.2 us
    ppermute x4, waiting for transfers between devices, shifted(): lax.ppermute(blocks[2], ('lat', 'lon'), [(i * lon + j, (i + step) % lat *...  12.3 us
    ppermute x9, waiting for transfers between devices, far_parts(): lax.ppermute(part, 'lon', [(i, (i + 2 * back) % ranks) for i in range(ran...  10.7 us
    ppermute x6, starting transfers between devices, routed(): return lax.ppermute(block, ('lat', 'lon'), pairs)  4.46 us
    ppermute x4, waiting for transfers between devices, shifted(): lax.ppermute(blocks[0], 'lat', [(i, (i + step) % lat) for i in range(lat)])  4.14 us
    ppermute x6, waiting for transfers between devices, routed(): return lax.ppermute(block, ('lat', 'lon'), pairs)  3.63 us
  transfers between devices with their start and end apart: 34, of which 12 were waited for; matrix products, arithmetic and copies ran while one was open for 0% of the time, Pallas kernels for 15%

profile of v8, /device:TPU:0, one launch (start us, length us, event | category | flops | bytes accessed | tf_op | source)
XLA Modules:
  0.0 107.3 jit_solution(12481707558747370086)
XLA Ops:
  0.7 3.1 %shard_map.293 = (bf16[112,512]{1,0:T(8,128)(2,1)S(1)}, bf16[112,512]{1,0:T(8,128)(2,1)S(1)}, bf16[48,512]{1,0:T(8,128)(2,1)S(1)}, bf16[8,576]{1,0:T(8,128)(2,1)...) custom-call(s32[4]{0:T(128)S(1)} %pad_add_fusion.refs_0_, ...), custom_call_target="tpu_custom_call" | custom-call | tf_op jit(solution)/shard_map/pallas_call | solution.py:419
  3.8 6.4 %collective-permute-start.2 = (bf16[48,512]{1,0:T(8,128)(2,1)S(1)}, bf16[48,512]{1,0:T(8,128)(2,1)S(1)}, u32[]{:S(2)}, u32[]{:S(2)}) collective-permute-start(bf16[48,512]{1,0:T(8,128)(2,1)S(1)} %get-tuple-element.56), channel_id=1, source_target_pairs={{0,31},{1,24},{2,25},{3,26},{4,27},{5,28},{6,29},{7,30},{8,7},{9,0... | collective-permute-start | bytes 147464 | tf_op jit(solution)/shard_map/ppermute | solution.py:437
  10.3 1.0 collective-permute-start.4
  11.3 2.8 %collective-permute-start.5 = (bf16[128,512]{1,0:T(8,128)(2,1)S(1)}, bf16[128,512]{1,0:T(8,128)(2,1)S(1)}, u32[]{:S(2)}, u32[]{:S(2)}) collective-permute-start(bf16[128,512]{1,0:T(8,128)(2,1)S(1)} %get-tuple-element.63), channel_id=1, source_target_pairs={{0,6},{1,7},{2,0},{3,1},{4,2},{5,3},{6,4},{7,5},{8,14},{9,15},{10,... | collective-permute-start | bytes 393224 | tf_op jit(solution)/shard_map/ppermute | solution.py:452
  14.1 0.5 collective-permute-start
  14.8 4.1 %collective-permute-done.refs_6_.refs_18_ = bf16[112,512]{1,0:T(8,128)(2,1)S(1)} collective-permute-done((bf16[112,512]{1,0:T(8,128)(2,1)S(1)}, bf16[112,512]{1,0:T(8,128)(2,1)S(1)}, u32[]{:S(2)}, u32[]{:S(2)}) %collective-permute-start) | collective-permute-done | bytes 114720 | tf_op jit(solution)/shard_map/ppermute | solution.py:435
  18.9 1.2 %collective-permute-done.1.refs_7_.refs_19_ = bf16[112,512]{1,0:T(8,128)(2,1)S(1)} collective-permute-done((bf16[112,512]{1,0:T(8,128)(2,1)S(1)}, bf16[112,512]{1,0:T(8,128)(2,1)S(1)}, u32[]{:S(2)}, u32[]{:S(2)}) %collective-permute-start.1) | collective-permute-done | bytes 114720 | tf_op jit(solution)/shard_map/ppermute | solution.py:436
  20.1 1.3 %collective-permute-done.4.refs_1_ = bf16[128,512]{1,0:T(8,128)(2,1)S(1)} collective-permute-done((bf16[128,512]{1,0:T(8,128)(2,1)S(1)}, bf16[128,512]{1,0:T(8,128)(2,1)S(1)}, u32[]{:S(2)}, u32[]{:S(2)}) %collective-permute-start.4) | collective-permute-done | bytes 131104 | tf_op jit(solution)/shard_map/ppermute | solution.py:452
  21.4 0.5 shard_map.295.refs_0_
  21.9 0.7 collective-permute-start.10
  22.6 3.4 %collective-permute-start.6 = (bf16[128,512]{1,0:T(8,128)(2,1)S(1)}, bf16[128,512]{1,0:T(8,128)(2,1)S(1)}, u32[]{:S(2)}, u32[]{:S(2)}) collective-permute-start(bf16[128,512]{1,0:T(8,128)(2,1)S(1)} %get-tuple-element.67), channel_id=1, source_target_pairs={{0,2},{1,3},{2,4},{3,5},{4,6},{5,7},{6,0},{7,1},{8,10},{9,11},{10,... | collective-permute-start | bytes 393224 | tf_op jit(solution)/shard_map/ppermute | solution.py:452
  26.0 2.2 %collective-permute-start.7 = (bf16[128,512]{1,0:T(8,128)(2,1)S(1)}, bf16[128,512]{1,0:T(8,128)(2,1)S(1)}, u32[]{:S(2)}, u32[]{:S(2)}) collective-permute-start(bf16[128,512]{1,0:T(8,128)(2,1)S(1)} %get-tuple-element.67), channel_id=1, source_target_pairs={{0,4},{1,5},{2,6},{3,7},{4,0},{5,1},{6,2},{7,3},{8,12},{9,13},{10,... | collective-permute-start | bytes 393224 | tf_op jit(solution)/shard_map/ppermute | solution.py:452
  28.4 6.9 %shard_map.294 = (bf16[576,512]{1,0:T(8,128)(2,1)S(1)}, bf16[112,512]{1,0:T(8,128)(2,1)S(1)}, bf16[112,512]{1,0:T(8,128)(2,1)S(1)}, bf16[48,512]{1,0:T(8,128)(2,...) custom-call(bf16[576,512]{1,0:T(8,128)(2,1)S(1)} %bitcast.9, ...), custom_call_target="tpu_custom_call" | custom-call | tf_op jit(solution)/shard_map/pallas_call | solution.py:419
  35.3 2.4 %collective-permute-done.7.refs_1_ = bf16[128,512]{1,0:T(8,128)(2,1)S(1)} collective-permute-done((bf16[128,512]{1,0:T(8,128)(2,1)S(1)}, bf16[128,512]{1,0:T(8,128)(2,1)S(1)}, u32[]{:S(2)}, u32[]{:S(2)}) %collective-permute-start.7) | collective-permute-done | bytes 131104 | tf_op jit(solution)/shard_map/ppermute | solution.py:452
  37.7 0.5 shard_map.296.refs_0_
  38.2 0.4 shard_map.297.refs_4_
  38.6 1.1 %collective-permute-start.15 = (bf16[6,128,512]{2,1,0:T(8,128)(2,1)S(1)}, bf16[6,128,512]{2,1,0:T(8,128)(2,1)S(1)}, u32[]{:S(2)}, u32[]{:S(2)}) collective-permute-start(bf16[6,128,512]{2,1,0:T(8,128)(2,1)S(1)} %shard_map.297.refs_4_), channel_id=1, source_target_pairs={{0,16},{1,9},{2,18},{3,11},{4,20},{5,13},{6,22},{7,15},{8,24},{9,1... | collective-permute-start | bytes 2359304 | tf_op jit(solution)/shard_map/ppermute | solution.py:462
  39.9 3.2 %collective-permute-start.11 = (bf16[128,512]{1,0:T(8,128)(2,1)S(1)}, bf16[128,512]{1,0:T(8,128)(2,1)S(1)}, u32[]{:S(2)}, u32[]{:S(2)}) collective-permute-start(bf16[128,512]{1,0:T(8,128)(2,1)S(1)} %get-tuple-element.73), channel_id=1, source_target_pairs={{0,2},{1,3},{2,4},{3,5},{4,6},{5,7},{6,0},{7,1},{8,10},{9,11},{10,... | collective-permute-start | bytes 393224 | tf_op jit(solution)/shard_map/ppermute | solution.py:452
  43.1 0.8 collective-permute-start.12
  43.9 1.6 %collective-permute-start.13 = (bf16[128,512]{1,0:T(8,128)(2,1)S(1)}, bf16[128,512]{1,0:T(8,128)(2,1)S(1)}, u32[]{:S(2)}, u32[]{:S(2)}) collective-permute-start(bf16[128,512]{1,0:T(8,128)(2,1)S(1)} %get-tuple-element.73), channel_id=1, source_target_pairs={{0,6},{1,7},{2,0},{3,1},{4,2},{5,3},{6,4},{7,5},{8,14},{9,15},{10,... | collective-permute-start | bytes 393224 | tf_op jit(solution)/shard_map/ppermute | solution.py:452
  45.5 2.4 %collective-permute-done.11.refs_0_ = bf16[128,512]{1,0:T(8,128)(2,1)S(1)} collective-permute-done((bf16[128,512]{1,0:T(8,128)(2,1)S(1)}, bf16[128,512]{1,0:T(8,128)(2,1)S(1)}, u32[]{:S(2)}, u32[]{:S(2)}) %collective-permute-start.11) | collective-permute-done | bytes 131104 | tf_op jit(solution)/shard_map/ppermute | solution.py:452
  47.9 4.7 %collective-permute-done.12.refs_1_ = bf16[128,512]{1,0:T(8,128)(2,1)S(1)} collective-permute-done((bf16[128,512]{1,0:T(8,128)(2,1)S(1)}, bf16[128,512]{1,0:T(8,128)(2,1)S(1)}, u32[]{:S(2)}, u32[]{:S(2)}) %collective-permute-start.12) | collective-permute-done | bytes 131104 | tf_op jit(solution)/shard_map/ppermute | solution.py:452
  52.5 1.6 %collective-permute-done.15.refs_5_ = bf16[6,128,512]{2,1,0:T(8,128)(2,1)S(1)} collective-permute-done((bf16[6,128,512]{2,1,0:T(8,128)(2,1)S(1)}, bf16[6,128,512]{2,1,0:T(8,128)(2,1)S(1)}, u32[]{:S(2)}, u32[]{:S(2)}) %collective-permute-start.15) | collective-permute-done | bytes 786464 | tf_op jit(solution)/shard_map/ppermute | solution.py:462
  54.2 0.5 shard_map.298.refs_0_
  54.7 0.4 shard_map.299.refs_9_
  55.1 1.0 collective-permute-start.17
  56.1 1.0 collective-permute-start.16
  57.1 1.6 %collective-permute-start.18 = (bf16[112,512]{1,0:T(8,128)(2,1)S(1)}, bf16[112,512]{1,0:T(8,128)(2,1)S(1)}, u32[]{:S(2)}, u32[]{:S(2)}) collective-permute-start(bf16[112,512]{1,0:T(8,128)(2,1)S(1)} %get-tuple-element.84), channel_id=1, source_target_pairs={{0,24},{8,0},{16,8},{24,16},{1,25},{9,1},{17,9},{25,17},{2,26},{10... | collective-permute-start | bytes 344072 | tf_op jit(solution)/shard_map/ppermute | solution.py:435
  58.7 1.6 %collective-permute-start.19 = (bf16[112,512]{1,0:T(8,128)(2,1)S(1)}, bf16[112,512]{1,0:T(8,128)(2,1)S(1)}, u32[]{:S(2)}, u32[]{:S(2)}) collective-permute-start(bf16[112,512]{1,0:T(8,128)(2,1)S(1)} %get-tuple-element.85), channel_id=1, source_target_pairs={{0,7},{1,0},{2,1},{3,2},{4,3},{5,4},{6,5},{7,6},{8,15},{9,8},{10,9... | collective-permute-start | bytes 344072 | tf_op jit(solution)/shard_map/ppermute | solution.py:436
  60.3 2.9 %collective-permute-start.20 = (bf16[48,512]{1,0:T(8,128)(2,1)S(1)}, bf16[48,512]{1,0:T(8,128)(2,1)S(1)}, u32[]{:S(2)}, u32[]{:S(2)}) collective-permute-start(bf16[48,512]{1,0:T(8,128)(2,1)S(1)} %get-tuple-element.86), channel_id=1, source_target_pairs={{0,31},{1,24},{2,25},{3,26},{4,27},{5,28},{6,29},{7,30},{8,7},{9,0... | collective-permute-start | bytes 147464 | tf_op jit(solution)/shard_map/ppermute | solution.py:437
  63.2 10.6 %collective-permute-done.20.refs_16_ = bf16[48,512]{1,0:T(8,128)(2,1)S(1)} collective-permute-done((bf16[48,512]{1,0:T(8,128)(2,1)S(1)}, bf16[48,512]{1,0:T(8,128)(2,1)S(1)}, u32[]{:S(2)}, u32[]{:S(2)}) %collective-permute-start.20) | collective-permute-done | bytes 49184 | tf_op jit(solution)/shard_map/ppermute | solution.py:437
  73.8 0.5 collective-permute-start.27
  74.4 0.5 collective-permute-start.29
  74.9 0.4 shard_map.301.refs_3_
  75.2 1.2 %collective-permute-start.24 = (bf16[6,128,512]{2,1,0:T(8,128)(2,1)S(1)}, bf16[6,128,512]{2,1,0:T(8,128)(2,1)S(1)}, u32[]{:S(2)}, u32[]{:S(2)}) collective-permute-start(bf16[6,128,512]{2,1,0:T(8,128)(2,1)S(1)} %shard_map.301.refs_3_), channel_id=1, source_target_pairs={{0,16},{1,9},{2,18},{3,11},{4,20},{5,13},{6,22},{7,15},{8,24},{9,1... | collective-permute-start | bytes 2359304 | tf_op jit(solution)/shard_map/ppermute | solution.py:462
  76.5 1.2 %collective-permute-start.21 = (bf16[112,512]{1,0:T(8,128)(2,1)S(1)}, bf16[112,512]{1,0:T(8,128)(2,1)S(1)}, u32[]{:S(2)}, u32[]{:S(2)}) collective-permute-start(bf16[112,512]{1,0:T(8,128)(2,1)S(1)} %get-tuple-element.88), channel_id=1, source_target_pairs={{0,8},{8,16},{16,24},{24,0},{1,9},{9,17},{17,25},{25,1},{2,10},{10... | collective-permute-start | bytes 344072 | tf_op jit(solution)/shard_map/ppermute | solution.py:435
  77.7 0.6 collective-permute-done.28.refs_11_
  78.3 3.6 %collective-permute-start.23 = (bf16[48,512]{1,0:T(8,128)(2,1)S(1)}, bf16[48,512]{1,0:T(8,128)(2,1)S(1)}, u32[]{:S(2)}, u32[]{:S(2)}) collective-permute-start(bf16[48,512]{1,0:T(8,128)(2,1)S(1)} %get-tuple-element.90), channel_id=1, source_target_pairs={{0,9},{1,10},{2,11},{3,12},{4,13},{5,14},{6,15},{7,8},{8,17},{9,18... | collective-permute-start | bytes 147464 | tf_op jit(solution)/shard_map/ppermute | solution.py:437
  81.9 0.3 collective-permute-start.25
  82.2 6.6 %shard_map.302 = (bf16[144,1024]{1,0:T(8,128)(2,1)S(1)}, bf16[2304,144]{1,0:T(8,128)(2,1)S(1)}) custom-call(s32[4]{0:T(128)S(1)} %pad_add_fusion.refs_0_, bf16[576,1024]{1,0:T(8,128)(2,1)S(1)} %copy-done.3, bf16[144,640]{1,0:T(8,128)(2,1)S(1)} %copy-done.5, bf16[12,128,512]{2,1,0:T(8,128)(2,1)S(1)} %get-tuple-element.69.refs_3_.refs_2_, ...), custom_call_target="tpu_custom_call" | custom-call | tf_op jit(solution)/shard_map/pallas_call | solution.py:419
  88.8 2.0 %collective-permute-done.24.refs_4_ = bf16[6,128,512]{2,1,0:T(8,128)(2,1)S(1)} collective-permute-done((bf16[6,128,512]{2,1,0:T(8,128)(2,1)S(1)}, bf16[6,128,512]{2,1,0:T(8,128)(2,1)S(1)}, u32[]{:S(2)}, u32[]{:S(2)}) %collective-permute-start.24) | collective-permute-done | bytes 786464 | tf_op jit(solution)/shard_map/ppermute | solution.py:462
  90.8 2.3 %collective-permute-done.30.refs_7_ = bf16[6,128,512]{2,1,0:T(8,128)(2,1)S(1)} collective-permute-done((bf16[6,128,512]{2,1,0:T(8,128)(2,1)S(1)}, bf16[6,128,512]{2,1,0:T(8,128)(2,1)S(1)}, u32[]{:S(2)}, u32[]{:S(2)}) %collective-permute-start.30) | collective-permute-done | bytes 786464 | tf_op jit(solution)/shard_map/ppermute | solution.py:446
  93.1 3.1 %shard_map.303 = (bf16[144,1024]{1,0:T(8,128)(2,1)S(1)}, bf16[48,1024]{1,0:T(8,128)(2,1)S(1)}, bf16[48,1024]{1,0:T(8,128)(2,1)S(1)}, bf16[48,1024]{1,0:T(8,128)(2,1)S(1)}) custom-call(s32[4]{0:T(128)S(1)} %pad_add_fusion.refs_0_, bf16[144,144]{1,0:T(8,128)(2,1)S(1)} %copy-done.6, bf16[12,128,512]{2,1,0:T(8,128)(2,1)S(1)} %get-tuple-element.69.refs_3_.refs_2_, ...), custom_call_target="tpu_custom_call" | custom-call | tf_op jit(solution)/shard_map/pallas_call | solution.py:419
  96.5 5.5 %collective-permute-start.33 = (bf16[48,1024]{1,0:T(8,128)(2,1)S(1)}, bf16[48,1024]{1,0:T(8,128)(2,1)S(1)}, u32[]{:S(2)}, u32[]{:S(2)}) collective-permute-start(bf16[48,1024]{1,0:T(8,128)(2,1)S(1)} %get-tuple-element.103), channel_id=1, source_target_pairs={{0,9},{1,10},{2,11},{3,12},{4,13},{5,14},{6,15},{7,8},{8,17},{9,18... | collective-permute-start | bytes 294920 | tf_op jit(solution)/shard_map/ppermute | solution.py:437
  102.0 1.9 %shard_map.300 = bf16[576,512]{1,0:T(8,128)(2,1)} custom-call(bf16[576,1024]{1,0:T(8,128)(2,1)S(1)} %copy-done.2, bf16[576,512]{1,0:T(8,128)(2,1)S(1)} %get-tuple-element.57.own_ref.refs_13_, bf16[112,512]{1,0:T(8,128)(2,1)S(1)} %collective-permute-done.21.lat_ref, bf16[112,512]{1,0:T(8,128)(2,1)S(1)} %collective-permute-done.22.lon_ref, ...), custom_call_target="tpu_custom_call" | custom-call | tf_op jit(solution)/shard_map/pallas_call | solution.py:419
  103.9 1.7 %collective-permute-done.33.both_ref = bf16[48,1024]{1,0:T(8,128)(2,1)S(1)} collective-permute-done((bf16[48,1024]{1,0:T(8,128)(2,1)S(1)}, bf16[48,1024]{1,0:T(8,128)(2,1)S(1)}, u32[]{:S(2)}, u32[]{:S(2)}) %collective-permute-start.33) | collective-permute-done | bytes 98336 | tf_op jit(solution)/shard_map/ppermute | solution.py:437
  105.6 0.6 shard_map.304
  106.3 1.0 copy.33
  (49 shorter events, 0.9 us)
Async XLA Ops:
  0.7 27.7 %copy-start = (bf16[2,12,24,512]{3,2,1,0:T(8,128)(2,1)S(1)}, bf16[2,12,24,512]{3,2,1,0:T(8,128)(2,1)}, u32[]{:S(2)}) copy-start(bf16[2,12,24,512]{3,2,1,0:T(8,128)(2,1)} %param.30) | copy-start | bytes 1769476
  0.7 27.7 %copy-start.1 = (bf16[512,1536]{1,0:T(8,128)(2,1)S(1)}, bf16[512,1536]{1,0:T(8,128)(2,1)}, u32[]{:S(2)}) copy-start(bf16[512,1536]{1,0:T(8,128)(2,1)} %refs_2_.2) | copy-start | bytes 4718596
  0.7 27.7 %copy-start.4 = (bf16[576,1024]{1,0:T(8,128)(2,1)S(1)}, bf16[576,1024]{1,0:T(8,128)(2,1)}, u32[]{:S(2)}) copy-start(bf16[576,1024]{1,0:T(8,128)(2,1)} %constant.93.clone.refs_1_) | copy-start | bytes 3538948
  3.8 10.8 %collective-permute-start.2 = (bf16[48,512]{1,0:T(8,128)(2,1)S(1)}, bf16[48,512]{1,0:T(8,128)(2,1)S(1)}, u32[]{:S(2)}, u32[]{:S(2)}) collective-permute-start(bf16[48,512]{1,0:T(8,128)(2,1)S(1)} %get-tuple-element.56), channel_id=1, source_target_pairs={{0,31},{1,24},{2,25},{3,26},{4,27},{5,28},{6,29},{7,30},{8,7},{9,0... | collective-permute-start | bytes 147464 | tf_op jit(solution)/shard_map/ppermute | solution.py:437
  10.3 9.9 %collective-permute-start.3 = (bf16[128,512]{1,0:T(8,128)(2,1)S(1)}, bf16[128,512]{1,0:T(8,128)(2,1)S(1)}, u32[]{:S(2)}, u32[]{:S(2)}) collective-permute-start(bf16[128,512]{1,0:T(8,128)(2,1)S(1)} %get-tuple-element.63), channel_id=1, source_target_pairs={{0,2},{1,3},{2,4},{3,5},{4,6},{5,7},{6,0},{7,1},{8,10},{9,11},{10,... | collective-permute-start | bytes 393224 | tf_op jit(solution)/shard_map/ppermute | solution.py:452
  10.3 11.1 %collective-permute-start.4 = (bf16[128,512]{1,0:T(8,128)(2,1)S(1)}, bf16[128,512]{1,0:T(8,128)(2,1)S(1)}, u32[]{:S(2)}, u32[]{:S(2)}) collective-permute-start(bf16[128,512]{1,0:T(8,128)(2,1)S(1)} %get-tuple-element.63), channel_id=1, source_target_pairs={{0,4},{1,5},{2,6},{3,7},{4,0},{5,1},{6,2},{7,3},{8,12},{9,13},{10,... | collective-permute-start | bytes 393224 | tf_op jit(solution)/shard_map/ppermute | solution.py:452
  11.3 10.1 %collective-permute-start.5 = (bf16[128,512]{1,0:T(8,128)(2,1)S(1)}, bf16[128,512]{1,0:T(8,128)(2,1)S(1)}, u32[]{:S(2)}, u32[]{:S(2)}) collective-permute-start(bf16[128,512]{1,0:T(8,128)(2,1)S(1)} %get-tuple-element.63), channel_id=1, source_target_pairs={{0,6},{1,7},{2,0},{3,1},{4,2},{5,3},{6,4},{7,5},{8,14},{9,15},{10,... | collective-permute-start | bytes 393224 | tf_op jit(solution)/shard_map/ppermute | solution.py:452
  14.1 4.8 %collective-permute-start = (bf16[112,512]{1,0:T(8,128)(2,1)S(1)}, bf16[112,512]{1,0:T(8,128)(2,1)S(1)}, u32[]{:S(2)}, u32[]{:S(2)}) collective-permute-start(bf16[112,512]{1,0:T(8,128)(2,1)S(1)} %get-tuple-element.54), channel_id=1, source_target_pairs={{0,24},{8,0},{16,8},{24,16},{1,25},{9,1},{17,9},{25,17},{2,26},{10... | collective-permute-start | bytes 344072 | tf_op jit(solution)/shard_map/ppermute | solution.py:435
  14.6 5.5 %collective-permute-start.1 = (bf16[112,512]{1,0:T(8,128)(2,1)S(1)}, bf16[112,512]{1,0:T(8,128)(2,1)S(1)}, u32[]{:S(2)}, u32[]{:S(2)}) collective-permute-start(bf16[112,512]{1,0:T(8,128)(2,1)S(1)} %get-tuple-element.55), channel_id=1, source_target_pairs={{0,7},{1,0},{2,1},{3,2},{4,3},{5,4},{6,5},{7,6},{8,15},{9,8},{10,9... | collective-permute-start | bytes 344072 | tf_op jit(solution)/shard_map/ppermute | solution.py:436
  21.9 15.7 %collective-permute-start.10 = (bf16[12,128,512]{2,1,0:T(8,128)(2,1)S(1)}, bf16[12,128,512]{2,1,0:T(8,128)(2,1)S(1)}, u32[]{:S(2)}, u32[]{:S(2)}) collective-permute-start(bf16[12,128,512]{2,1,0:T(8,128)(2,1)S(1)} %get-tuple-element.69.refs_3_.refs_2_), channel_id=1, source_target_pairs={{0,1},{1,0},{2,3},{3,2},{4,5},{5,4},{6,7},{7,6},{8,9},{9,8},{10,11... | collective-permute-start | bytes 4718600 | tf_op jit(solution)/shard_map/ppermute | solution.py:446
  22.6 15.1 %collective-permute-start.9 = (bf16[3,128,512]{2,1,0:T(8,128)(2,1)S(1)}, bf16[3,128,512]{2,1,0:T(8,128)(2,1)S(1)}, u32[]{:S(2)}, u32[]{:S(2)}) collective-permute-start(bf16[3,128,512]{2,1,0:T(8,128)(2,1)S(1)} %shard_map.295.refs_0_), channel_id=1, source_target_pairs={{0,8},{1,17},{2,10},{3,19},{4,12},{5,21},{6,14},{7,23},{8,0},{9,25... | collective-permute-start | bytes 1179656 | tf_op jit(solution)/shard_map/ppermute | solution.py:462
  22.6 12.7 %collective-permute-start.6 = (bf16[128,512]{1,0:T(8,128)(2,1)S(1)}, bf16[128,512]{1,0:T(8,128)(2,1)S(1)}, u32[]{:S(2)}, u32[]{:S(2)}) collective-permute-start(bf16[128,512]{1,0:T(8,128)(2,1)S(1)} %get-tuple-element.67), channel_id=1, source_target_pairs={{0,2},{1,3},{2,4},{3,5},{4,6},{5,7},{6,0},{7,1},{8,10},{9,11},{10,... | collective-permute-start | bytes 393224 | tf_op jit(solution)/shard_map/ppermute | solution.py:452
  26.0 11.6 %collective-permute-start.7 = (bf16[128,512]{1,0:T(8,128)(2,1)S(1)}, bf16[128,512]{1,0:T(8,128)(2,1)S(1)}, u32[]{:S(2)}, u32[]{:S(2)}) collective-permute-start(bf16[128,512]{1,0:T(8,128)(2,1)S(1)} %get-tuple-element.67), channel_id=1, source_target_pairs={{0,4},{1,5},{2,6},{3,7},{4,0},{5,1},{6,2},{7,3},{8,12},{9,13},{10,... | collective-permute-start | bytes 393224 | tf_op jit(solution)/shard_map/ppermute | solution.py:452
  28.3 9.4 %collective-permute-start.8 = (bf16[128,512]{1,0:T(8,128)(2,1)S(1)}, bf16[128,512]{1,0:T(8,128)(2,1)S(1)}, u32[]{:S(2)}, u32[]{:S(2)}) collective-permute-start(bf16[128,512]{1,0:T(8,128)(2,1)S(1)} %get-tuple-element.67), channel_id=1, source_target_pairs={{0,6},{1,7},{2,0},{3,1},{4,2},{5,3},{6,4},{7,5},{8,14},{9,15},{10,... | collective-permute-start | bytes 393224 | tf_op jit(solution)/shard_map/ppermute | solution.py:452
  38.6 15.5 %collective-permute-start.15 = (bf16[6,128,512]{2,1,0:T(8,128)(2,1)S(1)}, bf16[6,128,512]{2,1,0:T(8,128)(2,1)S(1)}, u32[]{:S(2)}, u32[]{:S(2)}) collective-permute-start(bf16[6,128,512]{2,1,0:T(8,128)(2,1)S(1)} %shard_map.297.refs_4_), channel_id=1, source_target_pairs={{0,16},{1,9},{2,18},{3,11},{4,20},{5,13},{6,22},{7,15},{8,24},{9,1... | collective-permute-start | bytes 2359304 | tf_op jit(solution)/shard_map/ppermute | solution.py:462
  39.8 12.7 %collective-permute-start.14 = (bf16[3,128,512]{2,1,0:T(8,128)(2,1)S(1)}, bf16[3,128,512]{2,1,0:T(8,128)(2,1)S(1)}, u32[]{:S(2)}, u32[]{:S(2)}) collective-permute-start(bf16[3,128,512]{2,1,0:T(8,128)(2,1)S(1)} %shard_map.296.refs_0_), channel_id=1, source_target_pairs={{0,8},{1,17},{2,10},{3,19},{4,12},{5,21},{6,14},{7,23},{8,0},{9,25... | collective-permute-start | bytes 1179656 | tf_op jit(solution)/shard_map/ppermute | solution.py:462
  39.9 8.0 %collective-permute-start.11 = (bf16[128,512]{1,0:T(8,128)(2,1)S(1)}, bf16[128,512]{1,0:T(8,128)(2,1)S(1)}, u32[]{:S(2)}, u32[]{:S(2)}) collective-permute-start(bf16[128,512]{1,0:T(8,128)(2,1)S(1)} %get-tuple-element.73), channel_id=1, source_target_pairs={{0,2},{1,3},{2,4},{3,5},{4,6},{5,7},{6,0},{7,1},{8,10},{9,11},{10,... | collective-permute-start | bytes 393224 | tf_op jit(solution)/shard_map/ppermute | solution.py:452
  43.1 9.4 %collective-permute-start.12 = (bf16[128,512]{1,0:T(8,128)(2,1)S(1)}, bf16[128,512]{1,0:T(8,128)(2,1)S(1)}, u32[]{:S(2)}, u32[]{:S(2)}) collective-permute-start(bf16[128,512]{1,0:T(8,128)(2,1)S(1)} %get-tuple-element.73), channel_id=1, source_target_pairs={{0,4},{1,5},{2,6},{3,7},{4,0},{5,1},{6,2},{7,3},{8,12},{9,13},{10,... | collective-permute-start | bytes 393224 | tf_op jit(solution)/shard_map/ppermute | solution.py:452
  43.9 8.6 %collective-permute-start.13 = (bf16[128,512]{1,0:T(8,128)(2,1)S(1)}, bf16[128,512]{1,0:T(8,128)(2,1)S(1)}, u32[]{:S(2)}, u32[]{:S(2)}) collective-permute-start(bf16[128,512]{1,0:T(8,128)(2,1)S(1)} %get-tuple-element.73), channel_id=1, source_target_pairs={{0,6},{1,7},{2,0},{3,1},{4,2},{5,3},{6,4},{7,5},{8,14},{9,15},{10,... | collective-permute-start | bytes 393224 | tf_op jit(solution)/shard_map/ppermute | solution.py:452
  55.1 27.1 %copy-start.3 = (bf16[576,1024]{1,0:T(8,128)(2,1)S(1)}, bf16[576,1024]{1,0:T(8,128)(2,1)}, u32[]{:S(2)}) copy-start(bf16[576,1024]{1,0:T(8,128)(2,1)} %constant.100.clone.refs_1_) | copy-start | bytes 3538948
  55.1 27.1 %copy-start.5 = (bf16[144,640]{1,0:T(8,128)(2,1)S(1)}, bf16[144,640]{1,0:T(8,128)(2,1)}, u32[]{:S(2)}) copy-start(bf16[144,640]{1,0:T(8,128)(2,1)} %constant.101.clone.refs_2_.select_hbm) | copy-start | bytes 552964
  55.1 19.1 %collective-permute-start.17 = (bf16[6,128,512]{2,1,0:T(8,128)(2,1)S(1)}, bf16[6,128,512]{2,1,0:T(8,128)(2,1)S(1)}, u32[]{:S(2)}, u32[]{:S(2)}) collective-permute-start(bf16[6,128,512]{2,1,0:T(8,128)(2,1)S(1)} %shard_map.299.refs_9_), channel_id=1, source_target_pairs={{0,16},{1,9},{2,18},{3,11},{4,20},{5,13},{6,22},{7,15},{8,24},{9,1... | collective-permute-start | bytes 2359304 | tf_op jit(solution)/shard_map/ppermute | solution.py:462
  56.1 18.1 %collective-permute-start.16 = (bf16[3,128,512]{2,1,0:T(8,128)(2,1)S(1)}, bf16[3,128,512]{2,1,0:T(8,128)(2,1)S(1)}, u32[]{:S(2)}, u32[]{:S(2)}) collective-permute-start(bf16[3,128,512]{2,1,0:T(8,128)(2,1)S(1)} %shard_map.298.refs_0_), channel_id=1, source_target_pairs={{0,8},{1,17},{2,10},{3,19},{4,12},{5,21},{6,14},{7,23},{8,0},{9,25... | collective-permute-start | bytes 1179656 | tf_op jit(solution)/shard_map/ppermute | solution.py:462
  57.1 16.6 %collective-permute-start.18 = (bf16[112,512]{1,0:T(8,128)(2,1)S(1)}, bf16[112,512]{1,0:T(8,128)(2,1)S(1)}, u32[]{:S(2)}, u32[]{:S(2)}) collective-permute-start(bf16[112,512]{1,0:T(8,128)(2,1)S(1)} %get-tuple-element.84), channel_id=1, source_target_pairs={{0,24},{8,0},{16,8},{24,16},{1,25},{9,1},{17,9},{25,17},{2,26},{10... | collective-permute-start | bytes 344072 | tf_op jit(solution)/shard_map/ppermute | solution.py:435
  58.7 15.6 %collective-permute-start.19 = (bf16[112,512]{1,0:T(8,128)(2,1)S(1)}, bf16[112,512]{1,0:T(8,128)(2,1)S(1)}, u32[]{:S(2)}, u32[]{:S(2)}) collective-permute-start(bf16[112,512]{1,0:T(8,128)(2,1)S(1)} %get-tuple-element.85), channel_id=1, source_target_pairs={{0,7},{1,0},{2,1},{3,2},{4,3},{5,4},{6,5},{7,6},{8,15},{9,8},{10,9... | collective-permute-start | bytes 344072 | tf_op jit(solution)/shard_map/ppermute | solution.py:436
  60.3 13.5 %collective-permute-start.20 = (bf16[48,512]{1,0:T(8,128)(2,1)S(1)}, bf16[48,512]{1,0:T(8,128)(2,1)S(1)}, u32[]{:S(2)}, u32[]{:S(2)}) collective-permute-start(bf16[48,512]{1,0:T(8,128)(2,1)S(1)} %get-tuple-element.86), channel_id=1, source_target_pairs={{0,31},{1,24},{2,25},{3,26},{4,27},{5,28},{6,29},{7,30},{8,7},{9,0... | collective-permute-start | bytes 147464 | tf_op jit(solution)/shard_map/ppermute | solution.py:437
  73.7 2.7 %collective-permute-start.26 = (bf16[6,128,512]{2,1,0:T(8,128)(2,1)S(1)}, bf16[6,128,512]{2,1,0:T(8,128)(2,1)S(1)}, u32[]{:S(2)}, u32[]{:S(2)}) collective-permute-start(bf16[6,128,512]{2,1,0:T(8,128)(2,1)S(1)} %shard_map.297.refs_4_), channel_id=1, source_target_pairs={{0,1},{1,0},{2,3},{3,2},{4,5},{5,4},{6,7},{7,6},{8,9},{9,8},{10,11... | collective-permute-start | bytes 2359304 | tf_op jit(solution)/shard_map/ppermute | solution.py:446
  73.8 3.9 %collective-permute-start.27 = (bf16[6,128,512]{2,1,0:T(8,128)(2,1)S(1)}, bf16[6,128,512]{2,1,0:T(8,128)(2,1)S(1)}, u32[]{:S(2)}, u32[]{:S(2)}) collective-permute-start(bf16[6,128,512]{2,1,0:T(8,128)(2,1)S(1)} %collective-permute-done.15.refs_5_), channel_id=1, source_target_pairs={{0,1},{1,0},{2,3},{3,2},{4,5},{5,4},{6,7},{7,6},{8,9},{9,8},{10,11... | collective-permute-start | bytes 2359304 | tf_op jit(solution)/shard_map/ppermute | solution.py:446
  74.3 4.0 %collective-permute-start.28 = (bf16[6,128,512]{2,1,0:T(8,128)(2,1)S(1)}, bf16[6,128,512]{2,1,0:T(8,128)(2,1)S(1)}, u32[]{:S(2)}, u32[]{:S(2)}) collective-permute-start(bf16[6,128,512]{2,1,0:T(8,128)(2,1)S(1)} %shard_map.299.refs_9_), channel_id=1, source_target_pairs={{0,1},{1,0},{2,3},{3,2},{4,5},{5,4},{6,7},{7,6},{8,9},{9,8},{10,11... | collective-permute-start | bytes 2359304 | tf_op jit(solution)/shard_map/ppermute | solution.py:446
  74.4 7.5 %collective-permute-start.29 = (bf16[6,128,512]{2,1,0:T(8,128)(2,1)S(1)}, bf16[6,128,512]{2,1,0:T(8,128)(2,1)S(1)}, u32[]{:S(2)}, u32[]{:S(2)}) collective-permute-start(bf16[6,128,512]{2,1,0:T(8,128)(2,1)S(1)} %collective-permute-done.17.refs_10_), channel_id=1, source_target_pairs={{0,1},{1,0},{2,3},{3,2},{4,5},{5,4},{6,7},{7,6},{8,9},{9,8},{10,11... | collective-permute-start | bytes 2359304 | tf_op jit(solution)/shard_map/ppermute | solution.py:446
  75.2 15.6 %collective-permute-start.24 = (bf16[6,128,512]{2,1,0:T(8,128)(2,1)S(1)}, bf16[6,128,512]{2,1,0:T(8,128)(2,1)S(1)}, u32[]{:S(2)}, u32[]{:S(2)}) collective-permute-start(bf16[6,128,512]{2,1,0:T(8,128)(2,1)S(1)} %shard_map.301.refs_3_), channel_id=1, source_target_pairs={{0,16},{1,9},{2,18},{3,11},{4,20},{5,13},{6,22},{7,15},{8,24},{9,1... | collective-permute-start | bytes 2359304 | tf_op jit(solution)/shard_map/ppermute | solution.py:462
  76.5 12.3 %collective-permute-start.21 = (bf16[112,512]{1,0:T(8,128)(2,1)S(1)}, bf16[112,512]{1,0:T(8,128)(2,1)S(1)}, u32[]{:S(2)}, u32[]{:S(2)}) collective-permute-start(bf16[112,512]{1,0:T(8,128)(2,1)S(1)} %get-tuple-element.88), channel_id=1, source_target_pairs={{0,8},{8,16},{16,24},{24,0},{1,9},{9,17},{17,25},{25,1},{2,10},{10... | collective-permute-start | bytes 344072 | tf_op jit(solution)/shard_map/ppermute | solution.py:435
  77.6 11.2 %collective-permute-start.22 = (bf16[112,512]{1,0:T(8,128)(2,1)S(1)}, bf16[112,512]{1,0:T(8,128)(2,1)S(1)}, u32[]{:S(2)}, u32[]{:S(2)}) collective-permute-start(bf16[112,512]{1,0:T(8,128)(2,1)S(1)} %get-tuple-element.89), channel_id=1, source_target_pairs={{0,1},{1,2},{2,3},{3,4},{4,5},{5,6},{6,7},{7,0},{8,9},{9,10},{10,1... | collective-permute-start | bytes 344072 | tf_op jit(solution)/shard_map/ppermute | solution.py:436
  78.3 10.5 %collective-permute-start.23 = (bf16[48,512]{1,0:T(8,128)(2,1)S(1)}, bf16[48,512]{1,0:T(8,128)(2,1)S(1)}, u32[]{:S(2)}, u32[]{:S(2)}) collective-permute-start(bf16[48,512]{1,0:T(8,128)(2,1)S(1)} %get-tuple-element.90), channel_id=1, source_target_pairs={{0,9},{1,10},{2,11},{3,12},{4,13},{5,14},{6,15},{7,8},{8,17},{9,18... | collective-permute-start | bytes 147464 | tf_op jit(solution)/shard_map/ppermute | solution.py:437
  81.9 8.9 %collective-permute-start.25 = (bf16[6,128,512]{2,1,0:T(8,128)(2,1)S(1)}, bf16[6,128,512]{2,1,0:T(8,128)(2,1)S(1)}, u32[]{:S(2)}, u32[]{:S(2)}) collective-permute-start(bf16[6,128,512]{2,1,0:T(8,128)(2,1)S(1)} %shard_map.301.refs_3_), channel_id=1, source_target_pairs={{0,1},{1,0},{2,3},{3,2},{4,5},{5,4},{6,7},{7,6},{8,9},{9,8},{10,11... | collective-permute-start | bytes 2359304 | tf_op jit(solution)/shard_map/ppermute | solution.py:446
  82.2 10.9 %copy-start.6 = (bf16[144,144]{1,0:T(8,128)(2,1)S(1)}, bf16[144,144]{1,0:T(8,128)(2,1)}, u32[]{:S(2)}) copy-start(bf16[144,144]{1,0:T(8,128)(2,1)} %constant.112.refs_1_) | copy-start | bytes 124420
  90.8 2.3 %collective-permute-start.30 = (bf16[6,128,512]{2,1,0:T(8,128)(2,1)S(1)}, bf16[6,128,512]{2,1,0:T(8,128)(2,1)S(1)}, u32[]{:S(2)}, u32[]{:S(2)}) collective-permute-start(bf16[6,128,512]{2,1,0:T(8,128)(2,1)S(1)} %collective-permute-done.24.refs_4_), channel_id=1, source_target_pairs={{0,1},{1,0},{2,3},{3,2},{4,5},{5,4},{6,7},{7,6},{8,9},{9,8},{10,11... | collective-permute-start | bytes 2359304 | tf_op jit(solution)/shard_map/ppermute | solution.py:446
  93.1 8.9 %copy-start.2 = (bf16[576,1024]{1,0:T(8,128)(2,1)S(1)}, bf16[576,1024]{1,0:T(8,128)(2,1)}, u32[]{:S(2)}) copy-start(bf16[576,1024]{1,0:T(8,128)(2,1)} %constant.102.clone.select_hbm) | copy-start | bytes 3538948
  96.2 7.7 %collective-permute-start.31 = (bf16[48,1024]{1,0:T(8,128)(2,1)S(1)}, bf16[48,1024]{1,0:T(8,128)(2,1)S(1)}, u32[]{:S(2)}, u32[]{:S(2)}) collective-permute-start(bf16[48,1024]{1,0:T(8,128)(2,1)S(1)} %get-tuple-element.101), channel_id=1, source_target_pairs={{0,8},{8,16},{16,24},{24,0},{1,9},{9,17},{17,25},{25,1},{2,10},{10... | collective-permute-start | bytes 294920 | tf_op jit(solution)/shard_map/ppermute | solution.py:435
  96.3 7.6 %collective-permute-start.32 = (bf16[48,1024]{1,0:T(8,128)(2,1)S(1)}, bf16[48,1024]{1,0:T(8,128)(2,1)S(1)}, u32[]{:S(2)}, u32[]{:S(2)}) collective-permute-start(bf16[48,1024]{1,0:T(8,128)(2,1)S(1)} %get-tuple-element.102), channel_id=1, source_target_pairs={{0,1},{1,2},{2,3},{3,4},{4,5},{5,6},{6,7},{7,0},{8,9},{9,10},{10,1... | collective-permute-start | bytes 294920 | tf_op jit(solution)/shard_map/ppermute | solution.py:436
  96.5 9.2 %collective-permute-start.33 = (bf16[48,1024]{1,0:T(8,128)(2,1)S(1)}, bf16[48,1024]{1,0:T(8,128)(2,1)S(1)}, u32[]{:S(2)}, u32[]{:S(2)}) collective-permute-start(bf16[48,1024]{1,0:T(8,128)(2,1)S(1)} %get-tuple-element.103), channel_id=1, source_target_pairs={{0,9},{1,10},{2,11},{3,12},{4,13},{5,14},{6,15},{7,8},{8,17},{9,18... | collective-permute-start | bytes 294920 | tf_op jit(solution)/shard_map/ppermute | solution.py:437
